TPU v7x, 32 devices: a whole 2x2x4 slice. The times are simulated.
32 devices in a mesh: expert: 8 (over z, y), shard: 4 (over x, core).
Axes of the slice: x: 2, y: 2, z: 4, core: 2. Of those that a mesh axis runs over, the one named last changes fastest.
Arguments:
- tokens: bfloat16 [4096, 768], P(('expert', 'shard')), may hold values from -6 to 6
- lengths: int32 [8, 3], P('expert'), may hold values from 1 to 448, 512 in all within a row
- routes: int32 [4096, 1], P(('expert', 'shard')), may hold values from 0 to 7; in each aligned block of 128 rows (0 to 127, 128 to 255, ...) at most 19 rows name the same one
- attention_in: bfloat16 [768, 2304], P('shard'), may hold values from -0.109375 to 0.109375
- attention_out: bfloat16 [768, 768], P('shard'), may hold values from -1.75 to 1.75
- position_bias: bfloat16 [12, 32], P('shard'), may hold values from -4 to 4
- first_gain: bfloat16 [768], P('shard'), may hold values from 0.5 to 1.5
- second_gain: bfloat16 [768], P('shard'), may hold values from 0.5 to 1.5
- router: float32 [768, 8], replicated, may hold values from -0.109375 to 0.109375
- expert_in: bfloat16 [8, 768, 3072], P('expert', None, 'shard'), may hold values from -0.21875 to 0.21875
- expert_out: bfloat16 [8, 3072, 768], P('expert', 'shard'), may hold values from -1.296875 to 1.296875
- cotangent: bfloat16 [4096, 768], P(('expert', 'shard')), may hold values from -6 to 6
Outputs:
- layer_out: bfloat16 [4096, 768], P(('expert', 'shard'))
- grad_tokens: bfloat16 [4096, 768], P(('expert', 'shard'))
- grad_attention_in: float32 [768, 2304], P('shard')
- grad_attention_out: float32 [768, 768], P('shard')
- grad_position_bias: float32 [12, 32], P('shard')
- grad_first_gain: float32 [768], P('shard')
- grad_second_gain: float32 [768], P('shard')
- grad_router: float32 [768, 8], P('shard')
- grad_expert_in: float32 [8, 768, 3072], P('expert', None, 'shard')
- grad_expert_out: float32 [8, 3072, 768], P('expert', 'shard')
Inputs may be any that keep to these rules, and one draw needn't show every extreme that they name: Each row holds the lengths of the 3 sequences that fill one group, and its largest is exactly 448. `routes`: among the tokens of one device no expert is named more than 19 times; in some device some expert is named exactly 19 times.
All inputs are finite; a program needn't handle non-finite values.
Results may differ from a plain program's by a relative error of at most 0.019.
Values may be sent and summed in bfloat16 or wider, within the bound.
No kernel may reach another device: no remote copies, remote signals or barrier semaphores. Data moves between devices by JAX's collectives and lax.ppermute only.
A program may use at most 128 MiB of HBM per device.

v0:
```python
import jax
import jax.numpy as jnp
from jax import lax
from jax.sharding import PartitionSpec as P

norm_eps = 1e-06
gelu_scale = 0.7978845608028654
gelu_cubic = 0.044715
big_negative = -1e30
far_steps = (12, 16, 23, 32, 46, 64, 91)


def bucket_index(offset):
    distance = jnp.abs(offset)
    far_level = jnp.full_like(distance, 8)
    for step_edge in far_steps:
        far_level = far_level + (distance >= step_edge).astype(jnp.int32)
    near = jnp.where(distance < 8, distance, far_level)
    return near + 16 * (offset > 0).astype(jnp.int32)


def gelu_tanh(value):
    inner = gelu_scale * (value + gelu_cubic * value * value * value)
    return 0.5 * value * (1.0 + jnp.tanh(inner))


def gelu_slope(value):
    inner = gelu_scale * (value + gelu_cubic * value * value * value)
    tanh_value = jnp.tanh(inner)
    return 0.5 * (1.0 + tanh_value) + 0.5 * value * (1.0 - tanh_value * tanh_value) * gelu_scale * (
        1.0 + 3.0 * gelu_cubic * value * value
    )


def rms_forward(value, gain):
    factor = lax.rsqrt(jnp.mean(value * value, axis=-1, keepdims=True) + norm_eps)
    return (value * factor * gain.astype(jnp.float32), factor)


def rms_backward(value, factor, gain, upstream):
    scaled = upstream * gain.astype(jnp.float32)
    grad_value = factor * scaled - value * factor * factor * factor * jnp.mean(
        scaled * value, axis=-1, keepdims=True
    )
    grad_gain = jnp.sum(upstream * value * factor, axis=0)
    return (grad_value, grad_gain)


def contract(left, right, left_dim, right_dim):
    return lax.dot_general(
        left, right, (((left_dim,), (right_dim,)), ((), ())), preferred_element_type=jnp.float32
    )


def local(
    tokens,
    lengths,
    routes,
    attention_in,
    attention_out,
    position_bias,
    first_gain,
    second_gain,
    router,
    expert_in,
    expert_out,
    cotangent,
):
    w_attn_in, w_attn_out, table, gain_one, gain_two = (
        lax.all_gather(attention_in, "shard", axis=0, tiled=True),
        lax.all_gather(attention_out, "shard", axis=0, tiled=True),
        lax.all_gather(position_bias, "shard", axis=0, tiled=True),
        lax.all_gather(first_gain, "shard", axis=0, tiled=True),
        lax.all_gather(second_gain, "shard", axis=0, tiled=True),
    )
    rows = tokens.shape[0]
    width = tokens.shape[1]
    heads = table.shape[0]
    bucket_count = table.shape[1]
    head_dim = width // heads
    pairs = heads // 2
    pair_width = 2 * head_dim
    group_rows = rows * lax.axis_size("shard")
    first_row = lax.axis_index("shard") * rows
    ends = jnp.cumsum(lengths[0])
    key_place = lax.iota(jnp.int32, group_rows)
    query_place = first_row + lax.iota(jnp.int32, rows)
    key_segment = jnp.sum((key_place[:, None] >= ends[None, :]).astype(jnp.int32), axis=1)
    query_segment = jnp.sum((query_place[:, None] >= ends[None, :]).astype(jnp.int32), axis=1)
    same_seq = query_segment[:, None] == key_segment[None, :]
    bucket = bucket_index(key_place[None, :] - query_place[:, None])
    relative_bucket_lookup = (
        lax.iota(jnp.int32, bucket_count)[:, None, None] == bucket[None, :, :]
    ).astype(jnp.bfloat16)
    inputs = tokens.astype(jnp.float32)
    normed, factor_one = rms_forward(inputs, gain_one)
    normed_low = normed.astype(jnp.bfloat16)
    projected = jnp.dot(normed_low, w_attn_in, preferred_element_type=jnp.float32).astype(
        jnp.bfloat16
    )
    queries = projected[:, :width]
    keys_local = projected[:, width : 2 * width]
    values_local = projected[:, 2 * width :]
    keys_all, values_all = (
        lax.all_gather(keys_local, "shard", axis=0, tiled=True),
        lax.all_gather(values_local, "shard", axis=0, tiled=True),
    )

    def by_pair(matrix):
        return jnp.swapaxes(matrix.reshape(matrix.shape[0], pairs, pair_width), 0, 1)

    def unpair(stacked):
        return jnp.swapaxes(stacked, 0, 1).reshape(stacked.shape[1], width)

    query_pairs = by_pair(queries)
    key_pairs = by_pair(keys_all)
    value_pairs = by_pair(values_all)
    table_pairs = table.reshape(pairs, 2, bucket_count)

    def pair_scores(query_pair, key_pair, bucket_lookup_pair):
        query_heads = query_pair.reshape(rows, 2, head_dim)
        key_heads = key_pair.reshape(group_rows, 2, head_dim)
        raw = jnp.einsum("qhd,khd->hqk", query_heads, key_heads, preferred_element_type=jnp.float32)
        raw = raw + jnp.einsum(
            "dy,yet->det",
            bucket_lookup_pair,
            relative_bucket_lookup,
            preferred_element_type=jnp.float32,
        )
        return jnp.where(same_seq[None], raw, big_negative)

    def forward_pair(operands):
        query_pair, key_pair, value_pair, bucket_lookup_pair = operands
        scores = pair_scores(query_pair, key_pair, bucket_lookup_pair)
        top_score = jnp.max(scores, axis=-1, keepdims=True)
        raised = jnp.exp(scores - top_score)
        total = jnp.sum(raised, axis=-1, keepdims=True)
        weights_low = (raised / total).astype(jnp.bfloat16)
        mixed_pair = jnp.einsum(
            "hqk,khd->qhd",
            weights_low,
            value_pair.reshape(group_rows, 2, head_dim),
            preferred_element_type=jnp.float32,
        )
        return (
            mixed_pair.reshape(rows, pair_width).astype(jnp.bfloat16),
            top_score + jnp.log(total),
        )

    mixed_pairs, log_totals = lax.map(
        forward_pair, (query_pairs, key_pairs, value_pairs, table_pairs)
    )
    mixed = unpair(mixed_pairs)
    first_hidden_state = inputs + jnp.dot(mixed, w_attn_out, preferred_element_type=jnp.float32)
    normed_two, factor_two = rms_forward(first_hidden_state, gain_two)
    logits = jnp.dot(
        normed_two, router, precision=lax.Precision.HIGHEST, preferred_element_type=jnp.float32
    )
    shifted = jnp.exp(logits - jnp.max(logits, axis=-1, keepdims=True))
    router_probs = shifted / jnp.sum(shifted, axis=-1, keepdims=True)
    experts = router.shape[1]
    route = routes[:, 0]
    chosen = (route[:, None] == lax.iota(jnp.int32, experts)[None, :]).astype(jnp.float32)
    gate = jnp.sum(router_probs * chosen, axis=1)
    lower = (lax.iota(jnp.int32, rows)[:, None] >= lax.iota(jnp.int32, rows)[None, :]).astype(
        jnp.float32
    )
    running = jnp.dot(
        lower, chosen, precision=lax.Precision.HIGHEST, preferred_element_type=jnp.float32
    )
    slot = jnp.sum((running - 1.0) * chosen, axis=1).astype(jnp.int32)
    capacity = max(2, 9 * rows // (8 * experts) + 1)
    target = route * capacity + slot
    buffer_place = lax.iota(jnp.int32, experts * capacity)
    scatter_table = (buffer_place[:, None] == target[None, :]).astype(jnp.bfloat16)
    collect_table = (target[:, None] == buffer_place[None, :]).astype(jnp.bfloat16)
    sent_rows = normed_two.astype(jnp.bfloat16)
    outgoing = jnp.dot(scatter_table, sent_rows, preferred_element_type=jnp.float32).astype(
        jnp.bfloat16
    )
    arrived = lax.all_to_all(
        outgoing.reshape(experts, capacity, width),
        "expert",
        split_axis=0,
        concat_axis=0,
        tiled=True,
    )
    arrived = arrived.reshape(experts * capacity, width)
    up_full, down_full = (
        lax.all_gather(expert_in, "shard", axis=2, tiled=True),
        lax.all_gather(expert_out, "shard", axis=1, tiled=True),
    )
    before = jnp.dot(arrived, up_full[0], preferred_element_type=jnp.float32)
    expert_hidden = gelu_tanh(before).astype(jnp.bfloat16)
    result = jnp.dot(expert_hidden, down_full[0], preferred_element_type=jnp.float32)
    returning = result.astype(jnp.bfloat16).reshape(experts, capacity, width)
    returned = lax.all_to_all(returning, "expert", split_axis=0, concat_axis=0, tiled=True).reshape(
        experts * capacity, width
    )
    expert_result = jnp.dot(collect_table, returned, preferred_element_type=jnp.float32)
    layer_out = (first_hidden_state + gate[:, None] * expert_result).astype(jnp.bfloat16)
    upstream = cotangent.astype(jnp.float32)
    grad_gate = jnp.sum(upstream * expert_result, axis=1)
    grad_result = (gate[:, None] * upstream).astype(jnp.bfloat16)
    outgoing_grad = jnp.dot(scatter_table, grad_result, preferred_element_type=jnp.float32).astype(
        jnp.bfloat16
    )
    arrived_grad = lax.all_to_all(
        outgoing_grad.reshape(experts, capacity, width),
        "expert",
        split_axis=0,
        concat_axis=0,
        tiled=True,
    )
    arrived_grad = arrived_grad.reshape(experts * capacity, width)
    grad_before = (contract(arrived_grad, down_full[0], 1, 1) * gelu_slope(before)).astype(
        jnp.bfloat16
    )
    grad_down = contract(expert_hidden, arrived_grad, 0, 0)[None]
    grad_up = contract(arrived, grad_before, 0, 0)[None]
    input_gradient_rows = contract(grad_before, up_full[0], 1, 1)
    back_grad = input_gradient_rows.astype(jnp.bfloat16).reshape(experts, capacity, width)
    returned_grad = lax.all_to_all(
        back_grad, "expert", split_axis=0, concat_axis=0, tiled=True
    ).reshape(experts * capacity, width)
    grad_sent = jnp.dot(collect_table, returned_grad, preferred_element_type=jnp.float32)
    grad_logits = (grad_gate * gate)[:, None] * (chosen - router_probs)
    grad_router = lax.dot_general(
        normed_two,
        grad_logits,
        (((0,), (0,)), ((), ())),
        precision=lax.Precision.HIGHEST,
        preferred_element_type=jnp.float32,
    )
    grad_normed_two = grad_sent + lax.dot_general(
        grad_logits,
        router,
        (((1,), (1,)), ((), ())),
        precision=lax.Precision.HIGHEST,
        preferred_element_type=jnp.float32,
    )
    grad_middle, grad_gain_two = rms_backward(
        first_hidden_state, factor_two, gain_two, grad_normed_two
    )
    grad_hidden = upstream + grad_middle
    grad_branch = grad_hidden.astype(jnp.bfloat16)
    grad_w_out_attn = contract(mixed, grad_branch, 0, 0)
    grad_mixed = contract(grad_branch, w_attn_out, 1, 1).astype(jnp.bfloat16)
    grad_mixed_pairs = by_pair(grad_mixed)

    def backward_pair(operands):
        query_pair, key_pair, value_pair, bucket_lookup_pair, grad_pair, log_total = operands
        scores = pair_scores(query_pair, key_pair, bucket_lookup_pair)
        weights = jnp.exp(scores - log_total)
        grad_heads = grad_pair.reshape(rows, 2, head_dim)
        value_heads = value_pair.reshape(group_rows, 2, head_dim)
        query_heads = query_pair.reshape(rows, 2, head_dim)
        key_heads = key_pair.reshape(group_rows, 2, head_dim)
        grad_weights = jnp.einsum(
            "qhd,khd->hqk", grad_heads, value_heads, preferred_element_type=jnp.float32
        )
        inner = jnp.sum(weights * grad_weights, axis=-1, keepdims=True)
        score_gradient = (weights * (grad_weights - inner)).astype(jnp.bfloat16)
        grad_query = jnp.einsum(
            "hqk,khd->qhd", score_gradient, key_heads, preferred_element_type=jnp.float32
        )
        grad_key = jnp.einsum(
            "hqk,qhd->khd", score_gradient, query_heads, preferred_element_type=jnp.float32
        )
        grad_value = jnp.einsum(
            "hqk,qhd->khd",
            weights.astype(jnp.bfloat16),
            grad_heads,
            preferred_element_type=jnp.float32,
        )
        grad_entries = jnp.einsum(
            "xfn,wfn->xw",
            score_gradient,
            relative_bucket_lookup,
            preferred_element_type=jnp.float32,
        )
        return (
            grad_query.reshape(rows, pair_width),
            grad_key.reshape(group_rows, pair_width),
            grad_value.reshape(group_rows, pair_width),
            grad_entries,
        )

    query_grads, key_grads, value_grads, entry_grads = lax.map(
        backward_pair,
        (query_pairs, key_pairs, value_pairs, table_pairs, grad_mixed_pairs, log_totals),
    )
    grad_keys, grad_values = (
        lax.psum_scatter(
            unpair(key_grads).astype(jnp.bfloat16), "shard", scatter_dimension=0, tiled=True
        ).astype(jnp.float32),
        lax.psum_scatter(
            unpair(value_grads).astype(jnp.bfloat16), "shard", scatter_dimension=0, tiled=True
        ).astype(jnp.float32),
    )
    grad_projected = jnp.concatenate([unpair(query_grads), grad_keys, grad_values], axis=1).astype(
        jnp.bfloat16
    )
    grad_w_in_attn = contract(normed_low, grad_projected, 0, 0)
    grad_normed = contract(grad_projected, w_attn_in, 1, 1)
    grad_input_norm, grad_gain_one = rms_backward(inputs, factor_one, gain_one, grad_normed)
    grad_tokens = (grad_hidden + grad_input_norm).astype(jnp.bfloat16)
    grad_table = entry_grads.reshape(heads, bucket_count)
    all_shares = (
        lax.psum_scatter(
            grad_w_in_attn.astype(jnp.bfloat16), "shard", scatter_dimension=0, tiled=True
        ).astype(jnp.float32),
        lax.psum_scatter(
            grad_w_out_attn.astype(jnp.bfloat16), "shard", scatter_dimension=0, tiled=True
        ).astype(jnp.float32),
        lax.psum_scatter(
            grad_table.astype(jnp.bfloat16), "shard", scatter_dimension=0, tiled=True
        ).astype(jnp.float32),
        lax.psum_scatter(
            grad_gain_one.astype(jnp.bfloat16), "shard", scatter_dimension=0, tiled=True
        ).astype(jnp.float32),
        lax.psum_scatter(
            grad_gain_two.astype(jnp.bfloat16), "shard", scatter_dimension=0, tiled=True
        ).astype(jnp.float32),
        lax.psum_scatter(
            grad_router.astype(jnp.bfloat16), "shard", scatter_dimension=0, tiled=True
        ).astype(jnp.float32),
        lax.psum_scatter(
            grad_up.astype(jnp.bfloat16), "shard", scatter_dimension=2, tiled=True
        ).astype(jnp.float32),
        lax.psum_scatter(
            grad_down.astype(jnp.bfloat16), "shard", scatter_dimension=1, tiled=True
        ).astype(jnp.float32),
    )
    weight_portions = all_shares[:6]
    grad_up_share = all_shares[6]
    grad_down_share = all_shares[7]
    totals = lax.psum(
        (
            weight_portions[0],
            weight_portions[1],
            weight_portions[2],
            weight_portions[3],
            weight_portions[4],
            weight_portions[5],
        ),
        "expert",
    )
    return (
        layer_out,
        grad_tokens,
        totals[0],
        totals[1],
        totals[2],
        totals[3],
        totals[4],
        totals[5],
        grad_up_share,
        grad_down_share,
    )


def solution(mesh):
    in_specs = (
        P(("expert", "shard"), None),
        P("expert", None),
        P(("expert", "shard"), None),
        P("shard", None),
        P("shard", None),
        P("shard", None),
        P("shard"),
        P("shard"),
        P(),
        P("expert", None, "shard"),
        P("expert", "shard", None),
        P(("expert", "shard"), None),
    )
    out_specs = (
        P(("expert", "shard"), None),
        P(("expert", "shard"), None),
        P("shard", None),
        P("shard", None),
        P("shard", None),
        P("shard"),
        P("shard"),
        P("shard", None),
        P("expert", None, "shard"),
        P("expert", "shard", None),
    )
    return jax.shard_map(local, mesh=mesh, in_specs=in_specs, out_specs=out_specs, check_vma=False)
```

profile of v0, /device:TPU:0, one launch (start us, length us, event | category | flops | bytes accessed | tf_op | source)
XLA Modules:
  0.0 497.5 jit_solution(15124953403332588687)
XLA Ops:
  12.6 8.3 %all-reduce.7 = (bf16[768]{0:T(1024)(128)(2,1)S(1)}, bf16[768]{0:T(1024)(128)(2,1)S(1)}) all-reduce(bf16[768]{0:T(1024)(128)(2,1)S(1)} %dynamic-update-slice, bf16[768]{0:T(1024)(128)(2,1)S(1)} %dynamic-update-slice.1), channel_id=1, replica_groups=mesh['expert'=8,'shard'=4] {'shard'}, use_global_device_ids=true, to_apply=%add | all-reduce | flops 1536 | bytes 6144
  21.0 5.1 %all-gather = bf16[4,3,32]{2,1,0:T(4,128)(2,1)S(1)} all-gather(bf16[1,3,32]{2,1,0:T(4,128)(2,1)S(1)} %bitcast.209), channel_id=1, replica_groups=mesh['expert'=8,'shard'=4] {'shard'}, dimensions={0}, use_global_device_ids=true | all-gather | bytes 960 | tf_op jit(solution)/shard_map/all_gather | solution.py:72
  26.8 16.4 %all-gather.6.cloned.1.call-done = bf16[768,2304]{1,0:T(8,128)(2,1)} async-done(((bf16[192,2304]{1,0:T(8,128)(2,1)}), bf16[768,2304]{1,0:T(8,128)(2,1)}) %all-gather.6.cloned.1.call-update) | async-done | bytes 3538960 | tf_op jit(solution)/shard_map/all_gather | solution.py:70
  45.9 8.6 %all_gather.29 = bf16[512,768]{1,0:T(8,128)(2,1)S(1)} all-gather(bf16[128,768]{1,0:T(8,128)(2,1)S(1)} %get-tuple-element.267), channel_id=1, replica_groups=mesh['expert'=8,'shard'=4] {'shard'}, dimensions={0}, use_global_device_ids=true | all-gather | bytes 983040 | tf_op jit(solution)/shard_map/all_gather | solution.py:106
  55.6 10.2 %all_gather.30 = bf16[512,768]{1,0:T(8,128)(2,1)S(1)} all-gather(bf16[128,768]{1,0:T(8,128)(2,1)S(1)} %get-tuple-element.265), channel_id=1, replica_groups=mesh['expert'=8,'shard'=4] {'shard'}, dimensions={0}, use_global_device_ids=true | all-gather | bytes 983040 | tf_op jit(solution)/shard_map/all_gather | solution.py:105
  66.1 18.8 %while.30 = (s32[]{:T(128)}, bf16[6,128,128]{1,2,0:T(8,128)(2,1)S(1)}, f32[6,2,128,1]{2,1,3,0:T(2,128)}, bf16[6,512,128]{1,2,0:T(8,128)(2,1)S(1)}, bf16[6,128,12...) while((s32[]{:T(128)}, ...), condition=%wide.region_7.8_spmd.clone, body=%wide.region_4.7_spmd.clone.sunk | while | flops 47267584 | bytes 4009097 | solution.py:150
  89.1 5.5 %all-to-all-start.2 = ((bf16[8,19,768]{2,1,0:T(8,128)(2,1)}), bf16[8,19,768]{2,1,0:T(8,128)(2,1)S(1)}, u32[]{:S(2)}, u32[]{:S(2)}) async-start(bf16[8,19,768]{2,1,0:T(8,128)(2,1)} %reshape.286), calls=%async_computation.2 | async-start | bytes 589824 | tf_op jit(solution)/shard_map/all_to_all | solution.py:208
  95.7 9.0 %all-to-all-done.2 = bf16[8,19,768]{2,1,0:T(8,128)(2,1)S(1)} async-done(((bf16[8,19,768]{2,1,0:T(8,128)(2,1)}), bf16[8,19,768]{2,1,0:T(8,128)(2,1)S(1)}, u32[]{:S(2)}, u32[]{:S(2)}) %all-to-all-start.2) | async-done | bytes 233504 | tf_op jit(solution)/shard_map/all_to_all | solution.py:208
  104.7 3.6 all-to-all-start
  109.1 8.9 %all-to-all-done = bf16[8,19,768]{2,1,0:T(8,128)(2,1)S(1)} async-done(((bf16[8,19,768]{2,1,0:T(8,128)(2,1)}), bf16[8,19,768]{2,1,0:T(8,128)(2,1)S(1)}, u32[]{:S(2)}, u32[]{:S(2)}) %all-to-all-start) | async-done | bytes 233504 | tf_op jit(solution)/shard_map/all_to_all | solution.py:181
  118.2 4.6 fusion.44
  122.8 18.9 %all-gather.12.cloned.1.call-done = bf16[1,3072,768]{2,1,0:T(8,128)(2,1)} async-done(((bf16[1,768,768]{2,1,0:T(8,128)(2,1)}), bf16[1,3072,768]{2,1,0:T(8,128)(2,1)}) %all-gather.12.cloned.1.call-update) | async-done | bytes 4718608 | tf_op jit(solution)/shard_map/all_gather | solution.py:191
  141.7 5.1 %fusion.51 = bf16[152,3072]{1,0:T(8,128)(2,1)S(1)} fusion(bf16[152,768]{1,0:T(8,128)(2,1)} %reshape.287, bf16[1,3072,768]{2,1,0:T(8,128)(2,1)} %all-gather.12.cloned.1.call-done, f32[152,3072]{1,0:T(8,128)} %fusion.44), kind=kOutput, calls=%fused_computation.65 | convolution fusion | flops 726097920 | bytes 7753728 | tf_op jit(solution)/shard_map/dot_general | solution.py:50
  149.3 5.5 %all-to-all-start.3 = ((bf16[8,19,768]{2,1,0:T(8,128)(2,1)}), bf16[8,19,768]{2,1,0:T(8,128)(2,1)}, u32[]{:S(2)}, u32[]{:S(2)}) async-start(bf16[8,19,768]{2,1,0:T(8,128)(2,1)} %reshape.288), calls=%async_computation.3 | async-start | bytes 589824 | tf_op jit(solution)/shard_map/all_to_all | solution.py:223
  154.9 4.8 fusion.62
  161.5 3.4 all-to-all-done.3
  164.9 4.1 all-to-all-start.1
  172.9 5.4 %all-to-all-done.1 = bf16[8,19,768]{2,1,0:T(8,128)(2,1)} async-done(((bf16[8,19,768]{2,1,0:T(8,128)(2,1)}), bf16[8,19,768]{2,1,0:T(8,128)(2,1)}, u32[]{:S(2)}, u32[]{:S(2)}) %all-to-all-start.1) | async-done | bytes 233504 | tf_op jit(solution)/shard_map/all_to_all | solution.py:197
  187.9 51.2 %while.31 = (s32[]{:T(128)}, bf16[6,128,128]{1,2,0:T(8,128)(2,1)}, bf16[6,512,128]{1,2,0:T(8,128)(2,1)}, bf16[6,512,128]{1,2,0:T(8,128)(2,1)}, bf16[6,2,32]{2,1,...) while((s32[]{:T(128)}, bf16[6,128,128]{1,2,0:T(8,128)(2,1)}, ...), condition=%wide.region_17.18_spmd.clone, body=%wide.region_15.17_spmd.clone.sunk | while | flops 110296832 | bytes 9020629 | solution.py:289
  245.7 17.3 %reduce-scatter.24.cloned.1.call-done = bf16[128,768]{1,0:T(8,128)(2,1)} async-done(((bf16[512,768]{1,0:T(8,128)(2,1)}), bf16[128,768]{1,0:T(8,128)(2,1)}) %reduce-scatter.24.cloned.1.call-update) | async-done | bytes 196624
  264.1 25.3 %reduce-scatter.22.cloned.1.call-done = bf16[128,768]{1,0:T(8,128)(2,1)} async-done(((bf16[512,768]{1,0:T(8,128)(2,1)}), bf16[128,768]{1,0:T(8,128)(2,1)}) %reduce-scatter.22.cloned.1.call-update) | async-done | bytes 196624
  290.6 3.0 convolution_convert_fusion.3
  294.5 3.6 fusion.46
  299.6 4.1 fusion.47
  305.1 7.2 %reduce-scatter.26.cloned.1.call-done = bf16[192,8]{1,0:T(8,128)(2,1)} async-done(((bf16[768,8]{1,0:T(8,128)(2,1)}), bf16[192,8]{1,0:T(8,128)(2,1)}) %reduce-scatter.26.cloned.1.call-update) | async-done | bytes 3088
  313.1 3.5 fusion.80
  316.6 5.9 %all-reduce.6 = (bf16[12,32]{1,0:T(8,128)(2,1)S(1)}, bf16[768]{0:T(1024)(128)(2,1)S(1)}, bf16[768]{0:T(1024)(128)(2,1)S(1)}) all-reduce(bf16[12,32]{1,0:T(8,128)(2,1)S(1)} %convert_element_type.283, bf16[768]{0:T(1024)(128)(2,1)S(1)} %get-tuple-element.196, ...), channel_id=6, replica_groups=mesh['expert'=8,'shard'=4] {'shard'}, use_global_device_ids=true, to_apply=%region_25.26.clone | all-reduce | flops 1920 | bytes 7680
  323.4 17.7 %reduce-scatter.16.cloned.1.call-done = bf16[192,768]{1,0:T(8,128)(2,1)} async-done(((bf16[768,768]{1,0:T(8,128)(2,1)}), bf16[192,768]{1,0:T(8,128)(2,1)}) %reduce-scatter.16.cloned.1.call-update) | async-done | bytes 294928 | tf_op jit(solution)/shard_map/reduce_scatter | solution.py:313
  341.2 43.2 %reduce-scatter.14.cloned.1.call-done = bf16[192,2304]{1,0:T(8,128)(2,1)} async-done(((bf16[768,2304]{1,0:T(8,128)(2,1)}), bf16[192,2304]{1,0:T(8,128)(2,1)}) %reduce-scatter.14.cloned.1.call-update) | async-done | bytes 884752 | tf_op jit(solution)/shard_map/reduce_scatter | solution.py:310
  384.4 100.9 %all-reduce.9 = (f32[192,2304]{1,0:T(8,128)}, f32[192,768]{1,0:T(8,128)}, f32[3,32]{1,0:T(4,128)}, f32[192]{0:T(256)}, f32[192]{0:T(256)}, /*index=5*/f32[192,8]{0,1:T(8,128)}) all-reduce(bf16[192,2304]{1,0:T(8,128)(2,1)} %reduce-scatter.14.cloned.1.call-done, ...), channel_id=1, replica_groups=mesh['expert'=8,'shard'=4] {'expert'}, use_global_device_ids=true, to_apply=%region_22.23 | all-reduce | flops 591840 | bytes 3552000 | tf_op jit(solution)/shard_map/psum | solution.py:338
  485.3 2.8 convert_element_type.293
  488.1 2.8 convert_element_type.296
  (320 shorter events, 115.7 us)
Async XLA Ops:
  7.2 80.2 %copy-start = (f32[768,8]{0,1:T(8,128)S(1)}, f32[768,8]{0,1:T(8,128)}, u32[]{:S(2)}) copy-start(f32[768,8]{0,1:T(8,128)} %param.24) | copy-start | bytes 73732
  7.2 4.9 copy-start.30
  7.2 5.1 %copy-start.31 = (bf16[192]{0:T(256)(128)(2,1)S(1)}, bf16[192]{0:T(256)(128)(2,1)}, u32[]{:S(2)}) copy-start(bf16[192]{0:T(256)(128)(2,1)} %param.23) | copy-start | bytes 1156
  7.2 13.6 %copy-start.2 = (bf16[128,768]{1,0:T(8,128)(2,1)S(1)}, bf16[128,768]{1,0:T(8,128)(2,1)}, u32[]{:S(2)}) copy-start(bf16[128,768]{1,0:T(8,128)(2,1)} %param.16) | copy-start | bytes 589828
  7.2 13.8 %copy-start.28 = (bf16[3,32]{1,0:T(4,128)(2,1)S(1)}, bf16[3,32]{1,0:T(4,128)(2,1)}, u32[]{:S(2)}) copy-start(bf16[3,32]{1,0:T(4,128)(2,1)} %param.21) | copy-start | bytes 580
  7.3 18.9 %copy-start.17 = (s32[128,1]{0,1:T(1,128)S(1)}, s32[128,1]{0,1:T(1,128)}, u32[]{:S(2)}) copy-start(s32[128,1]{0,1:T(1,128)} %param.18) | copy-start | bytes 1540
  7.3 35.9 %all-gather.6.cloned.1.call-start = ((), (), s32[]{:S(2)}) async-start(), calls=%async_computation.11 | async-start | bytes 4423680 | tf_op jit(solution)/shard_map/all_gather | solution.py:70
  8.0 77.0 %all-gather.8.cloned.1.call-start = ((), (), s32[]{:S(2)}) async-start(), calls=%async_computation.12 | async-start | bytes 1474560 | tf_op jit(solution)/shard_map/all_gather | solution.py:71
  8.8 109.4 %all-gather.10.cloned.1.call-start = ((), (), s32[]{:S(2)}) async-start(), calls=%async_computation.13 | async-start | bytes 5898240 | tf_op jit(solution)/shard_map/all_gather | solution.py:190
  9.5 132.2 %all-gather.12.cloned.1.call-start = ((), (), s32[]{:S(2)}) async-start(), calls=%async_computation.14 | async-start | bytes 5898240 | tf_op jit(solution)/shard_map/all_gather | solution.py:191
  26.3 19.6 %copy-start.32 = (f32[128]{0:T(128)}, f32[128]{0:T(128)S(1)}, u32[]{:S(2)}) copy-start(f32[128]{0:T(128)S(1)} %fusion.66) | copy-start | bytes 1540
  88.0 16.7 %copy-start.20 = (f32[128]{0:T(128)}, f32[128]{0:T(128)S(1)}, u32[]{:S(2)}) copy-start(f32[128]{0:T(128)S(1)} %select_reduce_fusion) | copy-start | bytes 1540
  89.1 15.6 %all-to-all-start.2 = ((bf16[8,19,768]{2,1,0:T(8,128)(2,1)}), bf16[8,19,768]{2,1,0:T(8,128)(2,1)S(1)}, u32[]{:S(2)}, u32[]{:S(2)}) async-start(bf16[8,19,768]{2,1,0:T(8,128)(2,1)} %reshape.286), calls=%async_computation.2 | async-start | bytes 589824 | tf_op jit(solution)/shard_map/all_to_all | solution.py:208
  104.7 13.4 %all-to-all-start = ((bf16[8,19,768]{2,1,0:T(8,128)(2,1)}), bf16[8,19,768]{2,1,0:T(8,128)(2,1)S(1)}, u32[]{:S(2)}, u32[]{:S(2)}) async-start(bf16[8,19,768]{2,1,0:T(8,128)(2,1)} %reshape.282), calls=%async_computation | async-start | bytes 589824 | tf_op jit(solution)/shard_map/all_to_all | solution.py:181
  118.2 4.6 copy-start.4
  141.7 5.1 %copy-start.1 = (bf16[1,768,3072]{2,1,0:T(8,128)(2,1)S(1)}, bf16[1,768,3072]{2,1,0:T(8,128)(2,1)}, u32[]{:S(2)}) copy-start(bf16[1,768,3072]{2,1,0:T(8,128)(2,1)} %all-gather.10.cloned.1.call-done) | copy-start | bytes 14155780
  149.3 15.6 %all-to-all-start.3 = ((bf16[8,19,768]{2,1,0:T(8,128)(2,1)}), bf16[8,19,768]{2,1,0:T(8,128)(2,1)}, u32[]{:S(2)}, u32[]{:S(2)}) async-start(bf16[8,19,768]{2,1,0:T(8,128)(2,1)} %reshape.288), calls=%async_computation.3 | async-start | bytes 589824 | tf_op jit(solution)/shard_map/all_to_all | solution.py:223
  154.9 14.4 %copy-start.33 = (f32[128]{0:T(128)S(1)}, f32[128]{0:T(128)}, u32[]{:S(2)}) copy-start(f32[128]{0:T(128)} %copy-done.32) | copy-start | bytes 1540
  159.7 20.4 %copy-start.8 = (bf16[128,768]{1,0:T(8,128)(2,1)S(1)}, bf16[128,768]{1,0:T(8,128)(2,1)}, u32[]{:S(2)}) copy-start(bf16[128,768]{1,0:T(8,128)(2,1)} %param.27) | copy-start | bytes 589828
  159.7 21.8 %copy-start.21 = (f32[128]{0:T(128)S(1)}, f32[128]{0:T(128)}, u32[]{:S(2)}) copy-start(f32[128]{0:T(128)} %copy-done.20) | copy-start | bytes 1540
  159.7 21.8 %copy-start.18 = (s32[128,1]{0,1:T(1,128)S(1)}, s32[128,1]{0,1:T(1,128)}, u32[]{:S(2)}) copy-start(s32[128,1]{0,1:T(1,128)} %param.18) | copy-start | bytes 1540
  164.9 13.4 %all-to-all-start.1 = ((bf16[8,19,768]{2,1,0:T(8,128)(2,1)}), bf16[8,19,768]{2,1,0:T(8,128)(2,1)}, u32[]{:S(2)}, u32[]{:S(2)}) async-start(bf16[8,19,768]{2,1,0:T(8,128)(2,1)} %reshape.284), calls=%async_computation.1 | async-start | bytes 589824 | tf_op jit(solution)/shard_map/all_to_all | solution.py:197
  169.0 94.0 %reduce-scatter.24.cloned.1.call-start = ((), (), s32[]{:S(2)}) async-start(), calls=%async_computation.20 | async-start | bytes 983040
  180.1 4.9 copy-start.3
  241.6 47.9 %reduce-scatter.22.cloned.1.call-start = ((), (), s32[]{:S(2)}) async-start(), calls=%async_computation.19 | async-start | bytes 983040
  242.8 69.5 %reduce-scatter.26.cloned.1.call-start = ((), (), s32[]{:S(2)}) async-start(), calls=%async_computation.21 | async-start | bytes 245760
  244.1 46.4 %copy-start.15 = (bf16[6,128,128]{1,2,0:T(8,128)(2,1)S(1)}, bf16[6,128,128]{1,2,0:T(8,128)(2,1)}, u32[]{:S(2)}) copy-start(bf16[6,128,128]{1,2,0:T(8,128)(2,1)} %get-tuple-element.130) | copy-start | bytes 589828
  244.1 97.0 %reduce-scatter.16.cloned.1.call-start = ((), (), s32[]{:S(2)}) async-start(), calls=%async_computation.16 | async-start | bytes 1474560 | tf_op jit(solution)/shard_map/reduce_scatter | solution.py:313
  245.7 138.7 %reduce-scatter.14.cloned.1.call-start = ((), (), s32[]{:S(2)}) async-start(), calls=%async_computation.15 | async-start | bytes 4423680 | tf_op jit(solution)/shard_map/reduce_scatter | solution.py:310
  293.6 191.7 %reduce-scatter.18.cloned.1.call-start = ((), (), s32[]{:S(2)}) async-start(), calls=%async_computation.17 | async-start | bytes 5898240 | tf_op jit(solution)/shard_map/reduce_scatter | solution.py:328
  298.1 190.0 %reduce-scatter.20.cloned.1.call-start = ((), (), s32[]{:S(2)}) async-start(), calls=%async_computation.18 | async-start | bytes 5898240 | tf_op jit(solution)/shard_map/reduce_scatter | solution.py:331
  303.7 9.5 %copy-start.16 = (bf16[6,128,128]{1,2,0:T(8,128)(2,1)S(1)}, bf16[6,128,128]{1,2,0:T(8,128)(2,1)}, u32[]{:S(2)}) copy-start(bf16[6,128,128]{1,2,0:T(8,128)(2,1)} %get-tuple-element.130) | copy-start | bytes 589828
  (22 other events, 47.1 us)
Sparse Core Ops, SparseCore 0:
  9.7 33.4 all-gather.5
  44.7 18.9 all-gather.7
  65.3 37.4 all-gather.9
  104.2 37.4 all-gather.11
  241.7 21.3 reduce-scatter.23
  266.2 23.2 reduce-scatter.21
  292.5 19.7 reduce-scatter.25
  315.4 25.7 reduce-scatter.15
  343.9 40.4 reduce-scatter.13
  386.7 47.8 reduce-scatter.17
  437.3 47.8 reduce-scatter.19
where the time goes:
time: 500 us; the launch traced here: 498 us
  waiting for transfers between devices  176 us (35%)
  blocking collectives  139 us (28%)
  matrix products  80.4 us (16%)
  local copies, waits for them, and re-layouts  49.6 us (10%)
  starting transfers between devices  19.4 us (4%)
  other arithmetic  16.6 us (3%)
  between operations  16.4 us (3%)
    psum x1, blocking collectives, local(): lax.psum((weight_portions[0], weight_portions[1], weight_portions[2], wei...  101 us
    unnamed x14, waiting for transfers between devices  52.6 us
    reduce_scatter x1, waiting for transfers between devices, local(): lax.psum_scatter(grad_w_in_attn.astype(jnp.bfloat16), 'shard', scatter_di...  43.2 us
    dot_general x8, matrix products, contract(): lax.dot_general(left, right, (((left_dim,), (right_dim,)), ((), ())), pre...  23.5 us
    all_gather x1, waiting for transfers between devices, local(): lax.all_gather(expert_out, 'shard', axis=1, tiled=True)  18.9 us
    reduce_scatter x1, waiting for transfers between devices, local(): lax.psum_scatter(grad_w_out_attn.astype(jnp.bfloat16), 'shard', scatter_d...  17.7 us
    all_gather x1, waiting for transfers between devices, local(): lax.all_gather(attention_in, 'shard', axis=0, tiled=True)  16.4 us
    unnamed x2, blocking collectives  14.2 us
  transfers between devices with their start and end apart: 15, of which 11 were waited for; matrix products, arithmetic and copies ran while one was open for 14% of the time, Pallas kernels for 0%

commit v1 on v0

v1 whole, which is shorter than its diff:
```python
import jax
import jax.numpy as jnp
from jax import lax
from jax.experimental import pallas as pl
from jax.experimental.pallas import tpu as pltpu
from jax.sharding import PartitionSpec as P

norm_eps = 1e-06
gelu_scale = 0.7978845608028654
gelu_cubic = 0.044715
big_negative = -1e30
near_steps = 8
far_steps = (12, 16, 23, 32, 46, 64, 91)
bf16 = jnp.bfloat16
f32 = jnp.float32
row_tile = 8
gain_rows = 16


def bucket_index(offset):
    distance = jnp.abs(offset)
    far_level = jnp.full_like(distance, near_steps)
    for step_edge in far_steps:
        far_level = far_level + (distance >= step_edge).astype(jnp.int32)
    near = jnp.where(distance < near_steps, distance, far_level)
    return near + 16 * (offset > 0).astype(jnp.int32)


def dot(left, right):
    return jnp.dot(left, right, preferred_element_type=f32)


def dot_nt(left, right):
    return lax.dot_general(left, right, (((1,), (1,)), ((), ())), preferred_element_type=f32)


def dot_tn(left, right):
    return lax.dot_general(left, right, (((0,), (0,)), ((), ())), preferred_element_type=f32)


def swap(value, axis, bit):
    size = lax.axis_size(axis)
    return lax.ppermute(value, axis, [(i, i ^ bit) for i in range(size)])


def gather_relative(value, axis):
    blocks = [value]
    bit = lax.axis_size(axis) // 2
    parts = {0: value}
    while bit:
        for p in list(parts):
            parts[p ^ bit] = swap(parts[p], axis, bit)
        bit //= 2
    return [parts[p] for p in range(lax.axis_size(axis))]


def exchange_relative(blocks, axis):
    return [blocks[0]] + [swap(block, axis, p) for p, block in enumerate(blocks) if p]


def call(kernel, out_shape, operands, spaces=None, scratch=(), flops=0, size=0):
    vmem = pl.BlockSpec(memory_space=pltpu.VMEM)
    smem = pl.BlockSpec(memory_space=pltpu.SMEM)
    spaces = spaces or ""
    in_specs = [smem if i < len(spaces) and spaces[i] == "s" else vmem for i in range(len(operands))]
    return pl.pallas_call(
        kernel,
        out_shape=out_shape,
        in_specs=in_specs,
        out_specs=jax.tree.map(lambda _: vmem, out_shape),
        scratch_shapes=list(scratch),
        compiler_params=pltpu.CompilerParams(vmem_limit_bytes=56 * 2**20),
        cost_estimate=pl.CostEstimate(flops=flops, bytes_accessed=size, transcendentals=0),
    )(*operands)


def shape(dims, dtype=bf16):
    return jax.ShapeDtypeStruct(tuple(dims), dtype)


def attention_forward(n, rows, width, heads, seqs, buckets, *refs):
    index, lengths, table = refs[:3]
    token_refs = refs[3 : 3 + n]
    weight_refs = refs[3 + n : 3 + 2 * n]
    normed_out, weight_out, projected_out, weights_out = refs[3 + 2 * n : 7 + 2 * n]
    mixed_out = refs[7 + 2 * n : 7 + 3 * n]
    tokens_scr, mixed_scr = refs[7 + 3 * n :]
    s = index[0]
    part = width // n
    head_dim = part // heads
    gain = jnp.zeros((1, width), f32)
    for p in range(n):
        place = s ^ p
        tokens_scr[place] = token_refs[p][:rows, :]
        gain = gain + token_refs[p][rows : rows + gain_rows, :].astype(f32)[0:1, :]
        weight_out[pl.ds(pl.multiple_of(place * part, part & -part), part), :] = weight_refs[p][...]
    for j in range(n):
        value = tokens_scr[j].astype(f32)
        factor = lax.rsqrt(jnp.mean(value * value, axis=-1, keepdims=True) + norm_eps)
        normed_out[j * rows : (j + 1) * rows, :] = (value * factor * gain).astype(bf16)
    projected_out[...] = dot(normed_out[...], weight_out[...]).astype(bf16)
    total_rows = n * rows
    key_place = lax.broadcasted_iota(jnp.int32, (1, total_rows), 1)
    key_segment = jnp.zeros((1, total_rows), jnp.int32)
    end = jnp.int32(0)
    ends = []
    for j in range(seqs):
        end = end + lengths[0, j]
        ends.append(end)
        key_segment = key_segment + (key_place >= end).astype(jnp.int32)
    base = lax.broadcasted_iota(jnp.int32, (rows, rows), 1) - lax.broadcasted_iota(
        jnp.int32, (rows, rows), 0
    )
    steps = {diff: bucket_index(base + diff * rows) for diff in (-1, 0, 1)}
    for h in range(heads):
        query = projected_out[:, h * head_dim : (h + 1) * head_dim]
        key = projected_out[:, part + h * head_dim : part + (h + 1) * head_dim]
        value = projected_out[:, 2 * part + h * head_dim : 2 * part + (h + 1) * head_dim]
        bias = {}
        for diff in (-1, 0, 1):
            block = jnp.zeros((rows, rows), f32)
            for b in range(buckets):
                block = jnp.where(steps[diff] == b, table[h, b], block)
            bias[diff] = block
        low_side = jnp.full((rows, rows), table[h, buckets // 2 - 1], f32)
        high_side = jnp.full((rows, rows), table[h, buckets - 1], f32)
        for i in range(n):
            scores = dot_nt(query[i * rows : (i + 1) * rows, :], key)
            side = [
                bias[j - i] if abs(j - i) <= 1 else (high_side if j > i else low_side)
                for j in range(n)
            ]
            scores = scores + jnp.concatenate(side, axis=1)
            query_place = i * rows + lax.broadcasted_iota(jnp.int32, (rows, 1), 0)
            query_segment = jnp.zeros((rows, 1), jnp.int32)
            for j in range(seqs):
                query_segment = query_segment + (query_place >= ends[j]).astype(jnp.int32)
            scores = jnp.where(query_segment == key_segment, scores, big_negative)
            top = jnp.max(scores, axis=-1, keepdims=True)
            raised = jnp.exp(scores - top)
            total = jnp.sum(raised, axis=-1, keepdims=True)
            weights = (raised * (1.0 / total)).astype(bf16)
            weights_out[h, i * rows : (i + 1) * rows, :] = weights
            mixed_scr[i, :, h * head_dim : (h + 1) * head_dim] = dot(weights, value).astype(bf16)
    for p in range(n):
        mixed_out[p][...] = mixed_scr[s ^ p]


def attention_backward(n, m, rows, width, heads, buckets, *refs):
    index, projected, normed, weight, weights = refs[:5]
    grad_refs = refs[5 : 5 + n]
    at = 5 + n
    share_out = refs[at : at + m]
    normed_grad_out = refs[at + m : at + m + n]
    table_out = refs[at + m + n]
    grad_scr, scores_scr, projected_scr, total_scr, normed_scr = refs[at + m + n + 1 :]
    s = index[0]
    e = index[1]
    part = width // n
    head_dim = part // heads
    for p in range(n):
        grad_scr[s ^ p] = grad_refs[p][...]
    base = lax.broadcasted_iota(jnp.int32, (rows, rows), 1) - lax.broadcasted_iota(
        jnp.int32, (rows, rows), 0
    )
    steps = {diff: bucket_index(base + diff * rows) for diff in (-1, 0, 1)}
    lane = lax.broadcasted_iota(jnp.int32, (row_tile, 128), 1)
    line = lax.broadcasted_iota(jnp.int32, (row_tile, 128), 0)
    table_total = jnp.zeros((row_tile, 128), f32)
    for h in range(heads):
        query = projected[:, h * head_dim : (h + 1) * head_dim]
        key = projected[:, part + h * head_dim : part + (h + 1) * head_dim]
        value = projected[:, 2 * part + h * head_dim : 2 * part + (h + 1) * head_dim]
        near = {diff: jnp.zeros((rows, rows), f32) for diff in (-1, 0, 1)}
        low_side = jnp.zeros((rows, rows), f32)
        high_side = jnp.zeros((rows, rows), f32)
        upstream = jnp.concatenate(
            [grad_scr[i, :, h * head_dim : (h + 1) * head_dim] for i in range(n)], axis=0
        )
        for i in range(n):
            weights_i = weights[h, i * rows : (i + 1) * rows, :].astype(f32)
            grad_weights = dot_nt(upstream[i * rows : (i + 1) * rows, :], value)
            inner = jnp.sum(weights_i * grad_weights, axis=-1, keepdims=True)
            grad_scores = weights_i * (grad_weights - inner)
            scores_scr[i * rows : (i + 1) * rows, :] = grad_scores.astype(bf16)
            for j in range(n):
                block = grad_scores[:, j * rows : (j + 1) * rows]
                if abs(j - i) <= 1:
                    near[j - i] = near[j - i] + block
                elif j > i:
                    high_side = high_side + block
                else:
                    low_side = low_side + block
        for b in range(buckets):
            amount = jnp.zeros((1, rows), f32)
            for diff in (-1, 0, 1):
                if diff < 0 and b >= buckets // 2 or diff > 0 and b < buckets // 2:
                    continue
                amount = amount + jnp.sum(
                    jnp.where(steps[diff] == b, near[diff], 0.0), axis=0, keepdims=True
                )
            if b == buckets - 1:
                amount = amount + jnp.sum(high_side, axis=0, keepdims=True)
            if b == buckets // 2 - 1:
                amount = amount + jnp.sum(low_side, axis=0, keepdims=True)
            amount = jnp.sum(amount, axis=1, keepdims=True)
            table_total = jnp.where((line == h) & (lane == b), amount, table_total)
        grad_scores_all = scores_scr[...]
        projected_scr[:, h * head_dim : (h + 1) * head_dim] = dot(grad_scores_all, key).astype(bf16)
        projected_scr[:, part + h * head_dim : part + (h + 1) * head_dim] = dot_tn(
            grad_scores_all, query
        ).astype(bf16)
        projected_scr[:, 2 * part + h * head_dim : 2 * part + (h + 1) * head_dim] = dot_tn(
            weights[h], upstream
        ).astype(bf16)
    table_out[...] = table_total
    grad_projected = projected_scr[...]
    total_scr[...] = dot_tn(normed[...], grad_projected)
    for d in range(m):
        piece = part // m
        for t in range(n):
            start = pl.multiple_of(t * part + (e ^ d) * piece if m > 1 else t * part, row_tile)
            share_out[d][t] = total_scr[pl.ds(start, piece), :].astype(bf16)
    normed_scr[...] = dot_nt(grad_projected, weight[...]).astype(bf16).reshape(n, rows, width)
    for p in range(n):
        normed_grad_out[p][...] = normed_scr[s ^ p]


def expert_forward(n, rows, *refs):
    row_refs = refs[:n]
    up, down, hidden_out, slope_out = refs[n : n + 4]
    keep_out, send_out = refs[n + 4 :]
    for p in range(n):
        before = dot(row_refs[p][...], up[0])
        square = before * before
        tanh_value = jnp.tanh(gelu_scale * before * (1.0 + gelu_cubic * square))
        half = 0.5 * (1.0 + tanh_value)
        hidden = (before * half).astype(bf16)
        slope = half + 0.5 * before * (1.0 - tanh_value * tanh_value) * gelu_scale * (
            1.0 + 3.0 * gelu_cubic * square
        )
        hidden_out[p * rows : (p + 1) * rows, :] = hidden
        slope_out[p * rows : (p + 1) * rows, :] = slope.astype(bf16)
        result = dot(hidden, down[0]).astype(bf16)
        target = send_out if p & 1 else keep_out
        at = (p >> 1) * rows
        target[at : at + rows, :] = result


def expert_backward(n, rows, *refs):
    grad_refs = refs[:n]
    up, down, slope, before_out = refs[n : n + 4]
    keep_out, send_out = refs[n + 4 :]
    for p in range(n):
        grad_hidden = dot_nt(grad_refs[p][...], down[0])
        grad_before = (grad_hidden * slope[p * rows : (p + 1) * rows, :].astype(f32)).astype(bf16)
        before_out[p * rows : (p + 1) * rows, :] = grad_before
        result = dot_nt(grad_before, up[0]).astype(bf16)
        target = send_out if p & 1 else keep_out
        at = (p >> 1) * rows
        target[at : at + rows, :] = result


def expert_weights(n, *refs):
    row_refs = refs[:n]
    grad_refs = refs[n : 2 * n]
    hidden, grad_before, up_out, down_out = refs[2 * n :]
    grads = jnp.concatenate([r[...] for r in grad_refs], axis=0)
    rows = jnp.concatenate([r[...] for r in row_refs], axis=0)
    down_out[0] = dot_tn(hidden[...], grads)
    up_out[0] = dot_tn(rows, grad_before[...])


def reduce_shard(keep, send, rows):
    came = swap(send, "shard", 1)
    forward = (keep[rows:].astype(f32) + came[rows:].astype(f32)).astype(bf16)
    own = keep[:rows].astype(f32) + came[:rows].astype(f32)
    return (own + swap(forward, "shard", 2).astype(f32)).astype(bf16)


def rms_factor(value):
    return lax.rsqrt(jnp.mean(value * value, axis=-1, keepdims=True) + norm_eps)


def rms_backward(value, factor, gain, upstream):
    scaled = upstream * gain
    grad_value = factor * scaled - value * factor * factor * factor * jnp.mean(
        scaled * value, axis=-1, keepdims=True
    )
    grad_gain = jnp.sum(upstream * value * factor, axis=0)
    return (grad_value, grad_gain)


def local(
    tokens,
    lengths,
    routes,
    attention_in,
    attention_out,
    position_bias,
    first_gain,
    second_gain,
    router,
    expert_in,
    expert_out,
    cotangent,
):
    n = lax.axis_size("shard")
    m = lax.axis_size("expert")
    s = lax.axis_index("shard")
    e = lax.axis_index("expert")
    index = jnp.stack([s, e]).astype(jnp.int32)
    rows, width = tokens.shape
    heads, buckets = position_bias.shape
    part = width // n
    seqs = lengths.shape[1]
    experts = router.shape[1]
    direct = m <= 8

    gains = jnp.zeros((gain_rows, width), bf16)
    gains = lax.dynamic_update_slice(gains, jnp.stack([first_gain, second_gain]), (0, s * part))
    token_blocks = gather_relative(jnp.concatenate([tokens, gains], axis=0), "shard")
    by_target = attention_in.reshape(part, 3, n, part).transpose(2, 0, 1, 3).reshape(n, part, 3 * part)
    weight_blocks = exchange_relative(
        [lax.dynamic_index_in_dim(by_target, s ^ p, 0, keepdims=False) for p in range(n)], "shard"
    )
    out_blocks = gather_relative(attention_out, "shard")
    gain_one, gain_two = (
        sum(block[rows + i : rows + i + 1].astype(f32) for block in token_blocks) for i in range(2)
    )

    group = n * rows
    head_flops = 2 * heads * group * group * (part // heads)
    answers = call(
        lambda *refs: attention_forward(n, rows, width, heads, seqs, buckets, *refs),
        (
            shape((group, width)),
            shape((width, 3 * part)),
            shape((group, 3 * part)),
            shape((heads, group, group)),
            *[shape((rows, part))] * n,
        ),
        (index, lengths, position_bias.astype(f32), *token_blocks, *weight_blocks),
        "sss",
        [pltpu.VMEM((n, rows, width), bf16), pltpu.VMEM((n, rows, part), bf16)],
        flops=2 * group * width * 3 * part + 8 * head_flops,
        size=8 * 2**20,
    )
    normed, weight, projected, weights = answers[:4]
    mixed_mine = answers[4:]
    mixed_blocks = exchange_relative(list(mixed_mine), "shard")

    inputs = tokens.astype(f32)
    hidden_one = inputs + sum(dot(mixed_blocks[p], out_blocks[p]) for p in range(n))
    factor_two = rms_factor(hidden_one)
    normed_two = hidden_one * factor_two * gain_two
    logits = jnp.dot(
        normed_two, router, precision=lax.Precision.HIGHEST, preferred_element_type=f32
    )
    shifted = jnp.exp(logits - jnp.max(logits, axis=-1, keepdims=True))
    probs = shifted / jnp.sum(shifted, axis=-1, keepdims=True)
    route = routes[:, 0]
    chosen = (route[:, None] == lax.iota(jnp.int32, experts)[None, :]).astype(f32)
    gate = jnp.sum(probs * chosen, axis=1)
    lower = (lax.iota(jnp.int32, rows)[:, None] >= lax.iota(jnp.int32, rows)[None, :]).astype(bf16)
    running = dot(lower, chosen.astype(bf16))
    slot = jnp.sum((running - 1.0) * chosen, axis=1).astype(jnp.int32)
    capacity = max(2, 9 * rows // (8 * experts) + 1)
    capacity = -(-capacity // row_tile) * row_tile
    holder = route ^ e if direct else route
    target = holder * capacity + slot
    places = experts * capacity
    collect = (target[:, None] == lax.iota(jnp.int32, places)[None, :]).astype(bf16)
    upstream = cotangent.astype(f32)
    grad_result = (gate[:, None] * upstream).astype(bf16)

    def send(value):
        if not direct:
            return lax.all_to_all(
                value.reshape(experts, capacity, width), "expert", 0, 0, tiled=True
            ).reshape(places, width)
        return jnp.concatenate(
            exchange_relative(
                [value[d * capacity : (d + 1) * capacity] for d in range(experts)], "expert"
            ),
            axis=0,
        )

    arrived = send(dot_tn(collect, normed_two.astype(bf16)).astype(bf16))
    row_blocks = gather_relative(arrived, "shard")
    arrived_grad = send(dot_tn(collect, grad_result).astype(bf16))
    grad_blocks = gather_relative(arrived_grad, "shard")

    units = expert_in.shape[2]
    all_rows = n * places
    expert_flops = 2 * all_rows * width * units
    hidden, slope, keep, out = call(
        lambda *refs: expert_forward(n, places, *refs),
        (
            shape((all_rows, units)),
            shape((all_rows, units)),
            shape((all_rows // 2, width)),
            shape((all_rows // 2, width)),
        ),
        (*row_blocks, expert_in, expert_out),
        flops=2 * expert_flops,
        size=6 * 2**20,
    )
    returned = send(reduce_shard(keep, out, places))
    grad_before, keep_grad, out_grad = call(
        lambda *refs: expert_backward(n, places, *refs),
        (
            shape((all_rows, units)),
            shape((all_rows // 2, width)),
            shape((all_rows // 2, width)),
        ),
        (*grad_blocks, expert_in, expert_out, slope),
        flops=2 * expert_flops,
        size=6 * 2**20,
    )
    returned_grad = send(reduce_shard(keep_grad, out_grad, places))
    grad_up, grad_down = call(
        lambda *refs: expert_weights(n, *refs),
        (shape(expert_in.shape, f32), shape(expert_out.shape, f32)),
        (*row_blocks, *grad_blocks, hidden, grad_before),
        flops=2 * expert_flops,
        size=9 * 2**20,
    )

    expert_result = dot(collect, returned)
    layer_out = (hidden_one + gate[:, None] * expert_result).astype(bf16)
    grad_gate = jnp.sum(upstream * expert_result, axis=1)
    grad_logits = (grad_gate * gate)[:, None] * (chosen - probs)
    grad_router = lax.dot_general(
        normed_two,
        grad_logits,
        (((0,), (0,)), ((), ())),
        precision=lax.Precision.HIGHEST,
        preferred_element_type=f32,
    )
    grad_normed_two = dot(collect, returned_grad) + lax.dot_general(
        grad_logits,
        router,
        (((1,), (1,)), ((), ())),
        precision=lax.Precision.HIGHEST,
        preferred_element_type=f32,
    )
    grad_middle, grad_gain_two = rms_backward(hidden_one, factor_two, gain_two, grad_normed_two)
    grad_hidden = upstream + grad_middle
    grad_branch = grad_hidden.astype(bf16)
    grad_mixed_blocks = exchange_relative(
        [dot_nt(grad_branch, out_blocks[p]).astype(bf16) for p in range(n)], "shard"
    )
    branch_blocks = gather_relative(grad_branch, "shard")
    holders = m if direct else 1

    answers = call(
        lambda *refs: attention_backward(n, holders, rows, width, heads, buckets, *refs),
        (
            *[shape((n, part // holders, 3 * part))] * holders,
            *[shape((rows, width))] * n,
            shape((row_tile, 128), f32),
        ),
        (index, projected, normed, weight, weights, *grad_mixed_blocks),
        "s",
        [
            pltpu.VMEM((n, rows, part), bf16),
            pltpu.VMEM((group, group), bf16),
            pltpu.VMEM((group, 3 * part), bf16),
            pltpu.VMEM((width, 3 * part), f32),
            pltpu.VMEM((n, rows, width), bf16),
        ],
        flops=8 * head_flops,
        size=8 * 2**20,
    )
    piece = part // m
    grad_weight_out = sum(dot_tn(mixed_mine[p], branch_blocks[p]) for p in range(n))

    shares = list(answers[:holders])
    normed_grads = answers[holders : holders + n]
    grad_table = answers[holders + n][:heads, :buckets]

    def spread(blocks):
        if direct:
            return exchange_relative(blocks, "expert")
        return list(lax.all_to_all(blocks, "expert", 0, 0, tiled=True))

    def gather(value):
        if direct:
            stacked = jnp.stack(gather_relative(value, "expert"))
            return stacked[lax.iota(jnp.int32, m) ^ e]
        return lax.all_gather(value, "expert", axis=0, tiled=False)

    if direct:
        out_shares = [
            lax.dynamic_slice_in_dim(grad_weight_out, (e ^ d) * piece, piece, 0).astype(bf16)
            for d in range(m)
        ]
    else:
        out_shares = grad_weight_out.astype(bf16).reshape(m, piece, width)
        shares = shares[0].reshape(n, m, piece, 3 * part).swapaxes(0, 1)
    total_out = sum(x.astype(f32) for x in spread(out_shares)).astype(bf16)
    grad_attention_out = gather(total_out).astype(f32).reshape(part, width)

    summed = sum(x.astype(f32) for x in spread(shares)).astype(bf16)
    mine = exchange_relative(
        [lax.dynamic_index_in_dim(summed, s ^ p, 0, keepdims=False) for p in range(n)], "shard"
    )
    mine = jnp.stack(mine)[lax.iota(jnp.int32, n) ^ s]
    mine = mine.reshape(n, piece, 3, part).transpose(1, 2, 0, 3).reshape(piece, 3 * width)
    grad_attention_in = gather(mine).astype(f32).reshape(part, 3 * width)

    grad_normed = sum(x.astype(f32) for x in exchange_relative(list(normed_grads), "shard"))
    grad_input_norm, grad_gain_one = rms_backward(inputs, rms_factor(inputs), gain_one, grad_normed)
    grad_tokens = (grad_hidden + grad_input_norm).astype(bf16)

    small = jnp.concatenate([grad_gain_one[:, None], grad_gain_two[:, None], grad_router], axis=1)
    small_total = lax.psum(small, ("expert", "shard"))
    small_mine = lax.dynamic_slice_in_dim(small_total, s * part, part, 0)
    table_total = lax.psum(grad_table, "expert")
    return (
        layer_out,
        grad_tokens,
        grad_attention_in,
        grad_attention_out,
        table_total,
        small_mine[:, 0],
        small_mine[:, 1],
        small_mine[:, 2:],
        grad_up,
        grad_down,
    )


def solution(mesh):
    in_specs = (
        P(("expert", "shard"), None),
        P("expert", None),
        P(("expert", "shard"), None),
        P("shard", None),
        P("shard", None),
        P("shard", None),
        P("shard"),
        P("shard"),
        P(),
        P("expert", None, "shard"),
        P("expert", "shard", None),
        P(("expert", "shard"), None),
    )
    out_specs = (
        P(("expert", "shard"), None),
        P(("expert", "shard"), None),
        P("shard", None),
        P("shard", None),
        P("shard", None),
        P("shard"),
        P("shard"),
        P("shard", None),
        P("expert", None, "shard"),
        P("expert", "shard", None),
    )
    return jax.shard_map(local, mesh=mesh, in_specs=in_specs, out_specs=out_specs, check_vma=False)
```

time: 500 us -> 304 us (0.61)
  waiting for transfers between devices: 176 us -> 64.9 us
  blocking collectives: 139 us -> 58.9 us
  starting transfers between devices: 19.4 us -> 95.5 us
  matrix products: 80.4 us -> 7.51 us
  Pallas kernels: 0 us -> 36.5 us
  local copies, waits for them, and re-layouts: 49.6 us -> 23 us
  between operations: 16.4 us -> 1.66 us
    ppermute x0 -> x90, starting transfers between devices: none -> 95.5 us  [swap(): return lax.ppermute(value, axis, [(i, i ^ bit) for i in range(size)])]
    dot_general x77 -> x17, matrix products: 77.8 us -> 5.46 us  [the longest x6 2.72 us: dot_tn(): lax.dot_general(left, right, (((0,), (0,)), ((), ())), preferred_element_...]
    ppermute x0 -> x90, waiting for transfers between devices: none -> 64.9 us  [swap(): return lax.ppermute(value, axis, [(i, i ^ bit) for i in range(size)])]
    reduce_scatter x4 -> x0, waiting for transfers between devices: 60.9 us -> none  [the longest x1 43.2 us: local(): lax.psum_scatter(grad_w_in_attn.astype(jnp.bfloat16), 'shard', scatter_di...]
    unnamed x14 -> x0, waiting for transfers between devices: 52.6 us -> none
    psum x1 -> x2, blocking collectives: 101 us -> 58.9 us  [the longest x1 37.8 us: local(): small_total = lax.psum(small, ('expert', 'shard'))]
    pallas_call x0 -> x5, Pallas kernels: none -> 36.5 us  [call(): pl.pallas_call(kernel, out_shape=out_shape, in_specs=in_specs, out_specs=...]
    all_gather x4 -> x0, waiting for transfers between devices: 35.3 us -> none  [the longest x1 18.9 us: local(): lax.all_gather(expert_out, 'shard', axis=1, tiled=True)]
  transfers between devices with their start and end apart: 15 -> 90, of which waited for: 11 -> 27; matrix products, arithmetic and copies ran while one was open for 14% -> 11% of each run, Pallas kernels for 0% -> 10%
where the time goes in v1:
time: 304 us; the launch traced here: 303 us
  starting transfers between devices  95.5 us (31%)
  waiting for transfers between devices  64.9 us (21%)
  blocking collectives  58.9 us (19%)
  Pallas kernels  36.5 us (12%)
  local copies, waits for them, and re-layouts  23 us (8%)
  other arithmetic  15.3 us (5%)
  matrix products  7.51 us (2%)
    ppermute x90, starting transfers between devices, swap(): return lax.ppermute(value, axis, [(i, i ^ bit) for i in range(size)])  95.5 us
    ppermute x90, waiting for transfers between devices, swap(): return lax.ppermute(value, axis, [(i, i ^ bit) for i in range(size)])  64.9 us
    psum x1, blocking collectives, local(): small_total = lax.psum(small, ('expert', 'shard'))  37.8 us
    pallas_call x5, Pallas kernels, call(): pl.pallas_call(kernel, out_shape=out_shape, in_specs=in_specs, out_specs=...  36.5 us
    psum x1, blocking collectives, local(): table_total = lax.psum(grad_table, 'expert')  21.2 us
    unnamed x111, local copies, waits for them, and re-layouts  8.31 us
  transfers between devices with their start and end apart: 90, of which 27 were waited for; matrix products, arithmetic and copies ran while one was open for 11% of the time, Pallas kernels for 10%

profile of v1, /device:TPU:0, one launch (start us, length us, event | category | flops | bytes accessed | tf_op | source)
XLA Modules:
  0.0 303.3 jit_solution(4938479471755302220)
XLA Ops:
  6.5 2.9 reshape.112
  16.5 10.0 %collective-permute-done.9 = bf16[192,768]{1,0:T(8,128)(2,1)S(1)} collective-permute-done((bf16[192,768]{1,0:T(8,128)(2,1)S(1)}, bf16[192,768]{1,0:T(8,128)(2,1)S(1)}, u32[]{:S(2)}, u32[]{:S(2)}) %collective-permute-start.9) | collective-permute-done | bytes 294944 | tf_op jit(solution)/shard_map/ppermute | solution.py:43
  26.5 4.1 %collective-permute-done.5.refs_10_ = bf16[192,576]{1,0:T(8,128)(2,1)S(1)} collective-permute-done((bf16[192,576]{1,0:T(8,128)(2,1)S(1)}, bf16[192,576]{1,0:T(8,128)(2,1)S(1)}, u32[]{:S(2)}, u32[]{:S(2)}) %collective-permute-start.5) | collective-permute-done | bytes 221216 | tf_op jit(solution)/shard_map/ppermute | solution.py:43
  31.4 9.7 %shard_map.195 = (bf16[512,768]{1,0:T(8,128)(2,1)}, bf16[768,576]{1,0:T(8,128)(2,1)}, bf16[512,576]{1,0:T(8,128)(2,1)}, bf16[3,512,512]{2,1,0:T(8,128)(2,1)}, bf...) custom-call(s32[2]{0:T(128)} %pad_add_fusion.refs_0_, ...), custom_call_target="tpu_custom_call" | custom-call | flops 1258291200 | bytes 8388608 | tf_op jit(solution)/shard_map/pallas_call | solution.py:66
  51.7 2.6 collective-permute-start.15
  56.6 3.7 %collective-permute-start.17 = (bf16[24,768]{1,0:T(8,128)(2,1)S(1)}, bf16[24,768]{1,0:T(8,128)(2,1)S(1)}, u32[]{:S(2)}, u32[]{:S(2)}) collective-permute-start(bf16[24,768]{1,0:T(8,128)(2,1)S(1)} %get-tuple-element.116), channel_id=1, source_target_pairs={{0,24},{4,28},{8,16},{12,20},{16,8},{20,12},{24,0},{28,4},{1,25},{... | collective-permute-start | bytes 110600 | tf_op jit(solution)/shard_map/ppermute | solution.py:43
  67.9 3.7 %collective-permute-start.36 = (bf16[24,768]{1,0:T(8,128)(2,1)S(1)}, bf16[24,768]{1,0:T(8,128)(2,1)S(1)}, u32[]{:S(2)}, u32[]{:S(2)}) collective-permute-start(bf16[24,768]{1,0:T(8,128)(2,1)S(1)} %get-tuple-element.100), channel_id=1, source_target_pairs={{0,24},{4,28},{8,16},{12,20},{16,8},{20,12},{24,0},{28,4},{1,25},{... | collective-permute-start | bytes 110600 | tf_op jit(solution)/shard_map/ppermute | solution.py:43
  71.8 2.3 collective-permute-done.35
  74.2 4.0 %collective-permute-done.37 = bf16[24,768]{1,0:T(8,128)(2,1)S(1)} collective-permute-done((bf16[24,768]{1,0:T(8,128)(2,1)S(1)}, bf16[24,768]{1,0:T(8,128)(2,1)S(1)}, u32[]{:S(2)}, u32[]{:S(2)}) %collective-permute-start.37) | collective-permute-done | bytes 36896 | tf_op jit(solution)/shard_map/ppermute | solution.py:43
  78.3 2.9 collective-permute-done.20.refs_2_
  81.7 3.2 %collective-permute-done.39.refs_2_.refs_6_ = bf16[192,768]{1,0:T(8,128)(2,1)S(1)} collective-permute-done((bf16[192,768]{1,0:T(8,128)(2,1)S(1)}, bf16[192,768]{1,0:T(8,128)(2,1)S(1)}, u32[]{:S(2)}, u32[]{:S(2)}) %collective-permute-start.39) | collective-permute-done | bytes 294944 | tf_op jit(solution)/shard_map/ppermute | solution.py:43
  86.5 6.8 %shard_map.196 = (bf16[768,768]{1,0:T(8,128)(2,1)}, bf16[768,768]{1,0:T(8,128)(2,1)}, bf16[384,768]{1,0:T(8,128)(2,1)}, bf16[384,768]{1,0:T(8,128)(2,1)}) custom-call(bf16[192,768]{1,0:T(8,128)(2,1)} %copy-done.20, bf16[192,768]{1,0:T(8,128)(2,1)} %copy-done.31, bf16[192,768]{1,0:T(8,128)(2,1)} %copy-done.29, bf16[192,768]{1,0:T(8,128)(2,1)} %copy-done.32, ...), custom_call_target="tpu_custom_call" | custom-call | flops 1811939328 | bytes 6291456 | tf_op jit(solution)/shard_map/pallas_call | solution.py:66
  94.7 6.2 %shard_map.197 = (bf16[768,768]{1,0:T(8,128)(2,1)}, bf16[384,768]{1,0:T(8,128)(2,1)}, bf16[384,768]{1,0:T(8,128)(2,1)}) custom-call(bf16[192,768]{1,0:T(8,128)(2,1)} %copy-done.19, bf16[192,768]{1,0:T(8,128)(2,1)} %copy-done.33, bf16[192,768]{1,0:T(8,128)(2,1)} %copy-done.30, bf16[192,768]{1,0:T(8,128)(2,1)} %copy-done.34, bf16[1,768,768]{2,1,0:T(8,128)(2,1)} %refs_4_.3, ...), custom_call_target="tpu_custom_call" | custom-call | flops 1811939328 | bytes 6291456 | tf_op jit(solution)/shard_map/pallas_call | solution.py:66
  106.1 6.5 %collective-permute-done.23 = bf16[192,768]{1,0:T(8,128)(2,1)S(1)} collective-permute-done((bf16[192,768]{1,0:T(8,128)(2,1)S(1)}, bf16[192,768]{1,0:T(8,128)(2,1)S(1)}, u32[]{:S(2)}, u32[]{:S(2)}) %collective-permute-start.23) | collective-permute-done | bytes 294944 | tf_op jit(solution)/shard_map/ppermute | solution.py:43
  114.6 2.8 collective-permute-start.26
  123.7 2.5 collective-permute-start.30
  127.0 2.7 collective-permute-start.45
  135.9 2.5 collective-permute-start.49
  139.7 2.9 collective-permute-done.49
  150.7 7.6 %shard_map.198 = (bf16[4,24,576]{2,1,0:T(8,128)(2,1)}, bf16[4,24,576]{2,1,0:T(8,128)(2,1)}, bf16[4,24,576]{2,1,0:T(8,128)(2,1)}, bf16[4,24,576]{2,1,0:T(8,128)(2...) custom-call(s32[2]{0:T(128)} %pad_add_fusion.refs_0_, ...), custom_call_target="tpu_custom_call" | custom-call | flops 805306368 | bytes 8388608 | tf_op jit(solution)/shard_map/pallas_call | solution.py:66
  158.3 2.6 collective-permute-start.62
  162.7 3.9 %collective-permute-start.59 = (bf16[4,24,576]{2,1,0:T(8,128)(2,1)}, bf16[4,24,576]{2,1,0:T(8,128)(2,1)S(1)}, u32[]{:S(2)}, u32[]{:S(2)}) collective-permute-start(bf16[4,24,576]{2,1,0:T(8,128)(2,1)} %get-tuple-element.61), channel_id=1, source_target_pairs={{0,16},{4,20},{8,24},{12,28},{16,0},{20,4},{24,8},{28,12},{1,17},{... | collective-permute-start | bytes 331784 | tf_op jit(solution)/shard_map/ppermute | solution.py:43
  170.7 6.2 %shard_map.199 = (f32[1,768,768]{2,1,0:T(8,128)}, f32[1,768,768]{2,1,0:T(8,128)}) custom-call(bf16[192,768]{1,0:T(8,128)(2,1)} %copy-done.20, bf16[192,768]{1,0:T(8,128)(2,1)} %copy-done.31, bf16[192,768]{1,0:T(8,128)(2,1)} %copy-done.29, bf16[192,768]{1,0:T(8,128)(2,1)} %copy-done.32, bf16[192,768]{1,0:T(8,128)(2,1)} %copy-done.19, ...), custom_call_target="tpu_custom_call" | custom-call | flops 1811939328 | bytes 9437184 | tf_op jit(solution)/shard_map/pallas_call | solution.py:66
  184.2 21.2 %psum.14 = f32[3,32]{1,0:T(4,128)} all-reduce(f32[3,32]{1,0:T(4,128)S(1)} %slice.204), channel_id=1, replica_groups=mesh['expert'=8,'shard'=4] {'expert'}, use_global_device_ids=true, to_apply=%region_9.10 | all-reduce | flops 96 | bytes 768 | tf_op jit(solution)/shard_map/psum | solution.py:520
  212.8 3.4 %collective-permute-done.54 = bf16[128,768]{1,0:T(8,128)(2,1)} collective-permute-done((bf16[128,768]{1,0:T(8,128)(2,1)}, bf16[128,768]{1,0:T(8,128)(2,1)}, u32[]{:S(2)}, u32[]{:S(2)}) %collective-permute-start.54) | collective-permute-done | bytes 196640 | tf_op jit(solution)/shard_map/ppermute | solution.py:43
  218.3 37.8 %psum.15 = f32[768,10]{0,1:T(8,128)} all-reduce(f32[768,10]{0,1:T(8,128)S(1)} %pad_maximum_fusion.2), channel_id=1, replica_groups=mesh['expert'=8,'shard'=4] {'expert','shard'}, use_global_device_ids=true, to_apply=%region_12.13 | all-reduce | flops 7680 | bytes 61440 | tf_op jit(solution)/shard_map/psum | solution.py:518
  263.6 2.9 collective-permute-start.71
  268.6 3.0 collective-permute-start.82
  274.8 2.5 collective-permute-start.79
  278.0 2.8 collective-permute-start.77
  287.1 3.2 %collective-permute-done.86 = bf16[24,768]{1,0:T(8,128)(2,1)S(1)} collective-permute-done((bf16[24,768]{1,0:T(8,128)(2,1)S(1)}, bf16[24,768]{1,0:T(8,128)(2,1)S(1)}, u32[]{:S(2)}, u32[]{:S(2)}) %collective-permute-start.86) | collective-permute-done | bytes 36896 | tf_op jit(solution)/shard_map/ppermute | solution.py:43
  293.9 3.9 %collective-permute-done.85 = bf16[24,768]{1,0:T(8,128)(2,1)S(1)} collective-permute-done((bf16[24,768]{1,0:T(8,128)(2,1)S(1)}, bf16[24,768]{1,0:T(8,128)(2,1)S(1)}, u32[]{:S(2)}, u32[]{:S(2)}) %collective-permute-start.85) | collective-permute-done | bytes 36896 | tf_op jit(solution)/shard_map/ppermute | solution.py:43
  (356 shorter events, 119.0 us)
Async XLA Ops:
  3.4 12.4 %collective-permute-start = (bf16[144,768]{1,0:T(8,128)(2,1)S(1)}, bf16[144,768]{1,0:T(8,128)(2,1)S(1)}, u32[]{:S(2)}, u32[]{:S(2)}) collective-permute-start(bf16[144,768]{1,0:T(8,128)(2,1)S(1)} %pad_maximum_fusion.refs_3_), channel_id=1, source_target_pairs={{0,1},{1,0},{2,3},{3,2},{4,5},{5,4},{6,7},{7,6},{8,9},{9,8},{10,11... | collective-permute-start | bytes 663560 | tf_op jit(solution)/shard_map/ppermute | solution.py:43
  4.2 11.6 %collective-permute-start.1 = (bf16[144,768]{1,0:T(8,128)(2,1)S(1)}, bf16[144,768]{1,0:T(8,128)(2,1)}, u32[]{:S(2)}, u32[]{:S(2)}) collective-permute-start(bf16[144,768]{1,0:T(8,128)(2,1)S(1)} %pad_maximum_fusion.refs_3_), channel_id=1, source_target_pairs={{0,2},{1,3},{2,0},{3,1},{4,6},{5,7},{6,4},{7,5},{8,10},{9,11},{10,... | collective-permute-start | bytes 663560 | tf_op jit(solution)/shard_map/ppermute | solution.py:43
  11.3 15.2 %collective-permute-start.4 = (bf16[192,576]{1,0:T(8,128)(2,1)S(1)}, bf16[192,576]{1,0:T(8,128)(2,1)}, u32[]{:S(2)}, u32[]{:S(2)}) collective-permute-start(bf16[192,576]{1,0:T(8,128)(2,1)S(1)} %bitcast.99), channel_id=1, source_target_pairs={{0,2},{1,3},{2,0},{3,1},{4,6},{5,7},{6,4},{7,5},{8,10},{9,11},{10,... | collective-permute-start | bytes 663560 | tf_op jit(solution)/shard_map/ppermute | solution.py:43
  11.6 14.8 %collective-permute-start.9 = (bf16[192,768]{1,0:T(8,128)(2,1)S(1)}, bf16[192,768]{1,0:T(8,128)(2,1)S(1)}, u32[]{:S(2)}, u32[]{:S(2)}) collective-permute-start(bf16[192,768]{1,0:T(8,128)(2,1)S(1)} %copy-done.3), channel_id=1, source_target_pairs={{0,2},{1,3},{2,0},{3,1},{4,6},{5,7},{6,4},{7,5},{8,10},{9,11},{10,... | collective-permute-start | bytes 884744 | tf_op jit(solution)/shard_map/ppermute | solution.py:43
  15.8 14.8 %collective-permute-start.5 = (bf16[192,576]{1,0:T(8,128)(2,1)S(1)}, bf16[192,576]{1,0:T(8,128)(2,1)S(1)}, u32[]{:S(2)}, u32[]{:S(2)}) collective-permute-start(bf16[192,576]{1,0:T(8,128)(2,1)S(1)} %bitcast.101), channel_id=1, source_target_pairs={{0,3},{1,2},{2,1},{3,0},{4,7},{5,6},{6,5},{7,4},{8,11},{9,10},{10,... | collective-permute-start | bytes 663560 | tf_op jit(solution)/shard_map/ppermute | solution.py:43
  15.8 14.7 %collective-permute-start.2 = (bf16[144,768]{1,0:T(8,128)(2,1)}, bf16[144,768]{1,0:T(8,128)(2,1)S(1)}, u32[]{:S(2)}, u32[]{:S(2)}) collective-permute-start(bf16[144,768]{1,0:T(8,128)(2,1)} %collective-permute-done.1.refs_5_), channel_id=1, source_target_pairs={{0,1},{1,0},{2,3},{3,2},{4,5},{5,4},{6,7},{7,6},{8,9},{9,8},{10,11... | collective-permute-start | bytes 663560 | tf_op jit(solution)/shard_map/ppermute | solution.py:43
  16.2 30.3 %collective-permute-start.7 = (bf16[192,768]{1,0:T(8,128)(2,1)S(1)}, bf16[192,768]{1,0:T(8,128)(2,1)S(1)}, u32[]{:S(2)}, u32[]{:S(2)}) collective-permute-start(bf16[192,768]{1,0:T(8,128)(2,1)S(1)} %copy-done.3), channel_id=1, source_target_pairs={{0,1},{1,0},{2,3},{3,2},{4,5},{5,4},{6,7},{7,6},{8,9},{9,8},{10,11... | collective-permute-start | bytes 884744 | tf_op jit(solution)/shard_map/ppermute | solution.py:43
  26.5 20.5 %collective-permute-start.11 = (bf16[192,768]{1,0:T(8,128)(2,1)S(1)}, bf16[192,768]{1,0:T(8,128)(2,1)S(1)}, u32[]{:S(2)}, u32[]{:S(2)}) collective-permute-start(bf16[192,768]{1,0:T(8,128)(2,1)S(1)} %collective-permute-done.9), channel_id=1, source_target_pairs={{0,1},{1,0},{2,3},{3,2},{4,5},{5,4},{6,7},{7,6},{8,9},{9,8},{10,11... | collective-permute-start | bytes 884744 | tf_op jit(solution)/shard_map/ppermute | solution.py:43
  49.7 10.5 %collective-permute-start.13 = (bf16[24,768]{1,0:T(8,128)(2,1)S(1)}, bf16[24,768]{1,0:T(8,128)(2,1)S(1)}, u32[]{:S(2)}, u32[]{:S(2)}) collective-permute-start(bf16[24,768]{1,0:T(8,128)(2,1)S(1)} %get-tuple-element.120), channel_id=1, source_target_pairs={{0,8},{4,12},{8,0},{12,4},{16,24},{20,28},{24,16},{28,20},{1,9},{5... | collective-permute-start | bytes 110600 | tf_op jit(solution)/shard_map/ppermute | solution.py:43
  51.7 10.3 %collective-permute-start.15 = (bf16[24,768]{1,0:T(8,128)(2,1)S(1)}, bf16[24,768]{1,0:T(8,128)(2,1)S(1)}, u32[]{:S(2)}, u32[]{:S(2)}) collective-permute-start(bf16[24,768]{1,0:T(8,128)(2,1)S(1)} %get-tuple-element.118), channel_id=1, source_target_pairs={{0,16},{4,20},{8,24},{12,28},{16,0},{20,4},{24,8},{28,12},{1,17},{... | collective-permute-start | bytes 110600 | tf_op jit(solution)/shard_map/ppermute | solution.py:43
  81.2 12.7 %collective-permute-start.38 = (bf16[192,768]{1,0:T(8,128)(2,1)S(1)}, bf16[192,768]{1,0:T(8,128)(2,1)S(1)}, u32[]{:S(2)}, u32[]{:S(2)}) collective-permute-start(bf16[192,768]{1,0:T(8,128)(2,1)S(1)} %constant_dynamic-update-slice_fusion.16.refs_0_.refs_4_), channel_id=1, source_target_pairs={{0,1},{1,0},{2,3},{3,2},{4,5},{5,4},{6,7},{7,6},{8,9},{9,8},{10,11... | collective-permute-start | bytes 884744 | tf_op jit(solution)/shard_map/ppermute | solution.py:43
  104.4 14.1 %collective-permute-start.42 = (bf16[192,768]{1,0:T(8,128)(2,1)S(1)}, bf16[192,768]{1,0:T(8,128)(2,1)S(1)}, u32[]{:S(2)}, u32[]{:S(2)}) collective-permute-start(bf16[192,768]{1,0:T(8,128)(2,1)S(1)} %add_convert_fusion.1), channel_id=1, source_target_pairs={{0,2},{1,3},{2,0},{3,1},{4,6},{5,7},{6,4},{7,5},{8,10},{9,11},{10,... | collective-permute-start | bytes 884744 | tf_op jit(solution)/shard_map/ppermute | solution.py:43
  114.6 11.6 %collective-permute-start.26 = (bf16[24,768]{1,0:T(8,128)(2,1)S(1)}, bf16[24,768]{1,0:T(8,128)(2,1)S(1)}, u32[]{:S(2)}, u32[]{:S(2)}) collective-permute-start(bf16[24,768]{1,0:T(8,128)(2,1)S(1)} %get-tuple-element.111), channel_id=1, source_target_pairs={{0,12},{4,8},{8,4},{12,0},{16,28},{20,24},{24,20},{28,16},{1,13},{... | collective-permute-start | bytes 110600 | tf_op jit(solution)/shard_map/ppermute | solution.py:43
  127.0 11.4 %collective-permute-start.45 = (bf16[24,768]{1,0:T(8,128)(2,1)S(1)}, bf16[24,768]{1,0:T(8,128)(2,1)S(1)}, u32[]{:S(2)}, u32[]{:S(2)}) collective-permute-start(bf16[24,768]{1,0:T(8,128)(2,1)S(1)} %get-tuple-element.95), channel_id=1, source_target_pairs={{0,12},{4,8},{8,4},{12,0},{16,28},{20,24},{24,20},{28,16},{1,13},{... | collective-permute-start | bytes 110600 | tf_op jit(solution)/shard_map/ppermute | solution.py:43
  162.7 15.1 %collective-permute-start.60 = (bf16[4,24,576]{2,1,0:T(8,128)(2,1)}, bf16[4,24,576]{2,1,0:T(8,128)(2,1)S(1)}, u32[]{:S(2)}, u32[]{:S(2)}) collective-permute-start(bf16[4,24,576]{2,1,0:T(8,128)(2,1)} %get-tuple-element.62), channel_id=1, source_target_pairs={{0,20},{4,16},{8,28},{12,24},{16,4},{20,0},{24,12},{28,8},{1,21},{... | collective-permute-start | bytes 331784 | tf_op jit(solution)/shard_map/ppermute | solution.py:43
  162.7 18.1 %collective-permute-start.59 = (bf16[4,24,576]{2,1,0:T(8,128)(2,1)}, bf16[4,24,576]{2,1,0:T(8,128)(2,1)S(1)}, u32[]{:S(2)}, u32[]{:S(2)}) collective-permute-start(bf16[4,24,576]{2,1,0:T(8,128)(2,1)} %get-tuple-element.61), channel_id=1, source_target_pairs={{0,16},{4,20},{8,24},{12,28},{16,0},{20,4},{24,8},{28,12},{1,17},{... | collective-permute-start | bytes 331784 | tf_op jit(solution)/shard_map/ppermute | solution.py:43
  166.6 14.2 %collective-permute-start.58 = (bf16[4,24,576]{2,1,0:T(8,128)(2,1)}, bf16[4,24,576]{2,1,0:T(8,128)(2,1)S(1)}, u32[]{:S(2)}, u32[]{:S(2)}) collective-permute-start(bf16[4,24,576]{2,1,0:T(8,128)(2,1)} %get-tuple-element.60), channel_id=1, source_target_pairs={{0,12},{4,8},{8,4},{12,0},{16,28},{20,24},{24,20},{28,16},{1,13},{... | collective-permute-start | bytes 331784 | tf_op jit(solution)/shard_map/ppermute | solution.py:43
  167.5 13.3 %collective-permute-start.57 = (bf16[4,24,576]{2,1,0:T(8,128)(2,1)}, bf16[4,24,576]{2,1,0:T(8,128)(2,1)S(1)}, u32[]{:S(2)}, u32[]{:S(2)}) collective-permute-start(bf16[4,24,576]{2,1,0:T(8,128)(2,1)} %get-tuple-element.59), channel_id=1, source_target_pairs={{0,8},{4,12},{8,0},{12,4},{16,24},{20,28},{24,16},{28,20},{1,9},{5... | collective-permute-start | bytes 331784 | tf_op jit(solution)/shard_map/ppermute | solution.py:43
  169.1 11.7 %collective-permute-start.56 = (bf16[4,24,576]{2,1,0:T(8,128)(2,1)}, bf16[4,24,576]{2,1,0:T(8,128)(2,1)S(1)}, u32[]{:S(2)}, u32[]{:S(2)}) collective-permute-start(bf16[4,24,576]{2,1,0:T(8,128)(2,1)} %get-tuple-element.58), channel_id=1, source_target_pairs={{0,4},{4,0},{8,12},{12,8},{16,20},{20,16},{24,28},{28,24},{1,5},{5... | collective-permute-start | bytes 331784 | tf_op jit(solution)/shard_map/ppermute | solution.py:43
  177.7 31.5 %collective-permute-start.74 = (bf16[128,768]{1,0:T(8,128)(2,1)S(1)}, bf16[128,768]{1,0:T(8,128)(2,1)}, u32[]{:S(2)}, u32[]{:S(2)}) collective-permute-start(bf16[128,768]{1,0:T(8,128)(2,1)S(1)} %fusion.58), channel_id=1, source_target_pairs={{0,2},{1,3},{2,0},{3,1},{4,6},{5,7},{6,4},{7,5},{8,10},{9,11},{10,... | collective-permute-start | bytes 589832 | tf_op jit(solution)/shard_map/ppermute | solution.py:43
  180.8 29.8 %collective-permute-start.73 = (bf16[128,768]{1,0:T(8,128)(2,1)S(1)}, bf16[128,768]{1,0:T(8,128)(2,1)S(1)}, u32[]{:S(2)}, u32[]{:S(2)}) collective-permute-start(bf16[128,768]{1,0:T(8,128)(2,1)S(1)} %fusion.58), channel_id=1, source_target_pairs={{0,1},{1,0},{2,3},{3,2},{4,5},{5,4},{6,7},{7,6},{8,9},{9,8},{10,11... | collective-permute-start | bytes 589832 | tf_op jit(solution)/shard_map/ppermute | solution.py:43
  181.0 24.4 %collective-permute-start.65 = (bf16[24,576]{1,0:T(8,128)(2,1)S(1)}, bf16[24,576]{1,0:T(8,128)(2,1)S(1)}, u32[]{:S(2)}, u32[]{:S(2)}) collective-permute-start(bf16[24,576]{1,0:T(8,128)(2,1)S(1)} %get-tuple-element.124), channel_id=1, source_target_pairs={{0,3},{1,2},{2,1},{3,0},{4,7},{5,6},{6,5},{7,4},{8,11},{9,10},{10,... | collective-permute-start | bytes 82952 | tf_op jit(solution)/shard_map/ppermute | solution.py:43
  182.1 23.3 %collective-permute-start.64 = (bf16[24,576]{1,0:T(8,128)(2,1)S(1)}, bf16[24,576]{1,0:T(8,128)(2,1)S(1)}, u32[]{:S(2)}, u32[]{:S(2)}) collective-permute-start(bf16[24,576]{1,0:T(8,128)(2,1)S(1)} %get-tuple-element.125), channel_id=1, source_target_pairs={{0,2},{1,3},{2,0},{3,1},{4,6},{5,7},{6,4},{7,5},{8,10},{9,11},{10,... | collective-permute-start | bytes 82952 | tf_op jit(solution)/shard_map/ppermute | solution.py:43
  183.2 23.3 %collective-permute-start.63 = (bf16[24,576]{1,0:T(8,128)(2,1)S(1)}, bf16[24,576]{1,0:T(8,128)(2,1)S(1)}, u32[]{:S(2)}, u32[]{:S(2)}) collective-permute-start(bf16[24,576]{1,0:T(8,128)(2,1)S(1)} %get-tuple-element.126), channel_id=1, source_target_pairs={{0,1},{1,0},{2,3},{3,2},{4,5},{5,4},{6,7},{7,6},{8,9},{9,8},{10,11... | collective-permute-start | bytes 82952 | tf_op jit(solution)/shard_map/ppermute | solution.py:43
  205.4 10.8 %collective-permute-start.54 = (bf16[128,768]{1,0:T(8,128)(2,1)}, bf16[128,768]{1,0:T(8,128)(2,1)}, u32[]{:S(2)}, u32[]{:S(2)}) collective-permute-start(bf16[128,768]{1,0:T(8,128)(2,1)} %get-tuple-element.55), channel_id=1, source_target_pairs={{0,2},{1,3},{2,0},{3,1},{4,6},{5,7},{6,4},{7,5},{8,10},{9,11},{10,... | collective-permute-start | bytes 589832 | tf_op jit(solution)/shard_map/ppermute | solution.py:43
  209.2 57.3 %collective-permute-start.66 = (bf16[24,2304]{1,0:T(8,128)(2,1)}, bf16[24,2304]{1,0:T(8,128)(2,1)}, u32[]{:S(2)}, u32[]{:S(2)}) collective-permute-start(bf16[24,2304]{1,0:T(8,128)(2,1)} %reshape.115), channel_id=1, source_target_pairs={{0,4},{4,0},{8,12},{12,8},{16,20},{20,16},{24,28},{28,24},{1,5},{5... | collective-permute-start | bytes 331784 | tf_op jit(solution)/shard_map/ppermute | solution.py:43
  210.5 55.9 %collective-permute-start.67 = (bf16[24,2304]{1,0:T(8,128)(2,1)}, bf16[24,2304]{1,0:T(8,128)(2,1)}, u32[]{:S(2)}, u32[]{:S(2)}) collective-permute-start(bf16[24,2304]{1,0:T(8,128)(2,1)} %reshape.115), channel_id=1, source_target_pairs={{0,8},{4,12},{8,0},{12,4},{16,24},{20,28},{24,16},{28,20},{1,9},{5... | collective-permute-start | bytes 331784 | tf_op jit(solution)/shard_map/ppermute | solution.py:43
  212.8 48.5 %collective-permute-start.69 = (bf16[24,2304]{1,0:T(8,128)(2,1)}, bf16[24,2304]{1,0:T(8,128)(2,1)}, u32[]{:S(2)}, u32[]{:S(2)}) collective-permute-start(bf16[24,2304]{1,0:T(8,128)(2,1)} %reshape.115), channel_id=1, source_target_pairs={{0,16},{4,20},{8,24},{12,28},{16,0},{20,4},{24,8},{28,12},{1,17},{... | collective-permute-start | bytes 331784 | tf_op jit(solution)/shard_map/ppermute | solution.py:43
  216.2 52.1 %collective-permute-start.75 = (bf16[128,768]{1,0:T(8,128)(2,1)}, bf16[128,768]{1,0:T(8,128)(2,1)S(1)}, u32[]{:S(2)}, u32[]{:S(2)}) collective-permute-start(bf16[128,768]{1,0:T(8,128)(2,1)} %collective-permute-done.74), channel_id=1, source_target_pairs={{0,1},{1,0},{2,3},{3,2},{4,5},{5,4},{6,7},{7,6},{8,9},{9,8},{10,11... | collective-permute-start | bytes 589832 | tf_op jit(solution)/shard_map/ppermute | solution.py:43
  261.3 13.6 %collective-permute-start.70 = (bf16[24,2304]{1,0:T(8,128)(2,1)}, bf16[24,2304]{1,0:T(8,128)(2,1)S(1)}, u32[]{:S(2)}, u32[]{:S(2)}) collective-permute-start(bf16[24,2304]{1,0:T(8,128)(2,1)} %collective-permute-done.69), channel_id=1, source_target_pairs={{0,4},{4,0},{8,12},{12,8},{16,20},{20,16},{24,28},{28,24},{1,5},{5... | collective-permute-start | bytes 331784 | tf_op jit(solution)/shard_map/ppermute | solution.py:43
  263.6 13.8 %collective-permute-start.71 = (bf16[24,2304]{1,0:T(8,128)(2,1)}, bf16[24,2304]{1,0:T(8,128)(2,1)S(1)}, u32[]{:S(2)}, u32[]{:S(2)}) collective-permute-start(bf16[24,2304]{1,0:T(8,128)(2,1)} %collective-permute-done.69), channel_id=1, source_target_pairs={{0,8},{4,12},{8,0},{12,4},{16,24},{20,28},{24,16},{28,20},{1,9},{5... | collective-permute-start | bytes 331784 | tf_op jit(solution)/shard_map/ppermute | solution.py:43
  280.9 17.0 %collective-permute-start.72 = (bf16[24,2304]{1,0:T(8,128)(2,1)S(1)}, bf16[24,2304]{1,0:T(8,128)(2,1)S(1)}, u32[]{:S(2)}, u32[]{:S(2)}) collective-permute-start(bf16[24,2304]{1,0:T(8,128)(2,1)S(1)} %collective-permute-done.71), channel_id=1, source_target_pairs={{0,4},{4,0},{8,12},{12,8},{16,20},{20,16},{24,28},{28,24},{1,5},{5... | collective-permute-start | bytes 331784 | tf_op jit(solution)/shard_map/ppermute | solution.py:43
  (95 other events, 787.3 us)

commit v2 on v1

--- a/solution.py
+++ b/solution.py
@@ -15,6 +15,7 @@
 f32 = jnp.float32
 row_tile = 8
 gain_rows = 16
+slot_tile = 4
 
 
 def bucket_index(offset):
@@ -78,13 +79,34 @@
     return jax.ShapeDtypeStruct(tuple(dims), dtype)
 
 
+def prepare_tokens(n, rows, part, index, tokens, gains, out):
+    out[:rows, :] = tokens[...]
+    out[rows:, :] = jnp.zeros((gain_rows, n * part), bf16)
+    for k in range(n):
+
+        @pl.when(index[0] == k)
+        def _():
+            out[rows:, k * part : (k + 1) * part] = gains[...]
+
+
+def prepare_weight(n, part, index, weight, *outs):
+    for k in range(n):
+
+        @pl.when(index[0] == k)
+        def _():
+            for p in range(n):
+                for kind in range(3):
+                    at = (kind * n + (k ^ p)) * part
+                    outs[p][:, kind * part : (kind + 1) * part] = weight[:, at : at + part]
+
+
 def attention_forward(n, rows, width, heads, seqs, buckets, *refs):
     index, lengths, table = refs[:3]
     token_refs = refs[3 : 3 + n]
     weight_refs = refs[3 + n : 3 + 2 * n]
-    normed_out, weight_out, projected_out, weights_out = refs[3 + 2 * n : 7 + 2 * n]
-    mixed_out = refs[7 + 2 * n : 7 + 3 * n]
-    tokens_scr, mixed_scr = refs[7 + 3 * n :]
+    normed_out, weight_out, projected_out, weights_out, unit_out = refs[3 + 2 * n : 8 + 2 * n]
+    mixed_out = refs[8 + 2 * n : 8 + 3 * n]
+    tokens_scr, mixed_scr = refs[8 + 3 * n :]
     s = index[0]
     part = width // n
     head_dim = part // heads
@@ -97,7 +119,9 @@
     for j in range(n):
         value = tokens_scr[j].astype(f32)
         factor = lax.rsqrt(jnp.mean(value * value, axis=-1, keepdims=True) + norm_eps)
-        normed_out[j * rows : (j + 1) * rows, :] = (value * factor * gain).astype(bf16)
+        unit = value * factor
+        unit_out[j * rows : (j + 1) * rows, :] = unit
+        normed_out[j * rows : (j + 1) * rows, :] = (unit * gain).astype(bf16)
     projected_out[...] = dot(normed_out[...], weight_out[...]).astype(bf16)
     total_rows = n * rows
     key_place = lax.broadcasted_iota(jnp.int32, (1, total_rows), 1)
@@ -147,13 +171,13 @@
 
 
 def attention_backward(n, m, rows, width, heads, buckets, *refs):
-    index, projected, normed, weight, weights = refs[:5]
-    grad_refs = refs[5 : 5 + n]
-    at = 5 + n
+    index, projected, normed, weight, weights, unit, small = refs[:7]
+    grad_refs = refs[7 : 7 + n]
+    at = 7 + n
     share_out = refs[at : at + m]
     normed_grad_out = refs[at + m : at + m + n]
-    table_out = refs[at + m + n]
-    grad_scr, scores_scr, projected_scr, total_scr, normed_scr = refs[at + m + n + 1 :]
+    gain_out, table_out = refs[at + m + n : at + m + n + 2]
+    grad_scr, scores_scr, projected_scr, total_scr, normed_scr = refs[at + m + n + 2 :]
     s = index[0]
     e = index[1]
     part = width // n
@@ -215,15 +239,43 @@
         ).astype(bf16)
     table_out[...] = table_total
     grad_projected = projected_scr[...]
-    total_scr[...] = dot_tn(normed[...], grad_projected)
+    normed_grad = dot_nt(grad_projected, weight[...])
+    normed_scr[...] = normed_grad.astype(bf16).reshape(n, rows, width)
+    for p in range(n):
+        normed_grad_out[p][...] = normed_scr[s ^ p]
+    grad_gain = jnp.sum(normed_grad * unit[...], axis=0, keepdims=True)
+    gain_out[...] = jnp.broadcast_to(grad_gain, gain_out.shape)
+    wide = 3 * part
+    total_scr[:, :wide] = dot_tn(normed[...], grad_projected)
+    piece = part // m
+    if m > 1:
+        extra = small.shape[1]
+        eye = lax.broadcasted_iota(jnp.int32, (128, 128), 0) == lax.broadcasted_iota(
+            jnp.int32, (128, 128), 1
+        )
+        first = lax.broadcasted_iota(jnp.int32, (128, extra), 1) == 0
+        for c in range(width // 128):
+            row = jnp.broadcast_to(grad_gain[:, c * 128 : (c + 1) * 128], (128, 128))
+            column = jnp.sum(jnp.where(eye, row, 0.0), axis=1, keepdims=True)
+            block = jnp.where(first, column, small[c * 128 : (c + 1) * 128, :])
+            total_scr[c * 128 : (c + 1) * 128, wide : wide + extra] = block
+        for d in range(m):
+            total_scr[d * piece : d * piece + row_tile, wide + extra - buckets : wide + extra] = (
+                table_total[:, :buckets]
+            )
     for d in range(m):
-        piece = part // m
         for t in range(n):
             start = pl.multiple_of(t * part + (e ^ d) * piece if m > 1 else t * part, row_tile)
             share_out[d][t] = total_scr[pl.ds(start, piece), :].astype(bf16)
-    normed_scr[...] = dot_nt(grad_projected, weight[...]).astype(bf16).reshape(n, rows, width)
-    for p in range(n):
-        normed_grad_out[p][...] = normed_scr[s ^ p]
+
+
+def assemble(m, piece, wide, narrow, index, *refs):
+    total_out, out_out, small_out = refs[m:]
+    for d in range(m):
+        start = pl.multiple_of((index[1] ^ d) * piece, row_tile)
+        total_out[pl.ds(start, piece), :] = refs[d][:, :wide].astype(f32)
+        out_out[pl.ds(start, piece), :] = refs[d][:, wide : wide + narrow].astype(f32)
+        small_out[pl.ds(start, piece), :] = refs[d][:, wide + narrow :].astype(f32)
 
 
 def expert_forward(n, rows, *refs):
@@ -317,14 +369,28 @@
     experts = router.shape[1]
     direct = m <= 8
 
-    gains = jnp.zeros((gain_rows, width), bf16)
-    gains = lax.dynamic_update_slice(gains, jnp.stack([first_gain, second_gain]), (0, s * part))
-    token_blocks = gather_relative(jnp.concatenate([tokens, gains], axis=0), "shard")
-    by_target = attention_in.reshape(part, 3, n, part).transpose(2, 0, 1, 3).reshape(n, part, 3 * part)
+    gains = jnp.pad(jnp.stack([first_gain, second_gain]), ((0, gain_rows - 2), (0, 0)))
+    own_tokens = call(
+        lambda *refs: prepare_tokens(n, rows, part, *refs),
+        shape((rows + gain_rows, width)),
+        (index, tokens, gains),
+        "s",
+    )
+    token_blocks = gather_relative(own_tokens, "shard")
+    own_weight, own_tokens = lax.optimization_barrier((attention_in, own_tokens))
     weight_blocks = exchange_relative(
-        [lax.dynamic_index_in_dim(by_target, s ^ p, 0, keepdims=False) for p in range(n)], "shard"
-    )
-    out_blocks = gather_relative(attention_out, "shard")
+        call(
+            lambda *refs: prepare_weight(n, part, *refs),
+            [shape((part, 3 * part))] * n,
+            (index, own_weight),
+            "s",
+        ),
+        "shard",
+    )
+    own_out, token_blocks, weight_blocks = lax.optimization_barrier(
+        (attention_out, token_blocks, weight_blocks)
+    )
+    out_blocks = gather_relative(own_out, "shard")
     gain_one, gain_two = (
         sum(block[rows + i : rows + i + 1].astype(f32) for block in token_blocks) for i in range(2)
     )
@@ -338,6 +404,7 @@
             shape((width, 3 * part)),
             shape((group, 3 * part)),
             shape((heads, group, group)),
+            shape((group, width), f32),
             *[shape((rows, part))] * n,
         ),
         (index, lengths, position_bias.astype(f32), *token_blocks, *weight_blocks),
@@ -346,8 +413,8 @@
         flops=2 * group * width * 3 * part + 8 * head_flops,
         size=8 * 2**20,
     )
-    normed, weight, projected, weights = answers[:4]
-    mixed_mine = answers[4:]
+    normed, weight, projected, weights, unit = answers[:5]
+    mixed_mine = answers[5:]
     mixed_blocks = exchange_relative(list(mixed_mine), "shard")
 
     inputs = tokens.astype(f32)
@@ -366,25 +433,40 @@
     running = dot(lower, chosen.astype(bf16))
     slot = jnp.sum((running - 1.0) * chosen, axis=1).astype(jnp.int32)
     capacity = max(2, 9 * rows // (8 * experts) + 1)
-    capacity = -(-capacity // row_tile) * row_tile
-    holder = route ^ e if direct else route
-    target = holder * capacity + slot
+    capacity = -(-capacity // slot_tile) * slot_tile
     places = experts * capacity
+    half = places // 2
+    if direct:
+        holder = route ^ e
+        target = (holder & 1) * half + (holder >> 1) * capacity + slot
+    else:
+        target = route * capacity + slot
     collect = (target[:, None] == lax.iota(jnp.int32, places)[None, :]).astype(bf16)
     upstream = cotangent.astype(f32)
     grad_result = (gate[:, None] * upstream).astype(bf16)
 
+    def plain(value):
+        return lax.all_to_all(
+            value.reshape(experts, capacity, width), "expert", 0, 0, tiled=True
+        ).reshape(places, width)
+
     def send(value):
         if not direct:
-            return lax.all_to_all(
-                value.reshape(experts, capacity, width), "expert", 0, 0, tiled=True
-            ).reshape(places, width)
-        return jnp.concatenate(
-            exchange_relative(
-                [value[d * capacity : (d + 1) * capacity] for d in range(experts)], "expert"
-            ),
-            axis=0,
-        )
+            return plain(value)
+        came = swap(value[half:], "expert", 1).reshape(m // 2, capacity, width)
+        own = value[:half].reshape(m // 2, capacity, width)
+        both = jnp.concatenate([own, came], axis=1)
+        blocks = [both[d] if d == 0 else swap(both[d], "expert", 2 * d) for d in range(m // 2)]
+        return jnp.concatenate(blocks, axis=0)
+
+    def give_back(value):
+        if not direct:
+            return plain(value)
+        both = value.reshape(m // 2, 2 * capacity, width)
+        blocks = [both[d] if d == 0 else swap(both[d], "expert", 2 * d) for d in range(m // 2)]
+        own = [block[:capacity] for block in blocks]
+        other = swap(jnp.concatenate([block[capacity:] for block in blocks]), "expert", 1)
+        return jnp.concatenate([*own, other])
 
     arrived = send(dot_tn(collect, normed_two.astype(bf16)).astype(bf16))
     row_blocks = gather_relative(arrived, "shard")
@@ -406,7 +488,7 @@
         flops=2 * expert_flops,
         size=6 * 2**20,
     )
-    returned = send(reduce_shard(keep, out, places))
+    returned = give_back(reduce_shard(keep, out, places))
     grad_before, keep_grad, out_grad = call(
         lambda *refs: expert_backward(n, places, *refs),
         (
@@ -418,7 +500,7 @@
         flops=2 * expert_flops,
         size=6 * 2**20,
     )
-    returned_grad = send(reduce_shard(keep_grad, out_grad, places))
+    returned_grad = give_back(reduce_shard(keep_grad, out_grad, places))
     grad_up, grad_down = call(
         lambda *refs: expert_weights(n, *refs),
         (shape(expert_in.shape, f32), shape(expert_out.shape, f32)),
@@ -451,82 +533,99 @@
     grad_mixed_blocks = exchange_relative(
         [dot_nt(grad_branch, out_blocks[p]).astype(bf16) for p in range(n)], "shard"
     )
-    branch_blocks = gather_relative(grad_branch, "shard")
+    own_branch, grad_mixed_blocks = lax.optimization_barrier((grad_branch, grad_mixed_blocks))
+    branch_blocks = gather_relative(own_branch, "shard")
+    grad_weight_out = sum(dot_tn(mixed_mine[p], branch_blocks[p]) for p in range(n)).astype(bf16)
+    total_out = lax.psum_scatter(grad_weight_out, "expert", scatter_dimension=0, tiled=True)
+
     holders = m if direct else 1
-
+    wide = 3 * part
+    extra = -wide % 128
+    while direct and extra < 2 + experts + buckets:
+        extra = extra + 128
+    small = jnp.concatenate([grad_gain_two[:, None], grad_router], axis=1)
     answers = call(
         lambda *refs: attention_backward(n, holders, rows, width, heads, buckets, *refs),
         (
-            *[shape((n, part // holders, 3 * part))] * holders,
+            *[shape((n, part // holders, wide + extra))] * holders,
             *[shape((rows, width))] * n,
+            shape((row_tile, width), f32),
             shape((row_tile, 128), f32),
         ),
-        (index, projected, normed, weight, weights, *grad_mixed_blocks),
+        (
+            index,
+            projected,
+            normed,
+            weight,
+            weights,
+            unit,
+            jnp.pad(small, ((0, 0), (1, extra - experts - 2))) if direct else small,
+            *grad_mixed_blocks,
+        ),
         "s",
         [
             pltpu.VMEM((n, rows, part), bf16),
             pltpu.VMEM((group, group), bf16),
-            pltpu.VMEM((group, 3 * part), bf16),
-            pltpu.VMEM((width, 3 * part), f32),
+            pltpu.VMEM((group, wide), bf16),
+            pltpu.VMEM((width, wide + extra), f32),
             pltpu.VMEM((n, rows, width), bf16),
         ],
         flops=8 * head_flops,
         size=8 * 2**20,
     )
-    piece = part // m
-    grad_weight_out = sum(dot_tn(mixed_mine[p], branch_blocks[p]) for p in range(n))
-
     shares = list(answers[:holders])
     normed_grads = answers[holders : holders + n]
-    grad_table = answers[holders + n][:heads, :buckets]
-
-    def spread(blocks):
-        if direct:
-            return exchange_relative(blocks, "expert")
-        return list(lax.all_to_all(blocks, "expert", 0, 0, tiled=True))
-
-    def gather(value):
-        if direct:
-            stacked = jnp.stack(gather_relative(value, "expert"))
-            return stacked[lax.iota(jnp.int32, m) ^ e]
-        return lax.all_gather(value, "expert", axis=0, tiled=False)
-
+    gain_row, table = answers[holders + n :]
+
+    piece = part // m
     if direct:
-        out_shares = [
-            lax.dynamic_slice_in_dim(grad_weight_out, (e ^ d) * piece, piece, 0).astype(bf16)
-            for d in range(m)
-        ]
+        came = exchange_relative(shares, "expert")
     else:
-        out_shares = grad_weight_out.astype(bf16).reshape(m, piece, width)
-        shares = shares[0].reshape(n, m, piece, 3 * part).swapaxes(0, 1)
-    total_out = sum(x.astype(f32) for x in spread(out_shares)).astype(bf16)
-    grad_attention_out = gather(total_out).astype(f32).reshape(part, width)
-
-    summed = sum(x.astype(f32) for x in spread(shares)).astype(bf16)
+        came = lax.all_to_all(
+            shares[0].reshape(n, m, piece, wide + extra).swapaxes(0, 1), "expert", 0, 0, tiled=True
+        )
+    summed = sum(x.astype(f32) for x in came)
+    table_total = summed[0, :heads, wide + extra - buckets :]
+    summed = summed.astype(bf16)
     mine = exchange_relative(
         [lax.dynamic_index_in_dim(summed, s ^ p, 0, keepdims=False) for p in range(n)], "shard"
     )
-    mine = jnp.stack(mine)[lax.iota(jnp.int32, n) ^ s]
+    small_mine = sum(block[:, wide:].astype(f32) for block in mine).astype(bf16)
+    mine = jnp.stack(mine)[lax.iota(jnp.int32, n) ^ s][:, :, :wide]
     mine = mine.reshape(n, piece, 3, part).transpose(1, 2, 0, 3).reshape(piece, 3 * width)
-    grad_attention_in = gather(mine).astype(f32).reshape(part, 3 * width)
+    if direct:
+        mine = jnp.concatenate([mine, total_out, small_mine], axis=1)
+        mine = jnp.pad(mine, ((0, 0), (0, -extra % 128)))
+        blocks = gather_relative(mine, "expert")
+        grad_attention_in, grad_attention_out, small_total = call(
+            lambda *refs: assemble(m, piece, 3 * width, width, *refs),
+            (
+                shape((part, 3 * width), f32),
+                shape((part, width), f32),
+                shape((part, mine.shape[1] - 4 * width), f32),
+            ),
+            (index, *blocks),
+            "s",
+        )
+    else:
+        grad_attention_in = lax.all_gather(mine, "expert", axis=0, tiled=True).astype(f32)
+        grad_attention_out = lax.all_gather(total_out, "expert", axis=0, tiled=True).astype(f32)
+        small = jnp.concatenate([gain_row[0][:, None], small], axis=1)
+        small_total = lax.psum_scatter(small, "shard", scatter_dimension=0, tiled=True)
+        small_total, table_total = lax.psum((small_total, table[:heads, :buckets]), "expert")
 
     grad_normed = sum(x.astype(f32) for x in exchange_relative(list(normed_grads), "shard"))
-    grad_input_norm, grad_gain_one = rms_backward(inputs, rms_factor(inputs), gain_one, grad_normed)
+    grad_input_norm, _ = rms_backward(inputs, rms_factor(inputs), gain_one, grad_normed)
     grad_tokens = (grad_hidden + grad_input_norm).astype(bf16)
-
-    small = jnp.concatenate([grad_gain_one[:, None], grad_gain_two[:, None], grad_router], axis=1)
-    small_total = lax.psum(small, ("expert", "shard"))
-    small_mine = lax.dynamic_slice_in_dim(small_total, s * part, part, 0)
-    table_total = lax.psum(grad_table, "expert")
     return (
         layer_out,
         grad_tokens,
         grad_attention_in,
         grad_attention_out,
         table_total,
-        small_mine[:, 0],
-        small_mine[:, 1],
-        small_mine[:, 2:],
+        small_total[:, 0],
+        small_total[:, 1],
+        small_total[:, 2 : 2 + experts],
         grad_up,
         grad_down,
     )

time: 304 us -> 278 us (0.914)
  blocking collectives: 58.9 us -> 0 us
  waiting for transfers between devices: 64.9 us -> 116 us
  starting transfers between devices: 95.5 us -> 73.8 us
  between operations: 1.66 us -> 14.9 us
  local copies, waits for them, and re-layouts: 23 us -> 13.3 us
  other arithmetic: 15.3 us -> 8.23 us
  Pallas kernels: 36.5 us -> 43.5 us
    psum x2 -> x0, blocking collectives: 58.9 us -> none  [the longest x1 37.8 us: local(): small_total = lax.psum(small, ('expert', 'shard'))]
    reduce_scatter x0 -> x1, waiting for transfers between devices: none -> 51.4 us  [local(): lax.psum_scatter(grad_weight_out, 'expert', scatter_dimension=0, tiled=True)]
    ppermute x90 -> x64, starting transfers between devices: 95.5 us -> 73.8 us  [swap(): return lax.ppermute(value, axis, [(i, i ^ bit) for i in range(size)])]
    pallas_call x5 -> x8, Pallas kernels: 36.5 us -> 43.5 us  [call(): pl.pallas_call(kernel, out_shape=out_shape, in_specs=in_specs, out_specs=...]
    unnamed x111 -> x77, local copies, waits for them, and re-layouts: 8.31 us -> 4.31 us
    reshape x2 -> x4, local copies, waits for them, and re-layouts: 4.07 us -> 0.11 us  [the longest x2 0.06 us: send(): came = swap(value[half:], 'expert', 1).reshape(m // 2, capacity, width)]
    ppermute x90 -> x64, waiting for transfers between devices: 64.9 us -> 64.2 us  [swap(): return lax.ppermute(value, axis, [(i, i ^ bit) for i in range(size)])]
  transfers between devices with their start and end apart: 90 -> 65, of which waited for: 27 -> 29; matrix products, arithmetic and copies ran while one was open for 11% -> 6% of each run, Pallas kernels for 10% -> 11%
where the time goes in v2:
time: 278 us; the launch traced here: 277 us
  waiting for transfers between devices  116 us (42%)
  starting transfers between devices  73.8 us (27%)
  Pallas kernels  43.5 us (16%)
  between operations  14.9 us (5%)
  local copies, waits for them, and re-layouts  13.3 us (5%)
  other arithmetic  8.23 us (3%)
  matrix products  8.01 us (3%)
    ppermute x64, starting transfers between devices, swap(): return lax.ppermute(value, axis, [(i, i ^ bit) for i in range(size)])  73.8 us
    ppermute x64, waiting for transfers between devices, swap(): return lax.ppermute(value, axis, [(i, i ^ bit) for i in range(size)])  64.2 us
    reduce_scatter x1, waiting for transfers between devices, local(): lax.psum_scatter(grad_weight_out, 'expert', scatter_dimension=0, tiled=True)  51.4 us
    pallas_call x8, Pallas kernels, call(): pl.pallas_call(kernel, out_shape=out_shape, in_specs=in_specs, out_specs=...  43.5 us
  transfers between devices with their start and end apart: 65, of which 29 were waited for; matrix products, arithmetic and copies ran while one was open for 6% of the time, Pallas kernels for 11%

profile of v2, /device:TPU:0, one launch (start us, length us, event | category | flops | bytes accessed | tf_op | source)
XLA Modules:
  0.0 277.3 jit_solution(8963774423018588793)
XLA Ops:
  11.5 2.9 %collective-permute-start.1 = (bf16[144,768]{1,0:T(8,128)(2,1)}, bf16[144,768]{1,0:T(8,128)(2,1)S(1)}, u32[]{:S(2)}, u32[]{:S(2)}) collective-permute-start(bf16[144,768]{1,0:T(8,128)(2,1)} %shard_map.195.refs_3_), channel_id=1, source_target_pairs={{0,2},{1,3},{2,0},{3,1},{4,6},{5,7},{6,4},{7,5},{8,10},{9,11},{10,... | collective-permute-start | bytes 663560 | tf_op jit(solution)/shard_map/ppermute | solution.py:44
  14.4 2.4 shard_map.196
  18.6 1.9 collective-permute-done.1.refs_5_
  21.5 4.8 %collective-permute-done.4.refs_9_ = bf16[192,576]{1,0:T(8,128)(2,1)S(1)} collective-permute-done((bf16[192,576]{1,0:T(8,128)(2,1)}, bf16[192,576]{1,0:T(8,128)(2,1)S(1)}, u32[]{:S(2)}, u32[]{:S(2)}) %collective-permute-start.4) | collective-permute-done | bytes 221216 | tf_op jit(solution)/shard_map/ppermute | solution.py:44
  26.3 3.7 %collective-permute-done.5.refs_10_ = bf16[192,576]{1,0:T(8,128)(2,1)S(1)} collective-permute-done((bf16[192,576]{1,0:T(8,128)(2,1)}, bf16[192,576]{1,0:T(8,128)(2,1)S(1)}, u32[]{:S(2)}, u32[]{:S(2)}) %collective-permute-start.5) | collective-permute-done | bytes 221216 | tf_op jit(solution)/shard_map/ppermute | solution.py:44
  34.0 10.2 %shard_map.197 = (bf16[512,768]{1,0:T(8,128)(2,1)}, bf16[768,576]{1,0:T(8,128)(2,1)}, bf16[512,576]{1,0:T(8,128)(2,1)}, bf16[3,512,512]{2,1,0:T(8,128)(2,1)}, f3...) custom-call(s32[2]{0:T(128)} %pad_add_fusion.refs_0_, ...), custom_call_target="tpu_custom_call" | custom-call | flops 1258291200 | bytes 8388608 | tf_op jit(solution)/shard_map/pallas_call | solution.py:67
  53.6 2.7 collective-permute-done.12
  56.4 4.0 %collective-permute-start.15 = (bf16[40,768]{1,0:T(8,128)(2,1)S(1)}, bf16[40,768]{1,0:T(8,128)(2,1)S(1)}, u32[]{:S(2)}, u32[]{:S(2)}) collective-permute-start(bf16[40,768]{1,0:T(8,128)(2,1)S(1)} %get-tuple-element.172), channel_id=1, source_target_pairs={{0,24},{4,28},{8,16},{12,20},{16,8},{20,12},{24,0},{28,4},{1,25},{... | collective-permute-start | bytes 184328 | tf_op jit(solution)/shard_map/ppermute | solution.py:44
  61.1 2.2 collective-permute-done.15
  63.3 2.2 collective-permute-done.14
  67.2 2.5 collective-permute-start.28
  69.7 2.0 collective-permute-start.26
  76.3 5.1 %collective-permute-done.30.refs_2_.refs_6_ = bf16[160,768]{1,0:T(8,128)(2,1)S(1)} collective-permute-done((bf16[160,768]{1,0:T(8,128)(2,1)S(1)}, bf16[160,768]{1,0:T(8,128)(2,1)S(1)}, u32[]{:S(2)}, u32[]{:S(2)}) %collective-permute-start.30) | collective-permute-done | bytes 245792 | tf_op jit(solution)/shard_map/ppermute | solution.py:44
  82.8 6.0 %shard_map.198 = (bf16[640,768]{1,0:T(8,128)(2,1)}, bf16[640,768]{1,0:T(8,128)(2,1)}, bf16[320,768]{1,0:T(8,128)(2,1)}, bf16[320,768]{1,0:T(8,128)(2,1)}) custom-call(bf16[160,768]{1,0:T(8,128)(2,1)} %copy-done.9, bf16[160,768]{1,0:T(8,128)(2,1)} %copy-done.31, bf16[160,768]{1,0:T(8,128)(2,1)} %copy-done.29, bf16[160,768]{1,0:T(8,128)(2,1)} %copy-done.32, ...), custom_call_target="tpu_custom_call" | custom-call | flops 1509949440 | bytes 6291456 | tf_op jit(solution)/shard_map/pallas_call | solution.py:67
  90.2 6.2 %shard_map.199 = (bf16[640,768]{1,0:T(8,128)(2,1)}, bf16[320,768]{1,0:T(8,128)(2,1)}, bf16[320,768]{1,0:T(8,128)(2,1)}) custom-call(bf16[160,768]{1,0:T(8,128)(2,1)} %copy-done.10, bf16[160,768]{1,0:T(8,128)(2,1)} %copy-done.33, bf16[160,768]{1,0:T(8,128)(2,1)} %copy-done.30, bf16[160,768]{1,0:T(8,128)(2,1)} %copy-done.34, bf16[1,768,768]{2,1,0:T(8,128)(2,1)} %refs_4_.3, ...), custom_call_target="tpu_custom_call" | custom-call | flops 1509949440 | bytes 6291456 | tf_op jit(solution)/shard_map/pallas_call | solution.py:67
  100.1 5.3 %collective-permute-done.20 = bf16[160,768]{1,0:T(8,128)(2,1)S(1)} collective-permute-done((bf16[160,768]{1,0:T(8,128)(2,1)S(1)}, bf16[160,768]{1,0:T(8,128)(2,1)S(1)}, u32[]{:S(2)}, u32[]{:S(2)}) %collective-permute-start.20) | collective-permute-done | bytes 245792 | tf_op jit(solution)/shard_map/ppermute | solution.py:44
  106.4 3.8 %collective-permute-done.33 = bf16[160,768]{1,0:T(8,128)(2,1)S(1)} collective-permute-done((bf16[160,768]{1,0:T(8,128)(2,1)S(1)}, bf16[160,768]{1,0:T(8,128)(2,1)S(1)}, u32[]{:S(2)}, u32[]{:S(2)}) %collective-permute-start.33) | collective-permute-done | bytes 245792 | tf_op jit(solution)/shard_map/ppermute | solution.py:44
  110.3 1.8 collective-permute-start.22
  113.9 2.6 collective-permute-start.35
  120.7 2.7 collective-permute-done.35
  138.3 8.2 %shard_map.200 = (bf16[4,24,640]{2,1,0:T(8,128)(2,1)}, bf16[4,24,640]{2,1,0:T(8,128)(2,1)}, bf16[4,24,640]{2,1,0:T(8,128)(2,1)}, bf16[4,24,640]{2,1,0:T(8,128)(2...) custom-call(s32[2]{0:T(128)} %pad_add_fusion.refs_0_, ...), custom_call_target="tpu_custom_call" | custom-call | flops 805306368 | bytes 8388608 | tf_op jit(solution)/shard_map/pallas_call | solution.py:67
  146.5 3.2 %collective-permute-start.50 = (bf16[4,24,640]{2,1,0:T(8,128)(2,1)}, bf16[4,24,640]{2,1,0:T(8,128)(2,1)S(1)}, u32[]{:S(2)}, u32[]{:S(2)}) collective-permute-start(bf16[4,24,640]{2,1,0:T(8,128)(2,1)} %get-tuple-element.105), channel_id=1, source_target_pairs={{0,28},{4,24},{8,20},{12,16},{16,12},{20,8},{24,4},{28,0},{1,29},{... | collective-permute-start | bytes 368648 | tf_op jit(solution)/shard_map/ppermute | solution.py:44
  149.7 1.8 collective-permute-start.49
  152.3 2.0 collective-permute-start.47
  155.7 10.5 %collective-permute-start.45 = (bf16[4,24,640]{2,1,0:T(8,128)(2,1)}, bf16[4,24,640]{2,1,0:T(8,128)(2,1)S(1)}, u32[]{:S(2)}, u32[]{:S(2)}) collective-permute-start(bf16[4,24,640]{2,1,0:T(8,128)(2,1)} %get-tuple-element.100), channel_id=1, source_target_pairs={{0,8},{4,12},{8,0},{12,4},{16,24},{20,28},{24,16},{28,20},{1,9},{5... | collective-permute-start | bytes 368648 | tf_op jit(solution)/shard_map/ppermute | solution.py:44
  167.9 5.9 %shard_map.202 = (f32[1,768,768]{2,1,0:T(8,128)}, f32[1,768,768]{2,1,0:T(8,128)}) custom-call(bf16[160,768]{1,0:T(8,128)(2,1)} %copy-done.9, bf16[160,768]{1,0:T(8,128)(2,1)} %copy-done.31, bf16[160,768]{1,0:T(8,128)(2,1)} %copy-done.29, bf16[160,768]{1,0:T(8,128)(2,1)} %copy-done.32, bf16[160,768]{1,0:T(8,128)(2,1)} %copy-done.10, ...), custom_call_target="tpu_custom_call" | custom-call | flops 1509949440 | bytes 9437184 | tf_op jit(solution)/shard_map/pallas_call | solution.py:67
  177.2 3.8 %collective-permute-done.55 = bf16[128,768]{1,0:T(8,128)(2,1)S(1)} collective-permute-done((bf16[128,768]{1,0:T(8,128)(2,1)S(1)}, bf16[128,768]{1,0:T(8,128)(2,1)S(1)}, u32[]{:S(2)}, u32[]{:S(2)}) %collective-permute-start.55) | collective-permute-done | bytes 196640 | tf_op jit(solution)/shard_map/ppermute | solution.py:44
  190.4 51.4 %reduce-scatter.2.cloned.1.call-done = bf16[24,768]{1,0:T(8,128)(2,1)} async-done(((bf16[192,768]{1,0:T(8,128)(2,1)}), bf16[24,768]{1,0:T(8,128)(2,1)}) %reduce-scatter.2.cloned.1.call-update) | async-done | bytes 36880 | tf_op jit(solution)/shard_map/reduce_scatter | solution.py:539
  245.8 4.8 %collective-permute-done.60.refs_5_ = bf16[24,3200]{1,0:T(8,128)(2,1)S(1)} collective-permute-done((bf16[24,3200]{1,0:T(8,128)(2,1)S(1)}, bf16[24,3200]{1,0:T(8,128)(2,1)S(1)}, u32[]{:S(2)}, u32[]{:S(2)}) %collective-permute-start.60) | collective-permute-done | bytes 153632 | tf_op jit(solution)/shard_map/ppermute | solution.py:44
  254.1 1.8 collective-permute-done.62.refs_7_
  258.3 3.4 %collective-permute-done.59.refs_4_ = bf16[24,3200]{1,0:T(8,128)(2,1)S(1)} collective-permute-done((bf16[24,3200]{1,0:T(8,128)(2,1)S(1)}, bf16[24,3200]{1,0:T(8,128)(2,1)S(1)}, u32[]{:S(2)}, u32[]{:S(2)}) %collective-permute-start.59) | collective-permute-done | bytes 153632 | tf_op jit(solution)/shard_map/ppermute | solution.py:44
  264.1 2.9 %shard_map.201 = (f32[192,2304]{1,0:T(8,128)}, f32[192,768]{1,0:T(8,128)}, f32[192,128]{1,0:T(8,128)}) custom-call(s32[2]{0:T(128)} %pad_add_fusion.refs_0_, bf16[24,3200]{1,0:T(8,128)(2,1)} %copy-done.5, bf16[24,3200]{1,0:T(8,128)(2,1)} %copy-done.14, bf16[24,3200]{1,0:T(8,128)(2,1)} %copy-done.12, bf16[24,3200]{1,0:T(8,128)(2,1)} %copy-done.16, ...), custom_call_target="tpu_custom_call" | custom-call | tf_op jit(solution)/shard_map/pallas_call | solution.py:67
  (269 shorter events, 87.5 us)
Async XLA Ops:
  7.2 234.6 %reduce-scatter.2.cloned.1.call-start = ((), (), s32[]{:S(2)}) async-start(), calls=%async_computation.1 | async-start | bytes 331776 | tf_op jit(solution)/shard_map/reduce_scatter | solution.py:539
  11.5 9.1 %collective-permute-start.1 = (bf16[144,768]{1,0:T(8,128)(2,1)}, bf16[144,768]{1,0:T(8,128)(2,1)S(1)}, u32[]{:S(2)}, u32[]{:S(2)}) collective-permute-start(bf16[144,768]{1,0:T(8,128)(2,1)} %shard_map.195.refs_3_), channel_id=1, source_target_pairs={{0,2},{1,3},{2,0},{3,1},{4,6},{5,7},{6,4},{7,5},{8,10},{9,11},{10,... | collective-permute-start | bytes 663560 | tf_op jit(solution)/shard_map/ppermute | solution.py:44
  17.3 9.0 %collective-permute-start.4 = (bf16[192,576]{1,0:T(8,128)(2,1)}, bf16[192,576]{1,0:T(8,128)(2,1)S(1)}, u32[]{:S(2)}, u32[]{:S(2)}) collective-permute-start(bf16[192,576]{1,0:T(8,128)(2,1)} %get-tuple-element.65), channel_id=1, source_target_pairs={{0,2},{1,3},{2,0},{3,1},{4,6},{5,7},{6,4},{7,5},{8,10},{9,11},{10,... | collective-permute-start | bytes 663560 | tf_op jit(solution)/shard_map/ppermute | solution.py:44
  17.3 12.7 %collective-permute-start.5 = (bf16[192,576]{1,0:T(8,128)(2,1)}, bf16[192,576]{1,0:T(8,128)(2,1)S(1)}, u32[]{:S(2)}, u32[]{:S(2)}) collective-permute-start(bf16[192,576]{1,0:T(8,128)(2,1)} %get-tuple-element.66), channel_id=1, source_target_pairs={{0,3},{1,2},{2,1},{3,0},{4,7},{5,6},{6,5},{7,4},{8,11},{9,10},{10,... | collective-permute-start | bytes 663560 | tf_op jit(solution)/shard_map/ppermute | solution.py:44
  20.6 9.5 %collective-permute-start.2 = (bf16[144,768]{1,0:T(8,128)(2,1)S(1)}, bf16[144,768]{1,0:T(8,128)(2,1)S(1)}, u32[]{:S(2)}, u32[]{:S(2)}) collective-permute-start(bf16[144,768]{1,0:T(8,128)(2,1)S(1)} %collective-permute-done.1.refs_5_), channel_id=1, source_target_pairs={{0,1},{1,0},{2,3},{3,2},{4,5},{5,4},{6,7},{7,6},{8,9},{9,8},{10,11... | collective-permute-start | bytes 663560 | tf_op jit(solution)/shard_map/ppermute | solution.py:44
  30.0 17.4 %collective-permute-start.9 = (bf16[192,768]{1,0:T(8,128)(2,1)}, bf16[192,768]{1,0:T(8,128)(2,1)S(1)}, u32[]{:S(2)}, u32[]{:S(2)}) collective-permute-start(bf16[192,768]{1,0:T(8,128)(2,1)} %param.16), channel_id=1, source_target_pairs={{0,2},{1,3},{2,0},{3,1},{4,6},{5,7},{6,4},{7,5},{8,10},{9,11},{10,... | collective-permute-start | bytes 884744 | tf_op jit(solution)/shard_map/ppermute | solution.py:44
  33.3 15.7 %collective-permute-start.7 = (bf16[192,768]{1,0:T(8,128)(2,1)}, bf16[192,768]{1,0:T(8,128)(2,1)S(1)}, u32[]{:S(2)}, u32[]{:S(2)}) collective-permute-start(bf16[192,768]{1,0:T(8,128)(2,1)} %param.16), channel_id=1, source_target_pairs={{0,1},{1,0},{2,3},{3,2},{4,5},{5,4},{6,7},{7,6},{8,9},{9,8},{10,11... | collective-permute-start | bytes 884744 | tf_op jit(solution)/shard_map/ppermute | solution.py:44
  53.2 7.9 %collective-permute-start.25 = (bf16[80,768]{1,0:T(8,128)(2,1)S(1)}, bf16[80,768]{1,0:T(8,128)(2,1)S(1)}, u32[]{:S(2)}, u32[]{:S(2)}) collective-permute-start(bf16[80,768]{1,0:T(8,128)(2,1)S(1)} %get-tuple-element.180), channel_id=1, source_target_pairs={{0,4},{4,0},{8,12},{12,8},{16,20},{20,16},{24,28},{28,24},{1,5},{5... | collective-permute-start | bytes 368648 | tf_op jit(solution)/shard_map/ppermute | solution.py:44
  65.6 10.1 %collective-permute-start.17 = (bf16[160,768]{1,0:T(8,128)(2,1)S(1)}, bf16[160,768]{1,0:T(8,128)(2,1)S(1)}, u32[]{:S(2)}, u32[]{:S(2)}) collective-permute-start(bf16[160,768]{1,0:T(8,128)(2,1)S(1)} %pad_maximum_fusion.refs_0_), channel_id=1, source_target_pairs={{0,2},{1,3},{2,0},{3,1},{4,6},{5,7},{6,4},{7,5},{8,10},{9,11},{10,... | collective-permute-start | bytes 737288 | tf_op jit(solution)/shard_map/ppermute | solution.py:44
  76.2 13.2 %collective-permute-start.29 = (bf16[160,768]{1,0:T(8,128)(2,1)S(1)}, bf16[160,768]{1,0:T(8,128)(2,1)S(1)}, u32[]{:S(2)}, u32[]{:S(2)}) collective-permute-start(bf16[160,768]{1,0:T(8,128)(2,1)S(1)} %pad_maximum_fusion.1.refs_0_.refs_4_), channel_id=1, source_target_pairs={{0,1},{1,0},{2,3},{3,2},{4,5},{5,4},{6,7},{7,6},{8,9},{9,8},{10,11... | collective-permute-start | bytes 737288 | tf_op jit(solution)/shard_map/ppermute | solution.py:44
  81.4 8.0 %collective-permute-start.31 = (bf16[160,768]{1,0:T(8,128)(2,1)S(1)}, bf16[160,768]{1,0:T(8,128)(2,1)S(1)}, u32[]{:S(2)}, u32[]{:S(2)}) collective-permute-start(bf16[160,768]{1,0:T(8,128)(2,1)S(1)} %collective-permute-done.30.refs_2_.refs_6_), channel_id=1, source_target_pairs={{0,1},{1,0},{2,3},{3,2},{4,5},{5,4},{6,7},{7,6},{8,9},{9,8},{10,11... | collective-permute-start | bytes 737288 | tf_op jit(solution)/shard_map/ppermute | solution.py:44
  88.9 7.6 %collective-permute-start.19 = (bf16[320,768]{1,0:T(8,128)(2,1)}, bf16[320,768]{1,0:T(8,128)(2,1)S(1)}, u32[]{:S(2)}, u32[]{:S(2)}) collective-permute-start(bf16[320,768]{1,0:T(8,128)(2,1)} %get-tuple-element.81), channel_id=1, source_target_pairs={{0,1},{1,0},{2,3},{3,2},{4,5},{5,4},{6,7},{7,6},{8,9},{9,8},{10,11... | collective-permute-start | bytes 1474568 | tf_op jit(solution)/shard_map/ppermute | solution.py:44
  96.5 8.8 %collective-permute-start.20 = (bf16[160,768]{1,0:T(8,128)(2,1)S(1)}, bf16[160,768]{1,0:T(8,128)(2,1)S(1)}, u32[]{:S(2)}, u32[]{:S(2)}) collective-permute-start(bf16[160,768]{1,0:T(8,128)(2,1)S(1)} %add_convert_fusion.3), channel_id=1, source_target_pairs={{0,2},{1,3},{2,0},{3,1},{4,6},{5,7},{6,4},{7,5},{8,10},{9,11},{10,... | collective-permute-start | bytes 737288 | tf_op jit(solution)/shard_map/ppermute | solution.py:44
  99.5 10.7 %collective-permute-start.33 = (bf16[160,768]{1,0:T(8,128)(2,1)S(1)}, bf16[160,768]{1,0:T(8,128)(2,1)S(1)}, u32[]{:S(2)}, u32[]{:S(2)}) collective-permute-start(bf16[160,768]{1,0:T(8,128)(2,1)S(1)} %add_convert_fusion.1), channel_id=1, source_target_pairs={{0,2},{1,3},{2,0},{3,1},{4,6},{5,7},{6,4},{7,5},{8,10},{9,11},{10,... | collective-permute-start | bytes 737288 | tf_op jit(solution)/shard_map/ppermute | solution.py:44
  105.5 11.1 %collective-permute-start.21 = (bf16[40,768]{1,0:T(8,128)(2,1)S(1)}, bf16[40,768]{1,0:T(8,128)(2,1)S(1)}, u32[]{:S(2)}, u32[]{:S(2)}) collective-permute-start(bf16[40,768]{1,0:T(8,128)(2,1)S(1)} %get-tuple-element.185), channel_id=1, source_target_pairs={{0,8},{4,12},{8,0},{12,4},{16,24},{20,28},{24,16},{28,20},{1,9},{5... | collective-permute-start | bytes 184328 | tf_op jit(solution)/shard_map/ppermute | solution.py:44
  110.3 8.5 %collective-permute-start.22 = (bf16[40,768]{1,0:T(8,128)(2,1)S(1)}, bf16[40,768]{1,0:T(8,128)(2,1)S(1)}, u32[]{:S(2)}, u32[]{:S(2)}) collective-permute-start(bf16[40,768]{1,0:T(8,128)(2,1)S(1)} %get-tuple-element.184), channel_id=1, source_target_pairs={{0,16},{4,20},{8,24},{12,28},{16,0},{20,4},{24,8},{28,12},{1,17},{... | collective-permute-start | bytes 184328 | tf_op jit(solution)/shard_map/ppermute | solution.py:44
  113.9 9.5 %collective-permute-start.35 = (bf16[40,768]{1,0:T(8,128)(2,1)S(1)}, bf16[40,768]{1,0:T(8,128)(2,1)S(1)}, u32[]{:S(2)}, u32[]{:S(2)}) collective-permute-start(bf16[40,768]{1,0:T(8,128)(2,1)S(1)} %get-tuple-element.177), channel_id=1, source_target_pairs={{0,16},{4,20},{8,24},{12,28},{16,0},{20,4},{24,8},{28,12},{1,17},{... | collective-permute-start | bytes 184328 | tf_op jit(solution)/shard_map/ppermute | solution.py:44
  146.5 9.2 %collective-permute-start.50 = (bf16[4,24,640]{2,1,0:T(8,128)(2,1)}, bf16[4,24,640]{2,1,0:T(8,128)(2,1)S(1)}, u32[]{:S(2)}, u32[]{:S(2)}) collective-permute-start(bf16[4,24,640]{2,1,0:T(8,128)(2,1)} %get-tuple-element.105), channel_id=1, source_target_pairs={{0,28},{4,24},{8,20},{12,16},{16,12},{20,8},{24,4},{28,0},{1,29},{... | collective-permute-start | bytes 368648 | tf_op jit(solution)/shard_map/ppermute | solution.py:44
  149.7 16.5 %collective-permute-start.49 = (bf16[4,24,640]{2,1,0:T(8,128)(2,1)}, bf16[4,24,640]{2,1,0:T(8,128)(2,1)S(1)}, u32[]{:S(2)}, u32[]{:S(2)}) collective-permute-start(bf16[4,24,640]{2,1,0:T(8,128)(2,1)} %get-tuple-element.104), channel_id=1, source_target_pairs={{0,24},{4,28},{8,16},{12,20},{16,8},{20,12},{24,0},{28,4},{1,25},{... | collective-permute-start | bytes 368648 | tf_op jit(solution)/shard_map/ppermute | solution.py:44
  151.6 22.3 %collective-permute-start.48 = (bf16[4,24,640]{2,1,0:T(8,128)(2,1)}, bf16[4,24,640]{2,1,0:T(8,128)(2,1)S(1)}, u32[]{:S(2)}, u32[]{:S(2)}) collective-permute-start(bf16[4,24,640]{2,1,0:T(8,128)(2,1)} %get-tuple-element.103), channel_id=1, source_target_pairs={{0,20},{4,16},{8,28},{12,24},{16,4},{20,0},{24,12},{28,8},{1,21},{... | collective-permute-start | bytes 368648 | tf_op jit(solution)/shard_map/ppermute | solution.py:44
  152.3 22.6 %collective-permute-start.47 = (bf16[4,24,640]{2,1,0:T(8,128)(2,1)}, bf16[4,24,640]{2,1,0:T(8,128)(2,1)S(1)}, u32[]{:S(2)}, u32[]{:S(2)}) collective-permute-start(bf16[4,24,640]{2,1,0:T(8,128)(2,1)} %get-tuple-element.102), channel_id=1, source_target_pairs={{0,16},{4,20},{8,24},{12,28},{16,0},{20,4},{24,8},{28,12},{1,17},{... | collective-permute-start | bytes 368648 | tf_op jit(solution)/shard_map/ppermute | solution.py:44
  154.3 20.6 %collective-permute-start.46 = (bf16[4,24,640]{2,1,0:T(8,128)(2,1)}, bf16[4,24,640]{2,1,0:T(8,128)(2,1)S(1)}, u32[]{:S(2)}, u32[]{:S(2)}) collective-permute-start(bf16[4,24,640]{2,1,0:T(8,128)(2,1)} %get-tuple-element.101), channel_id=1, source_target_pairs={{0,12},{4,8},{8,4},{12,0},{16,28},{20,24},{24,20},{28,16},{1,13},{... | collective-permute-start | bytes 368648 | tf_op jit(solution)/shard_map/ppermute | solution.py:44
  155.7 20.3 %collective-permute-start.45 = (bf16[4,24,640]{2,1,0:T(8,128)(2,1)}, bf16[4,24,640]{2,1,0:T(8,128)(2,1)S(1)}, u32[]{:S(2)}, u32[]{:S(2)}) collective-permute-start(bf16[4,24,640]{2,1,0:T(8,128)(2,1)} %get-tuple-element.100), channel_id=1, source_target_pairs={{0,8},{4,12},{8,0},{12,4},{16,24},{20,28},{24,16},{28,20},{1,9},{5... | collective-permute-start | bytes 368648 | tf_op jit(solution)/shard_map/ppermute | solution.py:44
  166.2 10.8 %collective-permute-start.44 = (bf16[4,24,640]{2,1,0:T(8,128)(2,1)}, bf16[4,24,640]{2,1,0:T(8,128)(2,1)S(1)}, u32[]{:S(2)}, u32[]{:S(2)}) collective-permute-start(bf16[4,24,640]{2,1,0:T(8,128)(2,1)} %get-tuple-element.99), channel_id=1, source_target_pairs={{0,4},{4,0},{8,12},{12,8},{16,20},{20,16},{24,28},{28,24},{1,5},{5... | collective-permute-start | bytes 368648 | tf_op jit(solution)/shard_map/ppermute | solution.py:44
  174.9 69.2 %collective-permute-start.43 = (bf16[128,768]{1,0:T(8,128)(2,1)}, bf16[128,768]{1,0:T(8,128)(2,1)S(1)}, u32[]{:S(2)}, u32[]{:S(2)}) collective-permute-start(bf16[128,768]{1,0:T(8,128)(2,1)} %get-tuple-element.97), channel_id=1, source_target_pairs={{0,3},{1,2},{2,1},{3,0},{4,7},{5,6},{6,5},{7,4},{8,11},{9,10},{10,... | collective-permute-start | bytes 589832 | tf_op jit(solution)/shard_map/ppermute | solution.py:44
  176.0 68.0 %collective-permute-start.42 = (bf16[128,768]{1,0:T(8,128)(2,1)}, bf16[128,768]{1,0:T(8,128)(2,1)S(1)}, u32[]{:S(2)}, u32[]{:S(2)}) collective-permute-start(bf16[128,768]{1,0:T(8,128)(2,1)} %get-tuple-element.96), channel_id=1, source_target_pairs={{0,2},{1,3},{2,0},{3,1},{4,6},{5,7},{6,4},{7,5},{8,10},{9,11},{10,... | collective-permute-start | bytes 589832 | tf_op jit(solution)/shard_map/ppermute | solution.py:44
  187.5 56.6 %collective-permute-start.41 = (bf16[128,768]{1,0:T(8,128)(2,1)}, bf16[128,768]{1,0:T(8,128)(2,1)S(1)}, u32[]{:S(2)}, u32[]{:S(2)}) collective-permute-start(bf16[128,768]{1,0:T(8,128)(2,1)} %get-tuple-element.95), channel_id=1, source_target_pairs={{0,1},{1,0},{2,3},{3,2},{4,5},{5,4},{6,7},{7,6},{8,9},{9,8},{10,11... | collective-permute-start | bytes 589832 | tf_op jit(solution)/shard_map/ppermute | solution.py:44
  242.6 8.1 %collective-permute-start.60 = (bf16[24,3200]{1,0:T(8,128)(2,1)S(1)}, bf16[24,3200]{1,0:T(8,128)(2,1)S(1)}, u32[]{:S(2)}, u32[]{:S(2)}) collective-permute-start(bf16[24,3200]{1,0:T(8,128)(2,1)S(1)} %fusion.32.refs_1_), channel_id=1, source_target_pairs={{0,16},{4,20},{8,24},{12,28},{16,0},{20,4},{24,8},{28,12},{1,17},{... | collective-permute-start | bytes 460808 | tf_op jit(solution)/shard_map/ppermute | solution.py:44
  244.3 8.4 %collective-permute-start.58 = (bf16[24,3200]{1,0:T(8,128)(2,1)S(1)}, bf16[24,3200]{1,0:T(8,128)(2,1)S(1)}, u32[]{:S(2)}, u32[]{:S(2)}) collective-permute-start(bf16[24,3200]{1,0:T(8,128)(2,1)S(1)} %fusion.32.refs_1_), channel_id=1, source_target_pairs={{0,8},{4,12},{8,0},{12,4},{16,24},{20,28},{24,16},{28,20},{1,9},{5... | collective-permute-start | bytes 460808 | tf_op jit(solution)/shard_map/ppermute | solution.py:44
  250.7 7.6 %collective-permute-start.57 = (bf16[24,3200]{1,0:T(8,128)(2,1)S(1)}, bf16[24,3200]{1,0:T(8,128)(2,1)S(1)}, u32[]{:S(2)}, u32[]{:S(2)}) collective-permute-start(bf16[24,3200]{1,0:T(8,128)(2,1)S(1)} %fusion.32.refs_1_), channel_id=1, source_target_pairs={{0,4},{4,0},{8,12},{12,8},{16,20},{20,16},{24,28},{28,24},{1,5},{5... | collective-permute-start | bytes 460808 | tf_op jit(solution)/shard_map/ppermute | solution.py:44
  252.0 9.7 %collective-permute-start.61 = (bf16[24,3200]{1,0:T(8,128)(2,1)S(1)}, bf16[24,3200]{1,0:T(8,128)(2,1)S(1)}, u32[]{:S(2)}, u32[]{:S(2)}) collective-permute-start(bf16[24,3200]{1,0:T(8,128)(2,1)S(1)} %collective-permute-done.60.refs_5_), channel_id=1, source_target_pairs={{0,4},{4,0},{8,12},{12,8},{16,20},{20,16},{24,28},{28,24},{1,5},{5... | collective-permute-start | bytes 460808 | tf_op jit(solution)/shard_map/ppermute | solution.py:44
  252.8 9.0 %collective-permute-start.59 = (bf16[24,3200]{1,0:T(8,128)(2,1)S(1)}, bf16[24,3200]{1,0:T(8,128)(2,1)S(1)}, u32[]{:S(2)}, u32[]{:S(2)}) collective-permute-start(bf16[24,3200]{1,0:T(8,128)(2,1)S(1)} %collective-permute-done.58.refs_3_), channel_id=1, source_target_pairs={{0,4},{4,0},{8,12},{12,8},{16,20},{20,16},{24,28},{28,24},{1,5},{5... | collective-permute-start | bytes 460808 | tf_op jit(solution)/shard_map/ppermute | solution.py:44
  (71 other events, 511.0 us)
Sparse Core Ops, SparseCore 0:
  183.5 58.2 reduce-scatter.1

commit v3 on v2

v3 whole, which is shorter than its diff:
```python
import jax
import jax.numpy as jnp
from jax import lax
from jax.experimental import pallas as pl
from jax.experimental.pallas import tpu as pltpu
from jax.sharding import PartitionSpec as P

norm_eps = 1e-06
gelu_scale = 0.7978845608028654
gelu_cubic = 0.044715
big_negative = -1e30
near_steps = 8
far_steps = (12, 16, 23, 32, 46, 64, 91)
bf16 = jnp.bfloat16
f32 = jnp.float32
row_tile = 8
pair = 1
slot_tile = 4


def bucket_index(offset):
    distance = jnp.abs(offset)
    far_level = jnp.full_like(distance, near_steps)
    for step_edge in far_steps:
        far_level = far_level + (distance >= step_edge).astype(jnp.int32)
    near = jnp.where(distance < near_steps, distance, far_level)
    return near + 16 * (offset > 0).astype(jnp.int32)


def dot(left, right):
    return jnp.dot(left, right, preferred_element_type=f32)


def dot_nt(left, right):
    return lax.dot_general(left, right, (((1,), (1,)), ((), ())), preferred_element_type=f32)


def dot_tn(left, right):
    return lax.dot_general(left, right, (((0,), (0,)), ((), ())), preferred_element_type=f32)


def swap(value, axis, bit):
    size = lax.axis_size(axis)
    return lax.ppermute(value, axis, [(i, i ^ bit) for i in range(size)])


def gather_relative(value, axis):
    blocks = [value]
    bit = lax.axis_size(axis) // 2
    parts = {0: value}
    while bit:
        for p in list(parts):
            parts[p ^ bit] = swap(parts[p], axis, bit)
        bit //= 2
    return [parts[p] for p in range(lax.axis_size(axis))]


def exchange_relative(blocks, axis):
    return [blocks[0]] + [swap(block, axis, p) for p, block in enumerate(blocks) if p]


def call(kernel, out_shape, operands, spaces="", scratch=(), work=0):
    vmem = pl.BlockSpec(memory_space=pltpu.VMEM)
    smem = pl.BlockSpec(memory_space=pltpu.SMEM)
    in_specs = [smem if spaces[i : i + 1] == "s" else vmem for i in range(len(operands))]
    return pl.pallas_call(
        kernel,
        out_shape=out_shape,
        in_specs=in_specs,
        out_specs=jax.tree.map(lambda _: vmem, out_shape),
        scratch_shapes=list(scratch),
        compiler_params=pltpu.CompilerParams(vmem_limit_bytes=56 * 2**20),
        cost_estimate=pl.CostEstimate(flops=work, bytes_accessed=0, transcendentals=0),
    )(*operands)


def shape(dims, dtype=bf16):
    return jax.ShapeDtypeStruct(tuple(dims), dtype)


def diagonal(size):
    return lax.broadcasted_iota(jnp.int32, (size, size), 0) == lax.broadcasted_iota(
        jnp.int32, (size, size), 1
    )


def to_column(row, size):
    return jnp.sum(jnp.where(diagonal(size), row, 0.0), axis=1, keepdims=True)


def to_row(column, size):
    return jnp.sum(jnp.where(diagonal(size), column, 0.0), axis=0, keepdims=True)


def prepare_weight(n, part, weight, gain_one, gain_two, *outs):
    wide = 3 * part
    s = lax.axis_index("shard")
    extra = outs[0].shape[1] - wide
    one, two = (to_column(gain[...].astype(f32), part) for gain in (gain_one, gain_two))
    lane = lax.broadcasted_iota(jnp.int32, (part, extra), 1)
    beside = jnp.where(lane == 0, one, jnp.where(lane == 1, two, 0.0)).astype(bf16)
    for p in range(n):
        outs[p][:, wide:] = beside
    for k in range(n):

        @pl.when(s == k)
        def _():
            for p in range(n):
                for kind in range(3):
                    at = (kind * n + (k ^ p)) * part
                    outs[p][:, kind * part : (kind + 1) * part] = weight[:, at : at + part]


def offsets(rows):
    return lax.broadcasted_iota(jnp.int32, (rows, rows), 1) - lax.broadcasted_iota(
        jnp.int32, (rows, rows), 0
    )


def near_buckets(diff, buckets):
    if diff == 0:
        return range(buckets)
    return range(buckets // 2, buckets) if diff > 0 else range(buckets // 2)


def attention_forward(n, rows, width, heads, seqs, buckets, *refs):
    lengths, table = refs[:2]
    token_refs = refs[2 : 2 + n]
    weight_refs = refs[2 + n : 2 + 2 * n]
    tokens_out, weight_out, projected_out, weights_out, gains_out, mixed_all = refs[
        2 + 2 * n : 8 + 2 * n
    ]
    mixed_out = refs[8 + 2 * n : 8 + 3 * n]
    (normed_scr,) = refs[8 + 3 * n :]
    s = lax.axis_index("shard")
    part = width // n
    wide = 3 * part
    head_dim = part // heads
    for p in range(n):
        tokens_out[s ^ p] = token_refs[p][...]
        weight_out[pl.ds(pl.multiple_of((s ^ p) * part, part & -part), part), :] = weight_refs[p][...]
    size = 128
    for c in range(width // size):
        beside = weight_out[c * size : (c + 1) * size, wide:].astype(f32)
        for i in range(2):
            gains_out[i : i + 1, c * size : (c + 1) * size] = to_row(beside[:, i : i + 1], size)
    gain = gains_out[0:1, :]
    for j in range(n):
        value = tokens_out[j].astype(f32)
        factor = lax.rsqrt(jnp.mean(value * value, axis=-1, keepdims=True) + norm_eps)
        normed_scr[j * rows : (j + 1) * rows, :] = (value * factor * gain).astype(bf16)
    projected_out[...] = dot(normed_scr[...], weight_out[:, :wide]).astype(bf16)
    total_rows = n * rows
    key_place = lax.broadcasted_iota(jnp.int32, (1, total_rows), 1)
    key_segment = jnp.zeros((1, total_rows), jnp.int32)
    end = jnp.int32(0)
    ends = []
    for j in range(seqs):
        end = end + lengths[0, j]
        ends.append(end)
        key_segment = key_segment + (key_place >= end).astype(jnp.int32)
    base = offsets(rows)
    steps = {diff: bucket_index(base + diff * rows) for diff in (-1, 0, 1)}
    for h in range(heads):
        query = projected_out[:, h * head_dim : (h + 1) * head_dim]
        key = projected_out[:, part + h * head_dim : part + (h + 1) * head_dim]
        value = projected_out[:, 2 * part + h * head_dim : 2 * part + (h + 1) * head_dim]
        bias = {}
        for diff in (-1, 0, 1):
            block = jnp.zeros((rows, rows), f32)
            for b in near_buckets(diff, buckets):
                block = jnp.where(steps[diff] == b, table[h, b], block)
            bias[diff] = block
        low_side = jnp.full((rows, rows), table[h, buckets // 2 - 1], f32)
        high_side = jnp.full((rows, rows), table[h, buckets - 1], f32)
        for i in range(n):
            scores = dot_nt(query[i * rows : (i + 1) * rows, :], key)
            side = [
                bias[j - i] if abs(j - i) <= 1 else (high_side if j > i else low_side)
                for j in range(n)
            ]
            scores = scores + jnp.concatenate(side, axis=1)
            query_place = i * rows + lax.broadcasted_iota(jnp.int32, (rows, 1), 0)
            query_segment = jnp.zeros((rows, 1), jnp.int32)
            for j in range(seqs):
                query_segment = query_segment + (query_place >= ends[j]).astype(jnp.int32)
            scores = jnp.where(query_segment == key_segment, scores, big_negative)
            top = jnp.max(scores, axis=-1, keepdims=True)
            raised = jnp.exp(scores - top)
            total = jnp.sum(raised, axis=-1, keepdims=True)
            weights = (raised * (1.0 / total)).astype(bf16)
            weights_out[h, i * rows : (i + 1) * rows, :] = weights
            mixed_all[i, :, h * head_dim : (h + 1) * head_dim] = dot(weights, value).astype(bf16)
    for p in range(n):
        mixed_out[p][...] = mixed_all[s ^ p]


def attention_backward(n, m, rows, width, heads, buckets, experts, *refs):
    projected, tokens, gains, weight, weights, mixed, weight_out, gain_two, router = refs[:9]
    branch_refs = refs[9 : 9 + n]
    at = 9 + n
    shares = 4 if m > 1 else 2
    share_out = refs[at : at + shares]
    normed_grad_out = refs[at + shares : at + shares + n]
    gain_out, table_out = refs[at + shares + n : at + shares + n + 2]
    branch_scr, scores_scr, projected_scr, total_scr, out_scr, normed_scr, send_scr = refs[
        at + shares + n + 2 :
    ]
    s = lax.axis_index("shard")
    e = lax.axis_index("expert")
    part = width // n
    wide = 3 * part
    group = n * rows
    head_dim = part // heads
    for p in range(n):
        branch_scr[s ^ p] = branch_refs[p][...]
    branch = branch_scr[...].reshape(group, width)
    grad_mixed = dot_nt(branch, weight_out[...]).astype(bf16)
    out_scr[...] = dot_tn(mixed[...].reshape(group, part), branch)
    base = offsets(rows)
    steps = {diff: bucket_index(base + diff * rows) for diff in (-1, 0, 1)}
    lane = lax.broadcasted_iota(jnp.int32, (row_tile, 128), 1)
    line = lax.broadcasted_iota(jnp.int32, (row_tile, 128), 0)
    table_total = jnp.zeros((row_tile, 128), f32)
    per_line = buckets // row_tile
    for h in range(heads):
        query = projected[:, h * head_dim : (h + 1) * head_dim]
        key = projected[:, part + h * head_dim : part + (h + 1) * head_dim]
        value = projected[:, 2 * part + h * head_dim : 2 * part + (h + 1) * head_dim]
        near = {diff: jnp.zeros((rows, rows), f32) for diff in (-1, 0, 1)}
        low_side = jnp.zeros((1, rows), f32)
        high_side = jnp.zeros((1, rows), f32)
        upstream = grad_mixed[:, h * head_dim : (h + 1) * head_dim]
        for i in range(n):
            weights_i = weights[h, i * rows : (i + 1) * rows, :].astype(f32)
            grad_weights = dot_nt(upstream[i * rows : (i + 1) * rows, :], value)
            inner = jnp.sum(weights_i * grad_weights, axis=-1, keepdims=True)
            grad_scores = weights_i * (grad_weights - inner)
            scores_scr[i * rows : (i + 1) * rows, :] = grad_scores.astype(bf16)
            for j in range(n):
                block = grad_scores[:, j * rows : (j + 1) * rows]
                if abs(j - i) <= 1:
                    near[j - i] = near[j - i] + block
                elif j > i:
                    high_side = high_side + jnp.sum(block, axis=0, keepdims=True)
                else:
                    low_side = low_side + jnp.sum(block, axis=0, keepdims=True)
        for b in range(buckets):
            amount = jnp.zeros((1, rows), f32)
            for diff in (-1, 0, 1):
                if b in near_buckets(diff, buckets):
                    amount = amount + jnp.sum(
                        jnp.where(steps[diff] == b, near[diff], 0.0), axis=0, keepdims=True
                    )
            if b == buckets - 1:
                amount = amount + high_side
            if b == buckets // 2 - 1:
                amount = amount + low_side
            amount = jnp.sum(amount, axis=1, keepdims=True)
            spot = (line == b // per_line) & (lane == h * per_line + b % per_line)
            table_total = jnp.where(spot, amount, table_total)
        grad_scores_all = scores_scr[...]
        projected_scr[:, h * head_dim : (h + 1) * head_dim] = dot(grad_scores_all, key).astype(bf16)
        projected_scr[:, part + h * head_dim : part + (h + 1) * head_dim] = (
            dot_tn(query, grad_scores_all).T.astype(bf16)
        )
        projected_scr[:, 2 * part + h * head_dim : 2 * part + (h + 1) * head_dim] = (
            dot_tn(upstream, weights[h]).T.astype(bf16)
        )
    table_out[...] = table_total
    grad_projected = projected_scr[...]
    normed_grad = dot_nt(grad_projected, weight[:, :wide])
    send_scr[...] = normed_grad.astype(bf16).reshape(n, rows, width)
    for p in range(n):
        normed_grad_out[p][...] = send_scr[s ^ p]
    gain = gains[0:1, :]
    grad_gain = jnp.zeros((1, width), f32)
    for j in range(n):
        value = tokens[j].astype(f32)
        unit = value * lax.rsqrt(jnp.mean(value * value, axis=-1, keepdims=True) + norm_eps)
        normed_scr[j * rows : (j + 1) * rows, :] = (unit * gain).astype(bf16)
        grad_gain = grad_gain + jnp.sum(
            normed_grad[j * rows : (j + 1) * rows, :] * unit, axis=0, keepdims=True
        )
    gain_out[...] = jnp.broadcast_to(grad_gain, gain_out.shape)
    total_scr[:, :wide] = dot_tn(normed_scr[...], grad_projected)
    full = total_scr.shape[1]
    if m == 1:
        for t in range(n):
            share_out[0][t] = total_scr[t * part : (t + 1) * part, :wide].astype(bf16)
        share_out[1][...] = out_scr[...].astype(bf16)
        return
    piece = part // m
    total_scr[:, wide:] = jnp.zeros((width, full - wide), f32)
    size = 128
    for c in range(width // size):
        here = slice(c * size, (c + 1) * size)
        total_scr[here, wide : wide + 1] = to_column(grad_gain[:, here], size)
        total_scr[here, wide + 1 : wide + 2] = to_column(gain_two[0:1, here], size)
    total_scr[:, wide + 2 : wide + 2 + experts] = router[...]
    at = wide + 2 + experts
    rest = (width - full) // n
    for t in range(n):
        total_scr[t * part : (t + 1) * part, at : at + rest] = out_scr[
            :, full + t * rest : full + (t + 1) * rest
        ]
    at = at + rest
    for d in range(m):
        total_scr[d * piece : d * piece + row_tile, at : at + heads * per_line] = table_total[
            :, : heads * per_line
        ]
    for d in range(m):
        target = share_out[(d & 1) + 2 * (d < m // 2)]
        place = (d >> 1) % (m // 4)
        start = (e ^ d) * piece
        for t in range(n):
            rows_at = pl.multiple_of(t * part + start, row_tile)
            target[place, t] = total_scr[pl.ds(rows_at, piece), :].astype(bf16)
        rows_at = pl.multiple_of(start, row_tile)
        target[place, n] = out_scr[pl.ds(rows_at, piece), :full].astype(bf16)


def assemble(n, m, part, piece, experts, *refs):
    total_out, out_out, small_out = refs[m:]
    s = lax.axis_index("shard")
    e = lax.axis_index("expert")
    wide = 3 * part
    full = refs[0].shape[2]
    at = wide + 2 + experts
    rest = (n * part - full) // n
    for d in range(m):
        start = pl.multiple_of((e ^ d) * piece, row_tile)
        own = pl.ds(start, piece)
        small = jnp.zeros((piece, full - wide), f32)
        for p in range(n):
            small = small + refs[d][p, :, wide:].astype(f32)
            out_out[own, full + p * rest : full + (p + 1) * rest] = refs[d][p, :, at : at + rest].astype(
                f32
            )
        out_out[own, :full] = refs[d][n].astype(f32)
        small_out[own, :] = small
    for k in range(n):

        @pl.when(s == k)
        def _():
            for d in range(m):
                own = pl.ds(pl.multiple_of((e ^ d) * piece, row_tile), piece)
                for p in range(n):
                    for kind in range(3):
                        to = (kind * n + (k ^ p)) * part
                        total_out[own, to : to + part] = refs[d][
                            p, :, kind * part : (kind + 1) * part
                        ].astype(f32)


def expert_forward(rows, own, came, up_own, up_pair, down_own, down_pair, *outs):
    hidden_out, slope_out, keep_out, send_out = outs
    for i, source in enumerate((own, came)):
        result = 0.0
        for k, (up, down) in enumerate(((up_own, down_own), (up_pair, down_pair))):
            before = dot(source[...], up[0])
            square = before * before
            tanh_value = jnp.tanh(gelu_scale * before * (1.0 + gelu_cubic * square))
            half = 0.5 * (1.0 + tanh_value)
            hidden = (before * half).astype(bf16)
            slope = half + 0.5 * before * (1.0 - tanh_value * tanh_value) * gelu_scale * (
                1.0 + 3.0 * gelu_cubic * square
            )
            hidden_out[k, i * rows : (i + 1) * rows, :] = hidden
            slope_out[k, i * rows : (i + 1) * rows, :] = slope.astype(bf16)
            result = result + dot(hidden, down[0])
        if i:
            send_out[...] = result.astype(bf16)
        else:
            keep_out[...] = result


def expert_backward(rows, own, came, up_own, up_pair, down_own, down_pair, slope, *outs):
    before_out, keep_out, send_out = outs
    grads = jnp.concatenate([own[...], came[...]], axis=0)
    result = 0.0
    for k, (up, down) in enumerate(((up_own, down_own), (up_pair, down_pair))):
        grad_before = (dot_nt(grads, down[0]) * slope[k].astype(f32)).astype(bf16)
        before_out[k] = grad_before
        result = result + dot_nt(grad_before, up[0])
    keep_out[...] = result[:rows]
    send_out[...] = result[rows:].astype(bf16)


def expert_weights(own, came, own_grad, came_grad, hidden, grad_before, *outs):
    up_out, down_out, up_send, down_send = outs
    grads = jnp.concatenate([own_grad[...], came_grad[...]], axis=0)
    rows = jnp.concatenate([own[...], came[...]], axis=0)
    up_send[0] = dot_tn(rows, grad_before[1]).astype(bf16)
    down_send[0] = dot_tn(hidden[1], grads).astype(bf16)
    up_out[0] = dot_tn(rows, grad_before[0])
    down_out[0] = dot_tn(hidden[0], grads)


def rms_factor(value):
    return lax.rsqrt(jnp.mean(value * value, axis=-1, keepdims=True) + norm_eps)


def rms_backward(value, factor, gain, upstream):
    scaled = upstream * gain
    grad_value = factor * scaled - value * factor * factor * factor * jnp.mean(
        scaled * value, axis=-1, keepdims=True
    )
    grad_gain = jnp.sum(upstream * value * factor, axis=0)
    return (grad_value, grad_gain)


def local(
    tokens,
    lengths,
    routes,
    attention_in,
    attention_out,
    position_bias,
    first_gain,
    second_gain,
    router,
    expert_in,
    expert_out,
    cotangent,
):
    n = lax.axis_size("shard")
    m = lax.axis_size("expert")
    s = lax.axis_index("shard")
    e = lax.axis_index("expert")
    rows, width = tokens.shape
    heads, buckets = position_bias.shape
    part = width // n
    wide = 3 * part
    group = n * rows
    seqs = lengths.shape[1]
    experts = router.shape[1]
    direct = m == 8
    full = wide + -wide % 128
    micro = 10**9

    token_blocks = gather_relative(tokens, "shard")
    weight_blocks = exchange_relative(
        call(
            lambda *refs: prepare_weight(n, part, *refs),
            [shape((part, full))] * n,
            (attention_in, first_gain.reshape(1, part), second_gain.reshape(1, part)),
        ),
        "shard",
    )
    own_out, own_up, own_down, token_blocks, weight_blocks = lax.optimization_barrier(
        (attention_out, expert_in, expert_out, token_blocks, weight_blocks)
    )
    out_blocks = gather_relative(own_out, "shard")
    pair_up = swap(own_up, "shard", pair)
    pair_down = swap(own_down, "shard", pair)

    answers = call(
        lambda *refs: attention_forward(n, rows, width, heads, seqs, buckets, *refs),
        (
            shape((n, rows, width)),
            shape((width, full)),
            shape((group, wide)),
            shape((heads, group, group)),
            shape((row_tile, width), f32),
            shape((n, rows, part)),
            *[shape((rows, part))] * n,
        ),
        (lengths, position_bias.astype(f32), *token_blocks, *weight_blocks),
        "ss",
        [pltpu.VMEM((group, width), bf16)],
        work=10 * micro,
    )
    tokens_all, weight, projected, weights, gains, mixed = answers[:6]
    mixed_blocks = exchange_relative(list(answers[6:]), "shard")
    gain_one, gain_two = gains[0:1], gains[1:2]

    inputs = tokens.astype(f32)
    hidden_one = inputs + sum(dot(mixed_blocks[p], out_blocks[p]) for p in range(n))
    factor_two = rms_factor(hidden_one)
    normed_two = hidden_one * factor_two * gain_two
    logits = jnp.dot(
        normed_two, router, precision=lax.Precision.HIGHEST, preferred_element_type=f32
    )
    shifted = jnp.exp(logits - jnp.max(logits, axis=-1, keepdims=True))
    probs = shifted / jnp.sum(shifted, axis=-1, keepdims=True)
    route = routes[:, 0]
    chosen = (route[:, None] == lax.iota(jnp.int32, experts)[None, :]).astype(f32)
    gate = jnp.sum(probs * chosen, axis=1)
    lower = (lax.iota(jnp.int32, rows)[:, None] >= lax.iota(jnp.int32, rows)[None, :]).astype(bf16)
    running = dot(lower, chosen.astype(bf16))
    slot = jnp.sum((running - 1.0) * chosen, axis=1).astype(jnp.int32)
    capacity = max(2, 9 * rows // (8 * experts) + 1)
    capacity = -(-capacity // slot_tile) * slot_tile
    places = experts * capacity
    half = places // 2
    if direct:
        holder = route ^ e
        target = (holder & 1) * half + (holder >> 1) * capacity + slot
    else:
        target = route * capacity + slot
    collect = (target[:, None] == lax.iota(jnp.int32, places)[None, :]).astype(bf16)
    upstream = cotangent.astype(f32)
    grad_result = (gate[:, None] * upstream).astype(bf16)

    def plain(value):
        return lax.all_to_all(
            value.reshape(experts, capacity, width), "expert", 0, 0, tiled=True
        ).reshape(places, width)

    def send(value):
        if not direct:
            return plain(dot_tn(collect, value).astype(bf16))
        came = swap(dot_tn(collect[:, half:], value).astype(bf16), "expert", 1)
        own = dot_tn(collect[:, :half], value).astype(bf16).reshape(m // 2, capacity, width)
        both = jnp.concatenate([own, came.reshape(m // 2, capacity, width)], axis=1)
        blocks = [both[d] if d == 0 else swap(both[d], "expert", 2 * d) for d in range(m // 2)]
        return jnp.concatenate(blocks, axis=0)

    def give_back(value):
        if not direct:
            return dot(collect, plain(value))
        both = value.reshape(m // 2, 2 * capacity, width)
        blocks = [both[d] if d == 0 else swap(both[d], "expert", 2 * d) for d in range(m // 2)]
        own = jnp.concatenate([block[:capacity] for block in blocks])
        other = swap(jnp.concatenate([block[capacity:] for block in blocks]), "expert", 1)
        return dot(collect[:, :half], own) + dot(collect[:, half:], other)

    def reduce_shard(keep, out):
        return (keep + swap(out, "shard", 2 * pair).astype(f32)).astype(bf16)

    arrived = send(normed_two.astype(bf16))
    row_blocks = (arrived, swap(arrived, "shard", 2 * pair))
    arrived_grad = send(grad_result)
    grad_blocks = (arrived_grad, swap(arrived_grad, "shard", 2 * pair))

    units = expert_in.shape[2]
    both_rows = 2 * places
    expert_weight = (own_up, pair_up, own_down, pair_down)
    hidden, slope, keep, out = call(
        lambda *refs: expert_forward(places, *refs),
        (
            shape((2, both_rows, units)),
            shape((2, both_rows, units)),
            shape((places, width), f32),
            shape((places, width)),
        ),
        (*row_blocks, *expert_weight),
        work=6 * micro,
    )
    expert_result = give_back(reduce_shard(keep, out))
    grad_before, keep_grad, out_grad = call(
        lambda *refs: expert_backward(places, *refs),
        (
            shape((2, both_rows, units)),
            shape((places, width), f32),
            shape((places, width)),
        ),
        (*grad_blocks, *expert_weight, slope),
        work=6 * micro,
    )
    grad_sent = give_back(reduce_shard(keep_grad, out_grad))
    grad_up, grad_down, up_send, down_send = call(
        expert_weights,
        (
            shape(expert_in.shape, f32),
            shape(expert_out.shape, f32),
            shape(expert_in.shape),
            shape(expert_out.shape),
        ),
        (*row_blocks, *grad_blocks, hidden, grad_before),
        work=6 * micro,
    )
    grad_up = grad_up + swap(up_send, "shard", pair).astype(f32)
    grad_down = grad_down + swap(down_send, "shard", pair).astype(f32)

    layer_out = (hidden_one + gate[:, None] * expert_result).astype(bf16)
    grad_gate = jnp.sum(upstream * expert_result, axis=1)
    grad_logits = (grad_gate * gate)[:, None] * (chosen - probs)
    grad_router = lax.dot_general(
        normed_two,
        grad_logits,
        (((0,), (0,)), ((), ())),
        precision=lax.Precision.HIGHEST,
        preferred_element_type=f32,
    )
    grad_normed_two = grad_sent + lax.dot_general(
        grad_logits,
        router,
        (((1,), (1,)), ((), ())),
        precision=lax.Precision.HIGHEST,
        preferred_element_type=f32,
    )
    grad_middle, grad_gain_two = rms_backward(hidden_one, factor_two, gain_two, grad_normed_two)
    grad_hidden = upstream + grad_middle
    branch_blocks = gather_relative(grad_hidden.astype(bf16), "shard")

    holders = m if direct else 1
    piece = part // m
    if direct:
        share_shapes = [shape((m // 4, n + 1, piece, full))] * 4
    else:
        share_shapes = [shape((n, part, wide)), shape((part, width))]
    answers = call(
        lambda *refs: attention_backward(n, holders, rows, width, heads, buckets, experts, *refs),
        (
            *share_shapes,
            *[shape((rows, width))] * n,
            shape((row_tile, width), f32),
            shape((row_tile, 128), f32),
        ),
        (
            projected,
            tokens_all,
            gains,
            weight,
            weights,
            mixed,
            own_out,
            grad_gain_two[None],
            grad_router,
            *branch_blocks,
        ),
        "",
        [
            pltpu.VMEM((n, rows, width), bf16),
            pltpu.VMEM((group, group), bf16),
            pltpu.VMEM((group, wide), bf16),
            pltpu.VMEM((width, full), f32),
            pltpu.VMEM((part, width), f32),
            pltpu.VMEM((group, width), bf16),
            pltpu.VMEM((n, rows, width), bf16),
        ],
        work=8 * micro,
    )
    shares = answers[: len(share_shapes)]
    normed_grads = answers[len(share_shapes) : len(share_shapes) + n]
    gain_row, table = answers[len(share_shapes) + n :]

    per_line = buckets // row_tile

    def biases(block):
        return block.reshape(row_tile, heads, per_line).swapaxes(0, 1).reshape(heads, buckets)

    grad_normed = sum(x.astype(f32) for x in exchange_relative(list(normed_grads), "shard"))
    grad_input_norm, _ = rms_backward(inputs, rms_factor(inputs), gain_one, grad_normed)
    grad_tokens = (grad_hidden + grad_input_norm).astype(bf16)
    if direct:
        far_keep, far_send, near_keep, near_send = shares
        far = far_keep.astype(f32) + swap(far_send, "expert", 1).astype(f32)
        near = near_keep.astype(f32) + swap(near_send, "expert", 1).astype(f32)
        came = [swap(far[d].astype(bf16), "expert", m // 2 + 2 * d) for d in range(m // 4)]
        came += [swap(near[d].astype(bf16), "expert", 2 * d) for d in range(1, m // 4)]
        summed = near[0] + sum(x.astype(f32) for x in came)
        at = wide + 2 + experts
        rest = (width - full) // n
        table_total = biases(
            summed[0, :row_tile, at + rest : at + rest + heads * per_line]
        )
        low = summed.astype(bf16)
        mine = exchange_relative(
            [lax.dynamic_index_in_dim(low, s ^ p, 0, keepdims=False) for p in range(n)], "shard"
        )
        lane = lax.iota(jnp.int32, full)[None, :]
        own_lane = (lane >= at) & (lane < at + rest)
        mine = jnp.stack(
            [jnp.where(own_lane, low[p], mine[p]) for p in range(n)] + [low[n]], axis=0
        )
        blocks = gather_relative(mine, "expert")
        grad_attention_in, grad_attention_out, small_total = call(
            lambda *refs: assemble(n, m, part, piece, experts, *refs),
            (shape((part, 3 * width), f32), shape((part, width), f32), shape((part, full - wide), f32)),
            (*blocks,),
        )
    else:
        came = lax.all_to_all(
            shares[0].reshape(n, m, piece, wide).swapaxes(0, 1), "expert", 0, 0, tiled=True
        )
        summed = sum(x.astype(f32) for x in came).astype(bf16)
        mine = lax.all_to_all(summed, "shard", 0, 0, tiled=True)
        mine = mine.reshape(n, piece, 3, part).transpose(1, 2, 0, 3).reshape(piece, 3 * width)
        came = lax.all_to_all(shares[1].reshape(m, piece, width), "expert", 0, 0, tiled=True)
        out_mine = sum(x.astype(f32) for x in came).astype(bf16)
        grad_attention_in = lax.all_gather(mine, "expert", axis=0, tiled=True).astype(f32)
        grad_attention_out = lax.all_gather(out_mine, "expert", axis=0, tiled=True).astype(f32)
        small = jnp.concatenate([gain_row[0][:, None], grad_gain_two[:, None], grad_router], axis=1)
        small_total = lax.psum_scatter(small, "shard", scatter_dimension=0, tiled=True)
        small_total, table_total = lax.psum(
            (small_total, biases(table[:, : heads * per_line])), "expert"
        )
    return (
        layer_out,
        grad_tokens,
        grad_attention_in,
        grad_attention_out,
        table_total,
        small_total[:, 0],
        small_total[:, 1],
        small_total[:, 2 : 2 + experts],
        grad_up,
        grad_down,
    )


def solution(mesh):
    in_specs = (
        P(("expert", "shard"), None),
        P("expert", None),
        P(("expert", "shard"), None),
        P("shard", None),
        P("shard", None),
        P("shard", None),
        P("shard"),
        P("shard"),
        P(),
        P("expert", None, "shard"),
        P("expert", "shard", None),
        P(("expert", "shard"), None),
    )
    out_specs = (
        P(("expert", "shard"), None),
        P(("expert", "shard"), None),
        P("shard", None),
        P("shard", None),
        P("shard", None),
        P("shard"),
        P("shard"),
        P("shard", None),
        P("expert", None, "shard"),
        P("expert", "shard", None),
    )
    return jax.shard_map(local, mesh=mesh, in_specs=in_specs, out_specs=out_specs, check_vma=False)
```

time: 278 us -> 201 us (0.72)
  waiting for transfers between devices: 116 us -> 72.8 us
  starting transfers between devices: 73.8 us -> 56 us
  between operations: 14.9 us -> 1.34 us
    reduce_scatter x1 -> x0, waiting for transfers between devices: 51.4 us -> none  [local(): lax.psum_scatter(grad_weight_out, 'expert', scatter_dimension=0, tiled=True)]
    ppermute x64 -> x57, starting transfers between devices: 73.8 us -> 56 us  [swap(): return lax.ppermute(value, axis, [(i, i ^ bit) for i in range(size)])]
    ppermute x64 -> x57, waiting for transfers between devices: 64.2 us -> 72.8 us  [swap(): return lax.ppermute(value, axis, [(i, i ^ bit) for i in range(size)])]
    reshape x6 -> x7, local copies, waits for them, and re-layouts: 0.39 us -> 3.22 us  [the longest x1 1.22 us: local(): first_gain.reshape(1, part)]
    pallas_call x8 -> x7, Pallas kernels: 43.5 us -> 43 us  [call(): pl.pallas_call(kernel, out_shape=out_shape, in_specs=in_specs, out_specs=...]
  transfers between devices with their start and end apart: 65 -> 57, of which waited for: 29 -> 28; matrix products, arithmetic and copies ran while one was open for 6% -> 10% of each run, Pallas kernels for 11% -> 15%
where the time goes in v3:
time: 201 us; the launch traced here: 200 us
  waiting for transfers between devices  72.8 us (36%)
  starting transfers between devices  56 us (28%)
  Pallas kernels  43 us (21%)
  local copies, waits for them, and re-layouts  11.8 us (6%)
  matrix products  7.59 us (4%)
  other arithmetic  7.57 us (4%)
    ppermute x57, waiting for transfers between devices, swap(): return lax.ppermute(value, axis, [(i, i ^ bit) for i in range(size)])  72.8 us
    ppermute x57, starting transfers between devices, swap(): return lax.ppermute(value, axis, [(i, i ^ bit) for i in range(size)])  56 us
    pallas_call x7, Pallas kernels, call(): pl.pallas_call(kernel, out_shape=out_shape, in_specs=in_specs, out_specs=...  43 us
  transfers between devices with their start and end apart: 57, of which 28 were waited for; matrix products, arithmetic and copies ran while one was open for 10% of the time, Pallas kernels for 15%

profile of v3, /device:TPU:0, one launch (start us, length us, event | category | flops | bytes accessed | tf_op | source)
XLA Modules:
  0.0 200.1 jit_solution(5415026554070148687)
XLA Ops:
  1.2 2.6 %collective-permute-start.1 = (bf16[128,768]{1,0:T(8,128)(2,1)}, bf16[128,768]{1,0:T(8,128)(2,1)S(1)}, u32[]{:S(2)}, u32[]{:S(2)}) collective-permute-start(bf16[128,768]{1,0:T(8,128)(2,1)} %refs_2_), channel_id=1, source_target_pairs={{0,2},{1,3},{2,0},{3,1},{4,6},{5,7},{6,4},{7,5},{8,10},{9,11},{10,... | collective-permute-start | bytes 589832 | tf_op jit(solution)/shard_map/ppermute | solution.py:44
  6.2 2.5 %shard_map.195 = (bf16[192,640]{1,0:T(8,128)(2,1)}, bf16[192,640]{1,0:T(8,128)(2,1)}, bf16[192,640]{1,0:T(8,128)(2,1)}, bf16[192,640]{1,0:T(8,128)(2,1)}) custom-call(bf16[192,2304]{1,0:T(8,128)(2,1)} %refs_0_.2, bf16[1,192]{1,0:T(2,128)(2,1)} %reshape.121.refs_1_, bf16[1,192]{1,0:T(2,128)(2,1)} %reshape.122.refs_2_), custom_call_target="tpu_custom_call" | custom-call | tf_op jit(solution)/shard_map/pallas_call | solution.py:66
  14.0 3.9 %collective-permute-done.4.refs_8_ = bf16[192,640]{1,0:T(8,128)(2,1)S(1)} collective-permute-done((bf16[192,640]{1,0:T(8,128)(2,1)}, bf16[192,640]{1,0:T(8,128)(2,1)S(1)}, u32[]{:S(2)}, u32[]{:S(2)}) %collective-permute-start.4) | collective-permute-done | bytes 245792 | tf_op jit(solution)/shard_map/ppermute | solution.py:44
  17.9 4.1 %collective-permute-done.5.refs_9_ = bf16[192,640]{1,0:T(8,128)(2,1)S(1)} collective-permute-done((bf16[192,640]{1,0:T(8,128)(2,1)}, bf16[192,640]{1,0:T(8,128)(2,1)S(1)}, u32[]{:S(2)}, u32[]{:S(2)}) %collective-permute-start.5) | collective-permute-done | bytes 245792 | tf_op jit(solution)/shard_map/ppermute | solution.py:44
  23.1 9.5 %shard_map.196 = (bf16[4,128,768]{2,1,0:T(8,128)(2,1)}, bf16[768,640]{1,0:T(8,128)(2,1)}, bf16[512,576]{1,0:T(8,128)(2,1)}, bf16[3,512,512]{2,1,0:T(8,128)(2,1)}...) custom-call(s32[1,3]{1,0:T(1,128)} %refs_0_.3, ...), custom_call_target="tpu_custom_call" | custom-call | flops 10000000000 | tf_op jit(solution)/shard_map/pallas_call | solution.py:66
  45.4 3.4 %collective-permute-done.12 = bf16[80,768]{1,0:T(8,128)(2,1)S(1)} collective-permute-done((bf16[80,768]{1,0:T(8,128)(2,1)S(1)}, bf16[80,768]{1,0:T(8,128)(2,1)S(1)}, u32[]{:S(2)}, u32[]{:S(2)}) %collective-permute-start.12) | collective-permute-done | bytes 122912 | tf_op jit(solution)/shard_map/ppermute | solution.py:44
  50.6 2.5 %collective-permute-start.15 = (bf16[40,768]{1,0:T(8,128)(2,1)S(1)}, bf16[40,768]{1,0:T(8,128)(2,1)S(1)}, u32[]{:S(2)}, u32[]{:S(2)}) collective-permute-start(bf16[40,768]{1,0:T(8,128)(2,1)S(1)} %get-tuple-element.144), channel_id=1, source_target_pairs={{0,24},{4,28},{8,16},{12,20},{16,8},{20,12},{24,0},{28,4},{1,25},{... | collective-permute-start | bytes 184328 | tf_op jit(solution)/shard_map/ppermute | solution.py:44
  54.0 2.8 %collective-permute-done.15 = bf16[40,768]{1,0:T(8,128)(2,1)S(1)} collective-permute-done((bf16[40,768]{1,0:T(8,128)(2,1)S(1)}, bf16[40,768]{1,0:T(8,128)(2,1)S(1)}, u32[]{:S(2)}, u32[]{:S(2)}) %collective-permute-start.15) | collective-permute-done | bytes 61472 | tf_op jit(solution)/shard_map/ppermute | solution.py:44
  56.8 2.1 %collective-permute-done.14 = bf16[40,768]{1,0:T(8,128)(2,1)S(1)} collective-permute-done((bf16[40,768]{1,0:T(8,128)(2,1)S(1)}, bf16[40,768]{1,0:T(8,128)(2,1)S(1)}, u32[]{:S(2)}, u32[]{:S(2)}) %collective-permute-start.14) | collective-permute-done | bytes 61472 | tf_op jit(solution)/shard_map/ppermute | solution.py:44
  60.6 2.7 %collective-permute-start.27 = (bf16[40,768]{1,0:T(8,128)(2,1)S(1)}, bf16[40,768]{1,0:T(8,128)(2,1)S(1)}, u32[]{:S(2)}, u32[]{:S(2)}) collective-permute-start(bf16[40,768]{1,0:T(8,128)(2,1)S(1)} %get-tuple-element.140), channel_id=1, source_target_pairs={{0,24},{4,28},{8,16},{12,20},{16,8},{20,12},{24,0},{28,4},{1,25},{... | collective-permute-start | bytes 184328 | tf_op jit(solution)/shard_map/ppermute | solution.py:44
  63.3 2.0 %collective-permute-done.25 = bf16[40,768]{1,0:T(8,128)(2,1)S(1)} collective-permute-done((bf16[40,768]{1,0:T(8,128)(2,1)S(1)}, bf16[40,768]{1,0:T(8,128)(2,1)S(1)}, u32[]{:S(2)}, u32[]{:S(2)}) %collective-permute-start.25) | collective-permute-done | bytes 61472 | tf_op jit(solution)/shard_map/ppermute | solution.py:44
  66.8 4.2 %collective-permute-done.26 = bf16[40,768]{1,0:T(8,128)(2,1)S(1)} collective-permute-done((bf16[40,768]{1,0:T(8,128)(2,1)S(1)}, bf16[40,768]{1,0:T(8,128)(2,1)S(1)}, u32[]{:S(2)}, u32[]{:S(2)}) %collective-permute-start.26) | collective-permute-done | bytes 61472 | tf_op jit(solution)/shard_map/ppermute | solution.py:44
  72.8 6.0 %shard_map.197 = (bf16[2,320,768]{2,1,0:T(8,128)(2,1)}, bf16[2,320,768]{2,1,0:T(8,128)(2,1)}, f32[160,768]{1,0:T(8,128)}, bf16[160,768]{1,0:T(8,128)(2,1)}) custom-call(bf16[160,768]{1,0:T(8,128)(2,1)} %copy-done.11, bf16[160,768]{1,0:T(8,128)(2,1)} %copy-done.25, bf16[1,768,768]{2,1,0:T(8,128)(2,1)} %refs_2_.2, bf16[1,768,768]{2,1,0:T(8,128)(2,1)} %copy-done.23, ...), custom_call_target="tpu_custom_call" | custom-call | flops 6000000000 | tf_op jit(solution)/shard_map/pallas_call | solution.py:66
  81.0 6.0 %shard_map.198 = (bf16[2,320,768]{2,1,0:T(8,128)(2,1)}, f32[160,768]{1,0:T(8,128)}, bf16[160,768]{1,0:T(8,128)(2,1)}) custom-call(bf16[160,768]{1,0:T(8,128)(2,1)} %copy-done.12, bf16[160,768]{1,0:T(8,128)(2,1)} %copy-done.26, bf16[1,768,768]{2,1,0:T(8,128)(2,1)} %refs_2_.2, bf16[1,768,768]{2,1,0:T(8,128)(2,1)} %copy-done.23, bf16[1,768,768]{2,1,0:T(8,128)(2,1)} %refs_4_.1, ...), custom_call_target="tpu_custom_call" | custom-call | flops 6000000000 | tf_op jit(solution)/shard_map/pallas_call | solution.py:66
  87.8 5.6 %collective-permute-done.29 = bf16[160,768]{1,0:T(8,128)(2,1)S(1)} collective-permute-done((bf16[160,768]{1,0:T(8,128)(2,1)}, bf16[160,768]{1,0:T(8,128)(2,1)S(1)}, u32[]{:S(2)}, u32[]{:S(2)}) %collective-permute-start.29) | collective-permute-done | bytes 245792 | tf_op jit(solution)/shard_map/ppermute | solution.py:44
  93.5 2.3 %collective-permute-start.22 = (bf16[40,768]{1,0:T(8,128)(2,1)S(1)}, bf16[40,768]{1,0:T(8,128)(2,1)S(1)}, u32[]{:S(2)}, u32[]{:S(2)}) collective-permute-start(bf16[40,768]{1,0:T(8,128)(2,1)S(1)} %get-tuple-element.154), channel_id=1, source_target_pairs={{0,24},{4,28},{8,16},{12,20},{16,8},{20,12},{24,0},{28,4},{1,25},{... | collective-permute-start | bytes 184328 | tf_op jit(solution)/shard_map/ppermute | solution.py:44
  95.8 2.1 %collective-permute-start.30 = (bf16[40,768]{1,0:T(8,128)(2,1)S(1)}, bf16[40,768]{1,0:T(8,128)(2,1)S(1)}, u32[]{:S(2)}, u32[]{:S(2)}) collective-permute-start(bf16[40,768]{1,0:T(8,128)(2,1)S(1)} %get-tuple-element.148), channel_id=1, source_target_pairs={{0,8},{4,12},{8,0},{12,4},{16,24},{20,28},{24,16},{28,20},{1,9},{5... | collective-permute-start | bytes 184328 | tf_op jit(solution)/shard_map/ppermute | solution.py:44
  98.0 2.3 %collective-permute-start.32 = (bf16[40,768]{1,0:T(8,128)(2,1)S(1)}, bf16[40,768]{1,0:T(8,128)(2,1)S(1)}, u32[]{:S(2)}, u32[]{:S(2)}) collective-permute-start(bf16[40,768]{1,0:T(8,128)(2,1)S(1)} %get-tuple-element.149), channel_id=1, source_target_pairs={{0,24},{4,28},{8,16},{12,20},{16,8},{20,12},{24,0},{28,4},{1,25},{... | collective-permute-start | bytes 184328 | tf_op jit(solution)/shard_map/ppermute | solution.py:44
  108.1 2.3 %collective-permute-done.33 = bf16[80,768]{1,0:T(8,128)(2,1)S(1)} collective-permute-done((bf16[80,768]{1,0:T(8,128)(2,1)S(1)}, bf16[80,768]{1,0:T(8,128)(2,1)S(1)}, u32[]{:S(2)}, u32[]{:S(2)}) %collective-permute-start.33) | collective-permute-done | bytes 122912 | tf_op jit(solution)/shard_map/ppermute | solution.py:44
  112.5 4.4 %collective-permute-done.35.refs_11_ = bf16[128,768]{1,0:T(8,128)(2,1)S(1)} collective-permute-done((bf16[128,768]{1,0:T(8,128)(2,1)S(1)}, bf16[128,768]{1,0:T(8,128)(2,1)S(1)}, u32[]{:S(2)}, u32[]{:S(2)}) %collective-permute-start.35) | collective-permute-done | bytes 196640 | tf_op jit(solution)/shard_map/ppermute | solution.py:44
  119.3 8.9 %shard_map.199 = (bf16[2,5,24,640]{3,2,1,0:T(8,128)(2,1)}, bf16[2,5,24,640]{3,2,1,0:T(8,128)(2,1)}, bf16[2,5,24,640]{3,2,1,0:T(8,128)(2,1)}, bf16[2,5,24,640]{3,...) custom-call(bf16[512,576]{1,0:T(8,128)(2,1)} %get-tuple-element.82.r, ...), custom_call_target="tpu_custom_call" | custom-call | flops 8000000000 | tf_op jit(solution)/shard_map/pallas_call | solution.py:66
  129.8 6.8 %shard_map.201 = (f32[1,768,768]{2,1,0:T(8,128)}, f32[1,768,768]{2,1,0:T(8,128)}, bf16[1,768,768]{2,1,0:T(8,128)(2,1)}, bf16[1,768,768]{2,1,0:T(8,128)(2,1)}) custom-call(bf16[160,768]{1,0:T(8,128)(2,1)} %copy-done.11, bf16[160,768]{1,0:T(8,128)(2,1)} %copy-done.25, bf16[160,768]{1,0:T(8,128)(2,1)} %copy-done.12, bf16[160,768]{1,0:T(8,128)(2,1)} %copy-done.26, ...), custom_call_target="tpu_custom_call" | custom-call | flops 6000000000 | tf_op jit(solution)/shard_map/pallas_call | solution.py:66
  139.8 7.4 %collective-permute-done.41 = bf16[2,5,24,640]{3,2,1,0:T(8,128)(2,1)S(1)} collective-permute-done((bf16[2,5,24,640]{3,2,1,0:T(8,128)(2,1)S(1)}, bf16[2,5,24,640]{3,2,1,0:T(8,128)(2,1)S(1)}, u32[]{:S(2)}, u32[]{:S(2)}) %collective-permute-start.41) | collective-permute-done | bytes 307232 | tf_op jit(solution)/shard_map/ppermute | solution.py:44
  147.6 2.7 %collective-permute-start.42 = (bf16[5,24,640]{2,1,0:T(8,128)(2,1)S(1)}, bf16[5,24,640]{2,1,0:T(8,128)(2,1)S(1)}, u32[]{:S(2)}, u32[]{:S(2)}) collective-permute-start(bf16[5,24,640]{2,1,0:T(8,128)(2,1)S(1)} %get-tuple-element.136), channel_id=1, source_target_pairs={{0,16},{4,20},{8,24},{12,28},{16,0},{20,4},{24,8},{28,12},{1,17},{... | collective-permute-start | bytes 460808 | tf_op jit(solution)/shard_map/ppermute | solution.py:44
  150.4 4.0 %collective-permute-done.39 = bf16[128,768]{1,0:T(8,128)(2,1)S(1)} collective-permute-done((bf16[128,768]{1,0:T(8,128)(2,1)S(1)}, bf16[128,768]{1,0:T(8,128)(2,1)S(1)}, u32[]{:S(2)}, u32[]{:S(2)}) %collective-permute-start.39) | collective-permute-done | bytes 196640 | tf_op jit(solution)/shard_map/ppermute | solution.py:44
  154.4 2.2 %collective-permute-start.43 = (bf16[5,24,640]{2,1,0:T(8,128)(2,1)S(1)}, bf16[5,24,640]{2,1,0:T(8,128)(2,1)S(1)}, u32[]{:S(2)}, u32[]{:S(2)}) collective-permute-start(bf16[5,24,640]{2,1,0:T(8,128)(2,1)S(1)} %get-tuple-element.137), channel_id=1, source_target_pairs={{0,24},{4,28},{8,16},{12,20},{16,8},{20,12},{24,0},{28,4},{1,25},{... | collective-permute-start | bytes 460808 | tf_op jit(solution)/shard_map/ppermute | solution.py:44
  158.5 3.7 %collective-permute-done.43 = bf16[5,24,640]{2,1,0:T(8,128)(2,1)S(1)} collective-permute-done((bf16[5,24,640]{2,1,0:T(8,128)(2,1)S(1)}, bf16[5,24,640]{2,1,0:T(8,128)(2,1)S(1)}, u32[]{:S(2)}, u32[]{:S(2)}) %collective-permute-start.43) | collective-permute-done | bytes 153632 | tf_op jit(solution)/shard_map/ppermute | solution.py:44
  164.6 2.9 %collective-permute-done.46 = bf16[24,640]{1,0:T(8,128)(2,1)S(1)} collective-permute-done((bf16[24,640]{1,0:T(8,128)(2,1)S(1)}, bf16[24,640]{1,0:T(8,128)(2,1)S(1)}, u32[]{:S(2)}, u32[]{:S(2)}) %collective-permute-start.46) | collective-permute-done | bytes 30752 | tf_op jit(solution)/shard_map/ppermute | solution.py:44
  167.6 4.4 %collective-permute-start.51 = (bf16[5,24,640]{2,1,0:T(8,128)(2,1)S(1)}, bf16[5,24,640]{2,1,0:T(8,128)(2,1)S(1)}, u32[]{:S(2)}, u32[]{:S(2)}) collective-permute-start(bf16[5,24,640]{2,1,0:T(8,128)(2,1)S(1)} %slice_dynamic-update-slice_fusion.refs_0_), channel_id=1, source_target_pairs={{0,16},{4,20},{8,24},{12,28},{16,0},{20,4},{24,8},{28,12},{1,17},{... | collective-permute-start | bytes 460808 | tf_op jit(solution)/shard_map/ppermute | solution.py:44
  173.2 5.3 %collective-permute-done.51.refs_4_ = bf16[5,24,640]{2,1,0:T(8,128)(2,1)S(1)} collective-permute-done((bf16[5,24,640]{2,1,0:T(8,128)(2,1)S(1)}, bf16[5,24,640]{2,1,0:T(8,128)(2,1)S(1)}, u32[]{:S(2)}, u32[]{:S(2)}) %collective-permute-start.51) | collective-permute-done | bytes 153632 | tf_op jit(solution)/shard_map/ppermute | solution.py:44
  187.3 2.4 %collective-permute-done.52.refs_5_ = bf16[5,24,640]{2,1,0:T(8,128)(2,1)S(1)} collective-permute-done((bf16[5,24,640]{2,1,0:T(8,128)(2,1)S(1)}, bf16[5,24,640]{2,1,0:T(8,128)(2,1)S(1)}, u32[]{:S(2)}, u32[]{:S(2)}) %collective-permute-start.52) | collective-permute-done | bytes 153632 | tf_op jit(solution)/shard_map/ppermute | solution.py:44
  193.6 3.1 %shard_map.200 = (f32[192,2304]{1,0:T(8,128)}, f32[192,768]{1,0:T(8,128)}, f32[192,64]{1,0:T(8,128)}) custom-call(bf16[5,24,640]{2,1,0:T(8,128)(2,1)} %copy-done.13, bf16[5,24,640]{2,1,0:T(8,128)(2,1)} %copy-done.18, bf16[5,24,640]{2,1,0:T(8,128)(2,1)} %copy-done.16, bf16[5,24,640]{2,1,0:T(8,128)(2,1)} %copy-done.20, bf16[5,24,640]{2,1,0:T(8,128)(2,1)} %copy-done.15, ...), custom_call_target="tpu_custom_call" | custom-call | tf_op jit(solution)/shard_map/pallas_call | solution.py:66
  (242 shorter events, 71.4 us)
Async XLA Ops:
  0.7 13.3 %collective-permute-start = (bf16[128,768]{1,0:T(8,128)(2,1)}, bf16[128,768]{1,0:T(8,128)(2,1)S(1)}, u32[]{:S(2)}, u32[]{:S(2)}) collective-permute-start(bf16[128,768]{1,0:T(8,128)(2,1)} %refs_2_), channel_id=1, source_target_pairs={{0,1},{1,0},{2,3},{3,2},{4,5},{5,4},{6,7},{7,6},{8,9},{9,8},{10,11... | collective-permute-start | bytes 589832 | tf_op jit(solution)/shard_map/ppermute | solution.py:44
  1.2 12.2 %collective-permute-start.1 = (bf16[128,768]{1,0:T(8,128)(2,1)}, bf16[128,768]{1,0:T(8,128)(2,1)S(1)}, u32[]{:S(2)}, u32[]{:S(2)}) collective-permute-start(bf16[128,768]{1,0:T(8,128)(2,1)} %refs_2_), channel_id=1, source_target_pairs={{0,2},{1,3},{2,0},{3,1},{4,6},{5,7},{6,4},{7,5},{8,10},{9,11},{10,... | collective-permute-start | bytes 589832 | tf_op jit(solution)/shard_map/ppermute | solution.py:44
  8.9 9.0 %collective-permute-start.4 = (bf16[192,640]{1,0:T(8,128)(2,1)}, bf16[192,640]{1,0:T(8,128)(2,1)S(1)}, u32[]{:S(2)}, u32[]{:S(2)}) collective-permute-start(bf16[192,640]{1,0:T(8,128)(2,1)} %get-tuple-element.59), channel_id=1, source_target_pairs={{0,2},{1,3},{2,0},{3,1},{4,6},{5,7},{6,4},{7,5},{8,10},{9,11},{10,... | collective-permute-start | bytes 737288 | tf_op jit(solution)/shard_map/ppermute | solution.py:44
  9.2 12.8 %collective-permute-start.5 = (bf16[192,640]{1,0:T(8,128)(2,1)}, bf16[192,640]{1,0:T(8,128)(2,1)S(1)}, u32[]{:S(2)}, u32[]{:S(2)}) collective-permute-start(bf16[192,640]{1,0:T(8,128)(2,1)} %get-tuple-element.60), channel_id=1, source_target_pairs={{0,3},{1,2},{2,1},{3,0},{4,7},{5,6},{6,5},{7,4},{8,11},{9,10},{10,... | collective-permute-start | bytes 737288 | tf_op jit(solution)/shard_map/ppermute | solution.py:44
  13.4 8.6 %collective-permute-start.2 = (bf16[128,768]{1,0:T(8,128)(2,1)S(1)}, bf16[128,768]{1,0:T(8,128)(2,1)S(1)}, u32[]{:S(2)}, u32[]{:S(2)}) collective-permute-start(bf16[128,768]{1,0:T(8,128)(2,1)S(1)} %collective-permute-done.1.refs_4_), channel_id=1, source_target_pairs={{0,1},{1,0},{2,3},{3,2},{4,5},{5,4},{6,7},{7,6},{8,9},{9,8},{10,11... | collective-permute-start | bytes 589832 | tf_op jit(solution)/shard_map/ppermute | solution.py:44
  21.9 15.2 %collective-permute-start.9 = (bf16[192,768]{1,0:T(8,128)(2,1)}, bf16[192,768]{1,0:T(8,128)(2,1)S(1)}, u32[]{:S(2)}, u32[]{:S(2)}) collective-permute-start(bf16[192,768]{1,0:T(8,128)(2,1)} %refs_6_), channel_id=1, source_target_pairs={{0,2},{1,3},{2,0},{3,1},{4,6},{5,7},{6,4},{7,5},{8,10},{9,11},{10,... | collective-permute-start | bytes 884744 | tf_op jit(solution)/shard_map/ppermute | solution.py:44
  22.3 17.0 %collective-permute-start.7 = (bf16[192,768]{1,0:T(8,128)(2,1)}, bf16[192,768]{1,0:T(8,128)(2,1)S(1)}, u32[]{:S(2)}, u32[]{:S(2)}) collective-permute-start(bf16[192,768]{1,0:T(8,128)(2,1)} %refs_6_), channel_id=1, source_target_pairs={{0,1},{1,0},{2,3},{3,2},{4,5},{5,4},{6,7},{7,6},{8,9},{9,8},{10,11... | collective-permute-start | bytes 884744 | tf_op jit(solution)/shard_map/ppermute | solution.py:44
  22.5 49.2 %collective-permute-start.17 = (bf16[1,768,768]{2,1,0:T(8,128)(2,1)}, bf16[1,768,768]{2,1,0:T(8,128)(2,1)S(1)}, u32[]{:S(2)}, u32[]{:S(2)}) collective-permute-start(bf16[1,768,768]{2,1,0:T(8,128)(2,1)} %refs_2_.2), channel_id=1, source_target_pairs={{0,1},{1,0},{2,3},{3,2},{4,5},{5,4},{6,7},{7,6},{8,9},{9,8},{10,11... | collective-permute-start | bytes 3538952 | tf_op jit(solution)/shard_map/ppermute | solution.py:44
  22.8 48.9 %collective-permute-start.18 = (bf16[1,768,768]{2,1,0:T(8,128)(2,1)}, bf16[1,768,768]{2,1,0:T(8,128)(2,1)}, u32[]{:S(2)}, u32[]{:S(2)}) collective-permute-start(bf16[1,768,768]{2,1,0:T(8,128)(2,1)} %refs_4_.1), channel_id=1, source_target_pairs={{0,1},{1,0},{2,3},{3,2},{4,5},{5,4},{6,7},{7,6},{8,9},{9,8},{10,11... | collective-permute-start | bytes 3538952 | tf_op jit(solution)/shard_map/ppermute | solution.py:44
  44.6 8.5 %collective-permute-start.24 = (bf16[80,768]{1,0:T(8,128)(2,1)S(1)}, bf16[80,768]{1,0:T(8,128)(2,1)S(1)}, u32[]{:S(2)}, u32[]{:S(2)}) collective-permute-start(bf16[80,768]{1,0:T(8,128)(2,1)S(1)} %convolution_convert_fusion), channel_id=1, source_target_pairs={{0,4},{4,0},{8,12},{12,8},{16,20},{20,16},{24,28},{28,24},{1,5},{5... | collective-permute-start | bytes 368648 | tf_op jit(solution)/shard_map/ppermute | solution.py:44
  58.9 12.8 %collective-permute-start.16 = (bf16[160,768]{1,0:T(8,128)(2,1)S(1)}, bf16[160,768]{1,0:T(8,128)(2,1)S(1)}, u32[]{:S(2)}, u32[]{:S(2)}) collective-permute-start(bf16[160,768]{1,0:T(8,128)(2,1)S(1)} %pad_maximum_fusion.refs_0_.own), channel_id=1, source_target_pairs={{0,2},{1,3},{2,0},{3,1},{4,6},{5,7},{6,4},{7,5},{8,10},{9,11},{10,... | collective-permute-start | bytes 737288 | tf_op jit(solution)/shard_map/ppermute | solution.py:44
  71.0 9.2 %collective-permute-start.28 = (bf16[160,768]{1,0:T(8,128)(2,1)S(1)}, bf16[160,768]{1,0:T(8,128)(2,1)S(1)}, u32[]{:S(2)}, u32[]{:S(2)}) collective-permute-start(bf16[160,768]{1,0:T(8,128)(2,1)S(1)} %pad_maximum_fusion.1.refs_0_.own_grad), channel_id=1, source_target_pairs={{0,2},{1,3},{2,0},{3,1},{4,6},{5,7},{6,4},{7,5},{8,10},{9,11},{10,... | collective-permute-start | bytes 737288 | tf_op jit(solution)/shard_map/ppermute | solution.py:44
  78.8 8.8 %collective-permute-start.19 = (bf16[160,768]{1,0:T(8,128)(2,1)}, bf16[160,768]{1,0:T(8,128)(2,1)S(1)}, u32[]{:S(2)}, u32[]{:S(2)}) collective-permute-start(bf16[160,768]{1,0:T(8,128)(2,1)} %get-tuple-element.78), channel_id=1, source_target_pairs={{0,2},{1,3},{2,0},{3,1},{4,6},{5,7},{6,4},{7,5},{8,10},{9,11},{10,... | collective-permute-start | bytes 737288 | tf_op jit(solution)/shard_map/ppermute | solution.py:44
  87.7 12.5 %collective-permute-start.20 = (bf16[40,768]{1,0:T(8,128)(2,1)S(1)}, bf16[40,768]{1,0:T(8,128)(2,1)S(1)}, u32[]{:S(2)}, u32[]{:S(2)}) collective-permute-start(bf16[40,768]{1,0:T(8,128)(2,1)S(1)} %get-tuple-element.153), channel_id=1, source_target_pairs={{0,8},{4,12},{8,0},{12,4},{16,24},{20,28},{24,16},{28,20},{1,9},{5... | collective-permute-start | bytes 184328 | tf_op jit(solution)/shard_map/ppermute | solution.py:44
  93.5 6.7 %collective-permute-start.22 = (bf16[40,768]{1,0:T(8,128)(2,1)S(1)}, bf16[40,768]{1,0:T(8,128)(2,1)S(1)}, u32[]{:S(2)}, u32[]{:S(2)}) collective-permute-start(bf16[40,768]{1,0:T(8,128)(2,1)S(1)} %get-tuple-element.154), channel_id=1, source_target_pairs={{0,24},{4,28},{8,16},{12,20},{16,8},{20,12},{24,0},{28,4},{1,25},{... | collective-permute-start | bytes 184328 | tf_op jit(solution)/shard_map/ppermute | solution.py:44
  95.8 6.9 %collective-permute-start.30 = (bf16[40,768]{1,0:T(8,128)(2,1)S(1)}, bf16[40,768]{1,0:T(8,128)(2,1)S(1)}, u32[]{:S(2)}, u32[]{:S(2)}) collective-permute-start(bf16[40,768]{1,0:T(8,128)(2,1)S(1)} %get-tuple-element.148), channel_id=1, source_target_pairs={{0,8},{4,12},{8,0},{12,4},{16,24},{20,28},{24,16},{28,20},{1,9},{5... | collective-permute-start | bytes 184328 | tf_op jit(solution)/shard_map/ppermute | solution.py:44
  128.2 10.0 %collective-permute-start.40 = (bf16[2,5,24,640]{3,2,1,0:T(8,128)(2,1)}, bf16[2,5,24,640]{3,2,1,0:T(8,128)(2,1)S(1)}, u32[]{:S(2)}, u32[]{:S(2)}) collective-permute-start(bf16[2,5,24,640]{3,2,1,0:T(8,128)(2,1)} %get-tuple-element.92), channel_id=1, source_target_pairs={{0,4},{4,0},{8,12},{12,8},{16,20},{20,16},{24,28},{28,24},{1,5},{5... | collective-permute-start | bytes 921608 | tf_op jit(solution)/shard_map/ppermute | solution.py:44
  136.7 42.0 %collective-permute-start.55 = (bf16[1,768,768]{2,1,0:T(8,128)(2,1)}, bf16[1,768,768]{2,1,0:T(8,128)(2,1)S(1)}, u32[]{:S(2)}, u32[]{:S(2)}) collective-permute-start(bf16[1,768,768]{2,1,0:T(8,128)(2,1)} %get-tuple-element.101), channel_id=1, source_target_pairs={{0,1},{1,0},{2,3},{3,2},{4,5},{5,4},{6,7},{7,6},{8,9},{9,8},{10,11... | collective-permute-start | bytes 3538952 | tf_op jit(solution)/shard_map/ppermute | solution.py:44
  136.9 47.7 %collective-permute-start.56 = (bf16[1,768,768]{2,1,0:T(8,128)(2,1)}, bf16[1,768,768]{2,1,0:T(8,128)(2,1)S(1)}, u32[]{:S(2)}, u32[]{:S(2)}) collective-permute-start(bf16[1,768,768]{2,1,0:T(8,128)(2,1)} %get-tuple-element.103), channel_id=1, source_target_pairs={{0,1},{1,0},{2,3},{3,2},{4,5},{5,4},{6,7},{7,6},{8,9},{9,8},{10,11... | collective-permute-start | bytes 3538952 | tf_op jit(solution)/shard_map/ppermute | solution.py:44
  137.2 10.3 %collective-permute-start.37 = (bf16[128,768]{1,0:T(8,128)(2,1)S(1)}, bf16[128,768]{1,0:T(8,128)(2,1)S(1)}, u32[]{:S(2)}, u32[]{:S(2)}) collective-permute-start(bf16[128,768]{1,0:T(8,128)(2,1)S(1)} %copy-done.35), channel_id=1, source_target_pairs={{0,1},{1,0},{2,3},{3,2},{4,5},{5,4},{6,7},{7,6},{8,9},{9,8},{10,11... | collective-permute-start | bytes 589832 | tf_op jit(solution)/shard_map/ppermute | solution.py:44
  137.4 10.2 %collective-permute-start.38 = (bf16[128,768]{1,0:T(8,128)(2,1)S(1)}, bf16[128,768]{1,0:T(8,128)(2,1)S(1)}, u32[]{:S(2)}, u32[]{:S(2)}) collective-permute-start(bf16[128,768]{1,0:T(8,128)(2,1)S(1)} %copy-done.33), channel_id=1, source_target_pairs={{0,2},{1,3},{2,0},{3,1},{4,6},{5,7},{6,4},{7,5},{8,10},{9,11},{10,... | collective-permute-start | bytes 589832 | tf_op jit(solution)/shard_map/ppermute | solution.py:44
  138.2 9.0 %collective-permute-start.41 = (bf16[2,5,24,640]{3,2,1,0:T(8,128)(2,1)S(1)}, bf16[2,5,24,640]{3,2,1,0:T(8,128)(2,1)S(1)}, u32[]{:S(2)}, u32[]{:S(2)}) collective-permute-start(bf16[2,5,24,640]{3,2,1,0:T(8,128)(2,1)S(1)} %copy-done.24), channel_id=1, source_target_pairs={{0,4},{4,0},{8,12},{12,8},{16,20},{20,16},{24,28},{28,24},{1,5},{5... | collective-permute-start | bytes 921608 | tf_op jit(solution)/shard_map/ppermute | solution.py:44
  147.2 7.2 %collective-permute-start.39 = (bf16[128,768]{1,0:T(8,128)(2,1)S(1)}, bf16[128,768]{1,0:T(8,128)(2,1)S(1)}, u32[]{:S(2)}, u32[]{:S(2)}) collective-permute-start(bf16[128,768]{1,0:T(8,128)(2,1)S(1)} %copy-done.31), channel_id=1, source_target_pairs={{0,3},{1,2},{2,1},{3,0},{4,7},{5,6},{6,5},{7,4},{8,11},{9,10},{10,... | collective-permute-start | bytes 589832 | tf_op jit(solution)/shard_map/ppermute | solution.py:44
  147.5 9.3 %collective-permute-start.44 = (bf16[5,24,640]{2,1,0:T(8,128)(2,1)S(1)}, bf16[5,24,640]{2,1,0:T(8,128)(2,1)S(1)}, u32[]{:S(2)}, u32[]{:S(2)}) collective-permute-start(bf16[5,24,640]{2,1,0:T(8,128)(2,1)S(1)} %fusion.23), channel_id=1, source_target_pairs={{0,8},{4,12},{8,0},{12,4},{16,24},{20,28},{24,16},{28,20},{1,9},{5... | collective-permute-start | bytes 460808 | tf_op jit(solution)/shard_map/ppermute | solution.py:44
  147.6 10.9 %collective-permute-start.42 = (bf16[5,24,640]{2,1,0:T(8,128)(2,1)S(1)}, bf16[5,24,640]{2,1,0:T(8,128)(2,1)S(1)}, u32[]{:S(2)}, u32[]{:S(2)}) collective-permute-start(bf16[5,24,640]{2,1,0:T(8,128)(2,1)S(1)} %get-tuple-element.136), channel_id=1, source_target_pairs={{0,16},{4,20},{8,24},{12,28},{16,0},{20,4},{24,8},{28,12},{1,17},{... | collective-permute-start | bytes 460808 | tf_op jit(solution)/shard_map/ppermute | solution.py:44
  154.4 7.8 %collective-permute-start.43 = (bf16[5,24,640]{2,1,0:T(8,128)(2,1)S(1)}, bf16[5,24,640]{2,1,0:T(8,128)(2,1)S(1)}, u32[]{:S(2)}, u32[]{:S(2)}) collective-permute-start(bf16[5,24,640]{2,1,0:T(8,128)(2,1)S(1)} %get-tuple-element.137), channel_id=1, source_target_pairs={{0,24},{4,28},{8,16},{12,20},{16,8},{20,12},{24,0},{28,4},{1,25},{... | collective-permute-start | bytes 460808 | tf_op jit(solution)/shard_map/ppermute | solution.py:44
  167.6 10.8 %collective-permute-start.51 = (bf16[5,24,640]{2,1,0:T(8,128)(2,1)S(1)}, bf16[5,24,640]{2,1,0:T(8,128)(2,1)S(1)}, u32[]{:S(2)}, u32[]{:S(2)}) collective-permute-start(bf16[5,24,640]{2,1,0:T(8,128)(2,1)S(1)} %slice_dynamic-update-slice_fusion.refs_0_), channel_id=1, source_target_pairs={{0,16},{4,20},{8,24},{12,28},{16,0},{20,4},{24,8},{28,12},{1,17},{... | collective-permute-start | bytes 460808 | tf_op jit(solution)/shard_map/ppermute | solution.py:44
  173.2 9.2 %collective-permute-start.49 = (bf16[5,24,640]{2,1,0:T(8,128)(2,1)S(1)}, bf16[5,24,640]{2,1,0:T(8,128)(2,1)S(1)}, u32[]{:S(2)}, u32[]{:S(2)}) collective-permute-start(bf16[5,24,640]{2,1,0:T(8,128)(2,1)S(1)} %slice_dynamic-update-slice_fusion.refs_0_), channel_id=1, source_target_pairs={{0,8},{4,12},{8,0},{12,4},{16,24},{20,28},{24,16},{28,20},{1,9},{5... | collective-permute-start | bytes 460808 | tf_op jit(solution)/shard_map/ppermute | solution.py:44
  180.3 6.9 %collective-permute-start.48 = (bf16[5,24,640]{2,1,0:T(8,128)(2,1)S(1)}, bf16[5,24,640]{2,1,0:T(8,128)(2,1)S(1)}, u32[]{:S(2)}, u32[]{:S(2)}) collective-permute-start(bf16[5,24,640]{2,1,0:T(8,128)(2,1)S(1)} %slice_dynamic-update-slice_fusion.refs_0_), channel_id=1, source_target_pairs={{0,4},{4,0},{8,12},{12,8},{16,20},{20,16},{24,28},{28,24},{1,5},{5... | collective-permute-start | bytes 460808 | tf_op jit(solution)/shard_map/ppermute | solution.py:44
  181.1 8.5 %collective-permute-start.52 = (bf16[5,24,640]{2,1,0:T(8,128)(2,1)S(1)}, bf16[5,24,640]{2,1,0:T(8,128)(2,1)S(1)}, u32[]{:S(2)}, u32[]{:S(2)}) collective-permute-start(bf16[5,24,640]{2,1,0:T(8,128)(2,1)S(1)} %collective-permute-done.51.refs_4_), channel_id=1, source_target_pairs={{0,4},{4,0},{8,12},{12,8},{16,20},{20,16},{24,28},{28,24},{1,5},{5... | collective-permute-start | bytes 460808 | tf_op jit(solution)/shard_map/ppermute | solution.py:44
  182.4 8.9 %collective-permute-start.50 = (bf16[5,24,640]{2,1,0:T(8,128)(2,1)S(1)}, bf16[5,24,640]{2,1,0:T(8,128)(2,1)S(1)}, u32[]{:S(2)}, u32[]{:S(2)}) collective-permute-start(bf16[5,24,640]{2,1,0:T(8,128)(2,1)S(1)} %collective-permute-done.49.refs_2_), channel_id=1, source_target_pairs={{0,4},{4,0},{8,12},{12,8},{16,20},{20,16},{24,28},{28,24},{1,5},{5... | collective-permute-start | bytes 460808 | tf_op jit(solution)/shard_map/ppermute | solution.py:44
  183.7 9.3 %collective-permute-start.54 = (bf16[5,24,640]{2,1,0:T(8,128)(2,1)S(1)}, bf16[5,24,640]{2,1,0:T(8,128)(2,1)S(1)}, u32[]{:S(2)}, u32[]{:S(2)}) collective-permute-start(bf16[5,24,640]{2,1,0:T(8,128)(2,1)S(1)} %collective-permute-done.53.refs_6_), channel_id=1, source_target_pairs={{0,4},{4,0},{8,12},{12,8},{16,20},{20,16},{24,28},{28,24},{1,5},{5... | collective-permute-start | bytes 460808 | tf_op jit(solution)/shard_map/ppermute | solution.py:44
  (64 other events, 422.6 us)

commit v4 on v3

--- a/solution.py
+++ b/solution.py
@@ -92,11 +92,11 @@
     return jnp.sum(jnp.where(diagonal(size), column, 0.0), axis=0, keepdims=True)
 
 
-def prepare_weight(n, part, weight, gain_one, gain_two, *outs):
+def prepare_weight(n, part, weight, gains, *outs):
     wide = 3 * part
     s = lax.axis_index("shard")
     extra = outs[0].shape[1] - wide
-    one, two = (to_column(gain[...].astype(f32), part) for gain in (gain_one, gain_two))
+    one, two = (to_column(gains[i : i + 1, :].astype(f32), part) for i in range(2))
     lane = lax.broadcasted_iota(jnp.int32, (part, extra), 1)
     beside = jnp.where(lane == 0, one, jnp.where(lane == 1, two, 0.0)).astype(bf16)
     for p in range(n):
@@ -353,44 +353,40 @@
                         ].astype(f32)
 
 
-def expert_forward(rows, own, came, up_own, up_pair, down_own, down_pair, *outs):
-    hidden_out, slope_out, keep_out, send_out = outs
-    for i, source in enumerate((own, came)):
-        result = 0.0
-        for k, (up, down) in enumerate(((up_own, down_own), (up_pair, down_pair))):
-            before = dot(source[...], up[0])
-            square = before * before
-            tanh_value = jnp.tanh(gelu_scale * before * (1.0 + gelu_cubic * square))
-            half = 0.5 * (1.0 + tanh_value)
-            hidden = (before * half).astype(bf16)
-            slope = half + 0.5 * before * (1.0 - tanh_value * tanh_value) * gelu_scale * (
-                1.0 + 3.0 * gelu_cubic * square
-            )
-            hidden_out[k, i * rows : (i + 1) * rows, :] = hidden
-            slope_out[k, i * rows : (i + 1) * rows, :] = slope.astype(bf16)
-            result = result + dot(hidden, down[0])
-        if i:
-            send_out[...] = result.astype(bf16)
-        else:
-            keep_out[...] = result
-
-
-def expert_backward(rows, own, came, up_own, up_pair, down_own, down_pair, slope, *outs):
-    before_out, keep_out, send_out = outs
-    grads = jnp.concatenate([own[...], came[...]], axis=0)
+def expert_forward(source, up_own, up_pair, down_own, down_pair, *outs):
+    hidden_out, slope_out, result_out = outs
     result = 0.0
     for k, (up, down) in enumerate(((up_own, down_own), (up_pair, down_pair))):
-        grad_before = (dot_nt(grads, down[0]) * slope[k].astype(f32)).astype(bf16)
+        before = dot(source[...], up[0])
+        square = before * before
+        tanh_value = jnp.tanh(gelu_scale * before * (1.0 + gelu_cubic * square))
+        half = 0.5 * (1.0 + tanh_value)
+        hidden = (before * half).astype(bf16)
+        slope = half + 0.5 * before * (1.0 - tanh_value * tanh_value) * gelu_scale * (
+            1.0 + 3.0 * gelu_cubic * square
+        )
+        hidden_out[k] = hidden
+        slope_out[k] = slope.astype(bf16)
+        result = result + dot(hidden, down[0])
+    result_out[...] = result.astype(result_out.dtype)
+
+
+def expert_backward(grads, up_own, up_pair, down_own, down_pair, slope, *outs):
+    before_out, result_out = outs
+    result = 0.0
+    for k, (up, down) in enumerate(((up_own, down_own), (up_pair, down_pair))):
+        grad_before = (dot_nt(grads[...], down[0]) * slope[k].astype(f32)).astype(bf16)
         before_out[k] = grad_before
         result = result + dot_nt(grad_before, up[0])
-    keep_out[...] = result[:rows]
-    send_out[...] = result[rows:].astype(bf16)
-
-
-def expert_weights(own, came, own_grad, came_grad, hidden, grad_before, *outs):
-    up_out, down_out, up_send, down_send = outs
-    grads = jnp.concatenate([own_grad[...], came_grad[...]], axis=0)
-    rows = jnp.concatenate([own[...], came[...]], axis=0)
+    result_out[...] = result.astype(result_out.dtype)
+
+
+def expert_weights(*refs):
+    rows, grads, hidden, grad_before = (
+        jnp.concatenate([own[...], came[...]], axis=-2)
+        for own, came in zip(refs[0:8:2], refs[1:8:2])
+    )
+    up_out, down_out, up_send, down_send = refs[8:]
     up_send[0] = dot_tn(rows, grad_before[1]).astype(bf16)
     down_send[0] = dot_tn(hidden[1], grads).astype(bf16)
     up_out[0] = dot_tn(rows, grad_before[0])
@@ -439,21 +435,25 @@
     full = wide + -wide % 128
     micro = 10**9
 
-    token_blocks = gather_relative(tokens, "shard")
+    far_tokens, pair_tokens = swap(tokens, "shard", 2 * pair), swap(tokens, "shard", pair)
     weight_blocks = exchange_relative(
         call(
             lambda *refs: prepare_weight(n, part, *refs),
             [shape((part, full))] * n,
-            (attention_in, first_gain.reshape(1, part), second_gain.reshape(1, part)),
+            (attention_in, jnp.stack([first_gain, second_gain])),
         ),
         "shard",
     )
-    own_out, own_up, own_down, token_blocks, weight_blocks = lax.optimization_barrier(
-        (attention_out, expert_in, expert_out, token_blocks, weight_blocks)
-    )
-    out_blocks = gather_relative(own_out, "shard")
+    far_tokens, own_up, own_down, table_scalars = lax.optimization_barrier(
+        (far_tokens, expert_in, expert_out, position_bias.astype(f32))
+    )
+    token_blocks = [tokens, pair_tokens, far_tokens, swap(far_tokens, "shard", pair)]
     pair_up = swap(own_up, "shard", pair)
     pair_down = swap(own_down, "shard", pair)
+    own_out, token_blocks, weight_blocks = lax.optimization_barrier(
+        (attention_out, token_blocks, weight_blocks)
+    )
+    far_out, pair_out = swap(own_out, "shard", 2 * pair), swap(own_out, "shard", pair)
 
     answers = call(
         lambda *refs: attention_forward(n, rows, width, heads, seqs, buckets, *refs),
@@ -466,13 +466,17 @@
             shape((n, rows, part)),
             *[shape((rows, part))] * n,
         ),
-        (lengths, position_bias.astype(f32), *token_blocks, *weight_blocks),
+        (lengths, table_scalars, *token_blocks, *weight_blocks),
         "ss",
         [pltpu.VMEM((group, width), bf16)],
         work=10 * micro,
     )
     tokens_all, weight, projected, weights, gains, mixed = answers[:6]
-    mixed_blocks = exchange_relative(list(answers[6:]), "shard")
+    mixed_mine, pair_up, pair_down, far_out, pair_out = lax.optimization_barrier(
+        (list(answers[6:]), pair_up, pair_down, far_out, pair_out)
+    )
+    mixed_blocks = exchange_relative(mixed_mine, "shard")
+    out_blocks = [own_out, pair_out, far_out, swap(far_out, "shard", pair)]
     gain_one, gain_two = gains[0:1], gains[1:2]
 
     inputs = tokens.astype(f32)
@@ -523,7 +527,8 @@
         both = value.reshape(m // 2, 2 * capacity, width)
         blocks = [both[d] if d == 0 else swap(both[d], "expert", 2 * d) for d in range(m // 2)]
         own = jnp.concatenate([block[:capacity] for block in blocks])
-        other = swap(jnp.concatenate([block[capacity:] for block in blocks]), "expert", 1)
+        other = jnp.concatenate([block[capacity:] for block in blocks])
+        other = swap(other, "expert", 1)
         return dot(collect[:, :half], own) + dot(collect[:, half:], other)
 
     def reduce_shard(keep, out):
@@ -535,44 +540,21 @@
     grad_blocks = (arrived_grad, swap(arrived_grad, "shard", 2 * pair))
 
     units = expert_in.shape[2]
-    both_rows = 2 * places
     expert_weight = (own_up, pair_up, own_down, pair_down)
-    hidden, slope, keep, out = call(
-        lambda *refs: expert_forward(places, *refs),
-        (
-            shape((2, both_rows, units)),
-            shape((2, both_rows, units)),
-            shape((places, width), f32),
-            shape((places, width)),
-        ),
-        (*row_blocks, *expert_weight),
-        work=6 * micro,
-    )
-    expert_result = give_back(reduce_shard(keep, out))
-    grad_before, keep_grad, out_grad = call(
-        lambda *refs: expert_backward(places, *refs),
-        (
-            shape((2, both_rows, units)),
-            shape((places, width), f32),
-            shape((places, width)),
-        ),
-        (*grad_blocks, *expert_weight, slope),
-        work=6 * micro,
-    )
-    grad_sent = give_back(reduce_shard(keep_grad, out_grad))
-    grad_up, grad_down, up_send, down_send = call(
-        expert_weights,
-        (
-            shape(expert_in.shape, f32),
-            shape(expert_out.shape, f32),
-            shape(expert_in.shape),
-            shape(expert_out.shape),
-        ),
-        (*row_blocks, *grad_blocks, hidden, grad_before),
-        work=6 * micro,
-    )
-    grad_up = grad_up + swap(up_send, "shard", pair).astype(f32)
-    grad_down = grad_down + swap(down_send, "shard", pair).astype(f32)
+    middle = shape((2, places, units))
+    kept, sent = shape((places, width), f32), shape((places, width))
+    forward = [
+        call(expert_forward, (middle, middle, end), (block, *expert_weight), work=3 * micro)
+        for block, end in zip(row_blocks, (kept, sent))
+    ]
+    backward = [
+        call(
+            expert_backward, (middle, end), (block, *expert_weight, ahead[1]), work=3 * micro
+        )
+        for block, end, ahead in zip(grad_blocks, (kept, sent), forward)
+    ]
+    expert_result = give_back(reduce_shard(*[half[2] for half in forward]))
+    grad_sent = give_back(reduce_shard(*[half[1] for half in backward]))
 
     layer_out = (hidden_one + gate[:, None] * expert_result).astype(bf16)
     grad_gate = jnp.sum(upstream * expert_result, axis=1)
@@ -593,8 +575,28 @@
     )
     grad_middle, grad_gain_two = rms_backward(hidden_one, factor_two, gain_two, grad_normed_two)
     grad_hidden = upstream + grad_middle
-    branch_blocks = gather_relative(grad_hidden.astype(bf16), "shard")
-
+    branch, late_rows = lax.optimization_barrier((grad_hidden.astype(bf16), row_blocks))
+    grad_up, grad_down, up_send, down_send = call(
+        expert_weights,
+        (
+            shape(expert_in.shape, f32),
+            shape(expert_out.shape, f32),
+            shape(expert_in.shape),
+            shape(expert_out.shape),
+        ),
+        (
+            *late_rows,
+            *grad_blocks,
+            *[half[0] for half in forward],
+            *[half[0] for half in backward],
+        ),
+        work=6 * micro,
+    )
+    far_branch, pair_branch = swap(branch, "shard", 2 * pair), swap(branch, "shard", pair)
+    far_branch, grad_router, gain_two_row, up_send, down_send = lax.optimization_barrier(
+        (far_branch, grad_router, grad_gain_two[None], up_send, down_send)
+    )
+    branch_blocks = [branch, pair_branch, far_branch, swap(far_branch, "shard", pair)]
     holders = m if direct else 1
     piece = part // m
     if direct:
@@ -617,7 +619,7 @@
             weights,
             mixed,
             own_out,
-            grad_gain_two[None],
+            gain_two_row,
             grad_router,
             *branch_blocks,
         ),
@@ -642,12 +644,17 @@
     def biases(block):
         return block.reshape(row_tile, heads, per_line).swapaxes(0, 1).reshape(heads, buckets)
 
-    grad_normed = sum(x.astype(f32) for x in exchange_relative(list(normed_grads), "shard"))
-    grad_input_norm, _ = rms_backward(inputs, rms_factor(inputs), gain_one, grad_normed)
-    grad_tokens = (grad_hidden + grad_input_norm).astype(bf16)
+    def finish_tokens(blocks):
+        grad_normed = sum(x.astype(f32) for x in exchange_relative(list(blocks), "shard"))
+        grad_input_norm, _ = rms_backward(inputs, rms_factor(inputs), gain_one, grad_normed)
+        return (grad_hidden + grad_input_norm).astype(bf16)
+
     if direct:
         far_keep, far_send, near_keep, near_send = shares
-        far = far_keep.astype(f32) + swap(far_send, "expert", 1).astype(f32)
+        far_came = swap(far_send, "expert", 1)
+        far = far_keep.astype(f32) + far_came.astype(f32)
+        normed_grads, far_came = lax.optimization_barrier((normed_grads, far_came))
+        grad_tokens = finish_tokens(normed_grads)
         near = near_keep.astype(f32) + swap(near_send, "expert", 1).astype(f32)
         came = [swap(far[d].astype(bf16), "expert", m // 2 + 2 * d) for d in range(m // 4)]
         came += [swap(near[d].astype(bf16), "expert", 2 * d) for d in range(1, m // 4)]
@@ -657,7 +664,7 @@
         table_total = biases(
             summed[0, :row_tile, at + rest : at + rest + heads * per_line]
         )
-        low = summed.astype(bf16)
+        low, up_send, down_send = lax.optimization_barrier((summed.astype(bf16), up_send, down_send))
         mine = exchange_relative(
             [lax.dynamic_index_in_dim(low, s ^ p, 0, keepdims=False) for p in range(n)], "shard"
         )
@@ -666,13 +673,32 @@
         mine = jnp.stack(
             [jnp.where(own_lane, low[p], mine[p]) for p in range(n)] + [low[n]], axis=0
         )
-        blocks = gather_relative(mine, "expert")
+        blocks = {0: mine, 1: swap(mine, "expert", 1), 4: swap(mine, "expert", 4)}
+        blocks[2] = swap(mine, "expert", 2)
+        blocks[4], blocks[1], grad_tokens = lax.optimization_barrier(
+            (blocks[4], blocks[1], grad_tokens)
+        )
+        blocks[6] = swap(blocks[4], "expert", 2)
+        blocks[5] = swap(blocks[4], "expert", 1)
+        blocks[3] = swap(blocks[2], "expert", 1)
+        blocks[6], grad_up, grad_down = lax.optimization_barrier(
+            (
+                blocks[6],
+                grad_up + swap(up_send, "shard", pair).astype(f32),
+                grad_down + swap(down_send, "shard", pair).astype(f32),
+            )
+        )
+        blocks[7] = swap(blocks[6], "expert", 1)
+        blocks = [blocks[d] for d in range(m)]
         grad_attention_in, grad_attention_out, small_total = call(
             lambda *refs: assemble(n, m, part, piece, experts, *refs),
             (shape((part, 3 * width), f32), shape((part, width), f32), shape((part, full - wide), f32)),
             (*blocks,),
         )
     else:
+        grad_tokens = finish_tokens(normed_grads)
+        grad_up = grad_up + swap(up_send, "shard", pair).astype(f32)
+        grad_down = grad_down + swap(down_send, "shard", pair).astype(f32)
         came = lax.all_to_all(
             shares[0].reshape(n, m, piece, wide).swapaxes(0, 1), "expert", 0, 0, tiled=True
         )

time: 201 us -> 208 us (1.035)
  Pallas kernels: 43 us -> 50.3 us
  other arithmetic: 7.57 us -> 11.5 us
  starting transfers between devices: 56 us -> 53.8 us
    pallas_call x7 -> x9, Pallas kernels: 43 us -> 50.3 us  [call(): pl.pallas_call(kernel, out_shape=out_shape, in_specs=in_specs, out_specs=...]
    reshape x2 -> x0, local copies, waits for them, and re-layouts: 2.44 us -> none  [the longest x1 1.22 us: local(): first_gain.reshape(1, part)]
    ppermute x57, starting transfers between devices: 56 us -> 53.8 us  [swap(): return lax.ppermute(value, axis, [(i, i ^ bit) for i in range(size)])]
    unnamed x79 -> x71, local copies, waits for them, and re-layouts: 4 us -> 4.35 us
  transfers between devices with their start and end apart: 57 -> 57, of which waited for: 28 -> 23; matrix products, arithmetic and copies ran while one was open for 10% -> 9% of each run, Pallas kernels for 15% -> 16%
where the time goes in v4:
time: 208 us
  waiting for transfers between devices  73.4 us (35%)
  starting transfers between devices  53.8 us (26%)
  Pallas kernels  50.3 us (24%)
  local copies, waits for them, and re-layouts  12 us (6%)
  other arithmetic  11.5 us (6%)
  matrix products  5.52 us (3%)
    ppermute x57, waiting for transfers between devices, swap(): return lax.ppermute(value, axis, [(i, i ^ bit) for i in range(size)])  73.4 us
    ppermute x57, starting transfers between devices, swap(): return lax.ppermute(value, axis, [(i, i ^ bit) for i in range(size)])  53.8 us
    pallas_call x9, Pallas kernels, call(): pl.pallas_call(kernel, out_shape=out_shape, in_specs=in_specs, out_specs=...  50.3 us
    unnamed x71, local copies, waits for them, and re-layouts  4.35 us
  transfers between devices with their start and end apart: 57, of which 23 were waited for; matrix products, arithmetic and copies ran while one was open for 9% of the time, Pallas kernels for 16%

profile of v4, /device:TPU:0, one launch (start us, length us, event | category | flops | bytes accessed | tf_op | source)
XLA Modules:
  0.0 207.8 jit_solution(8181280732009397414)
XLA Ops:
  0.7 3.0 %collective-permute-start = (bf16[128,768]{1,0:T(8,128)(2,1)}, bf16[128,768]{1,0:T(8,128)(2,1)S(1)}, u32[]{:S(2)}, u32[]{:S(2)}) collective-permute-start(bf16[128,768]{1,0:T(8,128)(2,1)} %refs_2_), channel_id=1, source_target_pairs={{0,2},{1,3},{2,0},{3,1},{4,6},{5,7},{6,4},{7,5},{8,10},{9,11},{10,... | collective-permute-start | bytes 589832 | tf_op jit(solution)/shard_map/ppermute | solution.py:44
  5.6 2.5 %shard_map.195 = (bf16[192,640]{1,0:T(8,128)(2,1)}, bf16[192,640]{1,0:T(8,128)(2,1)}, bf16[192,640]{1,0:T(8,128)(2,1)}, bf16[192,640]{1,0:T(8,128)(2,1)}) custom-call(bf16[192,2304]{1,0:T(8,128)(2,1)} %refs_0_.2, bf16[2,192]{1,0:T(2,128)(2,1)} %pad_maximum_fusion.6.refs_1_), custom_call_target="tpu_custom_call" | custom-call | tf_op jit(solution)/shard_map/pallas_call | solution.py:66
  14.2 3.4 %collective-permute-done.4.refs_8_ = bf16[192,640]{1,0:T(8,128)(2,1)S(1)} collective-permute-done((bf16[192,640]{1,0:T(8,128)(2,1)}, bf16[192,640]{1,0:T(8,128)(2,1)S(1)}, u32[]{:S(2)}, u32[]{:S(2)}) %collective-permute-start.4) | collective-permute-done | bytes 245792 | tf_op jit(solution)/shard_map/ppermute | solution.py:44
  17.6 3.3 %collective-permute-done.5.refs_9_ = bf16[192,640]{1,0:T(8,128)(2,1)S(1)} collective-permute-done((bf16[192,640]{1,0:T(8,128)(2,1)}, bf16[192,640]{1,0:T(8,128)(2,1)S(1)}, u32[]{:S(2)}, u32[]{:S(2)}) %collective-permute-start.5) | collective-permute-done | bytes 245792 | tf_op jit(solution)/shard_map/ppermute | solution.py:44
  21.9 9.5 %shard_map.196 = (bf16[4,128,768]{2,1,0:T(8,128)(2,1)}, bf16[768,640]{1,0:T(8,128)(2,1)}, bf16[512,576]{1,0:T(8,128)(2,1)}, bf16[3,512,512]{2,1,0:T(8,128)(2,1)}...) custom-call(s32[1,3]{1,0:T(1,128)} %refs_0_.3, ...), custom_call_target="tpu_custom_call" | custom-call | flops 10000000000 | tf_op jit(solution)/shard_map/pallas_call | solution.py:66
  36.8 2.2 %collective-permute-done.12 = bf16[128,192]{1,0:T(8,128)(2,1)S(1)} collective-permute-done((bf16[128,192]{1,0:T(8,128)(2,1)}, bf16[128,192]{1,0:T(8,128)(2,1)S(1)}, u32[]{:S(2)}, u32[]{:S(2)}) %collective-permute-start.12) | collective-permute-done | bytes 49184 | tf_op jit(solution)/shard_map/ppermute | solution.py:44
  43.6 3.8 %collective-permute-done.24 = bf16[80,768]{1,0:T(8,128)(2,1)S(1)} collective-permute-done((bf16[80,768]{1,0:T(8,128)(2,1)S(1)}, bf16[80,768]{1,0:T(8,128)(2,1)S(1)}, u32[]{:S(2)}, u32[]{:S(2)}) %collective-permute-start.24) | collective-permute-done | bytes 122912 | tf_op jit(solution)/shard_map/ppermute | solution.py:44
  49.1 2.6 %collective-permute-start.26 = (bf16[40,768]{1,0:T(8,128)(2,1)S(1)}, bf16[40,768]{1,0:T(8,128)(2,1)S(1)}, u32[]{:S(2)}, u32[]{:S(2)}) collective-permute-start(bf16[40,768]{1,0:T(8,128)(2,1)S(1)} %get-tuple-element.209), channel_id=1, source_target_pairs={{0,16},{4,20},{8,24},{12,28},{16,0},{20,4},{24,8},{28,12},{1,17},{... | collective-permute-start | bytes 184328 | tf_op jit(solution)/shard_map/ppermute | solution.py:44
  52.8 3.5 %collective-permute-start.16 = (bf16[40,768]{1,0:T(8,128)(2,1)S(1)}, bf16[40,768]{1,0:T(8,128)(2,1)S(1)}, u32[]{:S(2)}, u32[]{:S(2)}) collective-permute-start(bf16[40,768]{1,0:T(8,128)(2,1)S(1)} %get-tuple-element.213), channel_id=1, source_target_pairs={{0,16},{4,20},{8,24},{12,28},{16,0},{20,4},{24,8},{28,12},{1,17},{... | collective-permute-start | bytes 184328 | tf_op jit(solution)/shard_map/ppermute | solution.py:44
  58.6 2.2 %collective-permute-done.16 = bf16[40,768]{1,0:T(8,128)(2,1)S(1)} collective-permute-done((bf16[40,768]{1,0:T(8,128)(2,1)S(1)}, bf16[40,768]{1,0:T(8,128)(2,1)S(1)}, u32[]{:S(2)}, u32[]{:S(2)}) %collective-permute-start.16) | collective-permute-done | bytes 61472 | tf_op jit(solution)/shard_map/ppermute | solution.py:44
  63.0 4.6 %shard_map.197 = (bf16[2,160,768]{2,1,0:T(8,128)(2,1)}, bf16[2,160,768]{2,1,0:T(8,128)(2,1)}, f32[160,768]{1,0:T(8,128)}) custom-call(bf16[160,768]{1,0:T(8,128)(2,1)} %copy-done.9, bf16[1,768,768]{2,1,0:T(8,128)(2,1)} %up_own.3, bf16[1,768,768]{2,1,0:T(8,128)(2,1)} %copy-done.21, bf16[1,768,768]{2,1,0:T(8,128)(2,1)} %down_own.3, bf16[1,768,768]{2,1,0:T(8,128)(2,1)} %copy-done.22), custom_call_target="tpu_custom_call" | custom-call | flops 3000000000 | tf_op jit(solution)/shard_map/pallas_call | solution.py:66
  70.1 4.5 %shard_map.198 = (bf16[2,160,768]{2,1,0:T(8,128)(2,1)}, bf16[2,160,768]{2,1,0:T(8,128)(2,1)}, bf16[160,768]{1,0:T(8,128)(2,1)}) custom-call(bf16[160,768]{1,0:T(8,128)(2,1)} %copy-done.24, bf16[1,768,768]{2,1,0:T(8,128)(2,1)} %up_own.3, bf16[1,768,768]{2,1,0:T(8,128)(2,1)} %copy-done.21, bf16[1,768,768]{2,1,0:T(8,128)(2,1)} %down_own.3, ...), custom_call_target="tpu_custom_call" | custom-call | flops 3000000000 | tf_op jit(solution)/shard_map/pallas_call | solution.py:66
  75.3 5.0 %shard_map.200 = (bf16[2,160,768]{2,1,0:T(8,128)(2,1)}, bf16[160,768]{1,0:T(8,128)(2,1)}) custom-call(bf16[160,768]{1,0:T(8,128)(2,1)} %copy-done.23, bf16[1,768,768]{2,1,0:T(8,128)(2,1)} %up_own.3, bf16[1,768,768]{2,1,0:T(8,128)(2,1)} %copy-done.21, bf16[1,768,768]{2,1,0:T(8,128)(2,1)} %down_own.3, bf16[1,768,768]{2,1,0:T(8,128)(2,1)} %copy-done.22, ...), custom_call_target="tpu_custom_call" | custom-call | flops 3000000000 | tf_op jit(solution)/shard_map/pallas_call | solution.py:66
  81.0 5.3 %shard_map.199 = (bf16[2,160,768]{2,1,0:T(8,128)(2,1)}, f32[160,768]{1,0:T(8,128)}) custom-call(bf16[160,768]{1,0:T(8,128)(2,1)} %copy-done.8, bf16[1,768,768]{2,1,0:T(8,128)(2,1)} %up_own.3, bf16[1,768,768]{2,1,0:T(8,128)(2,1)} %copy-done.21, bf16[1,768,768]{2,1,0:T(8,128)(2,1)} %down_own.3, bf16[1,768,768]{2,1,0:T(8,128)(2,1)} %copy-done.22, ...), custom_call_target="tpu_custom_call" | custom-call | flops 3000000000 | tf_op jit(solution)/shard_map/pallas_call | solution.py:66
  88.9 3.6 %collective-permute-done.19 = bf16[160,768]{1,0:T(8,128)(2,1)S(1)} collective-permute-done((bf16[160,768]{1,0:T(8,128)(2,1)S(1)}, bf16[160,768]{1,0:T(8,128)(2,1)S(1)}, u32[]{:S(2)}, u32[]{:S(2)}) %collective-permute-start.19) | collective-permute-done | bytes 245792 | tf_op jit(solution)/shard_map/ppermute | solution.py:44
  92.6 2.1 %collective-permute-start.20 = (bf16[40,768]{1,0:T(8,128)(2,1)S(1)}, bf16[40,768]{1,0:T(8,128)(2,1)S(1)}, u32[]{:S(2)}, u32[]{:S(2)}) collective-permute-start(bf16[40,768]{1,0:T(8,128)(2,1)S(1)} %get-tuple-element.221), channel_id=1, source_target_pairs={{0,8},{4,12},{8,0},{12,4},{16,24},{20,28},{24,16},{28,20},{1,9},{5... | collective-permute-start | bytes 184328 | tf_op jit(solution)/shard_map/ppermute | solution.py:44
  94.8 2.4 %collective-permute-start.31 = (bf16[40,768]{1,0:T(8,128)(2,1)S(1)}, bf16[40,768]{1,0:T(8,128)(2,1)S(1)}, u32[]{:S(2)}, u32[]{:S(2)}) collective-permute-start(bf16[40,768]{1,0:T(8,128)(2,1)S(1)} %get-tuple-element.218), channel_id=1, source_target_pairs={{0,16},{4,20},{8,24},{12,28},{16,0},{20,4},{24,8},{28,12},{1,17},{... | collective-permute-start | bytes 184328 | tf_op jit(solution)/shard_map/ppermute | solution.py:44
  97.2 2.0 collective-permute-start.32
  99.2 1.9 collective-permute-start.22
  101.1 5.1 %collective-permute-done.21 = bf16[40,768]{1,0:T(8,128)(2,1)S(1)} collective-permute-done((bf16[40,768]{1,0:T(8,128)(2,1)S(1)}, bf16[40,768]{1,0:T(8,128)(2,1)S(1)}, u32[]{:S(2)}, u32[]{:S(2)}) %collective-permute-start.21) | collective-permute-done | bytes 61472 | tf_op jit(solution)/shard_map/ppermute | solution.py:44
  108.6 2.7 %collective-permute-done.23 = bf16[80,768]{1,0:T(8,128)(2,1)S(1)} collective-permute-done((bf16[80,768]{1,0:T(8,128)(2,1)S(1)}, bf16[80,768]{1,0:T(8,128)(2,1)S(1)}, u32[]{:S(2)}, u32[]{:S(2)}) %collective-permute-start.23) | collective-permute-done | bytes 122912 | tf_op jit(solution)/shard_map/ppermute | solution.py:44
  115.8 6.7 %shard_map.201 = (f32[1,768,768]{2,1,0:T(8,128)}, f32[1,768,768]{2,1,0:T(8,128)}, bf16[1,768,768]{2,1,0:T(8,128)(2,1)}, bf16[1,768,768]{2,1,0:T(8,128)(2,1)}) custom-call(bf16[160,768]{1,0:T(8,128)(2,1)} %copy-done.9, bf16[160,768]{1,0:T(8,128)(2,1)} %copy-done.24, bf16[160,768]{1,0:T(8,128)(2,1)} %copy-done.8, bf16[160,768]{1,0:T(8,128)(2,1)} %copy-done.23, ...), custom_call_target="tpu_custom_call" | custom-call | flops 6000000000 | tf_op jit(solution)/shard_map/pallas_call | solution.py:66
  125.2 8.9 %shard_map.202 = (bf16[2,5,24,640]{3,2,1,0:T(8,128)(2,1)}, bf16[2,5,24,640]{3,2,1,0:T(8,128)(2,1)}, bf16[2,5,24,640]{3,2,1,0:T(8,128)(2,1)}, bf16[2,5,24,640]{3,...) custom-call(bf16[512,576]{1,0:T(8,128)(2,1)} %get-tuple-element.123., ...), custom_call_target="tpu_custom_call" | custom-call | flops 8000000000 | tf_op jit(solution)/shard_map/pallas_call | solution.py:66
  136.3 8.3 %collective-permute-done.38 = bf16[2,5,24,640]{3,2,1,0:T(8,128)(2,1)S(1)} collective-permute-done((bf16[2,5,24,640]{3,2,1,0:T(8,128)(2,1)}, bf16[2,5,24,640]{3,2,1,0:T(8,128)(2,1)S(1)}, u32[]{:S(2)}, u32[]{:S(2)}) %collective-permute-start.38) | collective-permute-done | bytes 307232 | tf_op jit(solution)/shard_map/ppermute | solution.py:44
  147.2 2.1 collective-permute-start.40
  152.9 6.0 %collective-permute-done.39 = bf16[5,24,640]{2,1,0:T(8,128)(2,1)S(1)} collective-permute-done((bf16[5,24,640]{2,1,0:T(8,128)(2,1)S(1)}, bf16[5,24,640]{2,1,0:T(8,128)(2,1)S(1)}, u32[]{:S(2)}, u32[]{:S(2)}) %collective-permute-start.39) | collective-permute-done | bytes 153632 | tf_op jit(solution)/shard_map/ppermute | solution.py:44
  158.9 2.4 %collective-permute-done.41 = bf16[5,24,640]{2,1,0:T(8,128)(2,1)S(1)} collective-permute-done((bf16[5,24,640]{2,1,0:T(8,128)(2,1)S(1)}, bf16[5,24,640]{2,1,0:T(8,128)(2,1)S(1)}, u32[]{:S(2)}, u32[]{:S(2)}) %collective-permute-start.41) | collective-permute-done | bytes 153632 | tf_op jit(solution)/shard_map/ppermute | solution.py:44
  164.9 9.1 %collective-permute-done.43 = bf16[24,640]{1,0:T(8,128)(2,1)S(1)} collective-permute-done((bf16[24,640]{1,0:T(8,128)(2,1)S(1)}, bf16[24,640]{1,0:T(8,128)(2,1)S(1)}, u32[]{:S(2)}, u32[]{:S(2)}) %collective-permute-start.43) | collective-permute-done | bytes 30752 | tf_op jit(solution)/shard_map/ppermute | solution.py:44
  174.0 3.3 %collective-permute-done.44 = bf16[24,640]{1,0:T(8,128)(2,1)S(1)} collective-permute-done((bf16[24,640]{1,0:T(8,128)(2,1)S(1)}, bf16[24,640]{1,0:T(8,128)(2,1)S(1)}, u32[]{:S(2)}, u32[]{:S(2)}) %collective-permute-start.44) | collective-permute-done | bytes 30752 | tf_op jit(solution)/shard_map/ppermute | solution.py:44
  182.5 5.6 %collective-permute-done.45.refs_4_ = bf16[5,24,640]{2,1,0:T(8,128)(2,1)S(1)} collective-permute-done((bf16[5,24,640]{2,1,0:T(8,128)(2,1)S(1)}, bf16[5,24,640]{2,1,0:T(8,128)(2,1)S(1)}, u32[]{:S(2)}, u32[]{:S(2)}) %collective-permute-start.45) | collective-permute-done | bytes 153632 | tf_op jit(solution)/shard_map/ppermute | solution.py:44
  198.1 2.5 %collective-permute-done.56.refs_7_ = bf16[5,24,640]{2,1,0:T(8,128)(2,1)S(1)} collective-permute-done((bf16[5,24,640]{2,1,0:T(8,128)(2,1)S(1)}, bf16[5,24,640]{2,1,0:T(8,128)(2,1)S(1)}, u32[]{:S(2)}, u32[]{:S(2)}) %collective-permute-start.56) | collective-permute-done | bytes 153632 | tf_op jit(solution)/shard_map/ppermute | solution.py:44
  201.3 3.1 %shard_map.203 = (f32[192,2304]{1,0:T(8,128)}, f32[192,768]{1,0:T(8,128)}, f32[192,64]{1,0:T(8,128)}) custom-call(bf16[5,24,640]{2,1,0:T(8,128)(2,1)} %copy-done.10, bf16[5,24,640]{2,1,0:T(8,128)(2,1)} %copy-done.13, bf16[5,24,640]{2,1,0:T(8,128)(2,1)} %copy-done.14, bf16[5,24,640]{2,1,0:T(8,128)(2,1)} %copy-done.17, bf16[5,24,640]{2,1,0:T(8,128)(2,1)} %copy-done.12, ...), custom_call_target="tpu_custom_call" | custom-call | tf_op jit(solution)/shard_map/pallas_call | solution.py:66
  (238 shorter events, 73.0 us)
Async XLA Ops:
  0.7 11.4 %collective-permute-start = (bf16[128,768]{1,0:T(8,128)(2,1)}, bf16[128,768]{1,0:T(8,128)(2,1)S(1)}, u32[]{:S(2)}, u32[]{:S(2)}) collective-permute-start(bf16[128,768]{1,0:T(8,128)(2,1)} %refs_2_), channel_id=1, source_target_pairs={{0,2},{1,3},{2,0},{3,1},{4,6},{5,7},{6,4},{7,5},{8,10},{9,11},{10,... | collective-permute-start | bytes 589832 | tf_op jit(solution)/shard_map/ppermute | solution.py:44
  3.7 9.2 %collective-permute-start.1 = (bf16[128,768]{1,0:T(8,128)(2,1)}, bf16[128,768]{1,0:T(8,128)(2,1)S(1)}, u32[]{:S(2)}, u32[]{:S(2)}) collective-permute-start(bf16[128,768]{1,0:T(8,128)(2,1)} %refs_2_), channel_id=1, source_target_pairs={{0,1},{1,0},{2,3},{3,2},{4,5},{5,4},{6,7},{7,6},{8,9},{9,8},{10,11... | collective-permute-start | bytes 589832 | tf_op jit(solution)/shard_map/ppermute | solution.py:44
  8.6 9.0 %collective-permute-start.4 = (bf16[192,640]{1,0:T(8,128)(2,1)}, bf16[192,640]{1,0:T(8,128)(2,1)S(1)}, u32[]{:S(2)}, u32[]{:S(2)}) collective-permute-start(bf16[192,640]{1,0:T(8,128)(2,1)} %get-tuple-element.95), channel_id=1, source_target_pairs={{0,2},{1,3},{2,0},{3,1},{4,6},{5,7},{6,4},{7,5},{8,10},{9,11},{10,... | collective-permute-start | bytes 737288 | tf_op jit(solution)/shard_map/ppermute | solution.py:44
  8.7 12.3 %collective-permute-start.5 = (bf16[192,640]{1,0:T(8,128)(2,1)}, bf16[192,640]{1,0:T(8,128)(2,1)S(1)}, u32[]{:S(2)}, u32[]{:S(2)}) collective-permute-start(bf16[192,640]{1,0:T(8,128)(2,1)} %get-tuple-element.96), channel_id=1, source_target_pairs={{0,3},{1,2},{2,1},{3,0},{4,7},{5,6},{6,5},{7,4},{8,11},{9,10},{10,... | collective-permute-start | bytes 737288 | tf_op jit(solution)/shard_map/ppermute | solution.py:44
  12.1 19.4 %collective-permute-start.6 = (bf16[1,768,768]{2,1,0:T(8,128)(2,1)}, bf16[1,768,768]{2,1,0:T(8,128)(2,1)S(1)}, u32[]{:S(2)}, u32[]{:S(2)}) collective-permute-start(bf16[1,768,768]{2,1,0:T(8,128)(2,1)} %up_own.3), channel_id=1, source_target_pairs={{0,1},{1,0},{2,3},{3,2},{4,5},{5,4},{6,7},{7,6},{8,9},{9,8},{10,11... | collective-permute-start | bytes 3538952 | tf_op jit(solution)/shard_map/ppermute | solution.py:44
  12.9 18.6 %collective-permute-start.7 = (bf16[1,768,768]{2,1,0:T(8,128)(2,1)}, bf16[1,768,768]{2,1,0:T(8,128)(2,1)S(1)}, u32[]{:S(2)}, u32[]{:S(2)}) collective-permute-start(bf16[1,768,768]{2,1,0:T(8,128)(2,1)} %down_own.3), channel_id=1, source_target_pairs={{0,1},{1,0},{2,3},{3,2},{4,5},{5,4},{6,7},{7,6},{8,9},{9,8},{10,11... | collective-permute-start | bytes 3538952 | tf_op jit(solution)/shard_map/ppermute | solution.py:44
  21.0 10.5 %collective-permute-start.8 = (bf16[192,768]{1,0:T(8,128)(2,1)}, bf16[192,768]{1,0:T(8,128)(2,1)S(1)}, u32[]{:S(2)}, u32[]{:S(2)}) collective-permute-start(bf16[192,768]{1,0:T(8,128)(2,1)} %refs_6_), channel_id=1, source_target_pairs={{0,2},{1,3},{2,0},{3,1},{4,6},{5,7},{6,4},{7,5},{8,10},{9,11},{10,... | collective-permute-start | bytes 884744 | tf_op jit(solution)/shard_map/ppermute | solution.py:44
  21.6 9.9 %collective-permute-start.9 = (bf16[192,768]{1,0:T(8,128)(2,1)}, bf16[192,768]{1,0:T(8,128)(2,1)S(1)}, u32[]{:S(2)}, u32[]{:S(2)}) collective-permute-start(bf16[192,768]{1,0:T(8,128)(2,1)} %refs_6_), channel_id=1, source_target_pairs={{0,1},{1,0},{2,3},{3,2},{4,5},{5,4},{6,7},{7,6},{8,9},{9,8},{10,11... | collective-permute-start | bytes 884744 | tf_op jit(solution)/shard_map/ppermute | solution.py:44
  42.7 9.2 %collective-permute-start.14 = (bf16[80,768]{1,0:T(8,128)(2,1)S(1)}, bf16[80,768]{1,0:T(8,128)(2,1)S(1)}, u32[]{:S(2)}, u32[]{:S(2)}) collective-permute-start(bf16[80,768]{1,0:T(8,128)(2,1)S(1)} %convolution_convert_fusion.2), channel_id=1, source_target_pairs={{0,4},{4,0},{8,12},{12,8},{16,20},{20,16},{24,28},{28,24},{1,5},{5... | collective-permute-start | bytes 368648 | tf_op jit(solution)/shard_map/ppermute | solution.py:44
  47.5 8.8 %collective-permute-start.25 = (bf16[40,768]{1,0:T(8,128)(2,1)S(1)}, bf16[40,768]{1,0:T(8,128)(2,1)S(1)}, u32[]{:S(2)}, u32[]{:S(2)}) collective-permute-start(bf16[40,768]{1,0:T(8,128)(2,1)S(1)} %get-tuple-element.207), channel_id=1, source_target_pairs={{0,8},{4,12},{8,0},{12,4},{16,24},{20,28},{24,16},{28,20},{1,9},{5... | collective-permute-start | bytes 184328 | tf_op jit(solution)/shard_map/ppermute | solution.py:44
  58.0 16.7 %collective-permute-start.28 = (bf16[160,768]{1,0:T(8,128)(2,1)S(1)}, bf16[160,768]{1,0:T(8,128)(2,1)S(1)}, u32[]{:S(2)}, u32[]{:S(2)}) collective-permute-start(bf16[160,768]{1,0:T(8,128)(2,1)S(1)} %pad_maximum_fusion.1.grads.refs_2_), channel_id=1, source_target_pairs={{0,2},{1,3},{2,0},{3,1},{4,6},{5,7},{6,4},{7,5},{8,10},{9,11},{10,... | collective-permute-start | bytes 737288 | tf_op jit(solution)/shard_map/ppermute | solution.py:44
  94.7 13.1 %collective-permute-start.30 = (bf16[40,768]{1,0:T(8,128)(2,1)S(1)}, bf16[40,768]{1,0:T(8,128)(2,1)S(1)}, u32[]{:S(2)}, u32[]{:S(2)}) collective-permute-start(bf16[40,768]{1,0:T(8,128)(2,1)S(1)} %get-tuple-element.216), channel_id=1, source_target_pairs={{0,8},{4,12},{8,0},{12,4},{16,24},{20,28},{24,16},{28,20},{1,9},{5... | collective-permute-start | bytes 184328 | tf_op jit(solution)/shard_map/ppermute | solution.py:44
  94.8 13.1 %collective-permute-start.31 = (bf16[40,768]{1,0:T(8,128)(2,1)S(1)}, bf16[40,768]{1,0:T(8,128)(2,1)S(1)}, u32[]{:S(2)}, u32[]{:S(2)}) collective-permute-start(bf16[40,768]{1,0:T(8,128)(2,1)S(1)} %get-tuple-element.218), channel_id=1, source_target_pairs={{0,16},{4,20},{8,24},{12,28},{16,0},{20,4},{24,8},{28,12},{1,17},{... | collective-permute-start | bytes 184328 | tf_op jit(solution)/shard_map/ppermute | solution.py:44
  97.2 10.7 %collective-permute-start.32 = (bf16[40,768]{1,0:T(8,128)(2,1)S(1)}, bf16[40,768]{1,0:T(8,128)(2,1)S(1)}, u32[]{:S(2)}, u32[]{:S(2)}) collective-permute-start(bf16[40,768]{1,0:T(8,128)(2,1)S(1)} %get-tuple-element.217), channel_id=1, source_target_pairs={{0,24},{4,28},{8,16},{12,20},{16,8},{20,12},{24,0},{28,4},{1,25},{... | collective-permute-start | bytes 184328 | tf_op jit(solution)/shard_map/ppermute | solution.py:44
  113.8 9.1 %collective-permute-start.34 = (bf16[128,768]{1,0:T(8,128)(2,1)S(1)}, bf16[128,768]{1,0:T(8,128)(2,1)S(1)}, u32[]{:S(2)}, u32[]{:S(2)}) collective-permute-start(bf16[128,768]{1,0:T(8,128)(2,1)S(1)} %fusion.84.refs_9_), channel_id=1, source_target_pairs={{0,2},{1,3},{2,0},{3,1},{4,6},{5,7},{6,4},{7,5},{8,10},{9,11},{10,... | collective-permute-start | bytes 589832 | tf_op jit(solution)/shard_map/ppermute | solution.py:44
  115.2 9.2 %collective-permute-start.35 = (bf16[128,768]{1,0:T(8,128)(2,1)S(1)}, bf16[128,768]{1,0:T(8,128)(2,1)S(1)}, u32[]{:S(2)}, u32[]{:S(2)}) collective-permute-start(bf16[128,768]{1,0:T(8,128)(2,1)S(1)} %fusion.84.refs_9_), channel_id=1, source_target_pairs={{0,1},{1,0},{2,3},{3,2},{4,5},{5,4},{6,7},{7,6},{8,9},{9,8},{10,11... | collective-permute-start | bytes 589832 | tf_op jit(solution)/shard_map/ppermute | solution.py:44
  134.1 10.4 %collective-permute-start.38 = (bf16[2,5,24,640]{3,2,1,0:T(8,128)(2,1)}, bf16[2,5,24,640]{3,2,1,0:T(8,128)(2,1)S(1)}, u32[]{:S(2)}, u32[]{:S(2)}) collective-permute-start(bf16[2,5,24,640]{3,2,1,0:T(8,128)(2,1)} %get-tuple-element.147), channel_id=1, source_target_pairs={{0,4},{4,0},{8,12},{12,8},{16,20},{20,16},{24,28},{28,24},{1,5},{5... | collective-permute-start | bytes 921608 | tf_op jit(solution)/shard_map/ppermute | solution.py:44
  135.4 15.2 %collective-permute-start.37 = (bf16[2,5,24,640]{3,2,1,0:T(8,128)(2,1)}, bf16[2,5,24,640]{3,2,1,0:T(8,128)(2,1)S(1)}, u32[]{:S(2)}, u32[]{:S(2)}) collective-permute-start(bf16[2,5,24,640]{3,2,1,0:T(8,128)(2,1)} %get-tuple-element.145), channel_id=1, source_target_pairs={{0,4},{4,0},{8,12},{12,8},{16,20},{20,16},{24,28},{28,24},{1,5},{5... | collective-permute-start | bytes 921608 | tf_op jit(solution)/shard_map/ppermute | solution.py:44
  145.6 13.3 %collective-permute-start.39 = (bf16[5,24,640]{2,1,0:T(8,128)(2,1)S(1)}, bf16[5,24,640]{2,1,0:T(8,128)(2,1)S(1)}, u32[]{:S(2)}, u32[]{:S(2)}) collective-permute-start(bf16[5,24,640]{2,1,0:T(8,128)(2,1)S(1)} %get-tuple-element.204), channel_id=1, source_target_pairs={{0,16},{4,20},{8,24},{12,28},{16,0},{20,4},{24,8},{28,12},{1,17},{... | collective-permute-start | bytes 460808 | tf_op jit(solution)/shard_map/ppermute | solution.py:44
  147.2 11.7 %collective-permute-start.40 = (bf16[5,24,640]{2,1,0:T(8,128)(2,1)S(1)}, bf16[5,24,640]{2,1,0:T(8,128)(2,1)S(1)}, u32[]{:S(2)}, u32[]{:S(2)}) collective-permute-start(bf16[5,24,640]{2,1,0:T(8,128)(2,1)S(1)} %get-tuple-element.205), channel_id=1, source_target_pairs={{0,24},{4,28},{8,16},{12,20},{16,8},{20,12},{24,0},{28,4},{1,25},{... | collective-permute-start | bytes 460808 | tf_op jit(solution)/shard_map/ppermute | solution.py:44
  151.6 9.7 %collective-permute-start.41 = (bf16[5,24,640]{2,1,0:T(8,128)(2,1)S(1)}, bf16[5,24,640]{2,1,0:T(8,128)(2,1)S(1)}, u32[]{:S(2)}, u32[]{:S(2)}) collective-permute-start(bf16[5,24,640]{2,1,0:T(8,128)(2,1)S(1)} %fusion.24), channel_id=1, source_target_pairs={{0,8},{4,12},{8,0},{12,4},{16,24},{20,28},{24,16},{28,20},{1,9},{5... | collective-permute-start | bytes 460808 | tf_op jit(solution)/shard_map/ppermute | solution.py:44
  161.5 16.1 %collective-permute-start.47 = (bf16[128,768]{1,0:T(8,128)(2,1)}, bf16[128,768]{1,0:T(8,128)(2,1)S(1)}, u32[]{:S(2)}, u32[]{:S(2)}) collective-permute-start(bf16[128,768]{1,0:T(8,128)(2,1)} %get-tuple-element.156), channel_id=1, source_target_pairs={{0,1},{1,0},{2,3},{3,2},{4,5},{5,4},{6,7},{7,6},{8,9},{9,8},{10,11... | collective-permute-start | bytes 589832 | tf_op jit(solution)/shard_map/ppermute | solution.py:44
  162.0 16.6 %collective-permute-start.48 = (bf16[128,768]{1,0:T(8,128)(2,1)}, bf16[128,768]{1,0:T(8,128)(2,1)S(1)}, u32[]{:S(2)}, u32[]{:S(2)}) collective-permute-start(bf16[128,768]{1,0:T(8,128)(2,1)} %get-tuple-element.157), channel_id=1, source_target_pairs={{0,2},{1,3},{2,0},{3,1},{4,6},{5,7},{6,4},{7,5},{8,10},{9,11},{10,... | collective-permute-start | bytes 589832 | tf_op jit(solution)/shard_map/ppermute | solution.py:44
  162.7 17.0 %collective-permute-start.49 = (bf16[128,768]{1,0:T(8,128)(2,1)}, bf16[128,768]{1,0:T(8,128)(2,1)S(1)}, u32[]{:S(2)}, u32[]{:S(2)}) collective-permute-start(bf16[128,768]{1,0:T(8,128)(2,1)} %get-tuple-element.158), channel_id=1, source_target_pairs={{0,3},{1,2},{2,1},{3,0},{4,7},{5,6},{6,5},{7,4},{8,11},{9,10},{10,... | collective-permute-start | bytes 589832 | tf_op jit(solution)/shard_map/ppermute | solution.py:44
  163.5 26.9 %collective-permute-start.55 = (bf16[1,768,768]{2,1,0:T(8,128)(2,1)}, bf16[1,768,768]{2,1,0:T(8,128)(2,1)S(1)}, u32[]{:S(2)}, u32[]{:S(2)}) collective-permute-start(bf16[1,768,768]{2,1,0:T(8,128)(2,1)} %get-tuple-element.165), channel_id=1, source_target_pairs={{0,1},{1,0},{2,3},{3,2},{4,5},{5,4},{6,7},{7,6},{8,9},{9,8},{10,11... | collective-permute-start | bytes 3538952 | tf_op jit(solution)/shard_map/ppermute | solution.py:44
  164.2 9.8 %collective-permute-start.43 = (bf16[24,640]{1,0:T(8,128)(2,1)S(1)}, bf16[24,640]{1,0:T(8,128)(2,1)S(1)}, u32[]{:S(2)}, u32[]{:S(2)}) collective-permute-start(bf16[24,640]{1,0:T(8,128)(2,1)S(1)} %get-tuple-element.225), channel_id=1, source_target_pairs={{0,2},{1,3},{2,0},{3,1},{4,6},{5,7},{6,4},{7,5},{8,10},{9,11},{10,... | collective-permute-start | bytes 92168 | tf_op jit(solution)/shard_map/ppermute | solution.py:44
  177.3 14.7 %collective-permute-start.54 = (bf16[1,768,768]{2,1,0:T(8,128)(2,1)}, bf16[1,768,768]{2,1,0:T(8,128)(2,1)S(1)}, u32[]{:S(2)}, u32[]{:S(2)}) collective-permute-start(bf16[1,768,768]{2,1,0:T(8,128)(2,1)} %get-tuple-element.163), channel_id=1, source_target_pairs={{0,1},{1,0},{2,3},{3,2},{4,5},{5,4},{6,7},{7,6},{8,9},{9,8},{10,11... | collective-permute-start | bytes 3538952 | tf_op jit(solution)/shard_map/ppermute | solution.py:44
  177.6 10.5 %collective-permute-start.45 = (bf16[5,24,640]{2,1,0:T(8,128)(2,1)S(1)}, bf16[5,24,640]{2,1,0:T(8,128)(2,1)S(1)}, u32[]{:S(2)}, u32[]{:S(2)}) collective-permute-start(bf16[5,24,640]{2,1,0:T(8,128)(2,1)S(1)} %slice_dynamic-update-slice_fusion.refs_0_), channel_id=1, source_target_pairs={{0,16},{4,20},{8,24},{12,28},{16,0},{20,4},{24,8},{28,12},{1,17},{... | collective-permute-start | bytes 460808 | tf_op jit(solution)/shard_map/ppermute | solution.py:44
  178.6 9.5 %collective-permute-start.46 = (bf16[5,24,640]{2,1,0:T(8,128)(2,1)S(1)}, bf16[5,24,640]{2,1,0:T(8,128)(2,1)S(1)}, u32[]{:S(2)}, u32[]{:S(2)}) collective-permute-start(bf16[5,24,640]{2,1,0:T(8,128)(2,1)S(1)} %slice_dynamic-update-slice_fusion.refs_0_), channel_id=1, source_target_pairs={{0,4},{4,0},{8,12},{12,8},{16,20},{20,16},{24,28},{28,24},{1,5},{5... | collective-permute-start | bytes 460808 | tf_op jit(solution)/shard_map/ppermute | solution.py:44
  179.7 9.7 %collective-permute-start.50 = (bf16[5,24,640]{2,1,0:T(8,128)(2,1)S(1)}, bf16[5,24,640]{2,1,0:T(8,128)(2,1)S(1)}, u32[]{:S(2)}, u32[]{:S(2)}) collective-permute-start(bf16[5,24,640]{2,1,0:T(8,128)(2,1)S(1)} %slice_dynamic-update-slice_fusion.refs_0_), channel_id=1, source_target_pairs={{0,8},{4,12},{8,0},{12,4},{16,24},{20,28},{24,16},{28,20},{1,9},{5... | collective-permute-start | bytes 460808 | tf_op jit(solution)/shard_map/ppermute | solution.py:44
  188.2 8.4 %collective-permute-start.52 = (bf16[5,24,640]{2,1,0:T(8,128)(2,1)S(1)}, bf16[5,24,640]{2,1,0:T(8,128)(2,1)S(1)}, u32[]{:S(2)}, u32[]{:S(2)}) collective-permute-start(bf16[5,24,640]{2,1,0:T(8,128)(2,1)S(1)} %collective-permute-done.45.refs_4_), channel_id=1, source_target_pairs={{0,4},{4,0},{8,12},{12,8},{16,20},{20,16},{24,28},{28,24},{1,5},{5... | collective-permute-start | bytes 460808 | tf_op jit(solution)/shard_map/ppermute | solution.py:44
  189.4 8.7 %collective-permute-start.51 = (bf16[5,24,640]{2,1,0:T(8,128)(2,1)S(1)}, bf16[5,24,640]{2,1,0:T(8,128)(2,1)S(1)}, u32[]{:S(2)}, u32[]{:S(2)}) collective-permute-start(bf16[5,24,640]{2,1,0:T(8,128)(2,1)S(1)} %collective-permute-done.50.refs_2_), channel_id=1, source_target_pairs={{0,4},{4,0},{8,12},{12,8},{16,20},{20,16},{24,28},{28,24},{1,5},{5... | collective-permute-start | bytes 460808 | tf_op jit(solution)/shard_map/ppermute | solution.py:44
  (60 other events, 367.7 us)

commit v5 on v4

--- a/solution.py
+++ b/solution.py
@@ -131,7 +131,7 @@
         2 + 2 * n : 8 + 2 * n
     ]
     mixed_out = refs[8 + 2 * n : 8 + 3 * n]
-    (normed_scr,) = refs[8 + 3 * n :]
+    normed_scr, scores_scr = refs[8 + 3 * n :]
     s = lax.axis_index("shard")
     part = width // n
     wide = 3 * part
@@ -173,8 +173,9 @@
             bias[diff] = block
         low_side = jnp.full((rows, rows), table[h, buckets // 2 - 1], f32)
         high_side = jnp.full((rows, rows), table[h, buckets - 1], f32)
+        scores_scr[...] = dot_nt(query, key)
         for i in range(n):
-            scores = dot_nt(query[i * rows : (i + 1) * rows, :], key)
+            scores = scores_scr[i * rows : (i + 1) * rows, :]
             side = [
                 bias[j - i] if abs(j - i) <= 1 else (high_side if j > i else low_side)
                 for j in range(n)
@@ -190,7 +191,9 @@
             total = jnp.sum(raised, axis=-1, keepdims=True)
             weights = (raised * (1.0 / total)).astype(bf16)
             weights_out[h, i * rows : (i + 1) * rows, :] = weights
-            mixed_all[i, :, h * head_dim : (h + 1) * head_dim] = dot(weights, value).astype(bf16)
+        mixed_all[:, :, h * head_dim : (h + 1) * head_dim] = (
+            dot(weights_out[h], value).astype(bf16).reshape(n, rows, head_dim)
+        )
     for p in range(n):
         mixed_out[p][...] = mixed_all[s ^ p]
 
@@ -203,9 +206,9 @@
     share_out = refs[at : at + shares]
     normed_grad_out = refs[at + shares : at + shares + n]
     gain_out, table_out = refs[at + shares + n : at + shares + n + 2]
-    branch_scr, scores_scr, projected_scr, total_scr, out_scr, normed_scr, send_scr = refs[
-        at + shares + n + 2 :
-    ]
+    branch_scr, scores_scr, projected_scr, total_scr, out_scr, normed_scr, send_scr, weights_scr = (
+        refs[at + shares + n + 2 :]
+    )
     s = lax.axis_index("shard")
     e = lax.axis_index("expert")
     part = width // n
@@ -231,9 +234,10 @@
         low_side = jnp.zeros((1, rows), f32)
         high_side = jnp.zeros((1, rows), f32)
         upstream = grad_mixed[:, h * head_dim : (h + 1) * head_dim]
+        weights_scr[...] = dot_nt(upstream, value)
         for i in range(n):
             weights_i = weights[h, i * rows : (i + 1) * rows, :].astype(f32)
-            grad_weights = dot_nt(upstream[i * rows : (i + 1) * rows, :], value)
+            grad_weights = weights_scr[i * rows : (i + 1) * rows, :]
             inner = jnp.sum(weights_i * grad_weights, axis=-1, keepdims=True)
             grad_scores = weights_i * (grad_weights - inner)
             scores_scr[i * rows : (i + 1) * rows, :] = grad_scores.astype(bf16)
@@ -297,7 +301,7 @@
         here = slice(c * size, (c + 1) * size)
         total_scr[here, wide : wide + 1] = to_column(grad_gain[:, here], size)
         total_scr[here, wide + 1 : wide + 2] = to_column(gain_two[0:1, here], size)
-    total_scr[:, wide + 2 : wide + 2 + experts] = router[...]
+        total_scr[here, wide + 2 : wide + 2 + experts] = router[:, here].T
     at = wide + 2 + experts
     rest = (width - full) // n
     for t in range(n):
@@ -320,8 +324,14 @@
         target[place, n] = out_scr[pl.ds(rows_at, piece), :full].astype(bf16)
 
 
+def beside_columns(ref, p, wide):
+    last = ref[p, :, ref.shape[2] - 128 :]
+    skip = wide - (ref.shape[2] - 128)
+    return jnp.concatenate([last[:, skip:], last[:, :skip]], axis=1)
+
+
 def assemble(n, m, part, piece, experts, *refs):
-    total_out, out_out, small_out = refs[m:]
+    total_out, out_out, one_out, two_out, router_out, small_scr = refs[m:]
     s = lax.axis_index("shard")
     e = lax.axis_index("expert")
     wide = 3 * part
@@ -331,14 +341,18 @@
     for d in range(m):
         start = pl.multiple_of((e ^ d) * piece, row_tile)
         own = pl.ds(start, piece)
-        small = jnp.zeros((piece, full - wide), f32)
+        small = jnp.zeros((piece, 128), f32)
         for p in range(n):
-            small = small + refs[d][p, :, wide:].astype(f32)
+            small = small + beside_columns(refs[d], p, wide).astype(f32)
             out_out[own, full + p * rest : full + (p + 1) * rest] = refs[d][p, :, at : at + rest].astype(
                 f32
             )
         out_out[own, :full] = refs[d][n].astype(f32)
-        small_out[own, :] = small
+        small_scr[own, :] = small
+    small = small_scr[...].T
+    one_out[...] = small[0:1, :]
+    two_out[...] = small[1:2, :]
+    router_out[...] = small[2 : 2 + experts, :]
     for k in range(n):
 
         @pl.when(s == k)
@@ -353,11 +367,12 @@
                         ].astype(f32)
 
 
-def expert_forward(source, up_own, up_pair, down_own, down_pair, *outs):
-    hidden_out, slope_out, result_out = outs
+def expert_forward(rows, own, came, up_own, up_pair, down_own, down_pair, *outs):
+    hidden_out, slope_out, keep_out, send_out = outs
+    source = jnp.concatenate([own[...], came[...]], axis=0)
     result = 0.0
     for k, (up, down) in enumerate(((up_own, down_own), (up_pair, down_pair))):
-        before = dot(source[...], up[0])
+        before = dot(source, up[0])
         square = before * before
         tanh_value = jnp.tanh(gelu_scale * before * (1.0 + gelu_cubic * square))
         half = 0.5 * (1.0 + tanh_value)
@@ -368,25 +383,26 @@
         hidden_out[k] = hidden
         slope_out[k] = slope.astype(bf16)
         result = result + dot(hidden, down[0])
-    result_out[...] = result.astype(result_out.dtype)
-
-
-def expert_backward(grads, up_own, up_pair, down_own, down_pair, slope, *outs):
-    before_out, result_out = outs
+    keep_out[...] = result[:rows]
+    send_out[...] = result[rows:].astype(bf16)
+
+
+def expert_backward(rows, own, came, up_own, up_pair, down_own, down_pair, slope, *outs):
+    before_out, keep_out, send_out = outs
+    grads = jnp.concatenate([own[...], came[...]], axis=0)
     result = 0.0
     for k, (up, down) in enumerate(((up_own, down_own), (up_pair, down_pair))):
-        grad_before = (dot_nt(grads[...], down[0]) * slope[k].astype(f32)).astype(bf16)
+        grad_before = (dot_nt(grads, down[0]) * slope[k].astype(f32)).astype(bf16)
         before_out[k] = grad_before
         result = result + dot_nt(grad_before, up[0])
-    result_out[...] = result.astype(result_out.dtype)
-
-
-def expert_weights(*refs):
-    rows, grads, hidden, grad_before = (
-        jnp.concatenate([own[...], came[...]], axis=-2)
-        for own, came in zip(refs[0:8:2], refs[1:8:2])
-    )
-    up_out, down_out, up_send, down_send = refs[8:]
+    keep_out[...] = result[:rows]
+    send_out[...] = result[rows:].astype(bf16)
+
+
+def expert_weights(own, came, own_grad, came_grad, hidden, grad_before, *outs):
+    up_out, down_out, up_send, down_send = outs
+    grads = jnp.concatenate([own_grad[...], came_grad[...]], axis=0)
+    rows = jnp.concatenate([own[...], came[...]], axis=0)
     up_send[0] = dot_tn(rows, grad_before[1]).astype(bf16)
     down_send[0] = dot_tn(hidden[1], grads).astype(bf16)
     up_out[0] = dot_tn(rows, grad_before[0])
@@ -402,7 +418,7 @@
     grad_value = factor * scaled - value * factor * factor * factor * jnp.mean(
         scaled * value, axis=-1, keepdims=True
     )
-    grad_gain = jnp.sum(upstream * value * factor, axis=0)
+    grad_gain = jnp.sum(upstream * value * factor, axis=0, keepdims=True)
     return (grad_value, grad_gain)
 
 
@@ -468,7 +484,7 @@
         ),
         (lengths, table_scalars, *token_blocks, *weight_blocks),
         "ss",
-        [pltpu.VMEM((group, width), bf16)],
+        [pltpu.VMEM((group, width), bf16), pltpu.VMEM((group, group), f32)],
         work=10 * micro,
     )
     tokens_all, weight, projected, weights, gains, mixed = answers[:6]
@@ -512,56 +528,62 @@
             value.reshape(experts, capacity, width), "expert", 0, 0, tiled=True
         ).reshape(places, width)
 
-    def send(value):
+    def send(value, after=None):
         if not direct:
             return plain(dot_tn(collect, value).astype(bf16))
         came = swap(dot_tn(collect[:, half:], value).astype(bf16), "expert", 1)
         own = dot_tn(collect[:, :half], value).astype(bf16).reshape(m // 2, capacity, width)
         both = jnp.concatenate([own, came.reshape(m // 2, capacity, width)], axis=1)
+        if after is not None:
+            both, _ = lax.optimization_barrier((both, after))
         blocks = [both[d] if d == 0 else swap(both[d], "expert", 2 * d) for d in range(m // 2)]
         return jnp.concatenate(blocks, axis=0)
 
     def give_back(value):
         if not direct:
-            return dot(collect, plain(value))
+            return dot(collect, plain(value)), value
         both = value.reshape(m // 2, 2 * capacity, width)
         blocks = [both[d] if d == 0 else swap(both[d], "expert", 2 * d) for d in range(m // 2)]
         own = jnp.concatenate([block[:capacity] for block in blocks])
         other = jnp.concatenate([block[capacity:] for block in blocks])
         other = swap(other, "expert", 1)
-        return dot(collect[:, :half], own) + dot(collect[:, half:], other)
+        return dot(collect[:, :half], own) + dot(collect[:, half:], other), own
 
     def reduce_shard(keep, out):
         return (keep + swap(out, "shard", 2 * pair).astype(f32)).astype(bf16)
 
     arrived = send(normed_two.astype(bf16))
     row_blocks = (arrived, swap(arrived, "shard", 2 * pair))
-    arrived_grad = send(grad_result)
+    arrived_grad = send(grad_result, arrived)
     grad_blocks = (arrived_grad, swap(arrived_grad, "shard", 2 * pair))
 
     units = expert_in.shape[2]
     expert_weight = (own_up, pair_up, own_down, pair_down)
-    middle = shape((2, places, units))
+    middle = shape((2, 2 * places, units))
     kept, sent = shape((places, width), f32), shape((places, width))
-    forward = [
-        call(expert_forward, (middle, middle, end), (block, *expert_weight), work=3 * micro)
-        for block, end in zip(row_blocks, (kept, sent))
-    ]
-    backward = [
-        call(
-            expert_backward, (middle, end), (block, *expert_weight, ahead[1]), work=3 * micro
-        )
-        for block, end, ahead in zip(grad_blocks, (kept, sent), forward)
-    ]
-    expert_result = give_back(reduce_shard(*[half[2] for half in forward]))
-    grad_sent = give_back(reduce_shard(*[half[1] for half in backward]))
+    hidden, slope, *forward = call(
+        lambda *refs: expert_forward(places, *refs),
+        (middle, middle, kept, sent),
+        (*row_blocks, *expert_weight),
+        work=6 * micro,
+    )
+    grad_before, *backward = call(
+        lambda *refs: expert_backward(places, *refs),
+        (middle, kept, sent),
+        (*grad_blocks, *expert_weight, slope),
+        work=6 * micro,
+    )
+    expert_result, first_back = give_back(reduce_shard(*forward))
+    keep_grad, came_grad = backward[0], swap(backward[1], "shard", 2 * pair)
+    came_grad, _ = lax.optimization_barrier((came_grad, first_back))
+    grad_sent, _ = give_back((keep_grad + came_grad.astype(f32)).astype(bf16))
 
     layer_out = (hidden_one + gate[:, None] * expert_result).astype(bf16)
     grad_gate = jnp.sum(upstream * expert_result, axis=1)
     grad_logits = (grad_gate * gate)[:, None] * (chosen - probs)
     grad_router = lax.dot_general(
+        grad_logits,
         normed_two,
-        grad_logits,
         (((0,), (0,)), ((), ())),
         precision=lax.Precision.HIGHEST,
         preferred_element_type=f32,
@@ -587,14 +609,14 @@
         (
             *late_rows,
             *grad_blocks,
-            *[half[0] for half in forward],
-            *[half[0] for half in backward],
+            hidden,
+            grad_before,
         ),
         work=6 * micro,
     )
     far_branch, pair_branch = swap(branch, "shard", 2 * pair), swap(branch, "shard", pair)
     far_branch, grad_router, gain_two_row, up_send, down_send = lax.optimization_barrier(
-        (far_branch, grad_router, grad_gain_two[None], up_send, down_send)
+        (far_branch, grad_router, grad_gain_two, up_send, down_send)
     )
     branch_blocks = [branch, pair_branch, far_branch, swap(far_branch, "shard", pair)]
     holders = m if direct else 1
@@ -632,6 +654,7 @@
             pltpu.VMEM((part, width), f32),
             pltpu.VMEM((group, width), bf16),
             pltpu.VMEM((n, rows, width), bf16),
+            pltpu.VMEM((group, group), f32),
         ],
         work=8 * micro,
     )
@@ -664,7 +687,7 @@
         table_total = biases(
             summed[0, :row_tile, at + rest : at + rest + heads * per_line]
         )
-        low, up_send, down_send = lax.optimization_barrier((summed.astype(bf16), up_send, down_send))
+        low, grad_tokens = lax.optimization_barrier((summed.astype(bf16), grad_tokens))
         mine = exchange_relative(
             [lax.dynamic_index_in_dim(low, s ^ p, 0, keepdims=False) for p in range(n)], "shard"
         )
@@ -673,11 +696,10 @@
         mine = jnp.stack(
             [jnp.where(own_lane, low[p], mine[p]) for p in range(n)] + [low[n]], axis=0
         )
+        mine, up_send, down_send = lax.optimization_barrier((mine, up_send, down_send))
         blocks = {0: mine, 1: swap(mine, "expert", 1), 4: swap(mine, "expert", 4)}
         blocks[2] = swap(mine, "expert", 2)
-        blocks[4], blocks[1], grad_tokens = lax.optimization_barrier(
-            (blocks[4], blocks[1], grad_tokens)
-        )
+        blocks[4], blocks[1] = lax.optimization_barrier((blocks[4], blocks[1]))
         blocks[6] = swap(blocks[4], "expert", 2)
         blocks[5] = swap(blocks[4], "expert", 1)
         blocks[3] = swap(blocks[2], "expert", 1)
@@ -690,10 +712,18 @@
         )
         blocks[7] = swap(blocks[6], "expert", 1)
         blocks = [blocks[d] for d in range(m)]
-        grad_attention_in, grad_attention_out, small_total = call(
+        grad_attention_in, grad_attention_out, total_one, total_two, total_router = call(
             lambda *refs: assemble(n, m, part, piece, experts, *refs),
-            (shape((part, 3 * width), f32), shape((part, width), f32), shape((part, full - wide), f32)),
+            (
+                shape((part, 3 * width), f32),
+                shape((part, width), f32),
+                shape((1, part), f32),
+                shape((1, part), f32),
+                shape((experts, part), f32),
+            ),
             (*blocks,),
+            "",
+            [pltpu.VMEM((part, 128), f32)],
         )
     else:
         grad_tokens = finish_tokens(normed_grads)
@@ -709,20 +739,21 @@
         out_mine = sum(x.astype(f32) for x in came).astype(bf16)
         grad_attention_in = lax.all_gather(mine, "expert", axis=0, tiled=True).astype(f32)
         grad_attention_out = lax.all_gather(out_mine, "expert", axis=0, tiled=True).astype(f32)
-        small = jnp.concatenate([gain_row[0][:, None], grad_gain_two[:, None], grad_router], axis=1)
-        small_total = lax.psum_scatter(small, "shard", scatter_dimension=0, tiled=True)
+        small = jnp.concatenate([gain_row[0:1], grad_gain_two, grad_router], axis=0)
+        small_total = lax.psum_scatter(small, "shard", scatter_dimension=1, tiled=True)
         small_total, table_total = lax.psum(
             (small_total, biases(table[:, : heads * per_line])), "expert"
         )
+        total_one, total_two, total_router = small_total[0:1], small_total[1:2], small_total[2:]
     return (
         layer_out,
         grad_tokens,
         grad_attention_in,
         grad_attention_out,
         table_total,
-        small_total[:, 0],
-        small_total[:, 1],
-        small_total[:, 2 : 2 + experts],
+        total_one[0],
+        total_two[0],
+        total_router.T,
         grad_up,
         grad_down,
     )

time: 208 us -> 193 us (0.928)
  Pallas kernels: 50.3 us -> 40.1 us
  local copies, waits for them, and re-layouts: 12 us -> 7.75 us
    pallas_call x9 -> x7, Pallas kernels: 50.3 us -> 40.1 us  [call(): pl.pallas_call(kernel, out_shape=out_shape, in_specs=in_specs, out_specs=...]
    slice x2 -> x0, local copies, waits for them, and re-layouts: 2.73 us -> none  [the longest x1 1.76 us: local(): small_total[:, 1]]
    unnamed x71 -> x74, local copies, waits for them, and re-layouts: 4.35 us -> 3.74 us
  transfers between devices with their start and end apart: 57 -> 57, of which waited for: 23 -> 27; matrix products, arithmetic and copies ran while one was open for 9% -> 8% of each run, Pallas kernels for 16% -> 15%
where the time goes in v5:
time: 193 us; the launch traced here: 192 us
  waiting for transfers between devices  74.6 us (39%)
  starting transfers between devices  52.1 us (27%)
  Pallas kernels  40.1 us (21%)
  other arithmetic  10.3 us (5%)
  local copies, waits for them, and re-layouts  7.75 us (4%)
  matrix products  6.12 us (3%)
    ppermute x57, waiting for transfers between devices, swap(): return lax.ppermute(value, axis, [(i, i ^ bit) for i in range(size)])  74.6 us
    ppermute x57, starting transfers between devices, swap(): return lax.ppermute(value, axis, [(i, i ^ bit) for i in range(size)])  52.1 us
    pallas_call x7, Pallas kernels, call(): pl.pallas_call(kernel, out_shape=out_shape, in_specs=in_specs, out_specs=...  40.1 us
  transfers between devices with their start and end apart: 57, of which 27 were waited for; matrix products, arithmetic and copies ran while one was open for 8% of the time, Pallas kernels for 15%

profile of v5, /device:TPU:0, one launch (start us, length us, event | category | flops | bytes accessed | tf_op | source)
XLA Modules:
  0.0 192.3 jit_solution(1788219618867871222)
XLA Ops:
  0.7 3.0 %collective-permute-start = (bf16[128,768]{1,0:T(8,128)(2,1)}, bf16[128,768]{1,0:T(8,128)(2,1)S(1)}, u32[]{:S(2)}, u32[]{:S(2)}) collective-permute-start(bf16[128,768]{1,0:T(8,128)(2,1)} %refs_2_), channel_id=1, source_target_pairs={{0,2},{1,3},{2,0},{3,1},{4,6},{5,7},{6,4},{7,5},{8,10},{9,11},{10,... | collective-permute-start | bytes 589832 | tf_op jit(solution)/shard_map/ppermute | solution.py:44
  5.6 2.5 %shard_map.195 = (bf16[192,640]{1,0:T(8,128)(2,1)}, bf16[192,640]{1,0:T(8,128)(2,1)}, bf16[192,640]{1,0:T(8,128)(2,1)}, bf16[192,640]{1,0:T(8,128)(2,1)}) custom-call(bf16[192,2304]{1,0:T(8,128)(2,1)} %refs_0_.2, bf16[2,192]{1,0:T(2,128)(2,1)} %pad_maximum_fusion.7.refs_1_), custom_call_target="tpu_custom_call" | custom-call | tf_op jit(solution)/shard_map/pallas_call | solution.py:66
  14.2 3.4 %collective-permute-done.4.refs_8_ = bf16[192,640]{1,0:T(8,128)(2,1)S(1)} collective-permute-done((bf16[192,640]{1,0:T(8,128)(2,1)}, bf16[192,640]{1,0:T(8,128)(2,1)S(1)}, u32[]{:S(2)}, u32[]{:S(2)}) %collective-permute-start.4) | collective-permute-done | bytes 245792 | tf_op jit(solution)/shard_map/ppermute | solution.py:44
  17.6 3.3 %collective-permute-done.5.refs_9_ = bf16[192,640]{1,0:T(8,128)(2,1)S(1)} collective-permute-done((bf16[192,640]{1,0:T(8,128)(2,1)}, bf16[192,640]{1,0:T(8,128)(2,1)S(1)}, u32[]{:S(2)}, u32[]{:S(2)}) %collective-permute-start.5) | collective-permute-done | bytes 245792 | tf_op jit(solution)/shard_map/ppermute | solution.py:44
  21.9 7.0 %shard_map.196 = (bf16[4,128,768]{2,1,0:T(8,128)(2,1)}, bf16[768,640]{1,0:T(8,128)(2,1)}, bf16[512,576]{1,0:T(8,128)(2,1)}, bf16[3,512,512]{2,1,0:T(8,128)(2,1)}...) custom-call(s32[1,3]{1,0:T(1,128)} %refs_0_.3, ...), custom_call_target="tpu_custom_call" | custom-call | flops 10000000000 | tf_op jit(solution)/shard_map/pallas_call | solution.py:66
  28.9 2.0 %collective-permute-done.8 = bf16[192,768]{1,0:T(8,128)(2,1)S(1)} collective-permute-done((bf16[192,768]{1,0:T(8,128)(2,1)}, bf16[192,768]{1,0:T(8,128)(2,1)S(1)}, u32[]{:S(2)}, u32[]{:S(2)}) %collective-permute-start.8) | collective-permute-done | bytes 294944 | tf_op jit(solution)/shard_map/ppermute | solution.py:44
  41.6 5.7 %collective-permute-done.14 = bf16[80,768]{1,0:T(8,128)(2,1)S(1)} collective-permute-done((bf16[80,768]{1,0:T(8,128)(2,1)S(1)}, bf16[80,768]{1,0:T(8,128)(2,1)S(1)}, u32[]{:S(2)}, u32[]{:S(2)}) %collective-permute-start.14) | collective-permute-done | bytes 122912 | tf_op jit(solution)/shard_map/ppermute | solution.py:44
  49.3 2.6 %collective-permute-start.16 = (bf16[40,768]{1,0:T(8,128)(2,1)S(1)}, bf16[40,768]{1,0:T(8,128)(2,1)S(1)}, u32[]{:S(2)}, u32[]{:S(2)}) collective-permute-start(bf16[40,768]{1,0:T(8,128)(2,1)S(1)} %get-tuple-element.191), channel_id=1, source_target_pairs={{0,16},{4,20},{8,24},{12,28},{16,0},{20,4},{24,8},{28,12},{1,17},{... | collective-permute-start | bytes 184328 | tf_op jit(solution)/shard_map/ppermute | solution.py:44
  52.0 3.7 %collective-permute-done.16 = bf16[40,768]{1,0:T(8,128)(2,1)S(1)} collective-permute-done((bf16[40,768]{1,0:T(8,128)(2,1)S(1)}, bf16[40,768]{1,0:T(8,128)(2,1)S(1)}, u32[]{:S(2)}, u32[]{:S(2)}) %collective-permute-start.16) | collective-permute-done | bytes 61472 | tf_op jit(solution)/shard_map/ppermute | solution.py:44
  55.7 2.2 %collective-permute-done.17 = bf16[40,768]{1,0:T(8,128)(2,1)S(1)} collective-permute-done((bf16[40,768]{1,0:T(8,128)(2,1)S(1)}, bf16[40,768]{1,0:T(8,128)(2,1)S(1)}, u32[]{:S(2)}, u32[]{:S(2)}) %collective-permute-start.17) | collective-permute-done | bytes 61472 | tf_op jit(solution)/shard_map/ppermute | solution.py:44
  61.0 2.9 %collective-permute-start.27 = (bf16[40,768]{1,0:T(8,128)(2,1)S(1)}, bf16[40,768]{1,0:T(8,128)(2,1)S(1)}, u32[]{:S(2)}, u32[]{:S(2)}) collective-permute-start(bf16[40,768]{1,0:T(8,128)(2,1)S(1)} %get-tuple-element.198), channel_id=1, source_target_pairs={{0,24},{4,28},{8,16},{12,20},{16,8},{20,12},{24,0},{28,4},{1,25},{... | collective-permute-start | bytes 184328 | tf_op jit(solution)/shard_map/ppermute | solution.py:44
  64.7 2.4 %collective-permute-done.27 = bf16[40,768]{1,0:T(8,128)(2,1)S(1)} collective-permute-done((bf16[40,768]{1,0:T(8,128)(2,1)S(1)}, bf16[40,768]{1,0:T(8,128)(2,1)S(1)}, u32[]{:S(2)}, u32[]{:S(2)}) %collective-permute-start.27) | collective-permute-done | bytes 61472 | tf_op jit(solution)/shard_map/ppermute | solution.py:44
  68.5 6.0 %shard_map.197 = (bf16[2,320,768]{2,1,0:T(8,128)(2,1)}, bf16[2,320,768]{2,1,0:T(8,128)(2,1)}, f32[160,768]{1,0:T(8,128)}, bf16[160,768]{1,0:T(8,128)(2,1)}) custom-call(bf16[160,768]{1,0:T(8,128)(2,1)} %copy-done.9, bf16[160,768]{1,0:T(8,128)(2,1)} %copy-done.26, bf16[1,768,768]{2,1,0:T(8,128)(2,1)} %refs_2_.2, bf16[1,768,768]{2,1,0:T(8,128)(2,1)} %copy-done.24, ...), custom_call_target="tpu_custom_call" | custom-call | flops 6000000000 | tf_op jit(solution)/shard_map/pallas_call | solution.py:66
  76.7 5.8 %shard_map.198 = (bf16[2,320,768]{2,1,0:T(8,128)(2,1)}, f32[160,768]{1,0:T(8,128)}, bf16[160,768]{1,0:T(8,128)(2,1)}) custom-call(bf16[160,768]{1,0:T(8,128)(2,1)} %copy-done.10, bf16[160,768]{1,0:T(8,128)(2,1)} %copy-done.27, bf16[1,768,768]{2,1,0:T(8,128)(2,1)} %refs_2_.2, bf16[1,768,768]{2,1,0:T(8,128)(2,1)} %copy-done.24, bf16[1,768,768]{2,1,0:T(8,128)(2,1)} %refs_4_.1, ...), custom_call_target="tpu_custom_call" | custom-call | flops 6000000000 | tf_op jit(solution)/shard_map/pallas_call | solution.py:66
  83.9 2.7 %collective-permute-start.21 = (bf16[40,768]{1,0:T(8,128)(2,1)S(1)}, bf16[40,768]{1,0:T(8,128)(2,1)S(1)}, u32[]{:S(2)}, u32[]{:S(2)}) collective-permute-start(bf16[40,768]{1,0:T(8,128)(2,1)S(1)} %get-tuple-element.205), channel_id=1, source_target_pairs={{0,16},{4,20},{8,24},{12,28},{16,0},{20,4},{24,8},{28,12},{1,17},{... | collective-permute-start | bytes 184328 | tf_op jit(solution)/shard_map/ppermute | solution.py:44
  89.1 3.9 %collective-permute-done.22 = bf16[40,768]{1,0:T(8,128)(2,1)S(1)} collective-permute-done((bf16[40,768]{1,0:T(8,128)(2,1)S(1)}, bf16[40,768]{1,0:T(8,128)(2,1)S(1)}, u32[]{:S(2)}, u32[]{:S(2)}) %collective-permute-start.22) | collective-permute-done | bytes 61472 | tf_op jit(solution)/shard_map/ppermute | solution.py:44
  93.0 2.0 %collective-permute-start.23 = (bf16[80,768]{1,0:T(8,128)(2,1)S(1)}, bf16[80,768]{1,0:T(8,128)(2,1)S(1)}, u32[]{:S(2)}, u32[]{:S(2)}) collective-permute-start(bf16[80,768]{1,0:T(8,128)(2,1)S(1)} %pad_maximum_fusion.4), channel_id=1, source_target_pairs={{0,4},{4,0},{8,12},{12,8},{16,20},{20,16},{24,28},{28,24},{1,5},{5... | collective-permute-start | bytes 368648 | tf_op jit(solution)/shard_map/ppermute | solution.py:44
  96.6 3.1 %collective-permute-start.32 = (bf16[40,768]{1,0:T(8,128)(2,1)S(1)}, bf16[40,768]{1,0:T(8,128)(2,1)S(1)}, u32[]{:S(2)}, u32[]{:S(2)}) collective-permute-start(bf16[40,768]{1,0:T(8,128)(2,1)S(1)} %get-tuple-element.195), channel_id=1, source_target_pairs={{0,24},{4,28},{8,16},{12,20},{16,8},{20,12},{24,0},{28,4},{1,25},{... | collective-permute-start | bytes 184328 | tf_op jit(solution)/shard_map/ppermute | solution.py:44
  100.4 2.2 %collective-permute-done.32 = bf16[40,768]{1,0:T(8,128)(2,1)S(1)} collective-permute-done((bf16[40,768]{1,0:T(8,128)(2,1)S(1)}, bf16[40,768]{1,0:T(8,128)(2,1)S(1)}, u32[]{:S(2)}, u32[]{:S(2)}) %collective-permute-start.32) | collective-permute-done | bytes 61472 | tf_op jit(solution)/shard_map/ppermute | solution.py:44
  105.7 2.1 %collective-permute-done.33 = bf16[80,768]{1,0:T(8,128)(2,1)S(1)} collective-permute-done((bf16[80,768]{1,0:T(8,128)(2,1)S(1)}, bf16[80,768]{1,0:T(8,128)(2,1)S(1)}, u32[]{:S(2)}, u32[]{:S(2)}) %collective-permute-start.33) | collective-permute-done | bytes 122912 | tf_op jit(solution)/shard_map/ppermute | solution.py:44
  110.1 6.8 %shard_map.199 = (f32[1,768,768]{2,1,0:T(8,128)}, f32[1,768,768]{2,1,0:T(8,128)}, bf16[1,768,768]{2,1,0:T(8,128)(2,1)}, bf16[1,768,768]{2,1,0:T(8,128)(2,1)}) custom-call(bf16[160,768]{1,0:T(8,128)(2,1)} %copy-done.9, bf16[160,768]{1,0:T(8,128)(2,1)} %copy-done.26, bf16[160,768]{1,0:T(8,128)(2,1)} %copy-done.10, bf16[160,768]{1,0:T(8,128)(2,1)} %copy-done.27, ...), custom_call_target="tpu_custom_call" | custom-call | flops 6000000000 | tf_op jit(solution)/shard_map/pallas_call | solution.py:66
  119.7 8.8 %shard_map.200 = (bf16[2,5,24,640]{3,2,1,0:T(8,128)(2,1)}, bf16[2,5,24,640]{3,2,1,0:T(8,128)(2,1)}, bf16[2,5,24,640]{3,2,1,0:T(8,128)(2,1)}, bf16[2,5,24,640]{3,...) custom-call(bf16[512,576]{1,0:T(8,128)(2,1)} %get-tuple-element.125., ...), custom_call_target="tpu_custom_call" | custom-call | flops 8000000000 | tf_op jit(solution)/shard_map/pallas_call | solution.py:66
  130.7 8.3 %collective-permute-done.38 = bf16[2,5,24,640]{3,2,1,0:T(8,128)(2,1)S(1)} collective-permute-done((bf16[2,5,24,640]{3,2,1,0:T(8,128)(2,1)}, bf16[2,5,24,640]{3,2,1,0:T(8,128)(2,1)S(1)}, u32[]{:S(2)}, u32[]{:S(2)}) %collective-permute-start.38) | collective-permute-done | bytes 307232 | tf_op jit(solution)/shard_map/ppermute | solution.py:44
  140.1 3.2 %collective-permute-start.40 = (bf16[5,24,640]{2,1,0:T(8,128)(2,1)S(1)}, bf16[5,24,640]{2,1,0:T(8,128)(2,1)S(1)}, u32[]{:S(2)}, u32[]{:S(2)}) collective-permute-start(bf16[5,24,640]{2,1,0:T(8,128)(2,1)S(1)} %get-tuple-element.187), channel_id=1, source_target_pairs={{0,24},{4,28},{8,16},{12,20},{16,8},{20,12},{24,0},{28,4},{1,25},{... | collective-permute-start | bytes 460808 | tf_op jit(solution)/shard_map/ppermute | solution.py:44
  146.9 6.3 %collective-permute-done.39 = bf16[5,24,640]{2,1,0:T(8,128)(2,1)S(1)} collective-permute-done((bf16[5,24,640]{2,1,0:T(8,128)(2,1)S(1)}, bf16[5,24,640]{2,1,0:T(8,128)(2,1)S(1)}, u32[]{:S(2)}, u32[]{:S(2)}) %collective-permute-start.39) | collective-permute-done | bytes 153632 | tf_op jit(solution)/shard_map/ppermute | solution.py:44
  153.2 2.6 %collective-permute-done.41 = bf16[5,24,640]{2,1,0:T(8,128)(2,1)S(1)} collective-permute-done((bf16[5,24,640]{2,1,0:T(8,128)(2,1)S(1)}, bf16[5,24,640]{2,1,0:T(8,128)(2,1)S(1)}, u32[]{:S(2)}, u32[]{:S(2)}) %collective-permute-start.41) | collective-permute-done | bytes 153632 | tf_op jit(solution)/shard_map/ppermute | solution.py:44
  155.9 3.8 %collective-permute-done.44 = bf16[128,768]{1,0:T(8,128)(2,1)S(1)} collective-permute-done((bf16[128,768]{1,0:T(8,128)(2,1)}, bf16[128,768]{1,0:T(8,128)(2,1)S(1)}, u32[]{:S(2)}, u32[]{:S(2)}) %collective-permute-start.44) | collective-permute-done | bytes 196640 | tf_op jit(solution)/shard_map/ppermute | solution.py:44
  163.1 2.1 %collective-permute-done.46 = bf16[24,640]{1,0:T(8,128)(2,1)S(1)} collective-permute-done((bf16[24,640]{1,0:T(8,128)(2,1)S(1)}, bf16[24,640]{1,0:T(8,128)(2,1)S(1)}, u32[]{:S(2)}, u32[]{:S(2)}) %collective-permute-start.46) | collective-permute-done | bytes 30752 | tf_op jit(solution)/shard_map/ppermute | solution.py:44
  169.0 6.9 %collective-permute-done.48.refs_4_ = bf16[5,24,640]{2,1,0:T(8,128)(2,1)S(1)} collective-permute-done((bf16[5,24,640]{2,1,0:T(8,128)(2,1)S(1)}, bf16[5,24,640]{2,1,0:T(8,128)(2,1)S(1)}, u32[]{:S(2)}, u32[]{:S(2)}) %collective-permute-start.48) | collective-permute-done | bytes 153632 | tf_op jit(solution)/shard_map/ppermute | solution.py:44
  183.9 2.1 %collective-permute-done.51.refs_3_ = bf16[5,24,640]{2,1,0:T(8,128)(2,1)S(1)} collective-permute-done((bf16[5,24,640]{2,1,0:T(8,128)(2,1)S(1)}, bf16[5,24,640]{2,1,0:T(8,128)(2,1)S(1)}, u32[]{:S(2)}, u32[]{:S(2)}) %collective-permute-start.51) | collective-permute-done | bytes 153632 | tf_op jit(solution)/shard_map/ppermute | solution.py:44
  186.0 2.4 %collective-permute-done.56.refs_7_ = bf16[5,24,640]{2,1,0:T(8,128)(2,1)S(1)} collective-permute-done((bf16[5,24,640]{2,1,0:T(8,128)(2,1)S(1)}, bf16[5,24,640]{2,1,0:T(8,128)(2,1)S(1)}, u32[]{:S(2)}, u32[]{:S(2)}) %collective-permute-start.56) | collective-permute-done | bytes 153632 | tf_op jit(solution)/shard_map/ppermute | solution.py:44
  189.1 3.2 %shard_map.201 = (f32[192,2304]{1,0:T(8,128)}, f32[192,768]{1,0:T(8,128)}, f32[1,192]{1,0:T(1,128)}, f32[1,192]{1,0:T(1,128)}, f32[8,192]{1,0:T(8,128)}) custom-call(bf16[5,24,640]{2,1,0:T(8,128)(2,1)} %copy-done.11, bf16[5,24,640]{2,1,0:T(8,128)(2,1)} %copy-done.14, bf16[5,24,640]{2,1,0:T(8,128)(2,1)} %copy-done.15, bf16[5,24,640]{2,1,0:T(8,128)(2,1)} %copy-done.18, ...), custom_call_target="tpu_custom_call" | custom-call | tf_op jit(solution)/shard_map/pallas_call | solution.py:66
  (238 shorter events, 66.2 us)
Async XLA Ops:
  0.7 11.4 %collective-permute-start = (bf16[128,768]{1,0:T(8,128)(2,1)}, bf16[128,768]{1,0:T(8,128)(2,1)S(1)}, u32[]{:S(2)}, u32[]{:S(2)}) collective-permute-start(bf16[128,768]{1,0:T(8,128)(2,1)} %refs_2_), channel_id=1, source_target_pairs={{0,2},{1,3},{2,0},{3,1},{4,6},{5,7},{6,4},{7,5},{8,10},{9,11},{10,... | collective-permute-start | bytes 589832 | tf_op jit(solution)/shard_map/ppermute | solution.py:44
  3.7 9.2 %collective-permute-start.1 = (bf16[128,768]{1,0:T(8,128)(2,1)}, bf16[128,768]{1,0:T(8,128)(2,1)S(1)}, u32[]{:S(2)}, u32[]{:S(2)}) collective-permute-start(bf16[128,768]{1,0:T(8,128)(2,1)} %refs_2_), channel_id=1, source_target_pairs={{0,1},{1,0},{2,3},{3,2},{4,5},{5,4},{6,7},{7,6},{8,9},{9,8},{10,11... | collective-permute-start | bytes 589832 | tf_op jit(solution)/shard_map/ppermute | solution.py:44
  8.6 9.0 %collective-permute-start.4 = (bf16[192,640]{1,0:T(8,128)(2,1)}, bf16[192,640]{1,0:T(8,128)(2,1)S(1)}, u32[]{:S(2)}, u32[]{:S(2)}) collective-permute-start(bf16[192,640]{1,0:T(8,128)(2,1)} %get-tuple-element.97), channel_id=1, source_target_pairs={{0,2},{1,3},{2,0},{3,1},{4,6},{5,7},{6,4},{7,5},{8,10},{9,11},{10,... | collective-permute-start | bytes 737288 | tf_op jit(solution)/shard_map/ppermute | solution.py:44
  8.7 12.3 %collective-permute-start.5 = (bf16[192,640]{1,0:T(8,128)(2,1)}, bf16[192,640]{1,0:T(8,128)(2,1)S(1)}, u32[]{:S(2)}, u32[]{:S(2)}) collective-permute-start(bf16[192,640]{1,0:T(8,128)(2,1)} %get-tuple-element.98), channel_id=1, source_target_pairs={{0,3},{1,2},{2,1},{3,0},{4,7},{5,6},{6,5},{7,4},{8,11},{9,10},{10,... | collective-permute-start | bytes 737288 | tf_op jit(solution)/shard_map/ppermute | solution.py:44
  12.1 18.8 %collective-permute-start.6 = (bf16[1,768,768]{2,1,0:T(8,128)(2,1)}, bf16[1,768,768]{2,1,0:T(8,128)(2,1)S(1)}, u32[]{:S(2)}, u32[]{:S(2)}) collective-permute-start(bf16[1,768,768]{2,1,0:T(8,128)(2,1)} %refs_2_.2), channel_id=1, source_target_pairs={{0,1},{1,0},{2,3},{3,2},{4,5},{5,4},{6,7},{7,6},{8,9},{9,8},{10,11... | collective-permute-start | bytes 3538952 | tf_op jit(solution)/shard_map/ppermute | solution.py:44
  12.9 18.1 %collective-permute-start.7 = (bf16[1,768,768]{2,1,0:T(8,128)(2,1)}, bf16[1,768,768]{2,1,0:T(8,128)(2,1)S(1)}, u32[]{:S(2)}, u32[]{:S(2)}) collective-permute-start(bf16[1,768,768]{2,1,0:T(8,128)(2,1)} %refs_4_.1), channel_id=1, source_target_pairs={{0,1},{1,0},{2,3},{3,2},{4,5},{5,4},{6,7},{7,6},{8,9},{9,8},{10,11... | collective-permute-start | bytes 3538952 | tf_op jit(solution)/shard_map/ppermute | solution.py:44
  13.7 7.3 %collective-permute-start.2 = (bf16[128,768]{1,0:T(8,128)(2,1)S(1)}, bf16[128,768]{1,0:T(8,128)(2,1)S(1)}, u32[]{:S(2)}, u32[]{:S(2)}) collective-permute-start(bf16[128,768]{1,0:T(8,128)(2,1)S(1)} %collective-permute-done.refs_4_), channel_id=1, source_target_pairs={{0,1},{1,0},{2,3},{3,2},{4,5},{5,4},{6,7},{7,6},{8,9},{9,8},{10,11... | collective-permute-start | bytes 589832 | tf_op jit(solution)/shard_map/ppermute | solution.py:44
  21.0 10.0 %collective-permute-start.8 = (bf16[192,768]{1,0:T(8,128)(2,1)}, bf16[192,768]{1,0:T(8,128)(2,1)S(1)}, u32[]{:S(2)}, u32[]{:S(2)}) collective-permute-start(bf16[192,768]{1,0:T(8,128)(2,1)} %refs_6_), channel_id=1, source_target_pairs={{0,2},{1,3},{2,0},{3,1},{4,6},{5,7},{6,4},{7,5},{8,10},{9,11},{10,... | collective-permute-start | bytes 884744 | tf_op jit(solution)/shard_map/ppermute | solution.py:44
  21.6 9.3 %collective-permute-start.9 = (bf16[192,768]{1,0:T(8,128)(2,1)}, bf16[192,768]{1,0:T(8,128)(2,1)S(1)}, u32[]{:S(2)}, u32[]{:S(2)}) collective-permute-start(bf16[192,768]{1,0:T(8,128)(2,1)} %refs_6_), channel_id=1, source_target_pairs={{0,1},{1,0},{2,3},{3,2},{4,5},{5,4},{6,7},{7,6},{8,9},{9,8},{10,11... | collective-permute-start | bytes 884744 | tf_op jit(solution)/shard_map/ppermute | solution.py:44
  39.2 12.6 %collective-permute-start.24 = (bf16[80,768]{1,0:T(8,128)(2,1)S(1)}, bf16[80,768]{1,0:T(8,128)(2,1)S(1)}, u32[]{:S(2)}, u32[]{:S(2)}) collective-permute-start(bf16[80,768]{1,0:T(8,128)(2,1)S(1)} %convolution_convert_fusion), channel_id=1, source_target_pairs={{0,4},{4,0},{8,12},{12,8},{16,20},{20,16},{24,28},{28,24},{1,5},{5... | collective-permute-start | bytes 368648 | tf_op jit(solution)/shard_map/ppermute | solution.py:44
  57.9 9.9 %collective-permute-start.18 = (bf16[160,768]{1,0:T(8,128)(2,1)S(1)}, bf16[160,768]{1,0:T(8,128)(2,1)S(1)}, u32[]{:S(2)}, u32[]{:S(2)}) collective-permute-start(bf16[160,768]{1,0:T(8,128)(2,1)S(1)} %pad_maximum_fusion.refs_0_.own), channel_id=1, source_target_pairs={{0,2},{1,3},{2,0},{3,1},{4,6},{5,7},{6,4},{7,5},{8,10},{9,11},{10,... | collective-permute-start | bytes 737288 | tf_op jit(solution)/shard_map/ppermute | solution.py:44
  67.2 8.8 %collective-permute-start.28 = (bf16[160,768]{1,0:T(8,128)(2,1)S(1)}, bf16[160,768]{1,0:T(8,128)(2,1)S(1)}, u32[]{:S(2)}, u32[]{:S(2)}) collective-permute-start(bf16[160,768]{1,0:T(8,128)(2,1)S(1)} %pad_maximum_fusion.2.refs_0_.own_grad), channel_id=1, source_target_pairs={{0,2},{1,3},{2,0},{3,1},{4,6},{5,7},{6,4},{7,5},{8,10},{9,11},{10,... | collective-permute-start | bytes 737288 | tf_op jit(solution)/shard_map/ppermute | solution.py:44
  74.5 8.5 %collective-permute-start.19 = (bf16[160,768]{1,0:T(8,128)(2,1)}, bf16[160,768]{1,0:T(8,128)(2,1)S(1)}, u32[]{:S(2)}, u32[]{:S(2)}) collective-permute-start(bf16[160,768]{1,0:T(8,128)(2,1)} %get-tuple-element.124), channel_id=1, source_target_pairs={{0,2},{1,3},{2,0},{3,1},{4,6},{5,7},{6,4},{7,5},{8,10},{9,11},{10,... | collective-permute-start | bytes 737288 | tf_op jit(solution)/shard_map/ppermute | solution.py:44
  82.5 12.5 %collective-permute-start.29 = (bf16[160,768]{1,0:T(8,128)(2,1)}, bf16[160,768]{1,0:T(8,128)(2,1)S(1)}, u32[]{:S(2)}, u32[]{:S(2)}) collective-permute-start(bf16[160,768]{1,0:T(8,128)(2,1)} %get-tuple-element.133), channel_id=1, source_target_pairs={{0,2},{1,3},{2,0},{3,1},{4,6},{5,7},{6,4},{7,5},{8,10},{9,11},{10,... | collective-permute-start | bytes 737288 | tf_op jit(solution)/shard_map/ppermute | solution.py:44
  93.0 10.6 %collective-permute-start.23 = (bf16[80,768]{1,0:T(8,128)(2,1)S(1)}, bf16[80,768]{1,0:T(8,128)(2,1)S(1)}, u32[]{:S(2)}, u32[]{:S(2)}) collective-permute-start(bf16[80,768]{1,0:T(8,128)(2,1)S(1)} %pad_maximum_fusion.4), channel_id=1, source_target_pairs={{0,4},{4,0},{8,12},{12,8},{16,20},{20,16},{24,28},{28,24},{1,5},{5... | collective-permute-start | bytes 368648 | tf_op jit(solution)/shard_map/ppermute | solution.py:44
  108.6 8.9 %collective-permute-start.34 = (bf16[128,768]{1,0:T(8,128)(2,1)S(1)}, bf16[128,768]{1,0:T(8,128)(2,1)S(1)}, u32[]{:S(2)}, u32[]{:S(2)}) collective-permute-start(bf16[128,768]{1,0:T(8,128)(2,1)S(1)} %fusion.69.refs_9_), channel_id=1, source_target_pairs={{0,2},{1,3},{2,0},{3,1},{4,6},{5,7},{6,4},{7,5},{8,10},{9,11},{10,... | collective-permute-start | bytes 589832 | tf_op jit(solution)/shard_map/ppermute | solution.py:44
  110.1 7.9 %collective-permute-start.35 = (bf16[128,768]{1,0:T(8,128)(2,1)S(1)}, bf16[128,768]{1,0:T(8,128)(2,1)S(1)}, u32[]{:S(2)}, u32[]{:S(2)}) collective-permute-start(bf16[128,768]{1,0:T(8,128)(2,1)S(1)} %fusion.69.refs_9_), channel_id=1, source_target_pairs={{0,1},{1,0},{2,3},{3,2},{4,5},{5,4},{6,7},{7,6},{8,9},{9,8},{10,11... | collective-permute-start | bytes 589832 | tf_op jit(solution)/shard_map/ppermute | solution.py:44
  128.6 10.4 %collective-permute-start.38 = (bf16[2,5,24,640]{3,2,1,0:T(8,128)(2,1)}, bf16[2,5,24,640]{3,2,1,0:T(8,128)(2,1)S(1)}, u32[]{:S(2)}, u32[]{:S(2)}) collective-permute-start(bf16[2,5,24,640]{3,2,1,0:T(8,128)(2,1)} %get-tuple-element.148), channel_id=1, source_target_pairs={{0,4},{4,0},{8,12},{12,8},{16,20},{20,16},{24,28},{28,24},{1,5},{5... | collective-permute-start | bytes 921608 | tf_op jit(solution)/shard_map/ppermute | solution.py:44
  129.4 15.6 %collective-permute-start.37 = (bf16[2,5,24,640]{3,2,1,0:T(8,128)(2,1)}, bf16[2,5,24,640]{3,2,1,0:T(8,128)(2,1)S(1)}, u32[]{:S(2)}, u32[]{:S(2)}) collective-permute-start(bf16[2,5,24,640]{3,2,1,0:T(8,128)(2,1)} %get-tuple-element.146), channel_id=1, source_target_pairs={{0,4},{4,0},{8,12},{12,8},{16,20},{20,16},{24,28},{28,24},{1,5},{5... | collective-permute-start | bytes 921608 | tf_op jit(solution)/shard_map/ppermute | solution.py:44
  140.1 13.1 %collective-permute-start.39 = (bf16[5,24,640]{2,1,0:T(8,128)(2,1)S(1)}, bf16[5,24,640]{2,1,0:T(8,128)(2,1)S(1)}, u32[]{:S(2)}, u32[]{:S(2)}) collective-permute-start(bf16[5,24,640]{2,1,0:T(8,128)(2,1)S(1)} %get-tuple-element.186), channel_id=1, source_target_pairs={{0,16},{4,20},{8,24},{12,28},{16,0},{20,4},{24,8},{28,12},{1,17},{... | collective-permute-start | bytes 460808 | tf_op jit(solution)/shard_map/ppermute | solution.py:44
  140.1 13.0 %collective-permute-start.40 = (bf16[5,24,640]{2,1,0:T(8,128)(2,1)S(1)}, bf16[5,24,640]{2,1,0:T(8,128)(2,1)S(1)}, u32[]{:S(2)}, u32[]{:S(2)}) collective-permute-start(bf16[5,24,640]{2,1,0:T(8,128)(2,1)S(1)} %get-tuple-element.187), channel_id=1, source_target_pairs={{0,24},{4,28},{8,16},{12,20},{16,8},{20,12},{24,0},{28,4},{1,25},{... | collective-permute-start | bytes 460808 | tf_op jit(solution)/shard_map/ppermute | solution.py:44
  146.0 9.7 %collective-permute-start.41 = (bf16[5,24,640]{2,1,0:T(8,128)(2,1)S(1)}, bf16[5,24,640]{2,1,0:T(8,128)(2,1)S(1)}, u32[]{:S(2)}, u32[]{:S(2)}) collective-permute-start(bf16[5,24,640]{2,1,0:T(8,128)(2,1)S(1)} %fusion.24), channel_id=1, source_target_pairs={{0,8},{4,12},{8,0},{12,4},{16,24},{20,28},{24,16},{28,20},{1,9},{5... | collective-permute-start | bytes 460808 | tf_op jit(solution)/shard_map/ppermute | solution.py:44
  146.2 9.7 %collective-permute-start.42 = (bf16[128,768]{1,0:T(8,128)(2,1)}, bf16[128,768]{1,0:T(8,128)(2,1)S(1)}, u32[]{:S(2)}, u32[]{:S(2)}) collective-permute-start(bf16[128,768]{1,0:T(8,128)(2,1)} %get-tuple-element.154), channel_id=1, source_target_pairs={{0,1},{1,0},{2,3},{3,2},{4,5},{5,4},{6,7},{7,6},{8,9},{9,8},{10,11... | collective-permute-start | bytes 589832 | tf_op jit(solution)/shard_map/ppermute | solution.py:44
  146.2 9.7 %collective-permute-start.43 = (bf16[128,768]{1,0:T(8,128)(2,1)}, bf16[128,768]{1,0:T(8,128)(2,1)S(1)}, u32[]{:S(2)}, u32[]{:S(2)}) collective-permute-start(bf16[128,768]{1,0:T(8,128)(2,1)} %get-tuple-element.155), channel_id=1, source_target_pairs={{0,2},{1,3},{2,0},{3,1},{4,6},{5,7},{6,4},{7,5},{8,10},{9,11},{10,... | collective-permute-start | bytes 589832 | tf_op jit(solution)/shard_map/ppermute | solution.py:44
  166.2 12.2 %collective-permute-start.55 = (bf16[1,768,768]{2,1,0:T(8,128)(2,1)S(1)}, bf16[1,768,768]{2,1,0:T(8,128)(2,1)S(1)}, u32[]{:S(2)}, u32[]{:S(2)}) collective-permute-start(bf16[1,768,768]{2,1,0:T(8,128)(2,1)S(1)} %copy-done.23), channel_id=1, source_target_pairs={{0,1},{1,0},{2,3},{3,2},{4,5},{5,4},{6,7},{7,6},{8,9},{9,8},{10,11... | collective-permute-start | bytes 3538952 | tf_op jit(solution)/shard_map/ppermute | solution.py:44
  166.4 13.6 %collective-permute-start.54 = (bf16[1,768,768]{2,1,0:T(8,128)(2,1)S(1)}, bf16[1,768,768]{2,1,0:T(8,128)(2,1)S(1)}, u32[]{:S(2)}, u32[]{:S(2)}) collective-permute-start(bf16[1,768,768]{2,1,0:T(8,128)(2,1)S(1)} %copy-done.22), channel_id=1, source_target_pairs={{0,1},{1,0},{2,3},{3,2},{4,5},{5,4},{6,7},{7,6},{8,9},{9,8},{10,11... | collective-permute-start | bytes 3538952 | tf_op jit(solution)/shard_map/ppermute | solution.py:44
  166.8 9.0 %collective-permute-start.48 = (bf16[5,24,640]{2,1,0:T(8,128)(2,1)S(1)}, bf16[5,24,640]{2,1,0:T(8,128)(2,1)S(1)}, u32[]{:S(2)}, u32[]{:S(2)}) collective-permute-start(bf16[5,24,640]{2,1,0:T(8,128)(2,1)S(1)} %slice_dynamic-update-slice_fusion.refs_0_), channel_id=1, source_target_pairs={{0,16},{4,20},{8,24},{12,28},{16,0},{20,4},{24,8},{28,12},{1,17},{... | collective-permute-start | bytes 460808 | tf_op jit(solution)/shard_map/ppermute | solution.py:44
  167.7 8.1 %collective-permute-start.49 = (bf16[5,24,640]{2,1,0:T(8,128)(2,1)S(1)}, bf16[5,24,640]{2,1,0:T(8,128)(2,1)S(1)}, u32[]{:S(2)}, u32[]{:S(2)}) collective-permute-start(bf16[5,24,640]{2,1,0:T(8,128)(2,1)S(1)} %slice_dynamic-update-slice_fusion.refs_0_), channel_id=1, source_target_pairs={{0,4},{4,0},{8,12},{12,8},{16,20},{20,16},{24,28},{28,24},{1,5},{5... | collective-permute-start | bytes 460808 | tf_op jit(solution)/shard_map/ppermute | solution.py:44
  168.0 8.7 %collective-permute-start.50 = (bf16[5,24,640]{2,1,0:T(8,128)(2,1)S(1)}, bf16[5,24,640]{2,1,0:T(8,128)(2,1)S(1)}, u32[]{:S(2)}, u32[]{:S(2)}) collective-permute-start(bf16[5,24,640]{2,1,0:T(8,128)(2,1)S(1)} %slice_dynamic-update-slice_fusion.refs_0_), channel_id=1, source_target_pairs={{0,8},{4,12},{8,0},{12,4},{16,24},{20,28},{24,16},{28,20},{1,9},{5... | collective-permute-start | bytes 460808 | tf_op jit(solution)/shard_map/ppermute | solution.py:44
  175.8 6.7 %collective-permute-start.53 = (bf16[5,24,640]{2,1,0:T(8,128)(2,1)S(1)}, bf16[5,24,640]{2,1,0:T(8,128)(2,1)S(1)}, u32[]{:S(2)}, u32[]{:S(2)}) collective-permute-start(bf16[5,24,640]{2,1,0:T(8,128)(2,1)S(1)} %collective-permute-done.48.refs_4_), channel_id=1, source_target_pairs={{0,8},{4,12},{8,0},{12,4},{16,24},{20,28},{24,16},{28,20},{1,9},{5... | collective-permute-start | bytes 460808 | tf_op jit(solution)/shard_map/ppermute | solution.py:44
  175.9 7.9 %collective-permute-start.52 = (bf16[5,24,640]{2,1,0:T(8,128)(2,1)S(1)}, bf16[5,24,640]{2,1,0:T(8,128)(2,1)S(1)}, u32[]{:S(2)}, u32[]{:S(2)}) collective-permute-start(bf16[5,24,640]{2,1,0:T(8,128)(2,1)S(1)} %collective-permute-done.48.refs_4_), channel_id=1, source_target_pairs={{0,4},{4,0},{8,12},{12,8},{16,20},{20,16},{24,28},{28,24},{1,5},{5... | collective-permute-start | bytes 460808 | tf_op jit(solution)/shard_map/ppermute | solution.py:44
  176.7 9.3 %collective-permute-start.51 = (bf16[5,24,640]{2,1,0:T(8,128)(2,1)S(1)}, bf16[5,24,640]{2,1,0:T(8,128)(2,1)S(1)}, u32[]{:S(2)}, u32[]{:S(2)}) collective-permute-start(bf16[5,24,640]{2,1,0:T(8,128)(2,1)S(1)} %collective-permute-done.50.refs_2_), channel_id=1, source_target_pairs={{0,4},{4,0},{8,12},{12,8},{16,20},{20,16},{24,28},{28,24},{1,5},{5... | collective-permute-start | bytes 460808 | tf_op jit(solution)/shard_map/ppermute | solution.py:44
  (62 other events, 380.6 us)

commit v6 on v5

--- a/solution.py
+++ b/solution.py
@@ -127,11 +127,11 @@
     lengths, table = refs[:2]
     token_refs = refs[2 : 2 + n]
     weight_refs = refs[2 + n : 2 + 2 * n]
-    tokens_out, weight_out, projected_out, weights_out, gains_out, mixed_all = refs[
-        2 + 2 * n : 8 + 2 * n
+    tokens_out, weight_out, projected_out, weights_out, *gains_out, mixed_all = refs[
+        2 + 2 * n : 9 + 2 * n
     ]
-    mixed_out = refs[8 + 2 * n : 8 + 3 * n]
-    normed_scr, scores_scr = refs[8 + 3 * n :]
+    mixed_out = refs[9 + 2 * n : 9 + 3 * n]
+    normed_scr, scores_scr = refs[9 + 3 * n :]
     s = lax.axis_index("shard")
     part = width // n
     wide = 3 * part
@@ -143,8 +143,8 @@
     for c in range(width // size):
         beside = weight_out[c * size : (c + 1) * size, wide:].astype(f32)
         for i in range(2):
-            gains_out[i : i + 1, c * size : (c + 1) * size] = to_row(beside[:, i : i + 1], size)
-    gain = gains_out[0:1, :]
+            gains_out[i][:, c * size : (c + 1) * size] = to_row(beside[:, i : i + 1], size)
+    gain = gains_out[0][...]
     for j in range(n):
         value = tokens_out[j].astype(f32)
         factor = lax.rsqrt(jnp.mean(value * value, axis=-1, keepdims=True) + norm_eps)
@@ -277,7 +277,7 @@
     send_scr[...] = normed_grad.astype(bf16).reshape(n, rows, width)
     for p in range(n):
         normed_grad_out[p][...] = send_scr[s ^ p]
-    gain = gains[0:1, :]
+    gain = gains[...]
     grad_gain = jnp.zeros((1, width), f32)
     for j in range(n):
         value = tokens[j].astype(f32)
@@ -399,14 +399,20 @@
     send_out[...] = result[rows:].astype(bf16)
 
 
-def expert_weights(own, came, own_grad, came_grad, hidden, grad_before, *outs):
-    up_out, down_out, up_send, down_send = outs
+def weights_to_send(own, came, own_grad, came_grad, hidden, grad_before, up_send, down_send):
     grads = jnp.concatenate([own_grad[...], came_grad[...]], axis=0)
     rows = jnp.concatenate([own[...], came[...]], axis=0)
     up_send[0] = dot_tn(rows, grad_before[1]).astype(bf16)
     down_send[0] = dot_tn(hidden[1], grads).astype(bf16)
-    up_out[0] = dot_tn(rows, grad_before[0])
-    down_out[0] = dot_tn(hidden[0], grads)
+
+
+def weights_to_keep(
+    own, came, own_grad, came_grad, hidden, grad_before, up_came, down_came, up_out, down_out
+):
+    grads = jnp.concatenate([own_grad[...], came_grad[...]], axis=0)
+    rows = jnp.concatenate([own[...], came[...]], axis=0)
+    up_out[0] = dot_tn(rows, grad_before[0]) + up_came[0].astype(f32)
+    down_out[0] = dot_tn(hidden[0], grads) + down_came[0].astype(f32)
 
 
 def rms_factor(value):
@@ -478,7 +484,8 @@
             shape((width, full)),
             shape((group, wide)),
             shape((heads, group, group)),
-            shape((row_tile, width), f32),
+            shape((1, width), f32),
+            shape((1, width), f32),
             shape((n, rows, part)),
             *[shape((rows, part))] * n,
         ),
@@ -487,13 +494,12 @@
         [pltpu.VMEM((group, width), bf16), pltpu.VMEM((group, group), f32)],
         work=10 * micro,
     )
-    tokens_all, weight, projected, weights, gains, mixed = answers[:6]
+    tokens_all, weight, projected, weights, gain_one, gain_two, mixed = answers[:7]
     mixed_mine, pair_up, pair_down, far_out, pair_out = lax.optimization_barrier(
-        (list(answers[6:]), pair_up, pair_down, far_out, pair_out)
+        (list(answers[7:]), pair_up, pair_down, far_out, pair_out)
     )
     mixed_blocks = exchange_relative(mixed_mine, "shard")
     out_blocks = [own_out, pair_out, far_out, swap(far_out, "shard", pair)]
-    gain_one, gain_two = gains[0:1], gains[1:2]
 
     inputs = tokens.astype(f32)
     hidden_one = inputs + sum(dot(mixed_blocks[p], out_blocks[p]) for p in range(n))
@@ -528,33 +534,48 @@
             value.reshape(experts, capacity, width), "expert", 0, 0, tiled=True
         ).reshape(places, width)
 
-    def send(value, after=None):
+    def dispatch(forward, backward):
         if not direct:
-            return plain(dot_tn(collect, value).astype(bf16))
+            return [plain(dot_tn(collect, x).astype(bf16)) for x in (forward, backward)]
+        value = jnp.concatenate([forward, backward], axis=1)
         came = swap(dot_tn(collect[:, half:], value).astype(bf16), "expert", 1)
-        own = dot_tn(collect[:, :half], value).astype(bf16).reshape(m // 2, capacity, width)
-        both = jnp.concatenate([own, came.reshape(m // 2, capacity, width)], axis=1)
+        own = dot_tn(collect[:, :half], value).astype(bf16).reshape(m // 2, capacity, 2 * width)
+        both = jnp.concatenate([own, came.reshape(m // 2, capacity, 2 * width)], axis=1)
+        blocks = [both[d] if d == 0 else swap(both[d], "expert", 2 * d) for d in range(m // 2)]
+        return [
+            jnp.concatenate([block[:, i * width : (i + 1) * width] for block in blocks], axis=0)
+            for i in range(2)
+        ]
+
+    def among_pairs(value):
+        both = value.reshape(m // 2, 2 * capacity, width)
+        return [both[d] if d == 0 else swap(both[d], "expert", 2 * d) for d in range(m // 2)]
+
+    def give_back(forward, backward):
+        if not direct:
+            return [dot(collect, plain(x)) for x in (forward, backward)]
+        blocks = [among_pairs(forward)]
+        backward, _ = lax.optimization_barrier((backward, blocks[0]))
+        blocks.append(among_pairs(backward))
+        own, other = (
+            jnp.concatenate(
+                [jnp.concatenate([x[at : at + capacity] for x in side]) for side in blocks], axis=1
+            )
+            for at in (0, capacity)
+        )
+        total = dot(collect[:, :half], own) + dot(collect[:, half:], swap(other, "expert", 1))
+        return total[:, :width], total[:, width:]
+
+    def reduce_shard(keep, out, after=None):
+        came = swap(out, "shard", 2 * pair)
         if after is not None:
-            both, _ = lax.optimization_barrier((both, after))
-        blocks = [both[d] if d == 0 else swap(both[d], "expert", 2 * d) for d in range(m // 2)]
-        return jnp.concatenate(blocks, axis=0)
-
-    def give_back(value):
-        if not direct:
-            return dot(collect, plain(value)), value
-        both = value.reshape(m // 2, 2 * capacity, width)
-        blocks = [both[d] if d == 0 else swap(both[d], "expert", 2 * d) for d in range(m // 2)]
-        own = jnp.concatenate([block[:capacity] for block in blocks])
-        other = jnp.concatenate([block[capacity:] for block in blocks])
-        other = swap(other, "expert", 1)
-        return dot(collect[:, :half], own) + dot(collect[:, half:], other), own
-
-    def reduce_shard(keep, out):
-        return (keep + swap(out, "shard", 2 * pair).astype(f32)).astype(bf16)
-
-    arrived = send(normed_two.astype(bf16))
-    row_blocks = (arrived, swap(arrived, "shard", 2 * pair))
-    arrived_grad = send(grad_result, arrived)
+            came, _ = lax.optimization_barrier((came, after))
+        return (keep + came.astype(f32)).astype(bf16)
+
+    arrived, arrived_grad = dispatch(normed_two.astype(bf16), grad_result)
+    came = swap(arrived, "shard", 2 * pair)
+    came, arrived_grad = lax.optimization_barrier((came, arrived_grad))
+    row_blocks = (arrived, came)
     grad_blocks = (arrived_grad, swap(arrived_grad, "shard", 2 * pair))
 
     units = expert_in.shape[2]
@@ -573,10 +594,9 @@
         (*grad_blocks, *expert_weight, slope),
         work=6 * micro,
     )
-    expert_result, first_back = give_back(reduce_shard(*forward))
-    keep_grad, came_grad = backward[0], swap(backward[1], "shard", 2 * pair)
-    came_grad, _ = lax.optimization_barrier((came_grad, first_back))
-    grad_sent, _ = give_back((keep_grad + came_grad.astype(f32)).astype(bf16))
+    expert_result, grad_sent = give_back(
+        reduce_shard(*forward, backward[1]), reduce_shard(*backward)
+    )
 
     layer_out = (hidden_one + gate[:, None] * expert_result).astype(bf16)
     grad_gate = jnp.sum(upstream * expert_result, axis=1)
@@ -598,27 +618,22 @@
     grad_middle, grad_gain_two = rms_backward(hidden_one, factor_two, gain_two, grad_normed_two)
     grad_hidden = upstream + grad_middle
     branch, late_rows = lax.optimization_barrier((grad_hidden.astype(bf16), row_blocks))
-    grad_up, grad_down, up_send, down_send = call(
-        expert_weights,
-        (
-            shape(expert_in.shape, f32),
-            shape(expert_out.shape, f32),
-            shape(expert_in.shape),
-            shape(expert_out.shape),
-        ),
-        (
-            *late_rows,
-            *grad_blocks,
-            hidden,
-            grad_before,
-        ),
-        work=6 * micro,
+    sources = (*grad_blocks, hidden, grad_before)
+    up_send, down_send = call(
+        weights_to_send,
+        (shape(expert_in.shape), shape(expert_out.shape)),
+        (*late_rows, *sources),
+        work=4 * micro,
     )
     far_branch, pair_branch = swap(branch, "shard", 2 * pair), swap(branch, "shard", pair)
     far_branch, grad_router, gain_two_row, up_send, down_send = lax.optimization_barrier(
         (far_branch, grad_router, grad_gain_two, up_send, down_send)
     )
     branch_blocks = [branch, pair_branch, far_branch, swap(far_branch, "shard", pair)]
+    branch_blocks, up_send, down_send = lax.optimization_barrier(
+        (branch_blocks, up_send, down_send)
+    )
+    up_came, down_came = swap(up_send, "shard", pair), swap(down_send, "shard", pair)
     holders = m if direct else 1
     piece = part // m
     if direct:
@@ -636,7 +651,7 @@
         (
             projected,
             tokens_all,
-            gains,
+            gain_one,
             weight,
             weights,
             mixed,
@@ -661,7 +676,13 @@
     shares = answers[: len(share_shapes)]
     normed_grads = answers[len(share_shapes) : len(share_shapes) + n]
     gain_row, table = answers[len(share_shapes) + n :]
-
+    late_rows, normed_grads = lax.optimization_barrier((row_blocks, list(normed_grads)))
+    grad_up, grad_down = call(
+        weights_to_keep,
+        (shape(expert_in.shape, f32), shape(expert_out.shape, f32)),
+        (*late_rows, *sources, up_came, down_came),
+        work=4 * micro,
+    )
     per_line = buckets // row_tile
 
     def biases(block):
@@ -675,10 +696,15 @@
     if direct:
         far_keep, far_send, near_keep, near_send = shares
         far_came = swap(far_send, "expert", 1)
+        far_came, near_send, grad_up, grad_down = lax.optimization_barrier(
+            (far_came, near_send, grad_up, grad_down)
+        )
         far = far_keep.astype(f32) + far_came.astype(f32)
-        normed_grads, far_came = lax.optimization_barrier((normed_grads, far_came))
+        near_came, normed_grads = lax.optimization_barrier(
+            (swap(near_send, "expert", 1), normed_grads)
+        )
+        near = near_keep.astype(f32) + near_came.astype(f32)
         grad_tokens = finish_tokens(normed_grads)
-        near = near_keep.astype(f32) + swap(near_send, "expert", 1).astype(f32)
         came = [swap(far[d].astype(bf16), "expert", m // 2 + 2 * d) for d in range(m // 4)]
         came += [swap(near[d].astype(bf16), "expert", 2 * d) for d in range(1, m // 4)]
         summed = near[0] + sum(x.astype(f32) for x in came)
@@ -696,20 +722,13 @@
         mine = jnp.stack(
             [jnp.where(own_lane, low[p], mine[p]) for p in range(n)] + [low[n]], axis=0
         )
-        mine, up_send, down_send = lax.optimization_barrier((mine, up_send, down_send))
         blocks = {0: mine, 1: swap(mine, "expert", 1), 4: swap(mine, "expert", 4)}
         blocks[2] = swap(mine, "expert", 2)
-        blocks[4], blocks[1] = lax.optimization_barrier((blocks[4], blocks[1]))
+        blocks[2], blocks[1] = lax.optimization_barrier((blocks[2], blocks[1]))
+        blocks[3] = swap(blocks[2], "expert", 1)
+        blocks[4], blocks[3] = lax.optimization_barrier((blocks[4], blocks[3]))
         blocks[6] = swap(blocks[4], "expert", 2)
         blocks[5] = swap(blocks[4], "expert", 1)
-        blocks[3] = swap(blocks[2], "expert", 1)
-        blocks[6], grad_up, grad_down = lax.optimization_barrier(
-            (
-                blocks[6],
-                grad_up + swap(up_send, "shard", pair).astype(f32),
-                grad_down + swap(down_send, "shard", pair).astype(f32),
-            )
-        )
         blocks[7] = swap(blocks[6], "expert", 1)
         blocks = [blocks[d] for d in range(m)]
         grad_attention_in, grad_attention_out, total_one, total_two, total_router = call(
@@ -727,8 +746,6 @@
         )
     else:
         grad_tokens = finish_tokens(normed_grads)
-        grad_up = grad_up + swap(up_send, "shard", pair).astype(f32)
-        grad_down = grad_down + swap(down_send, "shard", pair).astype(f32)
         came = lax.all_to_all(
             shares[0].reshape(n, m, piece, wide).swapaxes(0, 1), "expert", 0, 0, tiled=True
         )

time: 193 us -> 191 us (0.990)
  other arithmetic: 10.3 us -> 6.59 us
  Pallas kernels: 40.1 us -> 43.5 us
    add x3 -> x1, other arithmetic: 4.29 us -> 0.07 us  [local(): near = near_keep.astype(f32) + near_came.astype(f32)]
    pallas_call x7 -> x8, Pallas kernels: 40.1 us -> 43.5 us  [call(): pl.pallas_call(kernel, out_shape=out_shape, in_specs=in_specs, out_specs=...]
    ppermute x57 -> x52, starting transfers between devices: 52.1 us -> 53.1 us  [swap(): return lax.ppermute(value, axis, [(i, i ^ bit) for i in range(size)])]
    ppermute x57 -> x52, waiting for transfers between devices: 74.6 us -> 73.7 us  [swap(): return lax.ppermute(value, axis, [(i, i ^ bit) for i in range(size)])]
  transfers between devices with their start and end apart: 57 -> 52, of which waited for: 27 -> 28; matrix products, arithmetic and copies ran while one was open for 8% -> 5% of each run, Pallas kernels for 15% -> 21%
where the time goes in v6:
time: 191 us; the launch traced here: 190 us
  waiting for transfers between devices  73.7 us (39%)
  starting transfers between devices  53.1 us (28%)
  Pallas kernels  43.5 us (23%)
  local copies, waits for them, and re-layouts  6.85 us (4%)
  other arithmetic  6.59 us (3%)
  matrix products  5.23 us (3%)
    ppermute x52, waiting for transfers between devices, swap(): return lax.ppermute(value, axis, [(i, i ^ bit) for i in range(size)])  73.7 us
    ppermute x52, starting transfers between devices, swap(): return lax.ppermute(value, axis, [(i, i ^ bit) for i in range(size)])  53.1 us
    pallas_call x8, Pallas kernels, call(): pl.pallas_call(kernel, out_shape=out_shape, in_specs=in_specs, out_specs=...  43.5 us
  transfers between devices with their start and end apart: 52, of which 28 were waited for; matrix products, arithmetic and copies ran while one was open for 5% of the time, Pallas kernels for 21%

profile of v6, /device:TPU:0, one launch (start us, length us, event | category | flops | bytes accessed | tf_op | source)
XLA Modules:
  0.0 190.2 jit_solution(2489872406135086494)
XLA Ops:
  0.7 3.0 %collective-permute-start = (bf16[128,768]{1,0:T(8,128)(2,1)}, bf16[128,768]{1,0:T(8,128)(2,1)S(1)}, u32[]{:S(2)}, u32[]{:S(2)}) collective-permute-start(bf16[128,768]{1,0:T(8,128)(2,1)} %refs_2_), channel_id=1, source_target_pairs={{0,2},{1,3},{2,0},{3,1},{4,6},{5,7},{6,4},{7,5},{8,10},{9,11},{10,... | collective-permute-start | bytes 589832 | tf_op jit(solution)/shard_map/ppermute | solution.py:44
  5.6 2.5 %shard_map.195 = (bf16[192,640]{1,0:T(8,128)(2,1)}, bf16[192,640]{1,0:T(8,128)(2,1)}, bf16[192,640]{1,0:T(8,128)(2,1)}, bf16[192,640]{1,0:T(8,128)(2,1)}) custom-call(bf16[192,2304]{1,0:T(8,128)(2,1)} %refs_0_.2, bf16[2,192]{1,0:T(2,128)(2,1)} %pad_maximum_fusion.6.refs_1_), custom_call_target="tpu_custom_call" | custom-call | tf_op jit(solution)/shard_map/pallas_call | solution.py:66
  14.1 3.5 %collective-permute-done.4.refs_8_ = bf16[192,640]{1,0:T(8,128)(2,1)S(1)} collective-permute-done((bf16[192,640]{1,0:T(8,128)(2,1)}, bf16[192,640]{1,0:T(8,128)(2,1)S(1)}, u32[]{:S(2)}, u32[]{:S(2)}) %collective-permute-start.4) | collective-permute-done | bytes 245792 | tf_op jit(solution)/shard_map/ppermute | solution.py:44
  17.6 3.3 %collective-permute-done.5.refs_9_ = bf16[192,640]{1,0:T(8,128)(2,1)S(1)} collective-permute-done((bf16[192,640]{1,0:T(8,128)(2,1)}, bf16[192,640]{1,0:T(8,128)(2,1)S(1)}, u32[]{:S(2)}, u32[]{:S(2)}) %collective-permute-start.5) | collective-permute-done | bytes 245792 | tf_op jit(solution)/shard_map/ppermute | solution.py:44
  21.9 7.0 %shard_map.196 = (bf16[4,128,768]{2,1,0:T(8,128)(2,1)}, bf16[768,640]{1,0:T(8,128)(2,1)}, bf16[512,576]{1,0:T(8,128)(2,1)}, bf16[3,512,512]{2,1,0:T(8,128)(2,1)}...) custom-call(s32[1,3]{1,0:T(1,128)} %refs_0_.3, ...), custom_call_target="tpu_custom_call" | custom-call | flops 10000000000 | tf_op jit(solution)/shard_map/pallas_call | solution.py:66
  28.9 2.0 %collective-permute-done.8 = bf16[192,768]{1,0:T(8,128)(2,1)S(1)} collective-permute-done((bf16[192,768]{1,0:T(8,128)(2,1)}, bf16[192,768]{1,0:T(8,128)(2,1)S(1)}, u32[]{:S(2)}, u32[]{:S(2)}) %collective-permute-start.8) | collective-permute-done | bytes 294944 | tf_op jit(solution)/shard_map/ppermute | solution.py:44
  40.6 5.9 %collective-permute-done.14 = bf16[80,1536]{1,0:T(8,128)(2,1)S(1)} collective-permute-done((bf16[80,1536]{1,0:T(8,128)(2,1)S(1)}, bf16[80,1536]{1,0:T(8,128)(2,1)S(1)}, u32[]{:S(2)}, u32[]{:S(2)}) %collective-permute-start.14) | collective-permute-done | bytes 245792 | tf_op jit(solution)/shard_map/ppermute | solution.py:44
  46.7 3.9 %collective-permute-start.17 = (bf16[40,1536]{1,0:T(8,128)(2,1)S(1)}, bf16[40,1536]{1,0:T(8,128)(2,1)S(1)}, u32[]{:S(2)}, u32[]{:S(2)}) collective-permute-start(bf16[40,1536]{1,0:T(8,128)(2,1)S(1)} %get-tuple-element.218), channel_id=1, source_target_pairs={{0,24},{4,28},{8,16},{12,20},{16,8},{20,12},{24,0},{28,4},{1,25},{... | collective-permute-start | bytes 368648 | tf_op jit(solution)/shard_map/ppermute | solution.py:44
  51.2 3.6 %collective-permute-done.17 = bf16[40,1536]{1,0:T(8,128)(2,1)S(1)} collective-permute-done((bf16[40,1536]{1,0:T(8,128)(2,1)S(1)}, bf16[40,1536]{1,0:T(8,128)(2,1)S(1)}, u32[]{:S(2)}, u32[]{:S(2)}) %collective-permute-start.17) | collective-permute-done | bytes 122912 | tf_op jit(solution)/shard_map/ppermute | solution.py:44
  54.9 5.5 %collective-permute-done.16 = bf16[40,1536]{1,0:T(8,128)(2,1)S(1)} collective-permute-done((bf16[40,1536]{1,0:T(8,128)(2,1)S(1)}, bf16[40,1536]{1,0:T(8,128)(2,1)S(1)}, u32[]{:S(2)}, u32[]{:S(2)}) %collective-permute-start.16) | collective-permute-done | bytes 122912 | tf_op jit(solution)/shard_map/ppermute | solution.py:44
  61.5 5.9 %collective-permute-done.18.refs_1_.came = bf16[160,768]{1,0:T(8,128)(2,1)S(1)} collective-permute-done((bf16[160,768]{1,0:T(8,128)(2,1)S(1)}, bf16[160,768]{1,0:T(8,128)(2,1)S(1)}, u32[]{:S(2)}, u32[]{:S(2)}) %collective-permute-start.18) | collective-permute-done | bytes 245792 | tf_op jit(solution)/shard_map/ppermute | solution.py:44
  68.5 6.0 %shard_map.197 = (bf16[2,320,768]{2,1,0:T(8,128)(2,1)}, bf16[2,320,768]{2,1,0:T(8,128)(2,1)}, f32[160,768]{1,0:T(8,128)}, bf16[160,768]{1,0:T(8,128)(2,1)}) custom-call(bf16[160,768]{1,0:T(8,128)(2,1)} %copy-done.9, bf16[160,768]{1,0:T(8,128)(2,1)} %copy-done.26, bf16[1,768,768]{2,1,0:T(8,128)(2,1)} %refs_2_.2, ...), custom_call_target="tpu_custom_call" | custom-call | flops 6000000000 | tf_op jit(solution)/shard_map/pallas_call | solution.py:66
  76.2 5.8 %shard_map.198 = (bf16[2,320,768]{2,1,0:T(8,128)(2,1)}, f32[160,768]{1,0:T(8,128)}, bf16[160,768]{1,0:T(8,128)(2,1)}) custom-call(bf16[160,768]{1,0:T(8,128)(2,1)} %copy-done.10, bf16[160,768]{1,0:T(8,128)(2,1)} %copy-done.27, bf16[1,768,768]{2,1,0:T(8,128)(2,1)} %refs_2_.2, bf16[1,768,768]{2,1,0:T(8,128)(2,1)} %collective-permute-done.6.refs_3_, ...), custom_call_target="tpu_custom_call" | custom-call | flops 6000000000 | tf_op jit(solution)/shard_map/pallas_call | solution.py:66
  83.1 2.4 %collective-permute-start.23 = (bf16[40,768]{1,0:T(8,128)(2,1)S(1)}, bf16[40,768]{1,0:T(8,128)(2,1)S(1)}, u32[]{:S(2)}, u32[]{:S(2)}) collective-permute-start(bf16[40,768]{1,0:T(8,128)(2,1)S(1)} %get-tuple-element.229), channel_id=1, source_target_pairs={{0,24},{4,28},{8,16},{12,20},{16,8},{20,12},{24,0},{28,4},{1,25},{... | collective-permute-start | bytes 184328 | tf_op jit(solution)/shard_map/ppermute | solution.py:44
  85.6 2.0 %collective-permute-start.22 = (bf16[40,768]{1,0:T(8,128)(2,1)S(1)}, bf16[40,768]{1,0:T(8,128)(2,1)S(1)}, u32[]{:S(2)}, u32[]{:S(2)}) collective-permute-start(bf16[40,768]{1,0:T(8,128)(2,1)S(1)} %get-tuple-element.230), channel_id=1, source_target_pairs={{0,16},{4,20},{8,24},{12,28},{16,0},{20,4},{24,8},{28,12},{1,17},{... | collective-permute-start | bytes 184328 | tf_op jit(solution)/shard_map/ppermute | solution.py:44
  92.8 2.0 %collective-permute-start.26 = (bf16[40,768]{1,0:T(8,128)(2,1)S(1)}, bf16[40,768]{1,0:T(8,128)(2,1)S(1)}, u32[]{:S(2)}, u32[]{:S(2)}) collective-permute-start(bf16[40,768]{1,0:T(8,128)(2,1)S(1)} %get-tuple-element.228), channel_id=1, source_target_pairs={{0,16},{4,20},{8,24},{12,28},{16,0},{20,4},{24,8},{28,12},{1,17},{... | collective-permute-start | bytes 184328 | tf_op jit(solution)/shard_map/ppermute | solution.py:44
  100.8 4.7 %collective-permute-done.28 = bf16[80,1536]{1,0:T(8,128)(2,1)S(1)} collective-permute-done((bf16[80,1536]{1,0:T(8,128)(2,1)S(1)}, bf16[80,1536]{1,0:T(8,128)(2,1)S(1)}, u32[]{:S(2)}, u32[]{:S(2)}) %collective-permute-start.28) | collective-permute-done | bytes 245792 | tf_op jit(solution)/shard_map/ppermute | solution.py:44
  109.2 4.4 %shard_map.199 = (bf16[1,768,768]{2,1,0:T(8,128)(2,1)}, bf16[1,768,768]{2,1,0:T(8,128)(2,1)}) custom-call(bf16[160,768]{1,0:T(8,128)(2,1)} %copy-done.9, bf16[160,768]{1,0:T(8,128)(2,1)} %copy-done.26, bf16[160,768]{1,0:T(8,128)(2,1)} %copy-done.10, bf16[160,768]{1,0:T(8,128)(2,1)} %copy-done.27, bf16[2,320,768]{2,1,0:T(8,128)(2,1)} %get-tuple-element.157.hidden, ...), custom_call_target="tpu_custom_call" | custom-call | flops 4000000000 | tf_op jit(solution)/shard_map/pallas_call | solution.py:66
  116.8 8.8 %shard_map.200 = (bf16[2,5,24,640]{3,2,1,0:T(8,128)(2,1)}, bf16[2,5,24,640]{3,2,1,0:T(8,128)(2,1)}, bf16[2,5,24,640]{3,2,1,0:T(8,128)(2,1)}, bf16[2,5,24,640]{3,...) custom-call(bf16[512,576]{1,0:T(8,128)(2,1)} %get-tuple-element.148., ...), custom_call_target="tpu_custom_call" | custom-call | flops 8000000000 | tf_op jit(solution)/shard_map/pallas_call | solution.py:66
  129.3 5.8 %shard_map.201 = (f32[1,768,768]{2,1,0:T(8,128)}, f32[1,768,768]{2,1,0:T(8,128)}) custom-call(bf16[160,768]{1,0:T(8,128)(2,1)} %copy-done.9, bf16[160,768]{1,0:T(8,128)(2,1)} %copy-done.26, bf16[160,768]{1,0:T(8,128)(2,1)} %copy-done.10, bf16[160,768]{1,0:T(8,128)(2,1)} %copy-done.27, bf16[2,320,768]{2,1,0:T(8,128)(2,1)} %get-tuple-element.157.hidden, ...), custom_call_target="tpu_custom_call" | custom-call | flops 4000000000 | tf_op jit(solution)/shard_map/pallas_call | solution.py:66
  137.1 2.5 %collective-permute-start.37 = (bf16[5,24,640]{2,1,0:T(8,128)(2,1)S(1)}, bf16[5,24,640]{2,1,0:T(8,128)(2,1)S(1)}, u32[]{:S(2)}, u32[]{:S(2)}) collective-permute-start(bf16[5,24,640]{2,1,0:T(8,128)(2,1)S(1)} %get-tuple-element.221), channel_id=1, source_target_pairs={{0,24},{4,28},{8,16},{12,20},{16,8},{20,12},{24,0},{28,4},{1,25},{... | collective-permute-start | bytes 460808 | tf_op jit(solution)/shard_map/ppermute | solution.py:44
  139.8 4.6 %collective-permute-done.35 = bf16[2,5,24,640]{3,2,1,0:T(8,128)(2,1)S(1)} collective-permute-done((bf16[2,5,24,640]{3,2,1,0:T(8,128)(2,1)S(1)}, bf16[2,5,24,640]{3,2,1,0:T(8,128)(2,1)S(1)}, u32[]{:S(2)}, u32[]{:S(2)}) %collective-permute-start.35) | collective-permute-done | bytes 307232 | tf_op jit(solution)/shard_map/ppermute | solution.py:44
  147.7 5.2 %collective-permute-done.36 = bf16[5,24,640]{2,1,0:T(8,128)(2,1)S(1)} collective-permute-done((bf16[5,24,640]{2,1,0:T(8,128)(2,1)S(1)}, bf16[5,24,640]{2,1,0:T(8,128)(2,1)S(1)}, u32[]{:S(2)}, u32[]{:S(2)}) %collective-permute-start.36) | collective-permute-done | bytes 153632 | tf_op jit(solution)/shard_map/ppermute | solution.py:44
  153.2 3.5 %collective-permute-done.40 = bf16[128,768]{1,0:T(8,128)(2,1)S(1)} collective-permute-done((bf16[128,768]{1,0:T(8,128)(2,1)S(1)}, bf16[128,768]{1,0:T(8,128)(2,1)S(1)}, u32[]{:S(2)}, u32[]{:S(2)}) %collective-permute-start.40) | collective-permute-done | bytes 196640 | tf_op jit(solution)/shard_map/ppermute | solution.py:44
  160.0 2.2 %collective-permute-done.43 = bf16[24,640]{1,0:T(8,128)(2,1)S(1)} collective-permute-done((bf16[24,640]{1,0:T(8,128)(2,1)S(1)}, bf16[24,640]{1,0:T(8,128)(2,1)S(1)}, u32[]{:S(2)}, u32[]{:S(2)}) %collective-permute-start.43) | collective-permute-done | bytes 30752 | tf_op jit(solution)/shard_map/ppermute | solution.py:44
  166.3 3.9 %collective-permute-done.45.refs_2_ = bf16[5,24,640]{2,1,0:T(8,128)(2,1)S(1)} collective-permute-done((bf16[5,24,640]{2,1,0:T(8,128)(2,1)S(1)}, bf16[5,24,640]{2,1,0:T(8,128)(2,1)S(1)}, u32[]{:S(2)}, u32[]{:S(2)}) %collective-permute-start.45) | collective-permute-done | bytes 153632 | tf_op jit(solution)/shard_map/ppermute | solution.py:44
  170.2 2.4 %collective-permute-start.48 = (bf16[5,24,640]{2,1,0:T(8,128)(2,1)S(1)}, bf16[5,24,640]{2,1,0:T(8,128)(2,1)S(1)}, u32[]{:S(2)}, u32[]{:S(2)}) collective-permute-start(bf16[5,24,640]{2,1,0:T(8,128)(2,1)S(1)} %collective-permute-done.45.refs_2_), channel_id=1, source_target_pairs={{0,4},{4,0},{8,12},{12,8},{16,20},{20,16},{24,28},{28,24},{1,5},{5... | collective-permute-start | bytes 460808 | tf_op jit(solution)/shard_map/ppermute | solution.py:44
  172.7 2.3 %collective-permute-done.47.refs_4_ = bf16[5,24,640]{2,1,0:T(8,128)(2,1)S(1)} collective-permute-done((bf16[5,24,640]{2,1,0:T(8,128)(2,1)S(1)}, bf16[5,24,640]{2,1,0:T(8,128)(2,1)S(1)}, u32[]{:S(2)}, u32[]{:S(2)}) %collective-permute-start.47) | collective-permute-done | bytes 153632 | tf_op jit(solution)/shard_map/ppermute | solution.py:44
  177.9 3.2 %collective-permute-done.50.refs_6_ = bf16[5,24,640]{2,1,0:T(8,128)(2,1)S(1)} collective-permute-done((bf16[5,24,640]{2,1,0:T(8,128)(2,1)S(1)}, bf16[5,24,640]{2,1,0:T(8,128)(2,1)S(1)}, u32[]{:S(2)}, u32[]{:S(2)}) %collective-permute-start.50) | collective-permute-done | bytes 153632 | tf_op jit(solution)/shard_map/ppermute | solution.py:44
  181.1 2.0 %collective-permute-start.51 = (bf16[5,24,640]{2,1,0:T(8,128)(2,1)S(1)}, bf16[5,24,640]{2,1,0:T(8,128)(2,1)S(1)}, u32[]{:S(2)}, u32[]{:S(2)}) collective-permute-start(bf16[5,24,640]{2,1,0:T(8,128)(2,1)S(1)} %collective-permute-done.50.refs_6_), channel_id=1, source_target_pairs={{0,4},{4,0},{8,12},{12,8},{16,20},{20,16},{24,28},{28,24},{1,5},{5... | collective-permute-start | bytes 460808 | tf_op jit(solution)/shard_map/ppermute | solution.py:44
  184.0 2.3 %collective-permute-done.51.refs_7_ = bf16[5,24,640]{2,1,0:T(8,128)(2,1)S(1)} collective-permute-done((bf16[5,24,640]{2,1,0:T(8,128)(2,1)S(1)}, bf16[5,24,640]{2,1,0:T(8,128)(2,1)S(1)}, u32[]{:S(2)}, u32[]{:S(2)}) %collective-permute-start.51) | collective-permute-done | bytes 153632 | tf_op jit(solution)/shard_map/ppermute | solution.py:44
  187.0 3.2 %shard_map.202 = (f32[192,2304]{1,0:T(8,128)}, f32[192,768]{1,0:T(8,128)}, f32[1,192]{1,0:T(1,128)}, f32[1,192]{1,0:T(1,128)}, f32[8,192]{1,0:T(8,128)}) custom-call(bf16[5,24,640]{2,1,0:T(8,128)(2,1)} %copy-done.11, bf16[5,24,640]{2,1,0:T(8,128)(2,1)} %copy-done.14, bf16[5,24,640]{2,1,0:T(8,128)(2,1)} %copy-done.13, bf16[5,24,640]{2,1,0:T(8,128)(2,1)} %copy-done.16, ...), custom_call_target="tpu_custom_call" | custom-call | tf_op jit(solution)/shard_map/pallas_call | solution.py:66
  (229 shorter events, 63.5 us)
Async XLA Ops:
  0.7 10.5 %collective-permute-start = (bf16[128,768]{1,0:T(8,128)(2,1)}, bf16[128,768]{1,0:T(8,128)(2,1)S(1)}, u32[]{:S(2)}, u32[]{:S(2)}) collective-permute-start(bf16[128,768]{1,0:T(8,128)(2,1)} %refs_2_), channel_id=1, source_target_pairs={{0,2},{1,3},{2,0},{3,1},{4,6},{5,7},{6,4},{7,5},{8,10},{9,11},{10,... | collective-permute-start | bytes 589832 | tf_op jit(solution)/shard_map/ppermute | solution.py:44
  3.7 8.3 %collective-permute-start.1 = (bf16[128,768]{1,0:T(8,128)(2,1)}, bf16[128,768]{1,0:T(8,128)(2,1)S(1)}, u32[]{:S(2)}, u32[]{:S(2)}) collective-permute-start(bf16[128,768]{1,0:T(8,128)(2,1)} %refs_2_), channel_id=1, source_target_pairs={{0,1},{1,0},{2,3},{3,2},{4,5},{5,4},{6,7},{7,6},{8,9},{9,8},{10,11... | collective-permute-start | bytes 589832 | tf_op jit(solution)/shard_map/ppermute | solution.py:44
  8.6 9.0 %collective-permute-start.4 = (bf16[192,640]{1,0:T(8,128)(2,1)}, bf16[192,640]{1,0:T(8,128)(2,1)S(1)}, u32[]{:S(2)}, u32[]{:S(2)}) collective-permute-start(bf16[192,640]{1,0:T(8,128)(2,1)} %get-tuple-element.113), channel_id=1, source_target_pairs={{0,2},{1,3},{2,0},{3,1},{4,6},{5,7},{6,4},{7,5},{8,10},{9,11},{10,... | collective-permute-start | bytes 737288 | tf_op jit(solution)/shard_map/ppermute | solution.py:44
  8.7 12.3 %collective-permute-start.5 = (bf16[192,640]{1,0:T(8,128)(2,1)}, bf16[192,640]{1,0:T(8,128)(2,1)S(1)}, u32[]{:S(2)}, u32[]{:S(2)}) collective-permute-start(bf16[192,640]{1,0:T(8,128)(2,1)} %get-tuple-element.114), channel_id=1, source_target_pairs={{0,3},{1,2},{2,1},{3,0},{4,7},{5,6},{6,5},{7,4},{8,11},{9,10},{10,... | collective-permute-start | bytes 737288 | tf_op jit(solution)/shard_map/ppermute | solution.py:44
  11.2 19.7 %collective-permute-start.6 = (bf16[1,768,768]{2,1,0:T(8,128)(2,1)}, bf16[1,768,768]{2,1,0:T(8,128)(2,1)}, u32[]{:S(2)}, u32[]{:S(2)}) collective-permute-start(bf16[1,768,768]{2,1,0:T(8,128)(2,1)} %refs_2_.2), channel_id=1, source_target_pairs={{0,1},{1,0},{2,3},{3,2},{4,5},{5,4},{6,7},{7,6},{8,9},{9,8},{10,11... | collective-permute-start | bytes 3538952 | tf_op jit(solution)/shard_map/ppermute | solution.py:44
  12.0 19.0 %collective-permute-start.7 = (bf16[1,768,768]{2,1,0:T(8,128)(2,1)}, bf16[1,768,768]{2,1,0:T(8,128)(2,1)}, u32[]{:S(2)}, u32[]{:S(2)}) collective-permute-start(bf16[1,768,768]{2,1,0:T(8,128)(2,1)} %refs_4_.1), channel_id=1, source_target_pairs={{0,1},{1,0},{2,3},{3,2},{4,5},{5,4},{6,7},{7,6},{8,9},{9,8},{10,11... | collective-permute-start | bytes 3538952 | tf_op jit(solution)/shard_map/ppermute | solution.py:44
  13.0 8.0 %collective-permute-start.2 = (bf16[128,768]{1,0:T(8,128)(2,1)S(1)}, bf16[128,768]{1,0:T(8,128)(2,1)S(1)}, u32[]{:S(2)}, u32[]{:S(2)}) collective-permute-start(bf16[128,768]{1,0:T(8,128)(2,1)S(1)} %collective-permute-done.refs_4_), channel_id=1, source_target_pairs={{0,1},{1,0},{2,3},{3,2},{4,5},{5,4},{6,7},{7,6},{8,9},{9,8},{10,11... | collective-permute-start | bytes 589832 | tf_op jit(solution)/shard_map/ppermute | solution.py:44
  21.0 10.0 %collective-permute-start.8 = (bf16[192,768]{1,0:T(8,128)(2,1)}, bf16[192,768]{1,0:T(8,128)(2,1)S(1)}, u32[]{:S(2)}, u32[]{:S(2)}) collective-permute-start(bf16[192,768]{1,0:T(8,128)(2,1)} %refs_6_), channel_id=1, source_target_pairs={{0,2},{1,3},{2,0},{3,1},{4,6},{5,7},{6,4},{7,5},{8,10},{9,11},{10,... | collective-permute-start | bytes 884744 | tf_op jit(solution)/shard_map/ppermute | solution.py:44
  21.6 9.3 %collective-permute-start.9 = (bf16[192,768]{1,0:T(8,128)(2,1)}, bf16[192,768]{1,0:T(8,128)(2,1)S(1)}, u32[]{:S(2)}, u32[]{:S(2)}) collective-permute-start(bf16[192,768]{1,0:T(8,128)(2,1)} %refs_6_), channel_id=1, source_target_pairs={{0,1},{1,0},{2,3},{3,2},{4,5},{5,4},{6,7},{7,6},{8,9},{9,8},{10,11... | collective-permute-start | bytes 884744 | tf_op jit(solution)/shard_map/ppermute | solution.py:44
  38.4 8.1 %collective-permute-start.14 = (bf16[80,1536]{1,0:T(8,128)(2,1)S(1)}, bf16[80,1536]{1,0:T(8,128)(2,1)S(1)}, u32[]{:S(2)}, u32[]{:S(2)}) collective-permute-start(bf16[80,1536]{1,0:T(8,128)(2,1)S(1)} %convolution_convert_fusion), channel_id=1, source_target_pairs={{0,4},{4,0},{8,12},{12,8},{16,20},{20,16},{24,28},{28,24},{1,5},{5... | collective-permute-start | bytes 737288 | tf_op jit(solution)/shard_map/ppermute | solution.py:44
  46.7 8.2 %collective-permute-start.17 = (bf16[40,1536]{1,0:T(8,128)(2,1)S(1)}, bf16[40,1536]{1,0:T(8,128)(2,1)S(1)}, u32[]{:S(2)}, u32[]{:S(2)}) collective-permute-start(bf16[40,1536]{1,0:T(8,128)(2,1)S(1)} %get-tuple-element.218), channel_id=1, source_target_pairs={{0,24},{4,28},{8,16},{12,20},{16,8},{20,12},{24,0},{28,4},{1,25},{... | collective-permute-start | bytes 368648 | tf_op jit(solution)/shard_map/ppermute | solution.py:44
  50.6 9.8 %collective-permute-start.16 = (bf16[40,1536]{1,0:T(8,128)(2,1)S(1)}, bf16[40,1536]{1,0:T(8,128)(2,1)S(1)}, u32[]{:S(2)}, u32[]{:S(2)}) collective-permute-start(bf16[40,1536]{1,0:T(8,128)(2,1)S(1)} %get-tuple-element.219), channel_id=1, source_target_pairs={{0,16},{4,20},{8,24},{12,28},{16,0},{20,4},{24,8},{28,12},{1,17},{... | collective-permute-start | bytes 368648 | tf_op jit(solution)/shard_map/ppermute | solution.py:44
  50.6 9.8 %collective-permute-start.15 = (bf16[40,1536]{1,0:T(8,128)(2,1)S(1)}, bf16[40,1536]{1,0:T(8,128)(2,1)S(1)}, u32[]{:S(2)}, u32[]{:S(2)}) collective-permute-start(bf16[40,1536]{1,0:T(8,128)(2,1)S(1)} %get-tuple-element.217), channel_id=1, source_target_pairs={{0,8},{4,12},{8,0},{12,4},{16,24},{20,28},{24,16},{28,20},{1,9},{5... | collective-permute-start | bytes 368648 | tf_op jit(solution)/shard_map/ppermute | solution.py:44
  60.5 7.0 %collective-permute-start.18 = (bf16[160,768]{1,0:T(8,128)(2,1)S(1)}, bf16[160,768]{1,0:T(8,128)(2,1)S(1)}, u32[]{:S(2)}, u32[]{:S(2)}) collective-permute-start(bf16[160,768]{1,0:T(8,128)(2,1)S(1)} %pad_maximum_fusion.3.refs_0_.own), channel_id=1, source_target_pairs={{0,2},{1,3},{2,0},{3,1},{4,6},{5,7},{6,4},{7,5},{8,10},{9,11},{10,... | collective-permute-start | bytes 737288 | tf_op jit(solution)/shard_map/ppermute | solution.py:44
  67.5 8.0 %collective-permute-start.20 = (bf16[160,768]{1,0:T(8,128)(2,1)S(1)}, bf16[160,768]{1,0:T(8,128)(2,1)S(1)}, u32[]{:S(2)}, u32[]{:S(2)}) collective-permute-start(bf16[160,768]{1,0:T(8,128)(2,1)S(1)} %pad_maximum_fusion.4.refs_0_.own_grad), channel_id=1, source_target_pairs={{0,2},{1,3},{2,0},{3,1},{4,6},{5,7},{6,4},{7,5},{8,10},{9,11},{10,... | collective-permute-start | bytes 737288 | tf_op jit(solution)/shard_map/ppermute | solution.py:44
  74.5 8.5 %collective-permute-start.19 = (bf16[160,768]{1,0:T(8,128)(2,1)}, bf16[160,768]{1,0:T(8,128)(2,1)S(1)}, u32[]{:S(2)}, u32[]{:S(2)}) collective-permute-start(bf16[160,768]{1,0:T(8,128)(2,1)} %get-tuple-element.141), channel_id=1, source_target_pairs={{0,2},{1,3},{2,0},{3,1},{4,6},{5,7},{6,4},{7,5},{8,10},{9,11},{10,... | collective-permute-start | bytes 737288 | tf_op jit(solution)/shard_map/ppermute | solution.py:44
  82.0 8.9 %collective-permute-start.24 = (bf16[160,768]{1,0:T(8,128)(2,1)}, bf16[160,768]{1,0:T(8,128)(2,1)S(1)}, u32[]{:S(2)}, u32[]{:S(2)}) collective-permute-start(bf16[160,768]{1,0:T(8,128)(2,1)} %get-tuple-element.144), channel_id=1, source_target_pairs={{0,2},{1,3},{2,0},{3,1},{4,6},{5,7},{6,4},{7,5},{8,10},{9,11},{10,... | collective-permute-start | bytes 737288 | tf_op jit(solution)/shard_map/ppermute | solution.py:44
  108.0 6.6 %collective-permute-start.29 = (bf16[128,768]{1,0:T(8,128)(2,1)S(1)}, bf16[128,768]{1,0:T(8,128)(2,1)S(1)}, u32[]{:S(2)}, u32[]{:S(2)}) collective-permute-start(bf16[128,768]{1,0:T(8,128)(2,1)S(1)} %fusion.68.refs_9_), channel_id=1, source_target_pairs={{0,2},{1,3},{2,0},{3,1},{4,6},{5,7},{6,4},{7,5},{8,10},{9,11},{10,... | collective-permute-start | bytes 589832 | tf_op jit(solution)/shard_map/ppermute | solution.py:44
  108.6 6.5 %collective-permute-start.30 = (bf16[128,768]{1,0:T(8,128)(2,1)S(1)}, bf16[128,768]{1,0:T(8,128)(2,1)S(1)}, u32[]{:S(2)}, u32[]{:S(2)}) collective-permute-start(bf16[128,768]{1,0:T(8,128)(2,1)S(1)} %fusion.68.refs_9_), channel_id=1, source_target_pairs={{0,1},{1,0},{2,3},{3,2},{4,5},{5,4},{6,7},{7,6},{8,9},{9,8},{10,11... | collective-permute-start | bytes 589832 | tf_op jit(solution)/shard_map/ppermute | solution.py:44
  116.1 11.1 %collective-permute-start.33 = (bf16[1,768,768]{2,1,0:T(8,128)(2,1)}, bf16[1,768,768]{2,1,0:T(8,128)(2,1)S(1)}, u32[]{:S(2)}, u32[]{:S(2)}) collective-permute-start(bf16[1,768,768]{2,1,0:T(8,128)(2,1)} %get-tuple-element.179), channel_id=1, source_target_pairs={{0,1},{1,0},{2,3},{3,2},{4,5},{5,4},{6,7},{7,6},{8,9},{9,8},{10,11... | collective-permute-start | bytes 3538952 | tf_op jit(solution)/shard_map/ppermute | solution.py:44
  116.5 10.7 %collective-permute-start.34 = (bf16[1,768,768]{2,1,0:T(8,128)(2,1)}, bf16[1,768,768]{2,1,0:T(8,128)(2,1)S(1)}, u32[]{:S(2)}, u32[]{:S(2)}) collective-permute-start(bf16[1,768,768]{2,1,0:T(8,128)(2,1)} %get-tuple-element.180), channel_id=1, source_target_pairs={{0,1},{1,0},{2,3},{3,2},{4,5},{5,4},{6,7},{7,6},{8,9},{9,8},{10,11... | collective-permute-start | bytes 3538952 | tf_op jit(solution)/shard_map/ppermute | solution.py:44
  125.6 9.8 %collective-permute-start.32 = (bf16[2,5,24,640]{3,2,1,0:T(8,128)(2,1)}, bf16[2,5,24,640]{3,2,1,0:T(8,128)(2,1)S(1)}, u32[]{:S(2)}, u32[]{:S(2)}) collective-permute-start(bf16[2,5,24,640]{3,2,1,0:T(8,128)(2,1)} %get-tuple-element.171), channel_id=1, source_target_pairs={{0,4},{4,0},{8,12},{12,8},{16,20},{20,16},{24,28},{28,24},{1,5},{5... | collective-permute-start | bytes 921608 | tf_op jit(solution)/shard_map/ppermute | solution.py:44
  135.5 9.0 %collective-permute-start.35 = (bf16[2,5,24,640]{3,2,1,0:T(8,128)(2,1)S(1)}, bf16[2,5,24,640]{3,2,1,0:T(8,128)(2,1)S(1)}, u32[]{:S(2)}, u32[]{:S(2)}) collective-permute-start(bf16[2,5,24,640]{3,2,1,0:T(8,128)(2,1)S(1)} %copy-done.25), channel_id=1, source_target_pairs={{0,4},{4,0},{8,12},{12,8},{16,20},{20,16},{24,28},{28,24},{1,5},{5... | collective-permute-start | bytes 921608 | tf_op jit(solution)/shard_map/ppermute | solution.py:44
  137.1 9.8 %collective-permute-start.37 = (bf16[5,24,640]{2,1,0:T(8,128)(2,1)S(1)}, bf16[5,24,640]{2,1,0:T(8,128)(2,1)S(1)}, u32[]{:S(2)}, u32[]{:S(2)}) collective-permute-start(bf16[5,24,640]{2,1,0:T(8,128)(2,1)S(1)} %get-tuple-element.221), channel_id=1, source_target_pairs={{0,24},{4,28},{8,16},{12,20},{16,8},{20,12},{24,0},{28,4},{1,25},{... | collective-permute-start | bytes 460808 | tf_op jit(solution)/shard_map/ppermute | solution.py:44
  139.6 13.3 %collective-permute-start.36 = (bf16[5,24,640]{2,1,0:T(8,128)(2,1)S(1)}, bf16[5,24,640]{2,1,0:T(8,128)(2,1)S(1)}, u32[]{:S(2)}, u32[]{:S(2)}) collective-permute-start(bf16[5,24,640]{2,1,0:T(8,128)(2,1)S(1)} %get-tuple-element.220), channel_id=1, source_target_pairs={{0,16},{4,20},{8,24},{12,28},{16,0},{20,4},{24,8},{28,12},{1,17},{... | collective-permute-start | bytes 460808 | tf_op jit(solution)/shard_map/ppermute | solution.py:44
  144.5 8.6 %collective-permute-start.38 = (bf16[5,24,640]{2,1,0:T(8,128)(2,1)S(1)}, bf16[5,24,640]{2,1,0:T(8,128)(2,1)S(1)}, u32[]{:S(2)}, u32[]{:S(2)}) collective-permute-start(bf16[5,24,640]{2,1,0:T(8,128)(2,1)S(1)} %fusion.38), channel_id=1, source_target_pairs={{0,8},{4,12},{8,0},{12,4},{16,24},{20,28},{24,16},{28,20},{1,9},{5... | collective-permute-start | bytes 460808 | tf_op jit(solution)/shard_map/ppermute | solution.py:44
  145.8 7.4 %collective-permute-start.41 = (bf16[128,768]{1,0:T(8,128)(2,1)}, bf16[128,768]{1,0:T(8,128)(2,1)S(1)}, u32[]{:S(2)}, u32[]{:S(2)}) collective-permute-start(bf16[128,768]{1,0:T(8,128)(2,1)} %get-tuple-element.194), channel_id=1, source_target_pairs={{0,3},{1,2},{2,1},{3,0},{4,7},{5,6},{6,5},{7,4},{8,11},{9,10},{10,... | collective-permute-start | bytes 589832 | tf_op jit(solution)/shard_map/ppermute | solution.py:44
  145.9 10.8 %collective-permute-start.40 = (bf16[128,768]{1,0:T(8,128)(2,1)S(1)}, bf16[128,768]{1,0:T(8,128)(2,1)S(1)}, u32[]{:S(2)}, u32[]{:S(2)}) collective-permute-start(bf16[128,768]{1,0:T(8,128)(2,1)S(1)} %copy-done.32), channel_id=1, source_target_pairs={{0,2},{1,3},{2,0},{3,1},{4,6},{5,7},{6,4},{7,5},{8,10},{9,11},{10,... | collective-permute-start | bytes 589832 | tf_op jit(solution)/shard_map/ppermute | solution.py:44
  146.9 9.7 %collective-permute-start.39 = (bf16[128,768]{1,0:T(8,128)(2,1)S(1)}, bf16[128,768]{1,0:T(8,128)(2,1)S(1)}, u32[]{:S(2)}, u32[]{:S(2)}) collective-permute-start(bf16[128,768]{1,0:T(8,128)(2,1)S(1)} %copy-done.31), channel_id=1, source_target_pairs={{0,1},{1,0},{2,3},{3,2},{4,5},{5,4},{6,7},{7,6},{8,9},{9,8},{10,11... | collective-permute-start | bytes 589832 | tf_op jit(solution)/shard_map/ppermute | solution.py:44
  162.7 7.5 %collective-permute-start.45 = (bf16[5,24,640]{2,1,0:T(8,128)(2,1)S(1)}, bf16[5,24,640]{2,1,0:T(8,128)(2,1)S(1)}, u32[]{:S(2)}, u32[]{:S(2)}) collective-permute-start(bf16[5,24,640]{2,1,0:T(8,128)(2,1)S(1)} %slice_dynamic-update-slice_fusion.refs_0_), channel_id=1, source_target_pairs={{0,8},{4,12},{8,0},{12,4},{16,24},{20,28},{24,16},{28,20},{1,9},{5... | collective-permute-start | bytes 460808 | tf_op jit(solution)/shard_map/ppermute | solution.py:44
  165.3 9.7 %collective-permute-start.47 = (bf16[5,24,640]{2,1,0:T(8,128)(2,1)S(1)}, bf16[5,24,640]{2,1,0:T(8,128)(2,1)S(1)}, u32[]{:S(2)}, u32[]{:S(2)}) collective-permute-start(bf16[5,24,640]{2,1,0:T(8,128)(2,1)S(1)} %slice_dynamic-update-slice_fusion.refs_0_), channel_id=1, source_target_pairs={{0,16},{4,20},{8,24},{12,28},{16,0},{20,4},{24,8},{28,12},{1,17},{... | collective-permute-start | bytes 460808 | tf_op jit(solution)/shard_map/ppermute | solution.py:44
  176.1 7.9 %collective-permute-start.49 = (bf16[5,24,640]{2,1,0:T(8,128)(2,1)S(1)}, bf16[5,24,640]{2,1,0:T(8,128)(2,1)S(1)}, u32[]{:S(2)}, u32[]{:S(2)}) collective-permute-start(bf16[5,24,640]{2,1,0:T(8,128)(2,1)S(1)} %collective-permute-done.47.refs_4_), channel_id=1, source_target_pairs={{0,4},{4,0},{8,12},{12,8},{16,20},{20,16},{24,28},{28,24},{1,5},{5... | collective-permute-start | bytes 460808 | tf_op jit(solution)/shard_map/ppermute | solution.py:44
  (59 other events, 393.8 us)

commit v7 on v6

--- a/solution.py
+++ b/solution.py
@@ -92,11 +92,13 @@
     return jnp.sum(jnp.where(diagonal(size), column, 0.0), axis=0, keepdims=True)
 
 
-def prepare_weight(n, part, weight, gains, *outs):
+def prepare_weight(n, part, weight, gain_one, gain_two, *outs):
     wide = 3 * part
     s = lax.axis_index("shard")
     extra = outs[0].shape[1] - wide
-    one, two = (to_column(gains[i : i + 1, :].astype(f32), part) for i in range(2))
+    one, two = (
+        to_column(gain[...].astype(f32).reshape(1, part), part) for gain in (gain_one, gain_two)
+    )
     lane = lax.broadcasted_iota(jnp.int32, (part, extra), 1)
     beside = jnp.where(lane == 0, one, jnp.where(lane == 1, two, 0.0)).astype(bf16)
     for p in range(n):
@@ -204,10 +206,10 @@
     at = 9 + n
     shares = 4 if m > 1 else 2
     share_out = refs[at : at + shares]
-    normed_grad_out = refs[at + shares : at + shares + n]
-    gain_out, table_out = refs[at + shares + n : at + shares + n + 2]
+    normed_grad_out = refs[at + shares : at + shares + 2]
+    gain_out, table_out = refs[at + shares + 2 : at + shares + 4]
     branch_scr, scores_scr, projected_scr, total_scr, out_scr, normed_scr, send_scr, weights_scr = (
-        refs[at + shares + n + 2 :]
+        refs[at + shares + 4 :]
     )
     s = lax.axis_index("shard")
     e = lax.axis_index("expert")
@@ -276,7 +278,7 @@
     normed_grad = dot_nt(grad_projected, weight[:, :wide])
     send_scr[...] = normed_grad.astype(bf16).reshape(n, rows, width)
     for p in range(n):
-        normed_grad_out[p][...] = send_scr[s ^ p]
+        normed_grad_out[p & 1][p >> 1] = send_scr[s ^ p]
     gain = gains[...]
     grad_gain = jnp.zeros((1, width), f32)
     for j in range(n):
@@ -462,7 +464,7 @@
         call(
             lambda *refs: prepare_weight(n, part, *refs),
             [shape((part, full))] * n,
-            (attention_in, jnp.stack([first_gain, second_gain])),
+            (attention_in, first_gain, second_gain),
         ),
         "shard",
     )
@@ -495,8 +497,8 @@
         work=10 * micro,
     )
     tokens_all, weight, projected, weights, gain_one, gain_two, mixed = answers[:7]
-    mixed_mine, pair_up, pair_down, far_out, pair_out = lax.optimization_barrier(
-        (list(answers[7:]), pair_up, pair_down, far_out, pair_out)
+    mixed_mine, pair_up, pair_down, pair_out = lax.optimization_barrier(
+        (list(answers[7:]), pair_up, pair_down, pair_out)
     )
     mixed_blocks = exchange_relative(mixed_mine, "shard")
     out_blocks = [own_out, pair_out, far_out, swap(far_out, "shard", pair)]
@@ -541,30 +543,33 @@
         came = swap(dot_tn(collect[:, half:], value).astype(bf16), "expert", 1)
         own = dot_tn(collect[:, :half], value).astype(bf16).reshape(m // 2, capacity, 2 * width)
         both = jnp.concatenate([own, came.reshape(m // 2, capacity, 2 * width)], axis=1)
-        blocks = [both[d] if d == 0 else swap(both[d], "expert", 2 * d) for d in range(m // 2)]
-        return [
-            jnp.concatenate([block[:, i * width : (i + 1) * width] for block in blocks], axis=0)
-            for i in range(2)
-        ]
-
-    def among_pairs(value):
-        both = value.reshape(m // 2, 2 * capacity, width)
+        first = among_pairs(both[:, :, :width])
+        second, first[-1] = lax.optimization_barrier((both[:, :, width:], first[-1]))
+        return [jnp.concatenate(x, axis=0) for x in (first, among_pairs(second))]
+
+    def among_pairs(both):
         return [both[d] if d == 0 else swap(both[d], "expert", 2 * d) for d in range(m // 2)]
 
-    def give_back(forward, backward):
+    def give_back(forward, backward, late, work):
         if not direct:
-            return [dot(collect, plain(x)) for x in (forward, backward)]
+            return [dot(collect, plain(x)) for x in (forward, backward)] + [work(late)]
+        forward, backward = (
+            x.reshape(m // 2, 2 * capacity, width) for x in (forward, backward)
+        )
         blocks = [among_pairs(forward)]
-        backward, _ = lax.optimization_barrier((backward, blocks[0]))
+        backward, blocks[0][-1] = lax.optimization_barrier((backward, blocks[0][-1]))
         blocks.append(among_pairs(backward))
+        late, blocks = lax.optimization_barrier((late, blocks))
         own, other = (
             jnp.concatenate(
                 [jnp.concatenate([x[at : at + capacity] for x in side]) for side in blocks], axis=1
             )
             for at in (0, capacity)
         )
-        total = dot(collect[:, :half], own) + dot(collect[:, half:], swap(other, "expert", 1))
-        return total[:, :width], total[:, width:]
+        beside = work(late)
+        other, beside = lax.optimization_barrier((swap(other, "expert", 1), beside))
+        total = dot(collect[:, :half], own) + dot(collect[:, half:], other)
+        return total[:, :width], total[:, width:], beside
 
     def reduce_shard(keep, out, after=None):
         came = swap(out, "shard", 2 * pair)
@@ -574,7 +579,6 @@
 
     arrived, arrived_grad = dispatch(normed_two.astype(bf16), grad_result)
     came = swap(arrived, "shard", 2 * pair)
-    came, arrived_grad = lax.optimization_barrier((came, arrived_grad))
     row_blocks = (arrived, came)
     grad_blocks = (arrived_grad, swap(arrived_grad, "shard", 2 * pair))
 
@@ -594,8 +598,17 @@
         (*grad_blocks, *expert_weight, slope),
         work=6 * micro,
     )
-    expert_result, grad_sent = give_back(
-        reduce_shard(*forward, backward[1]), reduce_shard(*backward)
+    sources = (*grad_blocks, hidden, grad_before)
+    expert_result, grad_sent, (up_send, down_send) = give_back(
+        reduce_shard(*forward, backward[1]),
+        reduce_shard(*backward),
+        row_blocks,
+        lambda rows_late: call(
+            weights_to_send,
+            (shape(expert_in.shape), shape(expert_out.shape)),
+            (*rows_late, *sources),
+            work=4 * micro,
+        ),
     )
 
     layer_out = (hidden_one + gate[:, None] * expert_result).astype(bf16)
@@ -617,17 +630,10 @@
     )
     grad_middle, grad_gain_two = rms_backward(hidden_one, factor_two, gain_two, grad_normed_two)
     grad_hidden = upstream + grad_middle
-    branch, late_rows = lax.optimization_barrier((grad_hidden.astype(bf16), row_blocks))
-    sources = (*grad_blocks, hidden, grad_before)
-    up_send, down_send = call(
-        weights_to_send,
-        (shape(expert_in.shape), shape(expert_out.shape)),
-        (*late_rows, *sources),
-        work=4 * micro,
-    )
+    branch = grad_hidden.astype(bf16)
     far_branch, pair_branch = swap(branch, "shard", 2 * pair), swap(branch, "shard", pair)
-    far_branch, grad_router, gain_two_row, up_send, down_send = lax.optimization_barrier(
-        (far_branch, grad_router, grad_gain_two, up_send, down_send)
+    far_branch, grad_router, gain_two_row = lax.optimization_barrier(
+        (far_branch, grad_router, grad_gain_two)
     )
     branch_blocks = [branch, pair_branch, far_branch, swap(far_branch, "shard", pair)]
     branch_blocks, up_send, down_send = lax.optimization_barrier(
@@ -644,7 +650,7 @@
         lambda *refs: attention_backward(n, holders, rows, width, heads, buckets, experts, *refs),
         (
             *share_shapes,
-            *[shape((rows, width))] * n,
+            *[shape((n // 2, rows, width))] * 2,
             shape((row_tile, width), f32),
             shape((row_tile, 128), f32),
         ),
@@ -674,37 +680,38 @@
         work=8 * micro,
     )
     shares = answers[: len(share_shapes)]
-    normed_grads = answers[len(share_shapes) : len(share_shapes) + n]
-    gain_row, table = answers[len(share_shapes) + n :]
-    late_rows, normed_grads = lax.optimization_barrier((row_blocks, list(normed_grads)))
-    grad_up, grad_down = call(
-        weights_to_keep,
-        (shape(expert_in.shape, f32), shape(expert_out.shape, f32)),
-        (*late_rows, *sources, up_came, down_came),
-        work=4 * micro,
-    )
+    normed_keep, normed_send, gain_row, table = answers[len(share_shapes) :]
+
+    def kept_weights(late_rows):
+        return call(
+            weights_to_keep,
+            (shape(expert_in.shape, f32), shape(expert_out.shape, f32)),
+            (*late_rows, *sources, up_came, down_came),
+            work=4 * micro,
+        )
+
     per_line = buckets // row_tile
 
     def biases(block):
         return block.reshape(row_tile, heads, per_line).swapaxes(0, 1).reshape(heads, buckets)
 
-    def finish_tokens(blocks):
-        grad_normed = sum(x.astype(f32) for x in exchange_relative(list(blocks), "shard"))
-        grad_input_norm, _ = rms_backward(inputs, rms_factor(inputs), gain_one, grad_normed)
-        return (grad_hidden + grad_input_norm).astype(bf16)
-
+    normed_sum = normed_keep.astype(f32) + swap(normed_send, "shard", pair).astype(f32)
+    far_sum = swap(normed_sum[1].astype(bf16), "shard", 2 * pair)
+    late, far_sum = lax.optimization_barrier((tokens, far_sum))
+    late = late.astype(f32)
+    grad_input_norm, _ = rms_backward(
+        late, rms_factor(late), gain_one, normed_sum[0] + far_sum.astype(f32)
+    )
+    grad_tokens = (grad_hidden + grad_input_norm).astype(bf16)
     if direct:
         far_keep, far_send, near_keep, near_send = shares
         far_came = swap(far_send, "expert", 1)
-        far_came, near_send, grad_up, grad_down = lax.optimization_barrier(
-            (far_came, near_send, grad_up, grad_down)
-        )
+        far_came, near_send, late_rows = lax.optimization_barrier((far_came, near_send, row_blocks))
         far = far_keep.astype(f32) + far_came.astype(f32)
-        near_came, normed_grads = lax.optimization_barrier(
-            (swap(near_send, "expert", 1), normed_grads)
+        near_came, (grad_up, grad_down) = lax.optimization_barrier(
+            (swap(near_send, "expert", 1), kept_weights(late_rows))
         )
         near = near_keep.astype(f32) + near_came.astype(f32)
-        grad_tokens = finish_tokens(normed_grads)
         came = [swap(far[d].astype(bf16), "expert", m // 2 + 2 * d) for d in range(m // 4)]
         came += [swap(near[d].astype(bf16), "expert", 2 * d) for d in range(1, m // 4)]
         summed = near[0] + sum(x.astype(f32) for x in came)
@@ -713,7 +720,7 @@
         table_total = biases(
             summed[0, :row_tile, at + rest : at + rest + heads * per_line]
         )
-        low, grad_tokens = lax.optimization_barrier((summed.astype(bf16), grad_tokens))
+        low = summed.astype(bf16)
         mine = exchange_relative(
             [lax.dynamic_index_in_dim(low, s ^ p, 0, keepdims=False) for p in range(n)], "shard"
         )
@@ -729,6 +736,7 @@
         blocks[4], blocks[3] = lax.optimization_barrier((blocks[4], blocks[3]))
         blocks[6] = swap(blocks[4], "expert", 2)
         blocks[5] = swap(blocks[4], "expert", 1)
+        blocks[6], grad_tokens = lax.optimization_barrier((blocks[6], grad_tokens))
         blocks[7] = swap(blocks[6], "expert", 1)
         blocks = [blocks[d] for d in range(m)]
         grad_attention_in, grad_attention_out, total_one, total_two, total_router = call(
@@ -745,7 +753,7 @@
             [pltpu.VMEM((part, 128), f32)],
         )
     else:
-        grad_tokens = finish_tokens(normed_grads)
+        grad_up, grad_down = kept_weights(row_blocks)
         came = lax.all_to_all(
             shares[0].reshape(n, m, piece, wide).swapaxes(0, 1), "expert", 0, 0, tiled=True
         )

time: 191 us -> 186 us (0.974)
  waiting for transfers between devices: 73.7 us -> 70.6 us
    ppermute x52 -> x54, waiting for transfers between devices: 73.7 us -> 70.6 us  [swap(): return lax.ppermute(value, axis, [(i, i ^ bit) for i in range(size)])]
    ppermute x52 -> x54, starting transfers between devices: 53.1 us -> 51.2 us  [swap(): return lax.ppermute(value, axis, [(i, i ^ bit) for i in range(size)])]
  transfers between devices with their start and end apart: 52 -> 54, of which waited for: 28 -> 26; matrix products, arithmetic and copies ran while one was open for 5% -> 6% of each run, Pallas kernels for 21% -> 17%
where the time goes in v7:
time: 186 us
  waiting for transfers between devices  70.6 us (38%)
  starting transfers between devices  51.2 us (28%)
  Pallas kernels  43.9 us (24%)
  other arithmetic  7.8 us (4%)
  local copies, waits for them, and re-layouts  6.07 us (3%)
  matrix products  5.19 us (3%)
    ppermute x54, waiting for transfers between devices, swap(): return lax.ppermute(value, axis, [(i, i ^ bit) for i in range(size)])  70.6 us
    ppermute x54, starting transfers between devices, swap(): return lax.ppermute(value, axis, [(i, i ^ bit) for i in range(size)])  51.2 us
    pallas_call x8, Pallas kernels, call(): pl.pallas_call(kernel, out_shape=out_shape, in_specs=in_specs, out_specs=...  43.9 us
  transfers between devices with their start and end apart: 54, of which 26 were waited for; matrix products, arithmetic and copies ran while one was open for 6% of the time, Pallas kernels for 17%

profile of v7, /device:TPU:0, one launch (start us, length us, event | category | flops | bytes accessed | tf_op | source)
XLA Modules:
  0.0 186.1 jit_solution(12404694044322792395)
XLA Ops:
  0.7 3.0 %collective-permute-start = (bf16[128,768]{1,0:T(8,128)(2,1)}, bf16[128,768]{1,0:T(8,128)(2,1)S(1)}, u32[]{:S(2)}, u32[]{:S(2)}) collective-permute-start(bf16[128,768]{1,0:T(8,128)(2,1)} %refs_2_.2), channel_id=1, source_target_pairs={{0,2},{1,3},{2,0},{3,1},{4,6},{5,7},{6,4},{7,5},{8,10},{9,11},{10,... | collective-permute-start | bytes 589832 | tf_op jit(solution)/shard_map/ppermute | solution.py:44
  3.7 2.5 %shard_map.195 = (bf16[192,640]{1,0:T(8,128)(2,1)}, bf16[192,640]{1,0:T(8,128)(2,1)}, bf16[192,640]{1,0:T(8,128)(2,1)}, bf16[192,640]{1,0:T(8,128)(2,1)}) custom-call(bf16[192,2304]{1,0:T(8,128)(2,1)} %refs_0_.2, bf16[192]{0:T(256)(128)(2,1)} %refs_1_.1, bf16[192]{0:T(256)(128)(2,1)} %refs_2_.1), custom_call_target="tpu_custom_call" | custom-call | tf_op jit(solution)/shard_map/pallas_call | solution.py:66
  12.3 3.5 %collective-permute-done.4.refs_8_ = bf16[192,640]{1,0:T(8,128)(2,1)S(1)} collective-permute-done((bf16[192,640]{1,0:T(8,128)(2,1)}, bf16[192,640]{1,0:T(8,128)(2,1)S(1)}, u32[]{:S(2)}, u32[]{:S(2)}) %collective-permute-start.4) | collective-permute-done | bytes 245792 | tf_op jit(solution)/shard_map/ppermute | solution.py:44
  15.8 3.3 %collective-permute-done.5.refs_9_ = bf16[192,640]{1,0:T(8,128)(2,1)S(1)} collective-permute-done((bf16[192,640]{1,0:T(8,128)(2,1)}, bf16[192,640]{1,0:T(8,128)(2,1)S(1)}, u32[]{:S(2)}, u32[]{:S(2)}) %collective-permute-start.5) | collective-permute-done | bytes 245792 | tf_op jit(solution)/shard_map/ppermute | solution.py:44
  21.0 7.0 %shard_map.196 = (bf16[4,128,768]{2,1,0:T(8,128)(2,1)}, bf16[768,640]{1,0:T(8,128)(2,1)}, bf16[512,576]{1,0:T(8,128)(2,1)}, bf16[3,512,512]{2,1,0:T(8,128)(2,1)}...) custom-call(s32[1,3]{1,0:T(1,128)} %refs_0_.3, ...), custom_call_target="tpu_custom_call" | custom-call | flops 10000000000 | tf_op jit(solution)/shard_map/pallas_call | solution.py:66
  38.1 6.1 %collective-permute-done.14 = bf16[80,1536]{1,0:T(8,128)(2,1)S(1)} collective-permute-done((bf16[80,1536]{1,0:T(8,128)(2,1)S(1)}, bf16[80,1536]{1,0:T(8,128)(2,1)S(1)}, u32[]{:S(2)}, u32[]{:S(2)}) %collective-permute-start.14) | collective-permute-done | bytes 245792 | tf_op jit(solution)/shard_map/ppermute | solution.py:44
  44.4 3.7 %collective-permute-start.17 = (bf16[40,768]{1,0:T(8,128)(2,1)S(1)}, bf16[40,768]{1,0:T(8,128)(2,1)S(1)}, u32[]{:S(2)}, u32[]{:S(2)}) collective-permute-start(bf16[40,768]{1,0:T(8,128)(2,1)S(1)} %get-tuple-element.217), channel_id=1, source_target_pairs={{0,24},{4,28},{8,16},{12,20},{16,8},{20,12},{24,0},{28,4},{1,25},{... | collective-permute-start | bytes 184328 | tf_op jit(solution)/shard_map/ppermute | solution.py:44
  48.9 2.1 %collective-permute-done.17 = bf16[40,768]{1,0:T(8,128)(2,1)S(1)} collective-permute-done((bf16[40,768]{1,0:T(8,128)(2,1)S(1)}, bf16[40,768]{1,0:T(8,128)(2,1)S(1)}, u32[]{:S(2)}, u32[]{:S(2)}) %collective-permute-start.17) | collective-permute-done | bytes 61472 | tf_op jit(solution)/shard_map/ppermute | solution.py:44
  51.0 2.2 %collective-permute-done.16 = bf16[40,768]{1,0:T(8,128)(2,1)S(1)} collective-permute-done((bf16[40,768]{1,0:T(8,128)(2,1)S(1)}, bf16[40,768]{1,0:T(8,128)(2,1)S(1)}, u32[]{:S(2)}, u32[]{:S(2)}) %collective-permute-start.16) | collective-permute-done | bytes 61472 | tf_op jit(solution)/shard_map/ppermute | solution.py:44
  54.3 2.4 %collective-permute-start.22 = (bf16[40,768]{1,0:T(8,128)(2,1)S(1)}, bf16[40,768]{1,0:T(8,128)(2,1)S(1)}, u32[]{:S(2)}, u32[]{:S(2)}) collective-permute-start(bf16[40,768]{1,0:T(8,128)(2,1)S(1)} %get-tuple-element.231), channel_id=1, source_target_pairs={{0,24},{4,28},{8,16},{12,20},{16,8},{20,12},{24,0},{28,4},{1,25},{... | collective-permute-start | bytes 184328 | tf_op jit(solution)/shard_map/ppermute | solution.py:44
  56.7 2.1 %collective-permute-start.20 = (bf16[40,768]{1,0:T(8,128)(2,1)S(1)}, bf16[40,768]{1,0:T(8,128)(2,1)S(1)}, u32[]{:S(2)}, u32[]{:S(2)}) collective-permute-start(bf16[40,768]{1,0:T(8,128)(2,1)S(1)} %get-tuple-element.233), channel_id=1, source_target_pairs={{0,8},{4,12},{8,0},{12,4},{16,24},{20,28},{24,16},{28,20},{1,9},{5... | collective-permute-start | bytes 184328 | tf_op jit(solution)/shard_map/ppermute | solution.py:44
  64.0 6.0 %shard_map.197 = (bf16[2,320,768]{2,1,0:T(8,128)(2,1)}, bf16[2,320,768]{2,1,0:T(8,128)(2,1)}, f32[160,768]{1,0:T(8,128)}, bf16[160,768]{1,0:T(8,128)(2,1)}) custom-call(bf16[160,768]{1,0:T(8,128)(2,1)} %copy-done.8, bf16[160,768]{1,0:T(8,128)(2,1)} %copy-done.25, bf16[1,768,768]{2,1,0:T(8,128)(2,1)} %refs_2_.4, ...), custom_call_target="tpu_custom_call" | custom-call | flops 6000000000 | tf_op jit(solution)/shard_map/pallas_call | solution.py:66
  71.7 5.8 %shard_map.198 = (bf16[2,320,768]{2,1,0:T(8,128)(2,1)}, f32[160,768]{1,0:T(8,128)}, bf16[160,768]{1,0:T(8,128)(2,1)}) custom-call(bf16[160,768]{1,0:T(8,128)(2,1)} %copy-done.9, bf16[160,768]{1,0:T(8,128)(2,1)} %copy-done.26, bf16[1,768,768]{2,1,0:T(8,128)(2,1)} %refs_2_.4, bf16[1,768,768]{2,1,0:T(8,128)(2,1)} %collective-permute-done.6.refs_3_, ...), custom_call_target="tpu_custom_call" | custom-call | flops 6000000000 | tf_op jit(solution)/shard_map/pallas_call | solution.py:66
  81.3 1.8 collective-permute-start.27
  84.0 3.3 %collective-permute-done.27 = bf16[40,768]{1,0:T(8,128)(2,1)S(1)} collective-permute-done((bf16[40,768]{1,0:T(8,128)(2,1)S(1)}, bf16[40,768]{1,0:T(8,128)(2,1)S(1)}, u32[]{:S(2)}, u32[]{:S(2)}) %collective-permute-start.27) | collective-permute-done | bytes 61472 | tf_op jit(solution)/shard_map/ppermute | solution.py:44
  91.8 2.9 %collective-permute-done.29 = bf16[40,768]{1,0:T(8,128)(2,1)S(1)} collective-permute-done((bf16[40,768]{1,0:T(8,128)(2,1)S(1)}, bf16[40,768]{1,0:T(8,128)(2,1)S(1)}, u32[]{:S(2)}, u32[]{:S(2)}) %collective-permute-start.29) | collective-permute-done | bytes 61472 | tf_op jit(solution)/shard_map/ppermute | solution.py:44
  98.3 4.6 %shard_map.199 = (bf16[1,768,768]{2,1,0:T(8,128)(2,1)}, bf16[1,768,768]{2,1,0:T(8,128)(2,1)}) custom-call(bf16[160,768]{1,0:T(8,128)(2,1)} %copy-done.8, bf16[160,768]{1,0:T(8,128)(2,1)} %copy-done.25, bf16[160,768]{1,0:T(8,128)(2,1)} %copy-done.9, bf16[160,768]{1,0:T(8,128)(2,1)} %copy-done.26, bf16[2,320,768]{2,1,0:T(8,128)(2,1)} %get-tuple-element.158.hidden, ...), custom_call_target="tpu_custom_call" | custom-call | flops 4000000000 | tf_op jit(solution)/shard_map/pallas_call | solution.py:66
  107.8 3.1 %collective-permute-done.32.refs_11_ = bf16[128,768]{1,0:T(8,128)(2,1)S(1)} collective-permute-done((bf16[128,768]{1,0:T(8,128)(2,1)S(1)}, bf16[128,768]{1,0:T(8,128)(2,1)S(1)}, u32[]{:S(2)}, u32[]{:S(2)}) %collective-permute-start.32) | collective-permute-done | bytes 196640 | tf_op jit(solution)/shard_map/ppermute | solution.py:44
  113.1 9.0 %shard_map.200 = (bf16[2,5,24,640]{3,2,1,0:T(8,128)(2,1)}, bf16[2,5,24,640]{3,2,1,0:T(8,128)(2,1)}, bf16[2,5,24,640]{3,2,1,0:T(8,128)(2,1)}, bf16[2,5,24,640]{3,...) custom-call(bf16[512,576]{1,0:T(8,128)(2,1)} %get-tuple-element.163., ...), custom_call_target="tpu_custom_call" | custom-call | flops 8000000000 | tf_op jit(solution)/shard_map/pallas_call | solution.py:66
  124.0 7.6 %collective-permute-done.35 = bf16[2,5,24,640]{3,2,1,0:T(8,128)(2,1)S(1)} collective-permute-done((bf16[2,5,24,640]{3,2,1,0:T(8,128)(2,1)}, bf16[2,5,24,640]{3,2,1,0:T(8,128)(2,1)S(1)}, u32[]{:S(2)}, u32[]{:S(2)}) %collective-permute-start.35) | collective-permute-done | bytes 307232 | tf_op jit(solution)/shard_map/ppermute | solution.py:44
  137.3 5.8 %shard_map.201 = (f32[1,768,768]{2,1,0:T(8,128)}, f32[1,768,768]{2,1,0:T(8,128)}) custom-call(bf16[160,768]{1,0:T(8,128)(2,1)} %copy-done.8, bf16[160,768]{1,0:T(8,128)(2,1)} %copy-done.25, bf16[160,768]{1,0:T(8,128)(2,1)} %copy-done.9, bf16[160,768]{1,0:T(8,128)(2,1)} %copy-done.26, bf16[2,320,768]{2,1,0:T(8,128)(2,1)} %get-tuple-element.158.hidden, ...), custom_call_target="tpu_custom_call" | custom-call | flops 4000000000 | tf_op jit(solution)/shard_map/pallas_call | solution.py:66
  143.9 3.0 %collective-permute-start.41 = (bf16[5,24,640]{2,1,0:T(8,128)(2,1)}, bf16[5,24,640]{2,1,0:T(8,128)(2,1)}, u32[]{:S(2)}, u32[]{:S(2)}) collective-permute-start(bf16[5,24,640]{2,1,0:T(8,128)(2,1)} %fusion.42), channel_id=1, source_target_pairs={{0,8},{4,12},{8,0},{12,4},{16,24},{20,28},{24,16},{28,20},{1,9},{5... | collective-permute-start | bytes 460808 | tf_op jit(solution)/shard_map/ppermute | solution.py:44
  147.0 2.5 %collective-permute-done.39 = bf16[5,24,640]{2,1,0:T(8,128)(2,1)} collective-permute-done((bf16[5,24,640]{2,1,0:T(8,128)(2,1)S(1)}, bf16[5,24,640]{2,1,0:T(8,128)(2,1)}, u32[]{:S(2)}, u32[]{:S(2)}) %collective-permute-start.39) | collective-permute-done | bytes 153632 | tf_op jit(solution)/shard_map/ppermute | solution.py:44
  149.5 2.9 %collective-permute-done.41 = bf16[5,24,640]{2,1,0:T(8,128)(2,1)} collective-permute-done((bf16[5,24,640]{2,1,0:T(8,128)(2,1)}, bf16[5,24,640]{2,1,0:T(8,128)(2,1)}, u32[]{:S(2)}, u32[]{:S(2)}) %collective-permute-start.41) | collective-permute-done | bytes 153632 | tf_op jit(solution)/shard_map/ppermute | solution.py:44
  155.6 2.0 %collective-permute-done.43 = bf16[24,640]{1,0:T(8,128)(2,1)S(1)} collective-permute-done((bf16[24,640]{1,0:T(8,128)(2,1)S(1)}, bf16[24,640]{1,0:T(8,128)(2,1)S(1)}, u32[]{:S(2)}, u32[]{:S(2)}) %collective-permute-start.43) | collective-permute-done | bytes 30752 | tf_op jit(solution)/shard_map/ppermute | solution.py:44
  159.0 2.2 %collective-permute-start.45 = (bf16[5,24,640]{2,1,0:T(8,128)(2,1)S(1)}, bf16[5,24,640]{2,1,0:T(8,128)(2,1)S(1)}, u32[]{:S(2)}, u32[]{:S(2)}) collective-permute-start(bf16[5,24,640]{2,1,0:T(8,128)(2,1)S(1)} %slice_dynamic-update-slice_fusion.refs_0_), channel_id=1, source_target_pairs={{0,16},{4,20},{8,24},{12,28},{16,0},{20,4},{24,8},{28,12},{1,17},{... | collective-permute-start | bytes 460808 | tf_op jit(solution)/shard_map/ppermute | solution.py:44
  161.2 5.1 %collective-permute-done.46.refs_2_ = bf16[5,24,640]{2,1,0:T(8,128)(2,1)S(1)} collective-permute-done((bf16[5,24,640]{2,1,0:T(8,128)(2,1)S(1)}, bf16[5,24,640]{2,1,0:T(8,128)(2,1)S(1)}, u32[]{:S(2)}, u32[]{:S(2)}) %collective-permute-start.46) | collective-permute-done | bytes 153632 | tf_op jit(solution)/shard_map/ppermute | solution.py:44
  166.4 2.6 %collective-permute-done.45.refs_4_ = bf16[5,24,640]{2,1,0:T(8,128)(2,1)S(1)} collective-permute-done((bf16[5,24,640]{2,1,0:T(8,128)(2,1)S(1)}, bf16[5,24,640]{2,1,0:T(8,128)(2,1)S(1)}, u32[]{:S(2)}, u32[]{:S(2)}) %collective-permute-start.45) | collective-permute-done | bytes 153632 | tf_op jit(solution)/shard_map/ppermute | solution.py:44
  169.0 2.7 %collective-permute-done.48.refs_3_ = bf16[5,24,640]{2,1,0:T(8,128)(2,1)S(1)} collective-permute-done((bf16[5,24,640]{2,1,0:T(8,128)(2,1)S(1)}, bf16[5,24,640]{2,1,0:T(8,128)(2,1)S(1)}, u32[]{:S(2)}, u32[]{:S(2)}) %collective-permute-start.48) | collective-permute-done | bytes 153632 | tf_op jit(solution)/shard_map/ppermute | solution.py:44
  173.0 3.9 %collective-permute-done.49.refs_6_ = bf16[5,24,640]{2,1,0:T(8,128)(2,1)S(1)} collective-permute-done((bf16[5,24,640]{2,1,0:T(8,128)(2,1)S(1)}, bf16[5,24,640]{2,1,0:T(8,128)(2,1)S(1)}, u32[]{:S(2)}, u32[]{:S(2)}) %collective-permute-start.49) | collective-permute-done | bytes 153632 | tf_op jit(solution)/shard_map/ppermute | solution.py:44
  179.1 3.0 %collective-permute-done.53.refs_7_ = bf16[5,24,640]{2,1,0:T(8,128)(2,1)S(1)} collective-permute-done((bf16[5,24,640]{2,1,0:T(8,128)(2,1)S(1)}, bf16[5,24,640]{2,1,0:T(8,128)(2,1)S(1)}, u32[]{:S(2)}, u32[]{:S(2)}) %collective-permute-start.53) | collective-permute-done | bytes 153632 | tf_op jit(solution)/shard_map/ppermute | solution.py:44
  182.8 3.2 %shard_map.202 = (f32[192,2304]{1,0:T(8,128)}, f32[192,768]{1,0:T(8,128)}, f32[1,192]{1,0:T(1,128)}, f32[1,192]{1,0:T(1,128)}, f32[8,192]{1,0:T(8,128)}) custom-call(bf16[5,24,640]{2,1,0:T(8,128)(2,1)} %copy-done.10, bf16[5,24,640]{2,1,0:T(8,128)(2,1)} %copy-done.13, bf16[5,24,640]{2,1,0:T(8,128)(2,1)} %copy-done.12, bf16[5,24,640]{2,1,0:T(8,128)(2,1)} %copy-done.15, ...), custom_call_target="tpu_custom_call" | custom-call | tf_op jit(solution)/shard_map/pallas_call | solution.py:66
  (224 shorter events, 63.8 us)
Async XLA Ops:
  0.7 8.7 %collective-permute-start = (bf16[128,768]{1,0:T(8,128)(2,1)}, bf16[128,768]{1,0:T(8,128)(2,1)S(1)}, u32[]{:S(2)}, u32[]{:S(2)}) collective-permute-start(bf16[128,768]{1,0:T(8,128)(2,1)} %refs_2_.2), channel_id=1, source_target_pairs={{0,2},{1,3},{2,0},{3,1},{4,6},{5,7},{6,4},{7,5},{8,10},{9,11},{10,... | collective-permute-start | bytes 589832 | tf_op jit(solution)/shard_map/ppermute | solution.py:44
  3.7 6.5 %collective-permute-start.1 = (bf16[128,768]{1,0:T(8,128)(2,1)}, bf16[128,768]{1,0:T(8,128)(2,1)S(1)}, u32[]{:S(2)}, u32[]{:S(2)}) collective-permute-start(bf16[128,768]{1,0:T(8,128)(2,1)} %refs_2_.2), channel_id=1, source_target_pairs={{0,1},{1,0},{2,3},{3,2},{4,5},{5,4},{6,7},{7,6},{8,9},{9,8},{10,11... | collective-permute-start | bytes 589832 | tf_op jit(solution)/shard_map/ppermute | solution.py:44
  6.7 9.0 %collective-permute-start.4 = (bf16[192,640]{1,0:T(8,128)(2,1)}, bf16[192,640]{1,0:T(8,128)(2,1)S(1)}, u32[]{:S(2)}, u32[]{:S(2)}) collective-permute-start(bf16[192,640]{1,0:T(8,128)(2,1)} %get-tuple-element.113), channel_id=1, source_target_pairs={{0,2},{1,3},{2,0},{3,1},{4,6},{5,7},{6,4},{7,5},{8,10},{9,11},{10,... | collective-permute-start | bytes 737288 | tf_op jit(solution)/shard_map/ppermute | solution.py:44
  6.8 12.3 %collective-permute-start.5 = (bf16[192,640]{1,0:T(8,128)(2,1)}, bf16[192,640]{1,0:T(8,128)(2,1)S(1)}, u32[]{:S(2)}, u32[]{:S(2)}) collective-permute-start(bf16[192,640]{1,0:T(8,128)(2,1)} %get-tuple-element.114), channel_id=1, source_target_pairs={{0,3},{1,2},{2,1},{3,0},{4,7},{5,6},{6,5},{7,4},{8,11},{9,10},{10,... | collective-permute-start | bytes 737288 | tf_op jit(solution)/shard_map/ppermute | solution.py:44
  9.3 18.6 %collective-permute-start.6 = (bf16[1,768,768]{2,1,0:T(8,128)(2,1)}, bf16[1,768,768]{2,1,0:T(8,128)(2,1)}, u32[]{:S(2)}, u32[]{:S(2)}) collective-permute-start(bf16[1,768,768]{2,1,0:T(8,128)(2,1)} %refs_2_.4), channel_id=1, source_target_pairs={{0,1},{1,0},{2,3},{3,2},{4,5},{5,4},{6,7},{7,6},{8,9},{9,8},{10,11... | collective-permute-start | bytes 3538952 | tf_op jit(solution)/shard_map/ppermute | solution.py:44
  10.1 17.8 %collective-permute-start.7 = (bf16[1,768,768]{2,1,0:T(8,128)(2,1)}, bf16[1,768,768]{2,1,0:T(8,128)(2,1)}, u32[]{:S(2)}, u32[]{:S(2)}) collective-permute-start(bf16[1,768,768]{2,1,0:T(8,128)(2,1)} %refs_4_.1), channel_id=1, source_target_pairs={{0,1},{1,0},{2,3},{3,2},{4,5},{5,4},{6,7},{7,6},{8,9},{9,8},{10,11... | collective-permute-start | bytes 3538952 | tf_op jit(solution)/shard_map/ppermute | solution.py:44
  11.1 8.0 %collective-permute-start.2 = (bf16[128,768]{1,0:T(8,128)(2,1)S(1)}, bf16[128,768]{1,0:T(8,128)(2,1)S(1)}, u32[]{:S(2)}, u32[]{:S(2)}) collective-permute-start(bf16[128,768]{1,0:T(8,128)(2,1)S(1)} %collective-permute-done.refs_4_), channel_id=1, source_target_pairs={{0,1},{1,0},{2,3},{3,2},{4,5},{5,4},{6,7},{7,6},{8,9},{9,8},{10,11... | collective-permute-start | bytes 589832 | tf_op jit(solution)/shard_map/ppermute | solution.py:44
  19.1 8.9 %collective-permute-start.8 = (bf16[192,768]{1,0:T(8,128)(2,1)}, bf16[192,768]{1,0:T(8,128)(2,1)S(1)}, u32[]{:S(2)}, u32[]{:S(2)}) collective-permute-start(bf16[192,768]{1,0:T(8,128)(2,1)} %refs_6_), channel_id=1, source_target_pairs={{0,1},{1,0},{2,3},{3,2},{4,5},{5,4},{6,7},{7,6},{8,9},{9,8},{10,11... | collective-permute-start | bytes 884744 | tf_op jit(solution)/shard_map/ppermute | solution.py:44
  20.0 9.9 %collective-permute-start.11 = (bf16[192,768]{1,0:T(8,128)(2,1)}, bf16[192,768]{1,0:T(8,128)(2,1)S(1)}, u32[]{:S(2)}, u32[]{:S(2)}) collective-permute-start(bf16[192,768]{1,0:T(8,128)(2,1)} %refs_6_), channel_id=1, source_target_pairs={{0,2},{1,3},{2,0},{3,1},{4,6},{5,7},{6,4},{7,5},{8,10},{9,11},{10,... | collective-permute-start | bytes 884744 | tf_op jit(solution)/shard_map/ppermute | solution.py:44
  36.2 8.0 %collective-permute-start.14 = (bf16[80,1536]{1,0:T(8,128)(2,1)S(1)}, bf16[80,1536]{1,0:T(8,128)(2,1)S(1)}, u32[]{:S(2)}, u32[]{:S(2)}) collective-permute-start(bf16[80,1536]{1,0:T(8,128)(2,1)S(1)} %convolution_convert_fusion), channel_id=1, source_target_pairs={{0,4},{4,0},{8,12},{12,8},{16,20},{20,16},{24,28},{28,24},{1,5},{5... | collective-permute-start | bytes 737288 | tf_op jit(solution)/shard_map/ppermute | solution.py:44
  44.4 6.6 %collective-permute-start.17 = (bf16[40,768]{1,0:T(8,128)(2,1)S(1)}, bf16[40,768]{1,0:T(8,128)(2,1)S(1)}, u32[]{:S(2)}, u32[]{:S(2)}) collective-permute-start(bf16[40,768]{1,0:T(8,128)(2,1)S(1)} %get-tuple-element.217), channel_id=1, source_target_pairs={{0,24},{4,28},{8,16},{12,20},{16,8},{20,12},{24,0},{28,4},{1,25},{... | collective-permute-start | bytes 184328 | tf_op jit(solution)/shard_map/ppermute | solution.py:44
  53.2 10.0 %collective-permute-start.18 = (bf16[160,768]{1,0:T(8,128)(2,1)S(1)}, bf16[160,768]{1,0:T(8,128)(2,1)S(1)}, u32[]{:S(2)}, u32[]{:S(2)}) collective-permute-start(bf16[160,768]{1,0:T(8,128)(2,1)S(1)} %pad_maximum_fusion.3.refs_0_.own), channel_id=1, source_target_pairs={{0,2},{1,3},{2,0},{3,1},{4,6},{5,7},{6,4},{7,5},{8,10},{9,11},{10,... | collective-permute-start | bytes 737288 | tf_op jit(solution)/shard_map/ppermute | solution.py:44
  54.3 6.1 %collective-permute-start.22 = (bf16[40,768]{1,0:T(8,128)(2,1)S(1)}, bf16[40,768]{1,0:T(8,128)(2,1)S(1)}, u32[]{:S(2)}, u32[]{:S(2)}) collective-permute-start(bf16[40,768]{1,0:T(8,128)(2,1)S(1)} %get-tuple-element.231), channel_id=1, source_target_pairs={{0,24},{4,28},{8,16},{12,20},{16,8},{20,12},{24,0},{28,4},{1,25},{... | collective-permute-start | bytes 184328 | tf_op jit(solution)/shard_map/ppermute | solution.py:44
  62.2 8.8 %collective-permute-start.23 = (bf16[160,768]{1,0:T(8,128)(2,1)S(1)}, bf16[160,768]{1,0:T(8,128)(2,1)S(1)}, u32[]{:S(2)}, u32[]{:S(2)}) collective-permute-start(bf16[160,768]{1,0:T(8,128)(2,1)S(1)} %pad_maximum_fusion.4.refs_0_.own_grad), channel_id=1, source_target_pairs={{0,2},{1,3},{2,0},{3,1},{4,6},{5,7},{6,4},{7,5},{8,10},{9,11},{10,... | collective-permute-start | bytes 737288 | tf_op jit(solution)/shard_map/ppermute | solution.py:44
  70.0 8.5 %collective-permute-start.19 = (bf16[160,768]{1,0:T(8,128)(2,1)}, bf16[160,768]{1,0:T(8,128)(2,1)S(1)}, u32[]{:S(2)}, u32[]{:S(2)}) collective-permute-start(bf16[160,768]{1,0:T(8,128)(2,1)} %get-tuple-element.140), channel_id=1, source_target_pairs={{0,2},{1,3},{2,0},{3,1},{4,6},{5,7},{6,4},{7,5},{8,10},{9,11},{10,... | collective-permute-start | bytes 737288 | tf_op jit(solution)/shard_map/ppermute | solution.py:44
  77.5 6.4 %collective-permute-start.26 = (bf16[160,768]{1,0:T(8,128)(2,1)}, bf16[160,768]{1,0:T(8,128)(2,1)S(1)}, u32[]{:S(2)}, u32[]{:S(2)}) collective-permute-start(bf16[160,768]{1,0:T(8,128)(2,1)} %get-tuple-element.143), channel_id=1, source_target_pairs={{0,2},{1,3},{2,0},{3,1},{4,6},{5,7},{6,4},{7,5},{8,10},{9,11},{10,... | collective-permute-start | bytes 737288 | tf_op jit(solution)/shard_map/ppermute | solution.py:44
  78.6 13.1 %collective-permute-start.24 = (bf16[40,768]{1,0:T(8,128)(2,1)S(1)}, bf16[40,768]{1,0:T(8,128)(2,1)S(1)}, u32[]{:S(2)}, u32[]{:S(2)}) collective-permute-start(bf16[40,768]{1,0:T(8,128)(2,1)S(1)} %get-tuple-element.228), channel_id=1, source_target_pairs={{0,8},{4,12},{8,0},{12,4},{16,24},{20,28},{24,16},{28,20},{1,9},{5... | collective-permute-start | bytes 184328 | tf_op jit(solution)/shard_map/ppermute | solution.py:44
  79.5 12.2 %collective-permute-start.25 = (bf16[40,768]{1,0:T(8,128)(2,1)S(1)}, bf16[40,768]{1,0:T(8,128)(2,1)S(1)}, u32[]{:S(2)}, u32[]{:S(2)}) collective-permute-start(bf16[40,768]{1,0:T(8,128)(2,1)S(1)} %get-tuple-element.227), channel_id=1, source_target_pairs={{0,16},{4,20},{8,24},{12,28},{16,0},{20,4},{24,8},{28,12},{1,17},{... | collective-permute-start | bytes 184328 | tf_op jit(solution)/shard_map/ppermute | solution.py:44
  96.7 6.4 %collective-permute-start.31 = (bf16[80,1536]{1,0:T(8,128)(2,1)S(1)}, bf16[80,1536]{1,0:T(8,128)(2,1)S(1)}, u32[]{:S(2)}, u32[]{:S(2)}) collective-permute-start(bf16[80,1536]{1,0:T(8,128)(2,1)S(1)} %maximum_maximum_fusion), channel_id=1, source_target_pairs={{0,4},{4,0},{8,12},{12,8},{16,20},{20,16},{24,28},{28,24},{1,5},{5... | collective-permute-start | bytes 737288 | tf_op jit(solution)/shard_map/ppermute | solution.py:44
  122.1 9.6 %collective-permute-start.35 = (bf16[2,5,24,640]{3,2,1,0:T(8,128)(2,1)}, bf16[2,5,24,640]{3,2,1,0:T(8,128)(2,1)S(1)}, u32[]{:S(2)}, u32[]{:S(2)}) collective-permute-start(bf16[2,5,24,640]{3,2,1,0:T(8,128)(2,1)} %get-tuple-element.179), channel_id=1, source_target_pairs={{0,4},{4,0},{8,12},{12,8},{16,20},{20,16},{24,28},{28,24},{1,5},{5... | collective-permute-start | bytes 921608 | tf_op jit(solution)/shard_map/ppermute | solution.py:44
  123.5 12.8 %collective-permute-start.37 = (bf16[1,768,768]{2,1,0:T(8,128)(2,1)S(1)}, bf16[1,768,768]{2,1,0:T(8,128)(2,1)S(1)}, u32[]{:S(2)}, u32[]{:S(2)}) collective-permute-start(bf16[1,768,768]{2,1,0:T(8,128)(2,1)S(1)} %copy-done.23), channel_id=1, source_target_pairs={{0,1},{1,0},{2,3},{3,2},{4,5},{5,4},{6,7},{7,6},{8,9},{9,8},{10,11... | collective-permute-start | bytes 3538952 | tf_op jit(solution)/shard_map/ppermute | solution.py:44
  123.5 13.9 %collective-permute-start.38 = (bf16[1,768,768]{2,1,0:T(8,128)(2,1)S(1)}, bf16[1,768,768]{2,1,0:T(8,128)(2,1)}, u32[]{:S(2)}, u32[]{:S(2)}) collective-permute-start(bf16[1,768,768]{2,1,0:T(8,128)(2,1)S(1)} %copy-done.22), channel_id=1, source_target_pairs={{0,1},{1,0},{2,3},{3,2},{4,5},{5,4},{6,7},{7,6},{8,9},{9,8},{10,11... | collective-permute-start | bytes 3538952 | tf_op jit(solution)/shard_map/ppermute | solution.py:44
  124.0 12.2 %collective-permute-start.50 = (bf16[2,128,768]{2,1,0:T(8,128)(2,1)}, bf16[2,128,768]{2,1,0:T(8,128)(2,1)S(1)}, u32[]{:S(2)}, u32[]{:S(2)}) collective-permute-start(bf16[2,128,768]{2,1,0:T(8,128)(2,1)} %get-tuple-element.194), channel_id=1, source_target_pairs={{0,1},{1,0},{2,3},{3,2},{4,5},{5,4},{6,7},{7,6},{8,9},{9,8},{10,11... | collective-permute-start | bytes 1179656 | tf_op jit(solution)/shard_map/ppermute | solution.py:44
  131.6 11.5 %collective-permute-start.36 = (bf16[2,5,24,640]{3,2,1,0:T(8,128)(2,1)}, bf16[2,5,24,640]{3,2,1,0:T(8,128)(2,1)S(1)}, u32[]{:S(2)}, u32[]{:S(2)}) collective-permute-start(bf16[2,5,24,640]{3,2,1,0:T(8,128)(2,1)} %get-tuple-element.181), channel_id=1, source_target_pairs={{0,4},{4,0},{8,12},{12,8},{16,20},{20,16},{24,28},{28,24},{1,5},{5... | collective-permute-start | bytes 921608 | tf_op jit(solution)/shard_map/ppermute | solution.py:44
  134.7 12.2 %collective-permute-start.40 = (bf16[5,24,640]{2,1,0:T(8,128)(2,1)}, bf16[5,24,640]{2,1,0:T(8,128)(2,1)S(1)}, u32[]{:S(2)}, u32[]{:S(2)}) collective-permute-start(bf16[5,24,640]{2,1,0:T(8,128)(2,1)} %get-tuple-element.221), channel_id=1, source_target_pairs={{0,24},{4,28},{8,16},{12,20},{16,8},{20,12},{24,0},{28,4},{1,25},{... | collective-permute-start | bytes 460808 | tf_op jit(solution)/shard_map/ppermute | solution.py:44
  136.1 13.3 %collective-permute-start.39 = (bf16[5,24,640]{2,1,0:T(8,128)(2,1)S(1)}, bf16[5,24,640]{2,1,0:T(8,128)(2,1)}, u32[]{:S(2)}, u32[]{:S(2)}) collective-permute-start(bf16[5,24,640]{2,1,0:T(8,128)(2,1)S(1)} %get-tuple-element.220), channel_id=1, source_target_pairs={{0,16},{4,20},{8,24},{12,28},{16,0},{20,4},{24,8},{28,12},{1,17},{... | collective-permute-start | bytes 460808 | tf_op jit(solution)/shard_map/ppermute | solution.py:44
  136.3 10.7 %collective-permute-start.51 = (bf16[128,768]{1,0:T(8,128)(2,1)S(1)}, bf16[128,768]{1,0:T(8,128)(2,1)S(1)}, u32[]{:S(2)}, u32[]{:S(2)}) collective-permute-start(bf16[128,768]{1,0:T(8,128)(2,1)S(1)} %fusion.37), channel_id=1, source_target_pairs={{0,2},{1,3},{2,0},{3,1},{4,6},{5,7},{6,4},{7,5},{8,10},{9,11},{10,... | collective-permute-start | bytes 589832 | tf_op jit(solution)/shard_map/ppermute | solution.py:44
  143.9 8.4 %collective-permute-start.41 = (bf16[5,24,640]{2,1,0:T(8,128)(2,1)}, bf16[5,24,640]{2,1,0:T(8,128)(2,1)}, u32[]{:S(2)}, u32[]{:S(2)}) collective-permute-start(bf16[5,24,640]{2,1,0:T(8,128)(2,1)} %fusion.42), channel_id=1, source_target_pairs={{0,8},{4,12},{8,0},{12,4},{16,24},{20,28},{24,16},{28,20},{1,9},{5... | collective-permute-start | bytes 460808 | tf_op jit(solution)/shard_map/ppermute | solution.py:44
  158.1 8.2 %collective-permute-start.46 = (bf16[5,24,640]{2,1,0:T(8,128)(2,1)S(1)}, bf16[5,24,640]{2,1,0:T(8,128)(2,1)S(1)}, u32[]{:S(2)}, u32[]{:S(2)}) collective-permute-start(bf16[5,24,640]{2,1,0:T(8,128)(2,1)S(1)} %slice_dynamic-update-slice_fusion.refs_0_), channel_id=1, source_target_pairs={{0,8},{4,12},{8,0},{12,4},{16,24},{20,28},{24,16},{28,20},{1,9},{5... | collective-permute-start | bytes 460808 | tf_op jit(solution)/shard_map/ppermute | solution.py:44
  158.3 8.0 %collective-permute-start.47 = (bf16[5,24,640]{2,1,0:T(8,128)(2,1)S(1)}, bf16[5,24,640]{2,1,0:T(8,128)(2,1)S(1)}, u32[]{:S(2)}, u32[]{:S(2)}) collective-permute-start(bf16[5,24,640]{2,1,0:T(8,128)(2,1)S(1)} %slice_dynamic-update-slice_fusion.refs_0_), channel_id=1, source_target_pairs={{0,4},{4,0},{8,12},{12,8},{16,20},{20,16},{24,28},{28,24},{1,5},{5... | collective-permute-start | bytes 460808 | tf_op jit(solution)/shard_map/ppermute | solution.py:44
  159.0 10.0 %collective-permute-start.45 = (bf16[5,24,640]{2,1,0:T(8,128)(2,1)S(1)}, bf16[5,24,640]{2,1,0:T(8,128)(2,1)S(1)}, u32[]{:S(2)}, u32[]{:S(2)}) collective-permute-start(bf16[5,24,640]{2,1,0:T(8,128)(2,1)S(1)} %slice_dynamic-update-slice_fusion.refs_0_), channel_id=1, source_target_pairs={{0,16},{4,20},{8,24},{12,28},{16,0},{20,4},{24,8},{28,12},{1,17},{... | collective-permute-start | bytes 460808 | tf_op jit(solution)/shard_map/ppermute | solution.py:44
  172.7 6.4 %collective-permute-start.52 = (bf16[5,24,640]{2,1,0:T(8,128)(2,1)S(1)}, bf16[5,24,640]{2,1,0:T(8,128)(2,1)S(1)}, u32[]{:S(2)}, u32[]{:S(2)}) collective-permute-start(bf16[5,24,640]{2,1,0:T(8,128)(2,1)S(1)} %collective-permute-done.45.refs_4_), channel_id=1, source_target_pairs={{0,4},{4,0},{8,12},{12,8},{16,20},{20,16},{24,28},{28,24},{1,5},{5... | collective-permute-start | bytes 460808 | tf_op jit(solution)/shard_map/ppermute | solution.py:44
  (58 other events, 371.4 us)

commit v8 on v7

--- a/solution.py
+++ b/solution.py
@@ -145,7 +145,10 @@
     for c in range(width // size):
         beside = weight_out[c * size : (c + 1) * size, wide:].astype(f32)
         for i in range(2):
-            gains_out[i][:, c * size : (c + 1) * size] = to_row(beside[:, i : i + 1], size)
+            row = to_row(beside[:, i : i + 1], size)
+            gains_out[i][:, c * size : (c + 1) * size] = jnp.broadcast_to(
+                row, (gains_out[i].shape[0], size)
+            )
     gain = gains_out[0][...]
     for j in range(n):
         value = tokens_out[j].astype(f32)
@@ -298,11 +301,12 @@
         return
     piece = part // m
     total_scr[:, wide:] = jnp.zeros((width, full - wide), f32)
+    grad_two = gain_two[...].reshape(1, width)
     size = 128
     for c in range(width // size):
         here = slice(c * size, (c + 1) * size)
         total_scr[here, wide : wide + 1] = to_column(grad_gain[:, here], size)
-        total_scr[here, wide + 1 : wide + 2] = to_column(gain_two[0:1, here], size)
+        total_scr[here, wide + 1 : wide + 2] = to_column(grad_two[:, here], size)
         total_scr[here, wide + 2 : wide + 2 + experts] = router[:, here].T
     at = wide + 2 + experts
     rest = (width - full) // n
@@ -426,7 +430,7 @@
     grad_value = factor * scaled - value * factor * factor * factor * jnp.mean(
         scaled * value, axis=-1, keepdims=True
     )
-    grad_gain = jnp.sum(upstream * value * factor, axis=0, keepdims=True)
+    grad_gain = jnp.sum(upstream * value * factor, axis=0)
     return (grad_value, grad_gain)
 
 
@@ -487,7 +491,7 @@
             shape((group, wide)),
             shape((heads, group, group)),
             shape((1, width), f32),
-            shape((1, width), f32),
+            shape((rows, width), f32),
             shape((n, rows, part)),
             *[shape((rows, part))] * n,
         ),
@@ -539,12 +543,19 @@
     def dispatch(forward, backward):
         if not direct:
             return [plain(dot_tn(collect, x).astype(bf16)) for x in (forward, backward)]
-        value = jnp.concatenate([forward, backward], axis=1)
-        came = swap(dot_tn(collect[:, half:], value).astype(bf16), "expert", 1)
-        own = dot_tn(collect[:, :half], value).astype(bf16).reshape(m // 2, capacity, 2 * width)
-        both = jnp.concatenate([own, came.reshape(m // 2, capacity, 2 * width)], axis=1)
-        first = among_pairs(both[:, :, :width])
-        second, first[-1] = lax.optimization_barrier((both[:, :, width:], first[-1]))
+        came = swap(dot_tn(collect[:, half:], forward).astype(bf16), "expert", 1)
+        came, other = lax.optimization_barrier(
+            (came, dot_tn(collect[:, half:], backward).astype(bf16))
+        )
+
+        def both(own, came):
+            own = dot_tn(collect[:, :half], own).astype(bf16).reshape(m // 2, capacity, width)
+            return jnp.concatenate([own, came.reshape(m // 2, capacity, width)], axis=1)
+
+        first = among_pairs(both(forward, came))
+        second, first[1] = lax.optimization_barrier(
+            (both(backward, swap(other, "expert", 1)), first[1])
+        )
         return [jnp.concatenate(x, axis=0) for x in (first, among_pairs(second))]
 
     def among_pairs(both):
@@ -557,7 +568,7 @@
             x.reshape(m // 2, 2 * capacity, width) for x in (forward, backward)
         )
         blocks = [among_pairs(forward)]
-        backward, blocks[0][-1] = lax.optimization_barrier((backward, blocks[0][-1]))
+        backward, blocks[0][1] = lax.optimization_barrier((backward, blocks[0][1]))
         blocks.append(among_pairs(backward))
         late, blocks = lax.optimization_barrier((late, blocks))
         own, other = (
@@ -706,14 +717,15 @@
     if direct:
         far_keep, far_send, near_keep, near_send = shares
         far_came = swap(far_send, "expert", 1)
-        far_came, near_send, late_rows = lax.optimization_barrier((far_came, near_send, row_blocks))
+        far_came, near_send, up_came, down_came = lax.optimization_barrier(
+            (far_came, near_send, up_came, down_came)
+        )
         far = far_keep.astype(f32) + far_came.astype(f32)
-        near_came, (grad_up, grad_down) = lax.optimization_barrier(
-            (swap(near_send, "expert", 1), kept_weights(late_rows))
-        )
+        near_came, late_rows = lax.optimization_barrier((swap(near_send, "expert", 1), row_blocks))
         near = near_keep.astype(f32) + near_came.astype(f32)
         came = [swap(far[d].astype(bf16), "expert", m // 2 + 2 * d) for d in range(m // 4)]
         came += [swap(near[d].astype(bf16), "expert", 2 * d) for d in range(1, m // 4)]
+        came, (grad_up, grad_down) = lax.optimization_barrier((came, kept_weights(late_rows)))
         summed = near[0] + sum(x.astype(f32) for x in came)
         at = wide + 2 + experts
         rest = (width - full) // n
@@ -764,7 +776,7 @@
         out_mine = sum(x.astype(f32) for x in came).astype(bf16)
         grad_attention_in = lax.all_gather(mine, "expert", axis=0, tiled=True).astype(f32)
         grad_attention_out = lax.all_gather(out_mine, "expert", axis=0, tiled=True).astype(f32)
-        small = jnp.concatenate([gain_row[0:1], grad_gain_two, grad_router], axis=0)
+        small = jnp.concatenate([gain_row[0:1], grad_gain_two[None], grad_router], axis=0)
         small_total = lax.psum_scatter(small, "shard", scatter_dimension=1, tiled=True)
         small_total, table_total = lax.psum(
             (small_total, biases(table[:, : heads * per_line])), "expert"

time: 186 us -> 177 us (0.952)
  waiting for transfers between devices: 70.6 us -> 63.4 us
  local copies, waits for them, and re-layouts: 6.07 us -> 3.66 us
    ppermute x54 -> x55, waiting for transfers between devices: 70.6 us -> 63.4 us  [swap(): return lax.ppermute(value, axis, [(i, i ^ bit) for i in range(size)])]
    ppermute x54 -> x55, starting transfers between devices: 51.2 us -> 52.2 us  [swap(): return lax.ppermute(value, axis, [(i, i ^ bit) for i in range(size)])]
  transfers between devices with their start and end apart: 54 -> 55, of which waited for: 26 -> 29; matrix products, arithmetic and copies ran while one was open for 6% -> 5% of each run, Pallas kernels for 17% -> 23%
where the time goes in v8:
time: 177 us; the launch traced here: 176 us
  waiting for transfers between devices  63.4 us (36%)
  starting transfers between devices  52.2 us (29%)
  Pallas kernels  43.9 us (25%)
  matrix products  5.99 us (3%)
  other arithmetic  5.98 us (3%)
  local copies, waits for them, and re-layouts  3.66 us (2%)
    ppermute x55, waiting for transfers between devices, swap(): return lax.ppermute(value, axis, [(i, i ^ bit) for i in range(size)])  63.4 us
    ppermute x55, starting transfers between devices, swap(): return lax.ppermute(value, axis, [(i, i ^ bit) for i in range(size)])  52.2 us
    pallas_call x8, Pallas kernels, call(): pl.pallas_call(kernel, out_shape=out_shape, in_specs=in_specs, out_specs=...  43.9 us
  transfers between devices with their start and end apart: 55, of which 29 were waited for; matrix products, arithmetic and copies ran while one was open for 5% of the time, Pallas kernels for 23%

profile of v8, /device:TPU:0, one launch (start us, length us, event | category | flops | bytes accessed | tf_op | source)
XLA Modules:
  0.0 176.5 jit_solution(4959573250286952028)
XLA Ops:
  0.7 3.0 %collective-permute-start = (bf16[128,768]{1,0:T(8,128)(2,1)}, bf16[128,768]{1,0:T(8,128)(2,1)S(1)}, u32[]{:S(2)}, u32[]{:S(2)}) collective-permute-start(bf16[128,768]{1,0:T(8,128)(2,1)} %refs_2_.2), channel_id=1, source_target_pairs={{0,2},{1,3},{2,0},{3,1},{4,6},{5,7},{6,4},{7,5},{8,10},{9,11},{10,... | collective-permute-start | bytes 589832 | tf_op jit(solution)/shard_map/ppermute | solution.py:44
  3.7 2.5 %shard_map.195 = (bf16[192,640]{1,0:T(8,128)(2,1)}, bf16[192,640]{1,0:T(8,128)(2,1)}, bf16[192,640]{1,0:T(8,128)(2,1)}, bf16[192,640]{1,0:T(8,128)(2,1)}) custom-call(bf16[192,2304]{1,0:T(8,128)(2,1)} %refs_0_.2, bf16[192]{0:T(256)(128)(2,1)} %refs_1_.1, bf16[192]{0:T(256)(128)(2,1)} %refs_2_.1), custom_call_target="tpu_custom_call" | custom-call | tf_op jit(solution)/shard_map/pallas_call | solution.py:66
  12.3 3.5 %collective-permute-done.4.refs_8_ = bf16[192,640]{1,0:T(8,128)(2,1)S(1)} collective-permute-done((bf16[192,640]{1,0:T(8,128)(2,1)}, bf16[192,640]{1,0:T(8,128)(2,1)S(1)}, u32[]{:S(2)}, u32[]{:S(2)}) %collective-permute-start.4) | collective-permute-done | bytes 245792 | tf_op jit(solution)/shard_map/ppermute | solution.py:44
  15.8 3.3 %collective-permute-done.5.refs_9_ = bf16[192,640]{1,0:T(8,128)(2,1)S(1)} collective-permute-done((bf16[192,640]{1,0:T(8,128)(2,1)}, bf16[192,640]{1,0:T(8,128)(2,1)S(1)}, u32[]{:S(2)}, u32[]{:S(2)}) %collective-permute-start.5) | collective-permute-done | bytes 245792 | tf_op jit(solution)/shard_map/ppermute | solution.py:44
  21.0 7.1 %shard_map.196 = (bf16[4,128,768]{2,1,0:T(8,128)(2,1)}, bf16[768,640]{1,0:T(8,128)(2,1)}, bf16[512,576]{1,0:T(8,128)(2,1)}, bf16[3,512,512]{2,1,0:T(8,128)(2,1)}...) custom-call(s32[1,3]{1,0:T(1,128)} %refs_0_.3, ...), custom_call_target="tpu_custom_call" | custom-call | flops 10000000000 | tf_op jit(solution)/shard_map/pallas_call | solution.py:66
  30.6 2.1 %collective-permute-done.10 = bf16[128,192]{1,0:T(8,128)(2,1)S(1)} collective-permute-done((bf16[128,192]{1,0:T(8,128)(2,1)}, bf16[128,192]{1,0:T(8,128)(2,1)S(1)}, u32[]{:S(2)}, u32[]{:S(2)}) %collective-permute-start.10) | collective-permute-done | bytes 49184 | tf_op jit(solution)/shard_map/ppermute | solution.py:44
  37.7 3.5 %collective-permute-done.14 = bf16[80,768]{1,0:T(8,128)(2,1)S(1)} collective-permute-done((bf16[80,768]{1,0:T(8,128)(2,1)S(1)}, bf16[80,768]{1,0:T(8,128)(2,1)S(1)}, u32[]{:S(2)}, u32[]{:S(2)}) %collective-permute-start.14) | collective-permute-done | bytes 122912 | tf_op jit(solution)/shard_map/ppermute | solution.py:44
  43.1 1.6 collective-permute-start.16
  44.8 2.6 %collective-permute-start.17 = (bf16[40,768]{1,0:T(8,128)(2,1)S(1)}, bf16[40,768]{1,0:T(8,128)(2,1)S(1)}, u32[]{:S(2)}, u32[]{:S(2)}) collective-permute-start(bf16[40,768]{1,0:T(8,128)(2,1)S(1)} %get-tuple-element.237), channel_id=1, source_target_pairs={{0,16},{4,20},{8,24},{12,28},{16,0},{20,4},{24,8},{28,12},{1,17},{... | collective-permute-start | bytes 184328 | tf_op jit(solution)/shard_map/ppermute | solution.py:44
  48.0 3.2 %collective-permute-done.17 = bf16[40,768]{1,0:T(8,128)(2,1)S(1)} collective-permute-done((bf16[40,768]{1,0:T(8,128)(2,1)S(1)}, bf16[40,768]{1,0:T(8,128)(2,1)S(1)}, u32[]{:S(2)}, u32[]{:S(2)}) %collective-permute-start.17) | collective-permute-done | bytes 61472 | tf_op jit(solution)/shard_map/ppermute | solution.py:44
  51.2 2.2 %collective-permute-done.18 = bf16[40,768]{1,0:T(8,128)(2,1)S(1)} collective-permute-done((bf16[40,768]{1,0:T(8,128)(2,1)S(1)}, bf16[40,768]{1,0:T(8,128)(2,1)S(1)}, u32[]{:S(2)}, u32[]{:S(2)}) %collective-permute-start.18) | collective-permute-done | bytes 61472 | tf_op jit(solution)/shard_map/ppermute | solution.py:44
  55.9 3.1 %collective-permute-start.23 = (bf16[40,768]{1,0:T(8,128)(2,1)S(1)}, bf16[40,768]{1,0:T(8,128)(2,1)S(1)}, u32[]{:S(2)}, u32[]{:S(2)}) collective-permute-start(bf16[40,768]{1,0:T(8,128)(2,1)S(1)} %get-tuple-element.247), channel_id=1, source_target_pairs={{0,24},{4,28},{8,16},{12,20},{16,8},{20,12},{24,0},{28,4},{1,25},{... | collective-permute-start | bytes 184328 | tf_op jit(solution)/shard_map/ppermute | solution.py:44
  59.7 2.2 %collective-permute-done.23 = bf16[40,768]{1,0:T(8,128)(2,1)S(1)} collective-permute-done((bf16[40,768]{1,0:T(8,128)(2,1)S(1)}, bf16[40,768]{1,0:T(8,128)(2,1)S(1)}, u32[]{:S(2)}, u32[]{:S(2)}) %collective-permute-start.23) | collective-permute-done | bytes 61472 | tf_op jit(solution)/shard_map/ppermute | solution.py:44
  63.8 6.0 %shard_map.197 = (bf16[2,320,768]{2,1,0:T(8,128)(2,1)}, bf16[2,320,768]{2,1,0:T(8,128)(2,1)}, f32[160,768]{1,0:T(8,128)}, bf16[160,768]{1,0:T(8,128)(2,1)}) custom-call(bf16[160,768]{1,0:T(8,128)(2,1)} %copy-done.9, bf16[160,768]{1,0:T(8,128)(2,1)} %copy-done.25, bf16[1,768,768]{2,1,0:T(8,128)(2,1)} %refs_2_.4, bf16[1,768,768]{2,1,0:T(8,128)(2,1)} %copy-done.23, ...), custom_call_target="tpu_custom_call" | custom-call | flops 6000000000 | tf_op jit(solution)/shard_map/pallas_call | solution.py:66
  71.5 5.8 %shard_map.198 = (bf16[2,320,768]{2,1,0:T(8,128)(2,1)}, f32[160,768]{1,0:T(8,128)}, bf16[160,768]{1,0:T(8,128)(2,1)}) custom-call(bf16[160,768]{1,0:T(8,128)(2,1)} %copy-done.10, bf16[160,768]{1,0:T(8,128)(2,1)} %copy-done.26, bf16[1,768,768]{2,1,0:T(8,128)(2,1)} %refs_2_.4, bf16[1,768,768]{2,1,0:T(8,128)(2,1)} %copy-done.23, bf16[1,768,768]{2,1,0:T(8,128)(2,1)} %refs_4_.1, ...), custom_call_target="tpu_custom_call" | custom-call | flops 6000000000 | tf_op jit(solution)/shard_map/pallas_call | solution.py:66
  79.1 2.9 %collective-permute-start.27 = (bf16[40,768]{1,0:T(8,128)(2,1)S(1)}, bf16[40,768]{1,0:T(8,128)(2,1)S(1)}, u32[]{:S(2)}, u32[]{:S(2)}) collective-permute-start(bf16[40,768]{1,0:T(8,128)(2,1)S(1)} %get-tuple-element.243), channel_id=1, source_target_pairs={{0,16},{4,20},{8,24},{12,28},{16,0},{20,4},{24,8},{28,12},{1,17},{... | collective-permute-start | bytes 184328 | tf_op jit(solution)/shard_map/ppermute | solution.py:44
  84.5 2.9 %collective-permute-start.30 = (bf16[40,768]{1,0:T(8,128)(2,1)S(1)}, bf16[40,768]{1,0:T(8,128)(2,1)S(1)}, u32[]{:S(2)}, u32[]{:S(2)}) collective-permute-start(bf16[40,768]{1,0:T(8,128)(2,1)S(1)} %get-tuple-element.239), channel_id=1, source_target_pairs={{0,16},{4,20},{8,24},{12,28},{16,0},{20,4},{24,8},{28,12},{1,17},{... | collective-permute-start | bytes 184328 | tf_op jit(solution)/shard_map/ppermute | solution.py:44
  89.7 3.8 %collective-permute-done.31 = bf16[40,768]{1,0:T(8,128)(2,1)S(1)} collective-permute-done((bf16[40,768]{1,0:T(8,128)(2,1)S(1)}, bf16[40,768]{1,0:T(8,128)(2,1)S(1)}, u32[]{:S(2)}, u32[]{:S(2)}) %collective-permute-start.31) | collective-permute-done | bytes 61472 | tf_op jit(solution)/shard_map/ppermute | solution.py:44
  94.2 4.5 %shard_map.199 = (bf16[1,768,768]{2,1,0:T(8,128)(2,1)}, bf16[1,768,768]{2,1,0:T(8,128)(2,1)}) custom-call(bf16[160,768]{1,0:T(8,128)(2,1)} %copy-done.9, bf16[160,768]{1,0:T(8,128)(2,1)} %copy-done.25, bf16[160,768]{1,0:T(8,128)(2,1)} %copy-done.10, bf16[160,768]{1,0:T(8,128)(2,1)} %copy-done.26, bf16[2,320,768]{2,1,0:T(8,128)(2,1)} %get-tuple-element.167.hidden, ...), custom_call_target="tpu_custom_call" | custom-call | flops 4000000000 | tf_op jit(solution)/shard_map/pallas_call | solution.py:66
  104.5 3.7 %collective-permute-done.33.refs_11_ = bf16[128,768]{1,0:T(8,128)(2,1)S(1)} collective-permute-done((bf16[128,768]{1,0:T(8,128)(2,1)S(1)}, bf16[128,768]{1,0:T(8,128)(2,1)S(1)}, u32[]{:S(2)}, u32[]{:S(2)}) %collective-permute-start.33) | collective-permute-done | bytes 196640 | tf_op jit(solution)/shard_map/ppermute | solution.py:44
  110.4 8.8 %shard_map.200 = (bf16[2,5,24,640]{3,2,1,0:T(8,128)(2,1)}, bf16[2,5,24,640]{3,2,1,0:T(8,128)(2,1)}, bf16[2,5,24,640]{3,2,1,0:T(8,128)(2,1)}, bf16[2,5,24,640]{3,...) custom-call(bf16[512,576]{1,0:T(8,128)(2,1)} %get-tuple-element.172., ...), custom_call_target="tpu_custom_call" | custom-call | flops 8000000000 | tf_op jit(solution)/shard_map/pallas_call | solution.py:66
  123.5 5.9 %collective-permute-done.52 = bf16[128,768]{1,0:T(8,128)(2,1)S(1)} collective-permute-done((bf16[128,768]{1,0:T(8,128)(2,1)S(1)}, bf16[128,768]{1,0:T(8,128)(2,1)S(1)}, u32[]{:S(2)}, u32[]{:S(2)}) %collective-permute-start.52) | collective-permute-done | bytes 196640 | tf_op jit(solution)/shard_map/ppermute | solution.py:44
  131.2 6.8 %collective-permute-done.39 = bf16[2,5,24,640]{3,2,1,0:T(8,128)(2,1)S(1)} collective-permute-done((bf16[2,5,24,640]{3,2,1,0:T(8,128)(2,1)S(1)}, bf16[2,5,24,640]{3,2,1,0:T(8,128)(2,1)S(1)}, u32[]{:S(2)}, u32[]{:S(2)}) %collective-permute-start.39) | collective-permute-done | bytes 307232 | tf_op jit(solution)/shard_map/ppermute | solution.py:44
  138.2 5.8 %shard_map.201 = (f32[1,768,768]{2,1,0:T(8,128)}, f32[1,768,768]{2,1,0:T(8,128)}) custom-call(bf16[160,768]{1,0:T(8,128)(2,1)} %copy-done.9, bf16[160,768]{1,0:T(8,128)(2,1)} %copy-done.25, bf16[160,768]{1,0:T(8,128)(2,1)} %copy-done.10, bf16[160,768]{1,0:T(8,128)(2,1)} %copy-done.26, bf16[2,320,768]{2,1,0:T(8,128)(2,1)} %get-tuple-element.167.hidden, ...), custom_call_target="tpu_custom_call" | custom-call | flops 4000000000 | tf_op jit(solution)/shard_map/pallas_call | solution.py:66
  146.5 2.0 %collective-permute-done.44 = bf16[24,640]{1,0:T(8,128)(2,1)S(1)} collective-permute-done((bf16[24,640]{1,0:T(8,128)(2,1)S(1)}, bf16[24,640]{1,0:T(8,128)(2,1)S(1)}, u32[]{:S(2)}, u32[]{:S(2)}) %collective-permute-start.44) | collective-permute-done | bytes 30752 | tf_op jit(solution)/shard_map/ppermute | solution.py:44
  149.1 1.9 %collective-permute-start.47 = (bf16[5,24,640]{2,1,0:T(8,128)(2,1)S(1)}, bf16[5,24,640]{2,1,0:T(8,128)(2,1)S(1)}, u32[]{:S(2)}, u32[]{:S(2)}) collective-permute-start(bf16[5,24,640]{2,1,0:T(8,128)(2,1)S(1)} %slice_dynamic-update-slice_fusion.refs_0_), channel_id=1, source_target_pairs={{0,8},{4,12},{8,0},{12,4},{16,24},{20,28},{24,16},{28,20},{1,9},{5... | collective-permute-start | bytes 460808 | tf_op jit(solution)/shard_map/ppermute | solution.py:44
  151.6 2.1 %collective-permute-start.46 = (bf16[5,24,640]{2,1,0:T(8,128)(2,1)S(1)}, bf16[5,24,640]{2,1,0:T(8,128)(2,1)S(1)}, u32[]{:S(2)}, u32[]{:S(2)}) collective-permute-start(bf16[5,24,640]{2,1,0:T(8,128)(2,1)S(1)} %slice_dynamic-update-slice_fusion.refs_0_), channel_id=1, source_target_pairs={{0,16},{4,20},{8,24},{12,28},{16,0},{20,4},{24,8},{28,12},{1,17},{... | collective-permute-start | bytes 460808 | tf_op jit(solution)/shard_map/ppermute | solution.py:44
  153.7 3.1 %collective-permute-done.47.refs_2_ = bf16[5,24,640]{2,1,0:T(8,128)(2,1)S(1)} collective-permute-done((bf16[5,24,640]{2,1,0:T(8,128)(2,1)S(1)}, bf16[5,24,640]{2,1,0:T(8,128)(2,1)S(1)}, u32[]{:S(2)}, u32[]{:S(2)}) %collective-permute-start.47) | collective-permute-done | bytes 153632 | tf_op jit(solution)/shard_map/ppermute | solution.py:44
  158.1 3.3 %collective-permute-done.46.refs_4_ = bf16[5,24,640]{2,1,0:T(8,128)(2,1)S(1)} collective-permute-done((bf16[5,24,640]{2,1,0:T(8,128)(2,1)S(1)}, bf16[5,24,640]{2,1,0:T(8,128)(2,1)S(1)}, u32[]{:S(2)}, u32[]{:S(2)}) %collective-permute-start.46) | collective-permute-done | bytes 153632 | tf_op jit(solution)/shard_map/ppermute | solution.py:44
  164.6 2.7 %collective-permute-done.50.refs_6_ = bf16[5,24,640]{2,1,0:T(8,128)(2,1)S(1)} collective-permute-done((bf16[5,24,640]{2,1,0:T(8,128)(2,1)S(1)}, bf16[5,24,640]{2,1,0:T(8,128)(2,1)S(1)}, u32[]{:S(2)}, u32[]{:S(2)}) %collective-permute-start.50) | collective-permute-done | bytes 153632 | tf_op jit(solution)/shard_map/ppermute | solution.py:44
  170.3 2.2 %collective-permute-done.54.refs_7_ = bf16[5,24,640]{2,1,0:T(8,128)(2,1)S(1)} collective-permute-done((bf16[5,24,640]{2,1,0:T(8,128)(2,1)S(1)}, bf16[5,24,640]{2,1,0:T(8,128)(2,1)S(1)}, u32[]{:S(2)}, u32[]{:S(2)}) %collective-permute-start.54) | collective-permute-done | bytes 153632 | tf_op jit(solution)/shard_map/ppermute | solution.py:44
  173.2 3.2 %shard_map.202 = (f32[192,2304]{1,0:T(8,128)}, f32[192,768]{1,0:T(8,128)}, f32[1,192]{1,0:T(1,128)}, f32[1,192]{1,0:T(1,128)}, f32[8,192]{1,0:T(8,128)}) custom-call(bf16[5,24,640]{2,1,0:T(8,128)(2,1)} %copy-done.11, bf16[5,24,640]{2,1,0:T(8,128)(2,1)} %copy-done.14, bf16[5,24,640]{2,1,0:T(8,128)(2,1)} %copy-done.13, bf16[5,24,640]{2,1,0:T(8,128)(2,1)} %copy-done.16, ...), custom_call_target="tpu_custom_call" | custom-call | tf_op jit(solution)/shard_map/pallas_call | solution.py:66
  (224 shorter events, 57.6 us)
Async XLA Ops:
  0.7 8.7 %collective-permute-start = (bf16[128,768]{1,0:T(8,128)(2,1)}, bf16[128,768]{1,0:T(8,128)(2,1)S(1)}, u32[]{:S(2)}, u32[]{:S(2)}) collective-permute-start(bf16[128,768]{1,0:T(8,128)(2,1)} %refs_2_.2), channel_id=1, source_target_pairs={{0,2},{1,3},{2,0},{3,1},{4,6},{5,7},{6,4},{7,5},{8,10},{9,11},{10,... | collective-permute-start | bytes 589832 | tf_op jit(solution)/shard_map/ppermute | solution.py:44
  3.7 6.5 %collective-permute-start.1 = (bf16[128,768]{1,0:T(8,128)(2,1)}, bf16[128,768]{1,0:T(8,128)(2,1)S(1)}, u32[]{:S(2)}, u32[]{:S(2)}) collective-permute-start(bf16[128,768]{1,0:T(8,128)(2,1)} %refs_2_.2), channel_id=1, source_target_pairs={{0,1},{1,0},{2,3},{3,2},{4,5},{5,4},{6,7},{7,6},{8,9},{9,8},{10,11... | collective-permute-start | bytes 589832 | tf_op jit(solution)/shard_map/ppermute | solution.py:44
  6.7 9.0 %collective-permute-start.4 = (bf16[192,640]{1,0:T(8,128)(2,1)}, bf16[192,640]{1,0:T(8,128)(2,1)S(1)}, u32[]{:S(2)}, u32[]{:S(2)}) collective-permute-start(bf16[192,640]{1,0:T(8,128)(2,1)} %get-tuple-element.120), channel_id=1, source_target_pairs={{0,2},{1,3},{2,0},{3,1},{4,6},{5,7},{6,4},{7,5},{8,10},{9,11},{10,... | collective-permute-start | bytes 737288 | tf_op jit(solution)/shard_map/ppermute | solution.py:44
  6.8 12.3 %collective-permute-start.5 = (bf16[192,640]{1,0:T(8,128)(2,1)}, bf16[192,640]{1,0:T(8,128)(2,1)S(1)}, u32[]{:S(2)}, u32[]{:S(2)}) collective-permute-start(bf16[192,640]{1,0:T(8,128)(2,1)} %get-tuple-element.121), channel_id=1, source_target_pairs={{0,3},{1,2},{2,1},{3,0},{4,7},{5,6},{6,5},{7,4},{8,11},{9,10},{10,... | collective-permute-start | bytes 737288 | tf_op jit(solution)/shard_map/ppermute | solution.py:44
  9.3 18.8 %collective-permute-start.6 = (bf16[1,768,768]{2,1,0:T(8,128)(2,1)}, bf16[1,768,768]{2,1,0:T(8,128)(2,1)S(1)}, u32[]{:S(2)}, u32[]{:S(2)}) collective-permute-start(bf16[1,768,768]{2,1,0:T(8,128)(2,1)} %refs_2_.4), channel_id=1, source_target_pairs={{0,1},{1,0},{2,3},{3,2},{4,5},{5,4},{6,7},{7,6},{8,9},{9,8},{10,11... | collective-permute-start | bytes 3538952 | tf_op jit(solution)/shard_map/ppermute | solution.py:44
  10.1 18.0 %collective-permute-start.7 = (bf16[1,768,768]{2,1,0:T(8,128)(2,1)}, bf16[1,768,768]{2,1,0:T(8,128)(2,1)}, u32[]{:S(2)}, u32[]{:S(2)}) collective-permute-start(bf16[1,768,768]{2,1,0:T(8,128)(2,1)} %refs_4_.1), channel_id=1, source_target_pairs={{0,1},{1,0},{2,3},{3,2},{4,5},{5,4},{6,7},{7,6},{8,9},{9,8},{10,11... | collective-permute-start | bytes 3538952 | tf_op jit(solution)/shard_map/ppermute | solution.py:44
  11.1 8.0 %collective-permute-start.2 = (bf16[128,768]{1,0:T(8,128)(2,1)S(1)}, bf16[128,768]{1,0:T(8,128)(2,1)S(1)}, u32[]{:S(2)}, u32[]{:S(2)}) collective-permute-start(bf16[128,768]{1,0:T(8,128)(2,1)S(1)} %collective-permute-done.refs_4_), channel_id=1, source_target_pairs={{0,1},{1,0},{2,3},{3,2},{4,5},{5,4},{6,7},{7,6},{8,9},{9,8},{10,11... | collective-permute-start | bytes 589832 | tf_op jit(solution)/shard_map/ppermute | solution.py:44
  19.1 9.0 %collective-permute-start.8 = (bf16[192,768]{1,0:T(8,128)(2,1)}, bf16[192,768]{1,0:T(8,128)(2,1)S(1)}, u32[]{:S(2)}, u32[]{:S(2)}) collective-permute-start(bf16[192,768]{1,0:T(8,128)(2,1)} %refs_6_), channel_id=1, source_target_pairs={{0,1},{1,0},{2,3},{3,2},{4,5},{5,4},{6,7},{7,6},{8,9},{9,8},{10,11... | collective-permute-start | bytes 884744 | tf_op jit(solution)/shard_map/ppermute | solution.py:44
  20.0 9.4 %collective-permute-start.11 = (bf16[192,768]{1,0:T(8,128)(2,1)}, bf16[192,768]{1,0:T(8,128)(2,1)S(1)}, u32[]{:S(2)}, u32[]{:S(2)}) collective-permute-start(bf16[192,768]{1,0:T(8,128)(2,1)} %refs_6_), channel_id=1, source_target_pairs={{0,2},{1,3},{2,0},{3,1},{4,6},{5,7},{6,4},{7,5},{8,10},{9,11},{10,... | collective-permute-start | bytes 884744 | tf_op jit(solution)/shard_map/ppermute | solution.py:44
  41.2 6.4 %collective-permute-start.15 = (bf16[80,768]{1,0:T(8,128)(2,1)S(1)}, bf16[80,768]{1,0:T(8,128)(2,1)S(1)}, u32[]{:S(2)}, u32[]{:S(2)}) collective-permute-start(bf16[80,768]{1,0:T(8,128)(2,1)S(1)} %convolution_convert_fusion.1), channel_id=1, source_target_pairs={{0,4},{4,0},{8,12},{12,8},{16,20},{20,16},{24,28},{28,24},{1,5},{5... | collective-permute-start | bytes 368648 | tf_op jit(solution)/shard_map/ppermute | solution.py:44
  44.8 6.4 %collective-permute-start.17 = (bf16[40,768]{1,0:T(8,128)(2,1)S(1)}, bf16[40,768]{1,0:T(8,128)(2,1)S(1)}, u32[]{:S(2)}, u32[]{:S(2)}) collective-permute-start(bf16[40,768]{1,0:T(8,128)(2,1)S(1)} %get-tuple-element.237), channel_id=1, source_target_pairs={{0,16},{4,20},{8,24},{12,28},{16,0},{20,4},{24,8},{28,12},{1,17},{... | collective-permute-start | bytes 184328 | tf_op jit(solution)/shard_map/ppermute | solution.py:44
  47.3 6.0 %collective-permute-start.18 = (bf16[40,768]{1,0:T(8,128)(2,1)S(1)}, bf16[40,768]{1,0:T(8,128)(2,1)S(1)}, u32[]{:S(2)}, u32[]{:S(2)}) collective-permute-start(bf16[40,768]{1,0:T(8,128)(2,1)S(1)} %get-tuple-element.236), channel_id=1, source_target_pairs={{0,24},{4,28},{8,16},{12,20},{16,8},{20,12},{24,0},{28,4},{1,25},{... | collective-permute-start | bytes 184328 | tf_op jit(solution)/shard_map/ppermute | solution.py:44
  53.4 9.7 %collective-permute-start.19 = (bf16[160,768]{1,0:T(8,128)(2,1)S(1)}, bf16[160,768]{1,0:T(8,128)(2,1)S(1)}, u32[]{:S(2)}, u32[]{:S(2)}) collective-permute-start(bf16[160,768]{1,0:T(8,128)(2,1)S(1)} %pad_maximum_fusion.1.refs_0_.own), channel_id=1, source_target_pairs={{0,2},{1,3},{2,0},{3,1},{4,6},{5,7},{6,4},{7,5},{8,10},{9,11},{10,... | collective-permute-start | bytes 737288 | tf_op jit(solution)/shard_map/ppermute | solution.py:44
  55.9 6.1 %collective-permute-start.23 = (bf16[40,768]{1,0:T(8,128)(2,1)S(1)}, bf16[40,768]{1,0:T(8,128)(2,1)S(1)}, u32[]{:S(2)}, u32[]{:S(2)}) collective-permute-start(bf16[40,768]{1,0:T(8,128)(2,1)S(1)} %get-tuple-element.247), channel_id=1, source_target_pairs={{0,24},{4,28},{8,16},{12,20},{16,8},{20,12},{24,0},{28,4},{1,25},{... | collective-permute-start | bytes 184328 | tf_op jit(solution)/shard_map/ppermute | solution.py:44
  62.0 8.8 %collective-permute-start.24 = (bf16[160,768]{1,0:T(8,128)(2,1)S(1)}, bf16[160,768]{1,0:T(8,128)(2,1)S(1)}, u32[]{:S(2)}, u32[]{:S(2)}) collective-permute-start(bf16[160,768]{1,0:T(8,128)(2,1)S(1)} %pad_maximum_fusion.2.refs_0_.own_grad), channel_id=1, source_target_pairs={{0,2},{1,3},{2,0},{3,1},{4,6},{5,7},{6,4},{7,5},{8,10},{9,11},{10,... | collective-permute-start | bytes 737288 | tf_op jit(solution)/shard_map/ppermute | solution.py:44
  69.8 8.6 %collective-permute-start.20 = (bf16[160,768]{1,0:T(8,128)(2,1)}, bf16[160,768]{1,0:T(8,128)(2,1)S(1)}, u32[]{:S(2)}, u32[]{:S(2)}) collective-permute-start(bf16[160,768]{1,0:T(8,128)(2,1)} %get-tuple-element.149), channel_id=1, source_target_pairs={{0,2},{1,3},{2,0},{3,1},{4,6},{5,7},{6,4},{7,5},{8,10},{9,11},{10,... | collective-permute-start | bytes 737288 | tf_op jit(solution)/shard_map/ppermute | solution.py:44
  77.3 6.4 %collective-permute-start.25 = (bf16[160,768]{1,0:T(8,128)(2,1)}, bf16[160,768]{1,0:T(8,128)(2,1)S(1)}, u32[]{:S(2)}, u32[]{:S(2)}) collective-permute-start(bf16[160,768]{1,0:T(8,128)(2,1)} %get-tuple-element.152), channel_id=1, source_target_pairs={{0,2},{1,3},{2,0},{3,1},{4,6},{5,7},{6,4},{7,5},{8,10},{9,11},{10,... | collective-permute-start | bytes 737288 | tf_op jit(solution)/shard_map/ppermute | solution.py:44
  79.1 9.1 %collective-permute-start.27 = (bf16[40,768]{1,0:T(8,128)(2,1)S(1)}, bf16[40,768]{1,0:T(8,128)(2,1)S(1)}, u32[]{:S(2)}, u32[]{:S(2)}) collective-permute-start(bf16[40,768]{1,0:T(8,128)(2,1)S(1)} %get-tuple-element.243), channel_id=1, source_target_pairs={{0,16},{4,20},{8,24},{12,28},{16,0},{20,4},{24,8},{28,12},{1,17},{... | collective-permute-start | bytes 184328 | tf_op jit(solution)/shard_map/ppermute | solution.py:44
  82.1 6.2 %collective-permute-start.28 = (bf16[40,768]{1,0:T(8,128)(2,1)S(1)}, bf16[40,768]{1,0:T(8,128)(2,1)S(1)}, u32[]{:S(2)}, u32[]{:S(2)}) collective-permute-start(bf16[40,768]{1,0:T(8,128)(2,1)S(1)} %get-tuple-element.242), channel_id=1, source_target_pairs={{0,24},{4,28},{8,16},{12,20},{16,8},{20,12},{24,0},{28,4},{1,25},{... | collective-permute-start | bytes 184328 | tf_op jit(solution)/shard_map/ppermute | solution.py:44
  87.5 6.0 %collective-permute-start.31 = (bf16[40,768]{1,0:T(8,128)(2,1)S(1)}, bf16[40,768]{1,0:T(8,128)(2,1)S(1)}, u32[]{:S(2)}, u32[]{:S(2)}) collective-permute-start(bf16[40,768]{1,0:T(8,128)(2,1)S(1)} %get-tuple-element.238), channel_id=1, source_target_pairs={{0,24},{4,28},{8,16},{12,20},{16,8},{20,12},{24,0},{28,4},{1,25},{... | collective-permute-start | bytes 184328 | tf_op jit(solution)/shard_map/ppermute | solution.py:44
  93.7 6.3 %collective-permute-start.32 = (bf16[80,1536]{1,0:T(8,128)(2,1)S(1)}, bf16[80,1536]{1,0:T(8,128)(2,1)S(1)}, u32[]{:S(2)}, u32[]{:S(2)}) collective-permute-start(bf16[80,1536]{1,0:T(8,128)(2,1)S(1)} %maximum_maximum_fusion), channel_id=1, source_target_pairs={{0,4},{4,0},{8,12},{12,8},{16,20},{20,16},{24,28},{28,24},{1,5},{5... | collective-permute-start | bytes 737288 | tf_op jit(solution)/shard_map/ppermute | solution.py:44
  109.7 19.7 %collective-permute-start.37 = (bf16[1,768,768]{2,1,0:T(8,128)(2,1)}, bf16[1,768,768]{2,1,0:T(8,128)(2,1)}, u32[]{:S(2)}, u32[]{:S(2)}) collective-permute-start(bf16[1,768,768]{2,1,0:T(8,128)(2,1)} %get-tuple-element.190), channel_id=1, source_target_pairs={{0,1},{1,0},{2,3},{3,2},{4,5},{5,4},{6,7},{7,6},{8,9},{9,8},{10,11... | collective-permute-start | bytes 3538952 | tf_op jit(solution)/shard_map/ppermute | solution.py:44
  109.8 19.5 %collective-permute-start.38 = (bf16[1,768,768]{2,1,0:T(8,128)(2,1)}, bf16[1,768,768]{2,1,0:T(8,128)(2,1)}, u32[]{:S(2)}, u32[]{:S(2)}) collective-permute-start(bf16[1,768,768]{2,1,0:T(8,128)(2,1)} %get-tuple-element.191), channel_id=1, source_target_pairs={{0,1},{1,0},{2,3},{3,2},{4,5},{5,4},{6,7},{7,6},{8,9},{9,8},{10,11... | collective-permute-start | bytes 3538952 | tf_op jit(solution)/shard_map/ppermute | solution.py:44
  119.4 9.9 %collective-permute-start.36 = (bf16[2,5,24,640]{3,2,1,0:T(8,128)(2,1)}, bf16[2,5,24,640]{3,2,1,0:T(8,128)(2,1)S(1)}, u32[]{:S(2)}, u32[]{:S(2)}) collective-permute-start(bf16[2,5,24,640]{3,2,1,0:T(8,128)(2,1)} %get-tuple-element.188), channel_id=1, source_target_pairs={{0,4},{4,0},{8,12},{12,8},{16,20},{20,16},{24,28},{28,24},{1,5},{5... | collective-permute-start | bytes 921608 | tf_op jit(solution)/shard_map/ppermute | solution.py:44
  122.3 7.0 %collective-permute-start.52 = (bf16[128,768]{1,0:T(8,128)(2,1)S(1)}, bf16[128,768]{1,0:T(8,128)(2,1)S(1)}, u32[]{:S(2)}, u32[]{:S(2)}) collective-permute-start(bf16[128,768]{1,0:T(8,128)(2,1)S(1)} %fusion.33), channel_id=1, source_target_pairs={{0,2},{1,3},{2,0},{3,1},{4,6},{5,7},{6,4},{7,5},{8,10},{9,11},{10,... | collective-permute-start | bytes 589832 | tf_op jit(solution)/shard_map/ppermute | solution.py:44
  129.4 8.6 %collective-permute-start.39 = (bf16[2,5,24,640]{3,2,1,0:T(8,128)(2,1)S(1)}, bf16[2,5,24,640]{3,2,1,0:T(8,128)(2,1)S(1)}, u32[]{:S(2)}, u32[]{:S(2)}) collective-permute-start(bf16[2,5,24,640]{3,2,1,0:T(8,128)(2,1)S(1)} %copy-done.24), channel_id=1, source_target_pairs={{0,4},{4,0},{8,12},{12,8},{16,20},{20,16},{24,28},{28,24},{1,5},{5... | collective-permute-start | bytes 921608 | tf_op jit(solution)/shard_map/ppermute | solution.py:44
  130.2 13.8 %collective-permute-start.40 = (bf16[5,24,640]{2,1,0:T(8,128)(2,1)S(1)}, bf16[5,24,640]{2,1,0:T(8,128)(2,1)S(1)}, u32[]{:S(2)}, u32[]{:S(2)}) collective-permute-start(bf16[5,24,640]{2,1,0:T(8,128)(2,1)S(1)} %get-tuple-element.233), channel_id=1, source_target_pairs={{0,16},{4,20},{8,24},{12,28},{16,0},{20,4},{24,8},{28,12},{1,17},{... | collective-permute-start | bytes 460808 | tf_op jit(solution)/shard_map/ppermute | solution.py:44
  130.3 13.7 %collective-permute-start.41 = (bf16[5,24,640]{2,1,0:T(8,128)(2,1)S(1)}, bf16[5,24,640]{2,1,0:T(8,128)(2,1)S(1)}, u32[]{:S(2)}, u32[]{:S(2)}) collective-permute-start(bf16[5,24,640]{2,1,0:T(8,128)(2,1)S(1)} %get-tuple-element.232), channel_id=1, source_target_pairs={{0,24},{4,28},{8,16},{12,20},{16,8},{20,12},{24,0},{28,4},{1,25},{... | collective-permute-start | bytes 460808 | tf_op jit(solution)/shard_map/ppermute | solution.py:44
  138.1 6.1 %collective-permute-start.42 = (bf16[5,24,640]{2,1,0:T(8,128)(2,1)S(1)}, bf16[5,24,640]{2,1,0:T(8,128)(2,1)S(1)}, u32[]{:S(2)}, u32[]{:S(2)}) collective-permute-start(bf16[5,24,640]{2,1,0:T(8,128)(2,1)S(1)} %fusion.34), channel_id=1, source_target_pairs={{0,8},{4,12},{8,0},{12,4},{16,24},{20,28},{24,16},{28,20},{1,9},{5... | collective-permute-start | bytes 460808 | tf_op jit(solution)/shard_map/ppermute | solution.py:44
  149.1 7.7 %collective-permute-start.47 = (bf16[5,24,640]{2,1,0:T(8,128)(2,1)S(1)}, bf16[5,24,640]{2,1,0:T(8,128)(2,1)S(1)}, u32[]{:S(2)}, u32[]{:S(2)}) collective-permute-start(bf16[5,24,640]{2,1,0:T(8,128)(2,1)S(1)} %slice_dynamic-update-slice_fusion.refs_0_), channel_id=1, source_target_pairs={{0,8},{4,12},{8,0},{12,4},{16,24},{20,28},{24,16},{28,20},{1,9},{5... | collective-permute-start | bytes 460808 | tf_op jit(solution)/shard_map/ppermute | solution.py:44
  151.6 9.8 %collective-permute-start.46 = (bf16[5,24,640]{2,1,0:T(8,128)(2,1)S(1)}, bf16[5,24,640]{2,1,0:T(8,128)(2,1)S(1)}, u32[]{:S(2)}, u32[]{:S(2)}) collective-permute-start(bf16[5,24,640]{2,1,0:T(8,128)(2,1)S(1)} %slice_dynamic-update-slice_fusion.refs_0_), channel_id=1, source_target_pairs={{0,16},{4,20},{8,24},{12,28},{16,0},{20,4},{24,8},{28,12},{1,17},{... | collective-permute-start | bytes 460808 | tf_op jit(solution)/shard_map/ppermute | solution.py:44
  163.9 6.4 %collective-permute-start.53 = (bf16[5,24,640]{2,1,0:T(8,128)(2,1)S(1)}, bf16[5,24,640]{2,1,0:T(8,128)(2,1)S(1)}, u32[]{:S(2)}, u32[]{:S(2)}) collective-permute-start(bf16[5,24,640]{2,1,0:T(8,128)(2,1)S(1)} %collective-permute-done.46.refs_4_), channel_id=1, source_target_pairs={{0,4},{4,0},{8,12},{12,8},{16,20},{20,16},{24,28},{28,24},{1,5},{5... | collective-permute-start | bytes 460808 | tf_op jit(solution)/shard_map/ppermute | solution.py:44
  (59 other events, 369.4 us)

commit v9 on v8

--- a/solution.py
+++ b/solution.py
@@ -207,13 +207,10 @@
     projected, tokens, gains, weight, weights, mixed, weight_out, gain_two, router = refs[:9]
     branch_refs = refs[9 : 9 + n]
     at = 9 + n
-    shares = 4 if m > 1 else 2
+    shares = 5 if m > 1 else 2
     share_out = refs[at : at + shares]
-    normed_grad_out = refs[at + shares : at + shares + 2]
-    gain_out, table_out = refs[at + shares + 2 : at + shares + 4]
-    branch_scr, scores_scr, projected_scr, total_scr, out_scr, normed_scr, send_scr, weights_scr = (
-        refs[at + shares + 4 :]
-    )
+    projected_scr, gain_out, table_out = refs[at + shares : at + shares + 3]
+    branch_scr, scores_scr, total_scr, out_scr, normed_scr, weights_scr = refs[at + shares + 3 :]
     s = lax.axis_index("shard")
     e = lax.axis_index("expert")
     part = width // n
@@ -278,21 +275,19 @@
         )
     table_out[...] = table_total
     grad_projected = projected_scr[...]
-    normed_grad = dot_nt(grad_projected, weight[:, :wide])
-    send_scr[...] = normed_grad.astype(bf16).reshape(n, rows, width)
-    for p in range(n):
-        normed_grad_out[p & 1][p >> 1] = send_scr[s ^ p]
     gain = gains[...]
-    grad_gain = jnp.zeros((1, width), f32)
     for j in range(n):
         value = tokens[j].astype(f32)
         unit = value * lax.rsqrt(jnp.mean(value * value, axis=-1, keepdims=True) + norm_eps)
         normed_scr[j * rows : (j + 1) * rows, :] = (unit * gain).astype(bf16)
-        grad_gain = grad_gain + jnp.sum(
-            normed_grad[j * rows : (j + 1) * rows, :] * unit, axis=0, keepdims=True
-        )
-    gain_out[...] = jnp.broadcast_to(grad_gain, gain_out.shape)
-    total_scr[:, :wide] = dot_tn(normed_scr[...], grad_projected)
+    grad_weight = dot_tn(normed_scr[...], grad_projected)
+    total_scr[:, :wide] = grad_weight
+    grad_gain = jnp.sum(grad_weight * weight[:, :wide].astype(f32), axis=1, keepdims=True)
+    grad_gain = grad_gain / weight[:, wide : wide + 1].astype(f32)
+    size = 128
+    for c in range(width // size):
+        here = slice(c * size, (c + 1) * size)
+        gain_out[:, here] = to_row(grad_gain[here], size)
     full = total_scr.shape[1]
     if m == 1:
         for t in range(n):
@@ -302,10 +297,9 @@
     piece = part // m
     total_scr[:, wide:] = jnp.zeros((width, full - wide), f32)
     grad_two = gain_two[...].reshape(1, width)
-    size = 128
+    total_scr[:, wide : wide + 1] = grad_gain
     for c in range(width // size):
         here = slice(c * size, (c + 1) * size)
-        total_scr[here, wide : wide + 1] = to_column(grad_gain[:, here], size)
         total_scr[here, wide + 1 : wide + 2] = to_column(grad_two[:, here], size)
         total_scr[here, wide + 2 : wide + 2 + experts] = router[:, here].T
     at = wide + 2 + experts
@@ -319,15 +313,27 @@
         total_scr[d * piece : d * piece + row_tile, at : at + heads * per_line] = table_total[
             :, : heads * per_line
         ]
+    near_keep, far_keep, near_send, far_send, last_send = share_out
     for d in range(m):
-        target = share_out[(d & 1) + 2 * (d < m // 2)]
         place = (d >> 1) % (m // 4)
+        target = (far_send if d & 1 else far_keep) if d >= m // 2 else (near_send if d & 1 else near_keep)
+        if d == m - 1:
+            target, place = last_send, 0
         start = (e ^ d) * piece
         for t in range(n):
             rows_at = pl.multiple_of(t * part + start, row_tile)
             target[place, t] = total_scr[pl.ds(rows_at, piece), :].astype(bf16)
         rows_at = pl.multiple_of(start, row_tile)
         target[place, n] = out_scr[pl.ds(rows_at, piece), :full].astype(bf16)
+
+
+def normed_backward(n, rows, projected, weight, keep_out, send_out, send_scr):
+    s = lax.axis_index("shard")
+    wide = projected.shape[1]
+    grad = dot_nt(projected[...], weight[:, :wide])
+    send_scr[...] = grad.astype(bf16).reshape(send_scr.shape)
+    for p in range(n):
+        (send_out if p & 1 else keep_out)[p >> 1] = send_scr[s ^ p]
 
 
 def beside_columns(ref, p, wide):
@@ -654,15 +660,17 @@
     holders = m if direct else 1
     piece = part // m
     if direct:
-        share_shapes = [shape((m // 4, n + 1, piece, full))] * 4
+        share_shapes = [
+            shape((held, n + 1, piece, full)) for held in (m // 4, m // 4, m // 4, m // 4 - 1, 1)
+        ]
     else:
         share_shapes = [shape((n, part, wide)), shape((part, width))]
     answers = call(
         lambda *refs: attention_backward(n, holders, rows, width, heads, buckets, experts, *refs),
         (
             *share_shapes,
-            *[shape((n // 2, rows, width))] * 2,
-            shape((row_tile, width), f32),
+            shape((group, wide)),
+            shape((1, width), f32),
             shape((row_tile, 128), f32),
         ),
         (
@@ -681,17 +689,15 @@
         [
             pltpu.VMEM((n, rows, width), bf16),
             pltpu.VMEM((group, group), bf16),
-            pltpu.VMEM((group, wide), bf16),
             pltpu.VMEM((width, full), f32),
             pltpu.VMEM((part, width), f32),
             pltpu.VMEM((group, width), bf16),
-            pltpu.VMEM((n, rows, width), bf16),
             pltpu.VMEM((group, group), f32),
         ],
         work=8 * micro,
     )
     shares = answers[: len(share_shapes)]
-    normed_keep, normed_send, gain_row, table = answers[len(share_shapes) :]
+    grad_projected, gain_row, table = answers[len(share_shapes) :]
 
     def kept_weights(late_rows):
         return call(
@@ -706,26 +712,45 @@
     def biases(block):
         return block.reshape(row_tile, heads, per_line).swapaxes(0, 1).reshape(heads, buckets)
 
-    normed_sum = normed_keep.astype(f32) + swap(normed_send, "shard", pair).astype(f32)
-    far_sum = swap(normed_sum[1].astype(bf16), "shard", 2 * pair)
-    late, far_sum = lax.optimization_barrier((tokens, far_sum))
-    late = late.astype(f32)
-    grad_input_norm, _ = rms_backward(
-        late, rms_factor(late), gain_one, normed_sum[0] + far_sum.astype(f32)
-    )
-    grad_tokens = (grad_hidden + grad_input_norm).astype(bf16)
+    def normed_gradients(projected):
+        return call(
+            lambda *refs: normed_backward(n, rows, *refs),
+            [shape((n // 2, rows, width))] * 2,
+            (projected, weight),
+            "",
+            [pltpu.VMEM((n, rows, width), bf16)],
+            work=2 * micro,
+        )
+
+    def finish_tokens(normed_keep, pair_came):
+        normed_sum = normed_keep.astype(f32) + pair_came.astype(f32)
+        far_sum = swap(normed_sum[1].astype(bf16), "shard", 2 * pair)
+        late, far_sum = lax.optimization_barrier((tokens, far_sum))
+        late = late.astype(f32)
+        grad_input_norm, _ = rms_backward(
+            late, rms_factor(late), gain_one, normed_sum[0] + far_sum.astype(f32)
+        )
+        return (grad_hidden + grad_input_norm).astype(bf16)
+
     if direct:
-        far_keep, far_send, near_keep, near_send = shares
+        near_keep, far_keep, near_send, far_send, last_send = shares
+        last_came = swap(last_send, "expert", 1)[0]
         far_came = swap(far_send, "expert", 1)
         far_came, near_send, up_came, down_came = lax.optimization_barrier(
             (far_came, near_send, up_came, down_came)
         )
-        far = far_keep.astype(f32) + far_came.astype(f32)
-        near_came, late_rows = lax.optimization_barrier((swap(near_send, "expert", 1), row_blocks))
+        last_came, late_rows = lax.optimization_barrier((last_came, row_blocks))
+        came = [swap((far_keep[-1].astype(f32) + last_came.astype(f32)).astype(bf16), "expert", m - 2)]
+        far = far_keep[:-1].astype(f32) + far_came.astype(f32)
+        near_came, (grad_up, grad_down), grad_projected = lax.optimization_barrier(
+            (swap(near_send, "expert", 1), kept_weights(late_rows), grad_projected)
+        )
+        normed_keep, normed_send = normed_gradients(grad_projected)
+        normed_came = swap(normed_send, "shard", pair)
         near = near_keep.astype(f32) + near_came.astype(f32)
-        came = [swap(far[d].astype(bf16), "expert", m // 2 + 2 * d) for d in range(m // 4)]
+        came += [swap(far[d].astype(bf16), "expert", m // 2 + 2 * d) for d in range(m // 4 - 1)]
         came += [swap(near[d].astype(bf16), "expert", 2 * d) for d in range(1, m // 4)]
-        came, (grad_up, grad_down) = lax.optimization_barrier((came, kept_weights(late_rows)))
+        came, normed_came = lax.optimization_barrier((came, normed_came))
         summed = near[0] + sum(x.astype(f32) for x in came)
         at = wide + 2 + experts
         rest = (width - full) // n
@@ -743,7 +768,10 @@
         )
         blocks = {0: mine, 1: swap(mine, "expert", 1), 4: swap(mine, "expert", 4)}
         blocks[2] = swap(mine, "expert", 2)
-        blocks[2], blocks[1] = lax.optimization_barrier((blocks[2], blocks[1]))
+        blocks[2], blocks[1], normed_came = lax.optimization_barrier(
+            (blocks[2], blocks[1], normed_came)
+        )
+        grad_tokens = finish_tokens(normed_keep, normed_came)
         blocks[3] = swap(blocks[2], "expert", 1)
         blocks[4], blocks[3] = lax.optimization_barrier((blocks[4], blocks[3]))
         blocks[6] = swap(blocks[4], "expert", 2)
@@ -766,6 +794,8 @@
         )
     else:
         grad_up, grad_down = kept_weights(row_blocks)
+        normed_keep, normed_send = normed_gradients(grad_projected)
+        grad_tokens = finish_tokens(normed_keep, swap(normed_send, "shard", pair))
         came = lax.all_to_all(
             shares[0].reshape(n, m, piece, wide).swapaxes(0, 1), "expert", 0, 0, tiled=True
         )

time: 177 us -> 185 us (1.045)
  Pallas kernels: 43.9 us -> 48.6 us
  waiting for transfers between devices: 63.4 us -> 65.3 us
    pallas_call x8 -> x9, Pallas kernels: 43.9 us -> 48.6 us  [call(): pl.pallas_call(kernel, out_shape=out_shape, in_specs=in_specs, out_specs=...]
    convert_element_type x1 -> x3, other arithmetic: 0.88 us -> 2.96 us  [the longest x1 1.14 us: local(): far[d].astype(bf16)]
    ppermute x55 -> x56, waiting for transfers between devices: 63.4 us -> 65.3 us  [swap(): return lax.ppermute(value, axis, [(i, i ^ bit) for i in range(size)])]
    ppermute x55 -> x56, starting transfers between devices: 52.2 us -> 53 us  [swap(): return lax.ppermute(value, axis, [(i, i ^ bit) for i in range(size)])]
  transfers between devices with their start and end apart: 55 -> 56, of which waited for: 29 -> 25; matrix products, arithmetic and copies ran while one was open for 5% -> 6% of each run, Pallas kernels for 23% -> 25%
where the time goes in v9:
time: 185 us
  waiting for transfers between devices  65.3 us (35%)
  starting transfers between devices  53 us (29%)
  Pallas kernels  48.6 us (26%)
  other arithmetic  6.95 us (4%)
  matrix products  5.99 us (3%)
  local copies, waits for them, and re-layouts  3.61 us (2%)
    ppermute x56, waiting for transfers between devices, swap(): return lax.ppermute(value, axis, [(i, i ^ bit) for i in range(size)])  65.3 us
    ppermute x56, starting transfers between devices, swap(): return lax.ppermute(value, axis, [(i, i ^ bit) for i in range(size)])  53 us
    pallas_call x9, Pallas kernels, call(): pl.pallas_call(kernel, out_shape=out_shape, in_specs=in_specs, out_specs=...  48.6 us
  transfers between devices with their start and end apart: 56, of which 25 were waited for; matrix products, arithmetic and copies ran while one was open for 6% of the time, Pallas kernels for 25%

profile of v9, /device:TPU:0, one launch (start us, length us, event | category | flops | bytes accessed | tf_op | source)
XLA Modules:
  0.0 184.9 jit_solution(2882474488767943336)
XLA Ops:
  0.7 3.0 %collective-permute-start = (bf16[128,768]{1,0:T(8,128)(2,1)}, bf16[128,768]{1,0:T(8,128)(2,1)S(1)}, u32[]{:S(2)}, u32[]{:S(2)}) collective-permute-start(bf16[128,768]{1,0:T(8,128)(2,1)} %refs_2_.2), channel_id=1, source_target_pairs={{0,2},{1,3},{2,0},{3,1},{4,6},{5,7},{6,4},{7,5},{8,10},{9,11},{10,... | collective-permute-start | bytes 589832 | tf_op jit(solution)/shard_map/ppermute | solution.py:44
  3.7 2.5 %shard_map.195 = (bf16[192,640]{1,0:T(8,128)(2,1)}, bf16[192,640]{1,0:T(8,128)(2,1)}, bf16[192,640]{1,0:T(8,128)(2,1)}, bf16[192,640]{1,0:T(8,128)(2,1)}) custom-call(bf16[192,2304]{1,0:T(8,128)(2,1)} %refs_0_.2, bf16[192]{0:T(256)(128)(2,1)} %refs_1_.1, bf16[192]{0:T(256)(128)(2,1)} %refs_2_.1), custom_call_target="tpu_custom_call" | custom-call | tf_op jit(solution)/shard_map/pallas_call | solution.py:66
  12.3 3.5 %collective-permute-done.4.refs_8_ = bf16[192,640]{1,0:T(8,128)(2,1)S(1)} collective-permute-done((bf16[192,640]{1,0:T(8,128)(2,1)}, bf16[192,640]{1,0:T(8,128)(2,1)S(1)}, u32[]{:S(2)}, u32[]{:S(2)}) %collective-permute-start.4) | collective-permute-done | bytes 245792 | tf_op jit(solution)/shard_map/ppermute | solution.py:44
  15.8 3.3 %collective-permute-done.5.refs_9_ = bf16[192,640]{1,0:T(8,128)(2,1)S(1)} collective-permute-done((bf16[192,640]{1,0:T(8,128)(2,1)}, bf16[192,640]{1,0:T(8,128)(2,1)S(1)}, u32[]{:S(2)}, u32[]{:S(2)}) %collective-permute-start.5) | collective-permute-done | bytes 245792 | tf_op jit(solution)/shard_map/ppermute | solution.py:44
  21.0 7.1 %shard_map.196 = (bf16[4,128,768]{2,1,0:T(8,128)(2,1)}, bf16[768,640]{1,0:T(8,128)(2,1)}, bf16[512,576]{1,0:T(8,128)(2,1)}, bf16[3,512,512]{2,1,0:T(8,128)(2,1)}...) custom-call(s32[1,3]{1,0:T(1,128)} %refs_0_.3, ...), custom_call_target="tpu_custom_call" | custom-call | flops 10000000000 | tf_op jit(solution)/shard_map/pallas_call | solution.py:66
  30.6 2.1 %collective-permute-done.10 = bf16[128,192]{1,0:T(8,128)(2,1)S(1)} collective-permute-done((bf16[128,192]{1,0:T(8,128)(2,1)}, bf16[128,192]{1,0:T(8,128)(2,1)S(1)}, u32[]{:S(2)}, u32[]{:S(2)}) %collective-permute-start.10) | collective-permute-done | bytes 49184 | tf_op jit(solution)/shard_map/ppermute | solution.py:44
  37.7 3.0 %collective-permute-done.14 = bf16[80,768]{1,0:T(8,128)(2,1)S(1)} collective-permute-done((bf16[80,768]{1,0:T(8,128)(2,1)S(1)}, bf16[80,768]{1,0:T(8,128)(2,1)S(1)}, u32[]{:S(2)}, u32[]{:S(2)}) %collective-permute-start.14) | collective-permute-done | bytes 122912 | tf_op jit(solution)/shard_map/ppermute | solution.py:44
  42.6 3.7 %collective-permute-start.18 = (bf16[40,768]{1,0:T(8,128)(2,1)S(1)}, bf16[40,768]{1,0:T(8,128)(2,1)S(1)}, u32[]{:S(2)}, u32[]{:S(2)}) collective-permute-start(bf16[40,768]{1,0:T(8,128)(2,1)S(1)} %get-tuple-element.246), channel_id=1, source_target_pairs={{0,24},{4,28},{8,16},{12,20},{16,8},{20,12},{24,0},{28,4},{1,25},{... | collective-permute-start | bytes 184328 | tf_op jit(solution)/shard_map/ppermute | solution.py:44
  47.2 3.4 %collective-permute-done.16 = bf16[40,768]{1,0:T(8,128)(2,1)S(1)} collective-permute-done((bf16[40,768]{1,0:T(8,128)(2,1)S(1)}, bf16[40,768]{1,0:T(8,128)(2,1)S(1)}, u32[]{:S(2)}, u32[]{:S(2)}) %collective-permute-start.16) | collective-permute-done | bytes 61472 | tf_op jit(solution)/shard_map/ppermute | solution.py:44
  52.7 2.1 %collective-permute-start.23 = (bf16[40,768]{1,0:T(8,128)(2,1)S(1)}, bf16[40,768]{1,0:T(8,128)(2,1)S(1)}, u32[]{:S(2)}, u32[]{:S(2)}) collective-permute-start(bf16[40,768]{1,0:T(8,128)(2,1)S(1)} %get-tuple-element.257), channel_id=1, source_target_pairs={{0,24},{4,28},{8,16},{12,20},{16,8},{20,12},{24,0},{28,4},{1,25},{... | collective-permute-start | bytes 184328 | tf_op jit(solution)/shard_map/ppermute | solution.py:44
  54.8 2.3 %collective-permute-start.21 = (bf16[40,768]{1,0:T(8,128)(2,1)S(1)}, bf16[40,768]{1,0:T(8,128)(2,1)S(1)}, u32[]{:S(2)}, u32[]{:S(2)}) collective-permute-start(bf16[40,768]{1,0:T(8,128)(2,1)S(1)} %get-tuple-element.259), channel_id=1, source_target_pairs={{0,8},{4,12},{8,0},{12,4},{16,24},{20,28},{24,16},{28,20},{1,9},{5... | collective-permute-start | bytes 184328 | tf_op jit(solution)/shard_map/ppermute | solution.py:44
  62.3 6.0 %shard_map.197 = (bf16[2,320,768]{2,1,0:T(8,128)(2,1)}, bf16[2,320,768]{2,1,0:T(8,128)(2,1)}, f32[160,768]{1,0:T(8,128)}, bf16[160,768]{1,0:T(8,128)(2,1)}) custom-call(bf16[160,768]{1,0:T(8,128)(2,1)} %copy-done.9, bf16[160,768]{1,0:T(8,128)(2,1)} %copy-done.28, bf16[1,768,768]{2,1,0:T(8,128)(2,1)} %refs_2_.4, bf16[1,768,768]{2,1,0:T(8,128)(2,1)} %copy-done.23, ...), custom_call_target="tpu_custom_call" | custom-call | flops 6000000000 | tf_op jit(solution)/shard_map/pallas_call | solution.py:66
  70.0 5.8 %shard_map.198 = (bf16[2,320,768]{2,1,0:T(8,128)(2,1)}, f32[160,768]{1,0:T(8,128)}, bf16[160,768]{1,0:T(8,128)(2,1)}) custom-call(bf16[160,768]{1,0:T(8,128)(2,1)} %copy-done.10, bf16[160,768]{1,0:T(8,128)(2,1)} %copy-done.29, bf16[1,768,768]{2,1,0:T(8,128)(2,1)} %refs_2_.4, bf16[1,768,768]{2,1,0:T(8,128)(2,1)} %copy-done.23, bf16[1,768,768]{2,1,0:T(8,128)(2,1)} %refs_4_.1, ...), custom_call_target="tpu_custom_call" | custom-call | flops 6000000000 | tf_op jit(solution)/shard_map/pallas_call | solution.py:66
  79.6 1.8 collective-permute-start.28
  86.8 2.3 %collective-permute-done.30 = bf16[40,768]{1,0:T(8,128)(2,1)S(1)} collective-permute-done((bf16[40,768]{1,0:T(8,128)(2,1)S(1)}, bf16[40,768]{1,0:T(8,128)(2,1)S(1)}, u32[]{:S(2)}, u32[]{:S(2)}) %collective-permute-start.30) | collective-permute-done | bytes 61472 | tf_op jit(solution)/shard_map/ppermute | solution.py:44
  89.1 1.9 %collective-permute-done.31 = bf16[40,768]{1,0:T(8,128)(2,1)S(1)} collective-permute-done((bf16[40,768]{1,0:T(8,128)(2,1)S(1)}, bf16[40,768]{1,0:T(8,128)(2,1)S(1)}, u32[]{:S(2)}, u32[]{:S(2)}) %collective-permute-start.31) | collective-permute-done | bytes 61472 | tf_op jit(solution)/shard_map/ppermute | solution.py:44
  91.8 4.5 %shard_map.199 = (bf16[1,768,768]{2,1,0:T(8,128)(2,1)}, bf16[1,768,768]{2,1,0:T(8,128)(2,1)}) custom-call(bf16[160,768]{1,0:T(8,128)(2,1)} %copy-done.9, bf16[160,768]{1,0:T(8,128)(2,1)} %copy-done.28, bf16[160,768]{1,0:T(8,128)(2,1)} %copy-done.10, bf16[160,768]{1,0:T(8,128)(2,1)} %copy-done.29, bf16[2,320,768]{2,1,0:T(8,128)(2,1)} %get-tuple-element.173.hidden, ...), custom_call_target="tpu_custom_call" | custom-call | flops 4000000000 | tf_op jit(solution)/shard_map/pallas_call | solution.py:66
  102.1 3.7 %collective-permute-done.33.refs_11_ = bf16[128,768]{1,0:T(8,128)(2,1)S(1)} collective-permute-done((bf16[128,768]{1,0:T(8,128)(2,1)S(1)}, bf16[128,768]{1,0:T(8,128)(2,1)S(1)}, u32[]{:S(2)}, u32[]{:S(2)}) %collective-permute-start.33) | collective-permute-done | bytes 196640 | tf_op jit(solution)/shard_map/ppermute | solution.py:44
  107.9 10.4 %shard_map.200 = (bf16[2,5,24,640]{3,2,1,0:T(8,128)(2,1)}, bf16[2,5,24,640]{3,2,1,0:T(8,128)(2,1)}, bf16[2,5,24,640]{3,2,1,0:T(8,128)(2,1)}, bf16[1,5,24,640]{3,...) custom-call(bf16[512,576]{1,0:T(8,128)(2,1)} %get-tuple-element.178., ...), custom_call_target="tpu_custom_call" | custom-call | flops 8000000000 | tf_op jit(solution)/shard_map/pallas_call | solution.py:66
  120.4 5.0 %collective-permute-done.40 = bf16[1,5,24,640]{3,2,1,0:T(8,128)(2,1)S(1)} collective-permute-done((bf16[1,5,24,640]{3,2,1,0:T(8,128)(2,1)}, bf16[1,5,24,640]{3,2,1,0:T(8,128)(2,1)S(1)}, u32[]{:S(2)}, u32[]{:S(2)}) %collective-permute-start.40) | collective-permute-done | bytes 153632 | tf_op jit(solution)/shard_map/ppermute | solution.py:44
  126.3 1.9 %collective-permute-start.41 = (bf16[5,24,640]{2,1,0:T(8,128)(2,1)S(1)}, bf16[5,24,640]{2,1,0:T(8,128)(2,1)S(1)}, u32[]{:S(2)}, u32[]{:S(2)}) collective-permute-start(bf16[5,24,640]{2,1,0:T(8,128)(2,1)S(1)} %fusion.17), channel_id=1, source_target_pairs={{0,24},{4,28},{8,16},{12,20},{16,8},{20,12},{24,0},{28,4},{1,25},{... | collective-permute-start | bytes 460808 | tf_op jit(solution)/shard_map/ppermute | solution.py:44
  130.2 5.8 %shard_map.201 = (f32[1,768,768]{2,1,0:T(8,128)}, f32[1,768,768]{2,1,0:T(8,128)}) custom-call(bf16[160,768]{1,0:T(8,128)(2,1)} %copy-done.9, bf16[160,768]{1,0:T(8,128)(2,1)} %copy-done.28, bf16[160,768]{1,0:T(8,128)(2,1)} %copy-done.10, bf16[160,768]{1,0:T(8,128)(2,1)} %copy-done.29, bf16[2,320,768]{2,1,0:T(8,128)(2,1)} %get-tuple-element.173.hidden, ...), custom_call_target="tpu_custom_call" | custom-call | flops 4000000000 | tf_op jit(solution)/shard_map/pallas_call | solution.py:66
  136.0 1.9 %collective-permute-done.39 = bf16[2,5,24,640]{3,2,1,0:T(8,128)(2,1)S(1)} collective-permute-done((bf16[2,5,24,640]{3,2,1,0:T(8,128)(2,1)}, bf16[2,5,24,640]{3,2,1,0:T(8,128)(2,1)S(1)}, u32[]{:S(2)}, u32[]{:S(2)}) %collective-permute-start.39) | collective-permute-done | bytes 307232 | tf_op jit(solution)/shard_map/ppermute | solution.py:44
  137.9 3.1 %shard_map.202 = (bf16[2,128,768]{2,1,0:T(8,128)(2,1)}, bf16[2,128,768]{2,1,0:T(8,128)(2,1)}) custom-call(bf16[512,576]{1,0:T(8,128)(2,1)} %get-tuple-element.211.refs_0_, bf16[768,640]{1,0:T(8,128)(2,1)} %get-tuple-element.181.refs_3_.refs_1_), custom_call_target="tpu_custom_call" | custom-call | flops 2000000000 | tf_op jit(solution)/shard_map/pallas_call | solution.py:66
  141.2 2.1 %collective-permute-start.43 = (bf16[5,24,640]{2,1,0:T(8,128)(2,1)S(1)}, bf16[5,24,640]{2,1,0:T(8,128)(2,1)S(1)}, u32[]{:S(2)}, u32[]{:S(2)}) collective-permute-start(bf16[5,24,640]{2,1,0:T(8,128)(2,1)S(1)} %fusion.36), channel_id=1, source_target_pairs={{0,8},{4,12},{8,0},{12,4},{16,24},{20,28},{24,16},{28,20},{1,9},{5... | collective-permute-start | bytes 460808 | tf_op jit(solution)/shard_map/ppermute | solution.py:44
  143.3 4.6 %collective-permute-done.43 = bf16[5,24,640]{2,1,0:T(8,128)(2,1)S(1)} collective-permute-done((bf16[5,24,640]{2,1,0:T(8,128)(2,1)S(1)}, bf16[5,24,640]{2,1,0:T(8,128)(2,1)S(1)}, u32[]{:S(2)}, u32[]{:S(2)}) %collective-permute-start.43) | collective-permute-done | bytes 153632 | tf_op jit(solution)/shard_map/ppermute | solution.py:44
  150.0 2.1 %collective-permute-done.46 = bf16[24,640]{1,0:T(8,128)(2,1)S(1)} collective-permute-done((bf16[24,640]{1,0:T(8,128)(2,1)S(1)}, bf16[24,640]{1,0:T(8,128)(2,1)S(1)}, u32[]{:S(2)}, u32[]{:S(2)}) %collective-permute-start.46) | collective-permute-done | bytes 30752 | tf_op jit(solution)/shard_map/ppermute | solution.py:44
  155.0 3.7 %collective-permute-done.49.refs_2_ = bf16[5,24,640]{2,1,0:T(8,128)(2,1)S(1)} collective-permute-done((bf16[5,24,640]{2,1,0:T(8,128)(2,1)S(1)}, bf16[5,24,640]{2,1,0:T(8,128)(2,1)S(1)}, u32[]{:S(2)}, u32[]{:S(2)}) %collective-permute-start.49) | collective-permute-done | bytes 153632 | tf_op jit(solution)/shard_map/ppermute | solution.py:44
  162.9 7.2 %collective-permute-done.48.refs_4_ = bf16[5,24,640]{2,1,0:T(8,128)(2,1)S(1)} collective-permute-done((bf16[5,24,640]{2,1,0:T(8,128)(2,1)S(1)}, bf16[5,24,640]{2,1,0:T(8,128)(2,1)S(1)}, u32[]{:S(2)}, u32[]{:S(2)}) %collective-permute-start.48) | collective-permute-done | bytes 153632 | tf_op jit(solution)/shard_map/ppermute | solution.py:44
  172.0 3.7 %collective-permute-done.52.refs_6_ = bf16[5,24,640]{2,1,0:T(8,128)(2,1)S(1)} collective-permute-done((bf16[5,24,640]{2,1,0:T(8,128)(2,1)S(1)}, bf16[5,24,640]{2,1,0:T(8,128)(2,1)S(1)}, u32[]{:S(2)}, u32[]{:S(2)}) %collective-permute-start.52) | collective-permute-done | bytes 153632 | tf_op jit(solution)/shard_map/ppermute | solution.py:44
  177.3 3.6 %collective-permute-done.55.refs_7_ = bf16[5,24,640]{2,1,0:T(8,128)(2,1)S(1)} collective-permute-done((bf16[5,24,640]{2,1,0:T(8,128)(2,1)S(1)}, bf16[5,24,640]{2,1,0:T(8,128)(2,1)S(1)}, u32[]{:S(2)}, u32[]{:S(2)}) %collective-permute-start.55) | collective-permute-done | bytes 153632 | tf_op jit(solution)/shard_map/ppermute | solution.py:44
  181.6 3.2 %shard_map.203 = (f32[192,2304]{1,0:T(8,128)}, f32[192,768]{1,0:T(8,128)}, f32[1,192]{1,0:T(1,128)}, f32[1,192]{1,0:T(1,128)}, f32[8,192]{1,0:T(8,128)}) custom-call(bf16[5,24,640]{2,1,0:T(8,128)(2,1)} %copy-done.11, bf16[5,24,640]{2,1,0:T(8,128)(2,1)} %copy-done.14, bf16[5,24,640]{2,1,0:T(8,128)(2,1)} %copy-done.13, bf16[5,24,640]{2,1,0:T(8,128)(2,1)} %copy-done.16, ...), custom_call_target="tpu_custom_call" | custom-call | tf_op jit(solution)/shard_map/pallas_call | solution.py:66
  (233 shorter events, 62.9 us)
Async XLA Ops:
  0.7 8.7 %collective-permute-start = (bf16[128,768]{1,0:T(8,128)(2,1)}, bf16[128,768]{1,0:T(8,128)(2,1)S(1)}, u32[]{:S(2)}, u32[]{:S(2)}) collective-permute-start(bf16[128,768]{1,0:T(8,128)(2,1)} %refs_2_.2), channel_id=1, source_target_pairs={{0,2},{1,3},{2,0},{3,1},{4,6},{5,7},{6,4},{7,5},{8,10},{9,11},{10,... | collective-permute-start | bytes 589832 | tf_op jit(solution)/shard_map/ppermute | solution.py:44
  3.7 6.5 %collective-permute-start.1 = (bf16[128,768]{1,0:T(8,128)(2,1)}, bf16[128,768]{1,0:T(8,128)(2,1)S(1)}, u32[]{:S(2)}, u32[]{:S(2)}) collective-permute-start(bf16[128,768]{1,0:T(8,128)(2,1)} %refs_2_.2), channel_id=1, source_target_pairs={{0,1},{1,0},{2,3},{3,2},{4,5},{5,4},{6,7},{7,6},{8,9},{9,8},{10,11... | collective-permute-start | bytes 589832 | tf_op jit(solution)/shard_map/ppermute | solution.py:44
  6.7 9.0 %collective-permute-start.4 = (bf16[192,640]{1,0:T(8,128)(2,1)}, bf16[192,640]{1,0:T(8,128)(2,1)S(1)}, u32[]{:S(2)}, u32[]{:S(2)}) collective-permute-start(bf16[192,640]{1,0:T(8,128)(2,1)} %get-tuple-element.126), channel_id=1, source_target_pairs={{0,2},{1,3},{2,0},{3,1},{4,6},{5,7},{6,4},{7,5},{8,10},{9,11},{10,... | collective-permute-start | bytes 737288 | tf_op jit(solution)/shard_map/ppermute | solution.py:44
  6.8 12.3 %collective-permute-start.5 = (bf16[192,640]{1,0:T(8,128)(2,1)}, bf16[192,640]{1,0:T(8,128)(2,1)S(1)}, u32[]{:S(2)}, u32[]{:S(2)}) collective-permute-start(bf16[192,640]{1,0:T(8,128)(2,1)} %get-tuple-element.127), channel_id=1, source_target_pairs={{0,3},{1,2},{2,1},{3,0},{4,7},{5,6},{6,5},{7,4},{8,11},{9,10},{10,... | collective-permute-start | bytes 737288 | tf_op jit(solution)/shard_map/ppermute | solution.py:44
  9.3 18.8 %collective-permute-start.6 = (bf16[1,768,768]{2,1,0:T(8,128)(2,1)}, bf16[1,768,768]{2,1,0:T(8,128)(2,1)S(1)}, u32[]{:S(2)}, u32[]{:S(2)}) collective-permute-start(bf16[1,768,768]{2,1,0:T(8,128)(2,1)} %refs_2_.4), channel_id=1, source_target_pairs={{0,1},{1,0},{2,3},{3,2},{4,5},{5,4},{6,7},{7,6},{8,9},{9,8},{10,11... | collective-permute-start | bytes 3538952 | tf_op jit(solution)/shard_map/ppermute | solution.py:44
  10.1 18.0 %collective-permute-start.7 = (bf16[1,768,768]{2,1,0:T(8,128)(2,1)}, bf16[1,768,768]{2,1,0:T(8,128)(2,1)}, u32[]{:S(2)}, u32[]{:S(2)}) collective-permute-start(bf16[1,768,768]{2,1,0:T(8,128)(2,1)} %refs_4_.1), channel_id=1, source_target_pairs={{0,1},{1,0},{2,3},{3,2},{4,5},{5,4},{6,7},{7,6},{8,9},{9,8},{10,11... | collective-permute-start | bytes 3538952 | tf_op jit(solution)/shard_map/ppermute | solution.py:44
  11.1 8.0 %collective-permute-start.2 = (bf16[128,768]{1,0:T(8,128)(2,1)S(1)}, bf16[128,768]{1,0:T(8,128)(2,1)S(1)}, u32[]{:S(2)}, u32[]{:S(2)}) collective-permute-start(bf16[128,768]{1,0:T(8,128)(2,1)S(1)} %collective-permute-done.refs_4_), channel_id=1, source_target_pairs={{0,1},{1,0},{2,3},{3,2},{4,5},{5,4},{6,7},{7,6},{8,9},{9,8},{10,11... | collective-permute-start | bytes 589832 | tf_op jit(solution)/shard_map/ppermute | solution.py:44
  19.1 9.0 %collective-permute-start.8 = (bf16[192,768]{1,0:T(8,128)(2,1)}, bf16[192,768]{1,0:T(8,128)(2,1)S(1)}, u32[]{:S(2)}, u32[]{:S(2)}) collective-permute-start(bf16[192,768]{1,0:T(8,128)(2,1)} %refs_6_), channel_id=1, source_target_pairs={{0,1},{1,0},{2,3},{3,2},{4,5},{5,4},{6,7},{7,6},{8,9},{9,8},{10,11... | collective-permute-start | bytes 884744 | tf_op jit(solution)/shard_map/ppermute | solution.py:44
  20.0 9.4 %collective-permute-start.11 = (bf16[192,768]{1,0:T(8,128)(2,1)}, bf16[192,768]{1,0:T(8,128)(2,1)S(1)}, u32[]{:S(2)}, u32[]{:S(2)}) collective-permute-start(bf16[192,768]{1,0:T(8,128)(2,1)} %refs_6_), channel_id=1, source_target_pairs={{0,2},{1,3},{2,0},{3,1},{4,6},{5,7},{6,4},{7,5},{8,10},{9,11},{10,... | collective-permute-start | bytes 884744 | tf_op jit(solution)/shard_map/ppermute | solution.py:44
  40.7 6.4 %collective-permute-start.15 = (bf16[80,768]{1,0:T(8,128)(2,1)S(1)}, bf16[80,768]{1,0:T(8,128)(2,1)S(1)}, u32[]{:S(2)}, u32[]{:S(2)}) collective-permute-start(bf16[80,768]{1,0:T(8,128)(2,1)S(1)} %convolution_convert_fusion.1), channel_id=1, source_target_pairs={{0,4},{4,0},{8,12},{12,8},{16,20},{20,16},{24,28},{28,24},{1,5},{5... | collective-permute-start | bytes 368648 | tf_op jit(solution)/shard_map/ppermute | solution.py:44
  42.6 8.0 %collective-permute-start.18 = (bf16[40,768]{1,0:T(8,128)(2,1)S(1)}, bf16[40,768]{1,0:T(8,128)(2,1)S(1)}, u32[]{:S(2)}, u32[]{:S(2)}) collective-permute-start(bf16[40,768]{1,0:T(8,128)(2,1)S(1)} %get-tuple-element.246), channel_id=1, source_target_pairs={{0,24},{4,28},{8,16},{12,20},{16,8},{20,12},{24,0},{28,4},{1,25},{... | collective-permute-start | bytes 184328 | tf_op jit(solution)/shard_map/ppermute | solution.py:44
  51.6 9.9 %collective-permute-start.19 = (bf16[160,768]{1,0:T(8,128)(2,1)S(1)}, bf16[160,768]{1,0:T(8,128)(2,1)S(1)}, u32[]{:S(2)}, u32[]{:S(2)}) collective-permute-start(bf16[160,768]{1,0:T(8,128)(2,1)S(1)} %pad_maximum_fusion.1.refs_0_.own), channel_id=1, source_target_pairs={{0,2},{1,3},{2,0},{3,1},{4,6},{5,7},{6,4},{7,5},{8,10},{9,11},{10,... | collective-permute-start | bytes 737288 | tf_op jit(solution)/shard_map/ppermute | solution.py:44
  60.4 8.9 %collective-permute-start.24 = (bf16[160,768]{1,0:T(8,128)(2,1)S(1)}, bf16[160,768]{1,0:T(8,128)(2,1)S(1)}, u32[]{:S(2)}, u32[]{:S(2)}) collective-permute-start(bf16[160,768]{1,0:T(8,128)(2,1)S(1)} %pad_maximum_fusion.2.refs_0_.own_grad), channel_id=1, source_target_pairs={{0,2},{1,3},{2,0},{3,1},{4,6},{5,7},{6,4},{7,5},{8,10},{9,11},{10,... | collective-permute-start | bytes 737288 | tf_op jit(solution)/shard_map/ppermute | solution.py:44
  68.3 8.6 %collective-permute-start.20 = (bf16[160,768]{1,0:T(8,128)(2,1)}, bf16[160,768]{1,0:T(8,128)(2,1)S(1)}, u32[]{:S(2)}, u32[]{:S(2)}) collective-permute-start(bf16[160,768]{1,0:T(8,128)(2,1)} %get-tuple-element.155), channel_id=1, source_target_pairs={{0,2},{1,3},{2,0},{3,1},{4,6},{5,7},{6,4},{7,5},{8,10},{9,11},{10,... | collective-permute-start | bytes 737288 | tf_op jit(solution)/shard_map/ppermute | solution.py:44
  75.8 6.4 %collective-permute-start.25 = (bf16[160,768]{1,0:T(8,128)(2,1)}, bf16[160,768]{1,0:T(8,128)(2,1)S(1)}, u32[]{:S(2)}, u32[]{:S(2)}) collective-permute-start(bf16[160,768]{1,0:T(8,128)(2,1)} %get-tuple-element.158), channel_id=1, source_target_pairs={{0,2},{1,3},{2,0},{3,1},{4,6},{5,7},{6,4},{7,5},{8,10},{9,11},{10,... | collective-permute-start | bytes 737288 | tf_op jit(solution)/shard_map/ppermute | solution.py:44
  78.0 8.8 %collective-permute-start.27 = (bf16[40,768]{1,0:T(8,128)(2,1)S(1)}, bf16[40,768]{1,0:T(8,128)(2,1)S(1)}, u32[]{:S(2)}, u32[]{:S(2)}) collective-permute-start(bf16[40,768]{1,0:T(8,128)(2,1)S(1)} %get-tuple-element.253), channel_id=1, source_target_pairs={{0,16},{4,20},{8,24},{12,28},{16,0},{20,4},{24,8},{28,12},{1,17},{... | collective-permute-start | bytes 184328 | tf_op jit(solution)/shard_map/ppermute | solution.py:44
  79.6 7.2 %collective-permute-start.28 = (bf16[40,768]{1,0:T(8,128)(2,1)S(1)}, bf16[40,768]{1,0:T(8,128)(2,1)S(1)}, u32[]{:S(2)}, u32[]{:S(2)}) collective-permute-start(bf16[40,768]{1,0:T(8,128)(2,1)S(1)} %get-tuple-element.252), channel_id=1, source_target_pairs={{0,24},{4,28},{8,16},{12,20},{16,8},{20,12},{24,0},{28,4},{1,25},{... | collective-permute-start | bytes 184328 | tf_op jit(solution)/shard_map/ppermute | solution.py:44
  91.2 6.3 %collective-permute-start.32 = (bf16[80,1536]{1,0:T(8,128)(2,1)S(1)}, bf16[80,1536]{1,0:T(8,128)(2,1)S(1)}, u32[]{:S(2)}, u32[]{:S(2)}) collective-permute-start(bf16[80,1536]{1,0:T(8,128)(2,1)S(1)} %maximum_maximum_fusion), channel_id=1, source_target_pairs={{0,4},{4,0},{8,12},{12,8},{16,20},{20,16},{24,28},{28,24},{1,5},{5... | collective-permute-start | bytes 737288 | tf_op jit(solution)/shard_map/ppermute | solution.py:44
  107.2 21.0 %collective-permute-start.37 = (bf16[1,768,768]{2,1,0:T(8,128)(2,1)S(1)}, bf16[1,768,768]{2,1,0:T(8,128)(2,1)S(1)}, u32[]{:S(2)}, u32[]{:S(2)}) collective-permute-start(bf16[1,768,768]{2,1,0:T(8,128)(2,1)S(1)} %copy-done.25), channel_id=1, source_target_pairs={{0,1},{1,0},{2,3},{3,2},{4,5},{5,4},{6,7},{7,6},{8,9},{9,8},{10,11... | collective-permute-start | bytes 3538952 | tf_op jit(solution)/shard_map/ppermute | solution.py:44
  107.4 20.9 %collective-permute-start.38 = (bf16[1,768,768]{2,1,0:T(8,128)(2,1)S(1)}, bf16[1,768,768]{2,1,0:T(8,128)(2,1)S(1)}, u32[]{:S(2)}, u32[]{:S(2)}) collective-permute-start(bf16[1,768,768]{2,1,0:T(8,128)(2,1)S(1)} %copy-done.24), channel_id=1, source_target_pairs={{0,1},{1,0},{2,3},{3,2},{4,5},{5,4},{6,7},{7,6},{8,9},{9,8},{10,11... | collective-permute-start | bytes 3538952 | tf_op jit(solution)/shard_map/ppermute | solution.py:44
  118.3 7.1 %collective-permute-start.40 = (bf16[1,5,24,640]{3,2,1,0:T(8,128)(2,1)}, bf16[1,5,24,640]{3,2,1,0:T(8,128)(2,1)S(1)}, u32[]{:S(2)}, u32[]{:S(2)}) collective-permute-start(bf16[1,5,24,640]{3,2,1,0:T(8,128)(2,1)} %get-tuple-element.199), channel_id=1, source_target_pairs={{0,4},{4,0},{8,12},{12,8},{16,20},{20,16},{24,28},{28,24},{1,5},{5... | collective-permute-start | bytes 460808 | tf_op jit(solution)/shard_map/ppermute | solution.py:44
  119.0 9.2 %collective-permute-start.36 = (bf16[1,5,24,640]{3,2,1,0:T(8,128)(2,1)}, bf16[1,5,24,640]{3,2,1,0:T(8,128)(2,1)S(1)}, u32[]{:S(2)}, u32[]{:S(2)}) collective-permute-start(bf16[1,5,24,640]{3,2,1,0:T(8,128)(2,1)} %get-tuple-element.194), channel_id=1, source_target_pairs={{0,4},{4,0},{8,12},{12,8},{16,20},{20,16},{24,28},{28,24},{1,5},{5... | collective-permute-start | bytes 460808 | tf_op jit(solution)/shard_map/ppermute | solution.py:44
  126.3 16.9 %collective-permute-start.41 = (bf16[5,24,640]{2,1,0:T(8,128)(2,1)S(1)}, bf16[5,24,640]{2,1,0:T(8,128)(2,1)S(1)}, u32[]{:S(2)}, u32[]{:S(2)}) collective-permute-start(bf16[5,24,640]{2,1,0:T(8,128)(2,1)S(1)} %fusion.17), channel_id=1, source_target_pairs={{0,24},{4,28},{8,16},{12,20},{16,8},{20,12},{24,0},{28,4},{1,25},{... | collective-permute-start | bytes 460808 | tf_op jit(solution)/shard_map/ppermute | solution.py:44
  129.4 13.9 %collective-permute-start.42 = (bf16[5,24,640]{2,1,0:T(8,128)(2,1)S(1)}, bf16[5,24,640]{2,1,0:T(8,128)(2,1)S(1)}, u32[]{:S(2)}, u32[]{:S(2)}) collective-permute-start(bf16[5,24,640]{2,1,0:T(8,128)(2,1)S(1)} %fusion.35), channel_id=1, source_target_pairs={{0,16},{4,20},{8,24},{12,28},{16,0},{20,4},{24,8},{28,12},{1,17},{... | collective-permute-start | bytes 460808 | tf_op jit(solution)/shard_map/ppermute | solution.py:44
  129.5 8.4 %collective-permute-start.39 = (bf16[2,5,24,640]{3,2,1,0:T(8,128)(2,1)}, bf16[2,5,24,640]{3,2,1,0:T(8,128)(2,1)S(1)}, u32[]{:S(2)}, u32[]{:S(2)}) collective-permute-start(bf16[2,5,24,640]{3,2,1,0:T(8,128)(2,1)} %get-tuple-element.198), channel_id=1, source_target_pairs={{0,4},{4,0},{8,12},{12,8},{16,20},{20,16},{24,28},{28,24},{1,5},{5... | collective-permute-start | bytes 921608 | tf_op jit(solution)/shard_map/ppermute | solution.py:44
  141.0 6.9 %collective-permute-start.44 = (bf16[2,128,768]{2,1,0:T(8,128)(2,1)}, bf16[2,128,768]{2,1,0:T(8,128)(2,1)S(1)}, u32[]{:S(2)}, u32[]{:S(2)}) collective-permute-start(bf16[2,128,768]{2,1,0:T(8,128)(2,1)} %get-tuple-element.212), channel_id=1, source_target_pairs={{0,1},{1,0},{2,3},{3,2},{4,5},{5,4},{6,7},{7,6},{8,9},{9,8},{10,11... | collective-permute-start | bytes 1179656 | tf_op jit(solution)/shard_map/ppermute | solution.py:44
  141.2 6.7 %collective-permute-start.43 = (bf16[5,24,640]{2,1,0:T(8,128)(2,1)S(1)}, bf16[5,24,640]{2,1,0:T(8,128)(2,1)S(1)}, u32[]{:S(2)}, u32[]{:S(2)}) collective-permute-start(bf16[5,24,640]{2,1,0:T(8,128)(2,1)S(1)} %fusion.36), channel_id=1, source_target_pairs={{0,8},{4,12},{8,0},{12,4},{16,24},{20,28},{24,16},{28,20},{1,9},{5... | collective-permute-start | bytes 460808 | tf_op jit(solution)/shard_map/ppermute | solution.py:44
  152.6 6.1 %collective-permute-start.49 = (bf16[5,24,640]{2,1,0:T(8,128)(2,1)S(1)}, bf16[5,24,640]{2,1,0:T(8,128)(2,1)S(1)}, u32[]{:S(2)}, u32[]{:S(2)}) collective-permute-start(bf16[5,24,640]{2,1,0:T(8,128)(2,1)S(1)} %slice_dynamic-update-slice_fusion.refs_0_), channel_id=1, source_target_pairs={{0,8},{4,12},{8,0},{12,4},{16,24},{20,28},{24,16},{28,20},{1,9},{5... | collective-permute-start | bytes 460808 | tf_op jit(solution)/shard_map/ppermute | solution.py:44
  160.3 10.6 %collective-permute-start.53 = (bf16[128,768]{1,0:T(8,128)(2,1)S(1)}, bf16[128,768]{1,0:T(8,128)(2,1)S(1)}, u32[]{:S(2)}, u32[]{:S(2)}) collective-permute-start(bf16[128,768]{1,0:T(8,128)(2,1)S(1)} %fusion.34), channel_id=1, source_target_pairs={{0,2},{1,3},{2,0},{3,1},{4,6},{5,7},{6,4},{7,5},{8,10},{9,11},{10,... | collective-permute-start | bytes 589832 | tf_op jit(solution)/shard_map/ppermute | solution.py:44
  161.3 8.8 %collective-permute-start.48 = (bf16[5,24,640]{2,1,0:T(8,128)(2,1)S(1)}, bf16[5,24,640]{2,1,0:T(8,128)(2,1)S(1)}, u32[]{:S(2)}, u32[]{:S(2)}) collective-permute-start(bf16[5,24,640]{2,1,0:T(8,128)(2,1)S(1)} %slice_dynamic-update-slice_fusion.refs_0_), channel_id=1, source_target_pairs={{0,16},{4,20},{8,24},{12,28},{16,0},{20,4},{24,8},{28,12},{1,17},{... | collective-permute-start | bytes 460808 | tf_op jit(solution)/shard_map/ppermute | solution.py:44
  162.2 7.9 %collective-permute-start.51 = (bf16[5,24,640]{2,1,0:T(8,128)(2,1)S(1)}, bf16[5,24,640]{2,1,0:T(8,128)(2,1)S(1)}, u32[]{:S(2)}, u32[]{:S(2)}) collective-permute-start(bf16[5,24,640]{2,1,0:T(8,128)(2,1)S(1)} %collective-permute-done.49.refs_2_), channel_id=1, source_target_pairs={{0,4},{4,0},{8,12},{12,8},{16,20},{20,16},{24,28},{28,24},{1,5},{5... | collective-permute-start | bytes 460808 | tf_op jit(solution)/shard_map/ppermute | solution.py:44
  170.2 7.1 %collective-permute-start.54 = (bf16[5,24,640]{2,1,0:T(8,128)(2,1)S(1)}, bf16[5,24,640]{2,1,0:T(8,128)(2,1)S(1)}, u32[]{:S(2)}, u32[]{:S(2)}) collective-permute-start(bf16[5,24,640]{2,1,0:T(8,128)(2,1)S(1)} %collective-permute-done.48.refs_4_), channel_id=1, source_target_pairs={{0,4},{4,0},{8,12},{12,8},{16,20},{20,16},{24,28},{28,24},{1,5},{5... | collective-permute-start | bytes 460808 | tf_op jit(solution)/shard_map/ppermute | solution.py:44
  (63 other events, 387.0 us)

commit v10 on v8

--- a/solution.py
+++ b/solution.py
@@ -207,7 +207,7 @@
     projected, tokens, gains, weight, weights, mixed, weight_out, gain_two, router = refs[:9]
     branch_refs = refs[9 : 9 + n]
     at = 9 + n
-    shares = 4 if m > 1 else 2
+    shares = 5 if m > 1 else 2
     share_out = refs[at : at + shares]
     normed_grad_out = refs[at + shares : at + shares + 2]
     gain_out, table_out = refs[at + shares + 2 : at + shares + 4]
@@ -319,9 +319,12 @@
         total_scr[d * piece : d * piece + row_tile, at : at + heads * per_line] = table_total[
             :, : heads * per_line
         ]
+    near_keep, far_keep, near_send, far_send, last_send = share_out
     for d in range(m):
-        target = share_out[(d & 1) + 2 * (d < m // 2)]
         place = (d >> 1) % (m // 4)
+        target = (far_send if d & 1 else far_keep) if d >= m // 2 else (near_send if d & 1 else near_keep)
+        if d == m - 1:
+            target, place = last_send, 0
         start = (e ^ d) * piece
         for t in range(n):
             rows_at = pl.multiple_of(t * part + start, row_tile)
@@ -654,7 +657,9 @@
     holders = m if direct else 1
     piece = part // m
     if direct:
-        share_shapes = [shape((m // 4, n + 1, piece, full))] * 4
+        share_shapes = [
+            shape((held, n + 1, piece, full)) for held in (m // 4, m // 4, m // 4, m // 4 - 1, 1)
+        ]
     else:
         share_shapes = [shape((n, part, wide)), shape((part, width))]
     answers = call(
@@ -706,26 +711,38 @@
     def biases(block):
         return block.reshape(row_tile, heads, per_line).swapaxes(0, 1).reshape(heads, buckets)
 
-    normed_sum = normed_keep.astype(f32) + swap(normed_send, "shard", pair).astype(f32)
-    far_sum = swap(normed_sum[1].astype(bf16), "shard", 2 * pair)
-    late, far_sum = lax.optimization_barrier((tokens, far_sum))
-    late = late.astype(f32)
-    grad_input_norm, _ = rms_backward(
-        late, rms_factor(late), gain_one, normed_sum[0] + far_sum.astype(f32)
-    )
-    grad_tokens = (grad_hidden + grad_input_norm).astype(bf16)
+    def far_normed(pair_came):
+        normed_sum = normed_keep.astype(f32) + pair_came.astype(f32)
+        return normed_sum[0], swap(normed_sum[1].astype(bf16), "shard", 2 * pair)
+
+    def finish_tokens(own_sum, far_sum):
+        late, far_sum = lax.optimization_barrier((tokens, far_sum))
+        late = late.astype(f32)
+        grad_input_norm, _ = rms_backward(
+            late, rms_factor(late), gain_one, own_sum + far_sum.astype(f32)
+        )
+        return (grad_hidden + grad_input_norm).astype(bf16)
+
+    normed_came = swap(normed_send, "shard", pair)
     if direct:
-        far_keep, far_send, near_keep, near_send = shares
+        near_keep, far_keep, near_send, far_send, last_send = shares
+        last_came = swap(last_send, "expert", 1)[0]
         far_came = swap(far_send, "expert", 1)
-        far_came, near_send, up_came, down_came = lax.optimization_barrier(
-            (far_came, near_send, up_came, down_came)
-        )
-        far = far_keep.astype(f32) + far_came.astype(f32)
-        near_came, late_rows = lax.optimization_barrier((swap(near_send, "expert", 1), row_blocks))
+        last_came, near_send, up_came, down_came = lax.optimization_barrier(
+            (last_came, near_send, up_came, down_came)
+        )
+        came = [swap((far_keep[-1].astype(f32) + last_came.astype(f32)).astype(bf16), "expert", m - 2)]
+        far = far_keep[:-1].astype(f32) + far_came.astype(f32)
+        near_came, late_rows, normed_came = lax.optimization_barrier(
+            (swap(near_send, "expert", 1), row_blocks, normed_came)
+        )
+        own_sum, far_sum = far_normed(normed_came)
         near = near_keep.astype(f32) + near_came.astype(f32)
-        came = [swap(far[d].astype(bf16), "expert", m // 2 + 2 * d) for d in range(m // 4)]
+        came += [swap(far[d].astype(bf16), "expert", m // 2 + 2 * d) for d in range(m // 4 - 1)]
         came += [swap(near[d].astype(bf16), "expert", 2 * d) for d in range(1, m // 4)]
         came, (grad_up, grad_down) = lax.optimization_barrier((came, kept_weights(late_rows)))
+        came, far_sum = lax.optimization_barrier((came, far_sum))
+        grad_tokens = finish_tokens(own_sum, far_sum)
         summed = near[0] + sum(x.astype(f32) for x in came)
         at = wide + 2 + experts
         rest = (width - full) // n
@@ -766,6 +783,7 @@
         )
     else:
         grad_up, grad_down = kept_weights(row_blocks)
+        grad_tokens = finish_tokens(*far_normed(normed_came))
         came = lax.all_to_all(
             shares[0].reshape(n, m, piece, wide).swapaxes(0, 1), "expert", 0, 0, tiled=True
         )

time: 177 us -> 178 us (level)
  waiting for transfers between devices: 63.4 us -> 67 us
  starting transfers between devices: 52.2 us -> 48.7 us
    ppermute x55 -> x56, waiting for transfers between devices: 63.4 us -> 67 us  [swap(): return lax.ppermute(value, axis, [(i, i ^ bit) for i in range(size)])]
    ppermute x55 -> x56, starting transfers between devices: 52.2 us -> 48.7 us  [swap(): return lax.ppermute(value, axis, [(i, i ^ bit) for i in range(size)])]
    convert_element_type x1 -> x3, other arithmetic: 0.88 us -> 2.81 us  [the longest x1 0.98 us: local(): (far_keep[-1].astype(f32) + last_came.astype(f32)).astype(bf16)]
  transfers between devices with their start and end apart: 55 -> 56, of which waited for: 29 -> 29; matrix products, arithmetic and copies ran while one was open for 5% -> 6% of each run, Pallas kernels for 23% -> 23%
where the time goes in v10:
time: 178 us; the launch traced here: 177 us
  waiting for transfers between devices  67 us (38%)
  starting transfers between devices  48.7 us (27%)
  Pallas kernels  43.9 us (25%)
  other arithmetic  6.82 us (4%)
  matrix products  5.99 us (3%)
  local copies, waits for them, and re-layouts  3.63 us (2%)
    ppermute x56, waiting for transfers between devices, swap(): return lax.ppermute(value, axis, [(i, i ^ bit) for i in range(size)])  67 us
    ppermute x56, starting transfers between devices, swap(): return lax.ppermute(value, axis, [(i, i ^ bit) for i in range(size)])  48.7 us
    pallas_call x8, Pallas kernels, call(): pl.pallas_call(kernel, out_shape=out_shape, in_specs=in_specs, out_specs=...  43.9 us
  transfers between devices with their start and end apart: 56, of which 29 were waited for; matrix products, arithmetic and copies ran while one was open for 6% of the time, Pallas kernels for 23%

profile of v10, /device:TPU:0, one launch (start us, length us, event | category | flops | bytes accessed | tf_op | source)
XLA Modules:
  0.0 177.4 jit_solution(13303546644220009594)
XLA Ops:
  0.7 3.0 %collective-permute-start = (bf16[128,768]{1,0:T(8,128)(2,1)}, bf16[128,768]{1,0:T(8,128)(2,1)S(1)}, u32[]{:S(2)}, u32[]{:S(2)}) collective-permute-start(bf16[128,768]{1,0:T(8,128)(2,1)} %refs_2_.2), channel_id=1, source_target_pairs={{0,2},{1,3},{2,0},{3,1},{4,6},{5,7},{6,4},{7,5},{8,10},{9,11},{10,... | collective-permute-start | bytes 589832 | tf_op jit(solution)/shard_map/ppermute | solution.py:44
  3.7 2.5 %shard_map.195 = (bf16[192,640]{1,0:T(8,128)(2,1)}, bf16[192,640]{1,0:T(8,128)(2,1)}, bf16[192,640]{1,0:T(8,128)(2,1)}, bf16[192,640]{1,0:T(8,128)(2,1)}) custom-call(bf16[192,2304]{1,0:T(8,128)(2,1)} %refs_0_.2, bf16[192]{0:T(256)(128)(2,1)} %refs_1_.1, bf16[192]{0:T(256)(128)(2,1)} %refs_2_.1), custom_call_target="tpu_custom_call" | custom-call | tf_op jit(solution)/shard_map/pallas_call | solution.py:66
  12.3 3.5 %collective-permute-done.4.refs_8_ = bf16[192,640]{1,0:T(8,128)(2,1)S(1)} collective-permute-done((bf16[192,640]{1,0:T(8,128)(2,1)}, bf16[192,640]{1,0:T(8,128)(2,1)S(1)}, u32[]{:S(2)}, u32[]{:S(2)}) %collective-permute-start.4) | collective-permute-done | bytes 245792 | tf_op jit(solution)/shard_map/ppermute | solution.py:44
  15.8 3.3 %collective-permute-done.5.refs_9_ = bf16[192,640]{1,0:T(8,128)(2,1)S(1)} collective-permute-done((bf16[192,640]{1,0:T(8,128)(2,1)}, bf16[192,640]{1,0:T(8,128)(2,1)S(1)}, u32[]{:S(2)}, u32[]{:S(2)}) %collective-permute-start.5) | collective-permute-done | bytes 245792 | tf_op jit(solution)/shard_map/ppermute | solution.py:44
  21.0 7.1 %shard_map.196 = (bf16[4,128,768]{2,1,0:T(8,128)(2,1)}, bf16[768,640]{1,0:T(8,128)(2,1)}, bf16[512,576]{1,0:T(8,128)(2,1)}, bf16[3,512,512]{2,1,0:T(8,128)(2,1)}...) custom-call(s32[1,3]{1,0:T(1,128)} %refs_0_.3, ...), custom_call_target="tpu_custom_call" | custom-call | flops 10000000000 | tf_op jit(solution)/shard_map/pallas_call | solution.py:66
  30.6 2.1 %collective-permute-done.10 = bf16[128,192]{1,0:T(8,128)(2,1)S(1)} collective-permute-done((bf16[128,192]{1,0:T(8,128)(2,1)}, bf16[128,192]{1,0:T(8,128)(2,1)S(1)}, u32[]{:S(2)}, u32[]{:S(2)}) %collective-permute-start.10) | collective-permute-done | bytes 49184 | tf_op jit(solution)/shard_map/ppermute | solution.py:44
  37.7 3.5 %collective-permute-done.14 = bf16[80,768]{1,0:T(8,128)(2,1)S(1)} collective-permute-done((bf16[80,768]{1,0:T(8,128)(2,1)S(1)}, bf16[80,768]{1,0:T(8,128)(2,1)S(1)}, u32[]{:S(2)}, u32[]{:S(2)}) %collective-permute-start.14) | collective-permute-done | bytes 122912 | tf_op jit(solution)/shard_map/ppermute | solution.py:44
  44.8 2.6 %collective-permute-start.17 = (bf16[40,768]{1,0:T(8,128)(2,1)S(1)}, bf16[40,768]{1,0:T(8,128)(2,1)S(1)}, u32[]{:S(2)}, u32[]{:S(2)}) collective-permute-start(bf16[40,768]{1,0:T(8,128)(2,1)S(1)} %get-tuple-element.247), channel_id=1, source_target_pairs={{0,16},{4,20},{8,24},{12,28},{16,0},{20,4},{24,8},{28,12},{1,17},{... | collective-permute-start | bytes 184328 | tf_op jit(solution)/shard_map/ppermute | solution.py:44
  48.0 3.2 %collective-permute-done.17 = bf16[40,768]{1,0:T(8,128)(2,1)S(1)} collective-permute-done((bf16[40,768]{1,0:T(8,128)(2,1)S(1)}, bf16[40,768]{1,0:T(8,128)(2,1)S(1)}, u32[]{:S(2)}, u32[]{:S(2)}) %collective-permute-start.17) | collective-permute-done | bytes 61472 | tf_op jit(solution)/shard_map/ppermute | solution.py:44
  51.2 2.2 %collective-permute-done.18 = bf16[40,768]{1,0:T(8,128)(2,1)S(1)} collective-permute-done((bf16[40,768]{1,0:T(8,128)(2,1)S(1)}, bf16[40,768]{1,0:T(8,128)(2,1)S(1)}, u32[]{:S(2)}, u32[]{:S(2)}) %collective-permute-start.18) | collective-permute-done | bytes 61472 | tf_op jit(solution)/shard_map/ppermute | solution.py:44
  55.9 3.1 %collective-permute-start.23 = (bf16[40,768]{1,0:T(8,128)(2,1)S(1)}, bf16[40,768]{1,0:T(8,128)(2,1)S(1)}, u32[]{:S(2)}, u32[]{:S(2)}) collective-permute-start(bf16[40,768]{1,0:T(8,128)(2,1)S(1)} %get-tuple-element.257), channel_id=1, source_target_pairs={{0,24},{4,28},{8,16},{12,20},{16,8},{20,12},{24,0},{28,4},{1,25},{... | collective-permute-start | bytes 184328 | tf_op jit(solution)/shard_map/ppermute | solution.py:44
  59.7 2.2 %collective-permute-done.23 = bf16[40,768]{1,0:T(8,128)(2,1)S(1)} collective-permute-done((bf16[40,768]{1,0:T(8,128)(2,1)S(1)}, bf16[40,768]{1,0:T(8,128)(2,1)S(1)}, u32[]{:S(2)}, u32[]{:S(2)}) %collective-permute-start.23) | collective-permute-done | bytes 61472 | tf_op jit(solution)/shard_map/ppermute | solution.py:44
  63.8 6.0 %shard_map.197 = (bf16[2,320,768]{2,1,0:T(8,128)(2,1)}, bf16[2,320,768]{2,1,0:T(8,128)(2,1)}, f32[160,768]{1,0:T(8,128)}, bf16[160,768]{1,0:T(8,128)(2,1)}) custom-call(bf16[160,768]{1,0:T(8,128)(2,1)} %copy-done.9, bf16[160,768]{1,0:T(8,128)(2,1)} %copy-done.25, bf16[1,768,768]{2,1,0:T(8,128)(2,1)} %refs_2_.4, bf16[1,768,768]{2,1,0:T(8,128)(2,1)} %copy-done.23, ...), custom_call_target="tpu_custom_call" | custom-call | flops 6000000000 | tf_op jit(solution)/shard_map/pallas_call | solution.py:66
  71.5 5.8 %shard_map.198 = (bf16[2,320,768]{2,1,0:T(8,128)(2,1)}, f32[160,768]{1,0:T(8,128)}, bf16[160,768]{1,0:T(8,128)(2,1)}) custom-call(bf16[160,768]{1,0:T(8,128)(2,1)} %copy-done.10, bf16[160,768]{1,0:T(8,128)(2,1)} %copy-done.26, bf16[1,768,768]{2,1,0:T(8,128)(2,1)} %refs_2_.4, bf16[1,768,768]{2,1,0:T(8,128)(2,1)} %copy-done.23, bf16[1,768,768]{2,1,0:T(8,128)(2,1)} %refs_4_.1, ...), custom_call_target="tpu_custom_call" | custom-call | flops 6000000000 | tf_op jit(solution)/shard_map/pallas_call | solution.py:66
  79.1 2.9 %collective-permute-start.27 = (bf16[40,768]{1,0:T(8,128)(2,1)S(1)}, bf16[40,768]{1,0:T(8,128)(2,1)S(1)}, u32[]{:S(2)}, u32[]{:S(2)}) collective-permute-start(bf16[40,768]{1,0:T(8,128)(2,1)S(1)} %get-tuple-element.253), channel_id=1, source_target_pairs={{0,16},{4,20},{8,24},{12,28},{16,0},{20,4},{24,8},{28,12},{1,17},{... | collective-permute-start | bytes 184328 | tf_op jit(solution)/shard_map/ppermute | solution.py:44
  84.5 2.9 %collective-permute-start.30 = (bf16[40,768]{1,0:T(8,128)(2,1)S(1)}, bf16[40,768]{1,0:T(8,128)(2,1)S(1)}, u32[]{:S(2)}, u32[]{:S(2)}) collective-permute-start(bf16[40,768]{1,0:T(8,128)(2,1)S(1)} %get-tuple-element.249), channel_id=1, source_target_pairs={{0,16},{4,20},{8,24},{12,28},{16,0},{20,4},{24,8},{28,12},{1,17},{... | collective-permute-start | bytes 184328 | tf_op jit(solution)/shard_map/ppermute | solution.py:44
  89.7 3.8 %collective-permute-done.31 = bf16[40,768]{1,0:T(8,128)(2,1)S(1)} collective-permute-done((bf16[40,768]{1,0:T(8,128)(2,1)S(1)}, bf16[40,768]{1,0:T(8,128)(2,1)S(1)}, u32[]{:S(2)}, u32[]{:S(2)}) %collective-permute-start.31) | collective-permute-done | bytes 61472 | tf_op jit(solution)/shard_map/ppermute | solution.py:44
  94.2 4.5 %shard_map.199 = (bf16[1,768,768]{2,1,0:T(8,128)(2,1)}, bf16[1,768,768]{2,1,0:T(8,128)(2,1)}) custom-call(bf16[160,768]{1,0:T(8,128)(2,1)} %copy-done.9, bf16[160,768]{1,0:T(8,128)(2,1)} %copy-done.25, bf16[160,768]{1,0:T(8,128)(2,1)} %copy-done.10, bf16[160,768]{1,0:T(8,128)(2,1)} %copy-done.26, bf16[2,320,768]{2,1,0:T(8,128)(2,1)} %get-tuple-element.173.hidden, ...), custom_call_target="tpu_custom_call" | custom-call | flops 4000000000 | tf_op jit(solution)/shard_map/pallas_call | solution.py:66
  104.5 3.7 %collective-permute-done.33.refs_11_ = bf16[128,768]{1,0:T(8,128)(2,1)S(1)} collective-permute-done((bf16[128,768]{1,0:T(8,128)(2,1)S(1)}, bf16[128,768]{1,0:T(8,128)(2,1)S(1)}, u32[]{:S(2)}, u32[]{:S(2)}) %collective-permute-start.33) | collective-permute-done | bytes 196640 | tf_op jit(solution)/shard_map/ppermute | solution.py:44
  110.3 8.8 %shard_map.200 = (bf16[2,5,24,640]{3,2,1,0:T(8,128)(2,1)}, bf16[2,5,24,640]{3,2,1,0:T(8,128)(2,1)}, bf16[2,5,24,640]{3,2,1,0:T(8,128)(2,1)}, bf16[1,5,24,640]{3,...) custom-call(bf16[512,576]{1,0:T(8,128)(2,1)} %get-tuple-element.178., ...), custom_call_target="tpu_custom_call" | custom-call | flops 8000000000 | tf_op jit(solution)/shard_map/pallas_call | solution.py:66
  121.4 4.9 %collective-permute-done.36 = bf16[1,5,24,640]{3,2,1,0:T(8,128)(2,1)S(1)} collective-permute-done((bf16[1,5,24,640]{3,2,1,0:T(8,128)(2,1)}, bf16[1,5,24,640]{3,2,1,0:T(8,128)(2,1)S(1)}, u32[]{:S(2)}, u32[]{:S(2)}) %collective-permute-start.36) | collective-permute-done | bytes 153632 | tf_op jit(solution)/shard_map/ppermute | solution.py:44
  127.0 2.6 %collective-permute-done.42 = bf16[1,5,24,640]{3,2,1,0:T(8,128)(2,1)S(1)} collective-permute-done((bf16[1,5,24,640]{3,2,1,0:T(8,128)(2,1)}, bf16[1,5,24,640]{3,2,1,0:T(8,128)(2,1)S(1)}, u32[]{:S(2)}, u32[]{:S(2)}) %collective-permute-start.42) | collective-permute-done | bytes 153632 | tf_op jit(solution)/shard_map/ppermute | solution.py:44
  132.5 2.9 %collective-permute-done.39 = bf16[2,5,24,640]{3,2,1,0:T(8,128)(2,1)S(1)} collective-permute-done((bf16[2,5,24,640]{3,2,1,0:T(8,128)(2,1)}, bf16[2,5,24,640]{3,2,1,0:T(8,128)(2,1)S(1)}, u32[]{:S(2)}, u32[]{:S(2)}) %collective-permute-start.39) | collective-permute-done | bytes 307232 | tf_op jit(solution)/shard_map/ppermute | solution.py:44
  136.8 5.8 %shard_map.201 = (f32[1,768,768]{2,1,0:T(8,128)}, f32[1,768,768]{2,1,0:T(8,128)}) custom-call(bf16[160,768]{1,0:T(8,128)(2,1)} %copy-done.9, bf16[160,768]{1,0:T(8,128)(2,1)} %copy-done.25, bf16[160,768]{1,0:T(8,128)(2,1)} %copy-done.10, bf16[160,768]{1,0:T(8,128)(2,1)} %copy-done.26, bf16[2,320,768]{2,1,0:T(8,128)(2,1)} %get-tuple-element.173.hidden, ...), custom_call_target="tpu_custom_call" | custom-call | flops 4000000000 | tf_op jit(solution)/shard_map/pallas_call | solution.py:66
  146.4 1.9 %collective-permute-done.47 = bf16[24,640]{1,0:T(8,128)(2,1)S(1)} collective-permute-done((bf16[24,640]{1,0:T(8,128)(2,1)S(1)}, bf16[24,640]{1,0:T(8,128)(2,1)S(1)}, u32[]{:S(2)}, u32[]{:S(2)}) %collective-permute-start.47) | collective-permute-done | bytes 30752 | tf_op jit(solution)/shard_map/ppermute | solution.py:44
  150.1 2.1 %collective-permute-start.49 = (bf16[5,24,640]{2,1,0:T(8,128)(2,1)S(1)}, bf16[5,24,640]{2,1,0:T(8,128)(2,1)S(1)}, u32[]{:S(2)}, u32[]{:S(2)}) collective-permute-start(bf16[5,24,640]{2,1,0:T(8,128)(2,1)S(1)} %slice_dynamic-update-slice_fusion.refs_0_), channel_id=1, source_target_pairs={{0,16},{4,20},{8,24},{12,28},{16,0},{20,4},{24,8},{28,12},{1,17},{... | collective-permute-start | bytes 460808 | tf_op jit(solution)/shard_map/ppermute | solution.py:44
  152.2 5.5 %collective-permute-done.50.refs_2_ = bf16[5,24,640]{2,1,0:T(8,128)(2,1)S(1)} collective-permute-done((bf16[5,24,640]{2,1,0:T(8,128)(2,1)S(1)}, bf16[5,24,640]{2,1,0:T(8,128)(2,1)S(1)}, u32[]{:S(2)}, u32[]{:S(2)}) %collective-permute-start.50) | collective-permute-done | bytes 153632 | tf_op jit(solution)/shard_map/ppermute | solution.py:44
  157.8 2.1 %collective-permute-done.49.refs_4_ = bf16[5,24,640]{2,1,0:T(8,128)(2,1)S(1)} collective-permute-done((bf16[5,24,640]{2,1,0:T(8,128)(2,1)S(1)}, bf16[5,24,640]{2,1,0:T(8,128)(2,1)S(1)}, u32[]{:S(2)}, u32[]{:S(2)}) %collective-permute-start.49) | collective-permute-done | bytes 153632 | tf_op jit(solution)/shard_map/ppermute | solution.py:44
  159.8 3.1 %collective-permute-done.52.refs_3_ = bf16[5,24,640]{2,1,0:T(8,128)(2,1)S(1)} collective-permute-done((bf16[5,24,640]{2,1,0:T(8,128)(2,1)S(1)}, bf16[5,24,640]{2,1,0:T(8,128)(2,1)S(1)}, u32[]{:S(2)}, u32[]{:S(2)}) %collective-permute-start.52) | collective-permute-done | bytes 153632 | tf_op jit(solution)/shard_map/ppermute | solution.py:44
  164.1 4.0 %collective-permute-done.53.refs_6_ = bf16[5,24,640]{2,1,0:T(8,128)(2,1)S(1)} collective-permute-done((bf16[5,24,640]{2,1,0:T(8,128)(2,1)S(1)}, bf16[5,24,640]{2,1,0:T(8,128)(2,1)S(1)}, u32[]{:S(2)}, u32[]{:S(2)}) %collective-permute-start.53) | collective-permute-done | bytes 153632 | tf_op jit(solution)/shard_map/ppermute | solution.py:44
  170.4 3.0 %collective-permute-done.55.refs_7_ = bf16[5,24,640]{2,1,0:T(8,128)(2,1)S(1)} collective-permute-done((bf16[5,24,640]{2,1,0:T(8,128)(2,1)S(1)}, bf16[5,24,640]{2,1,0:T(8,128)(2,1)S(1)}, u32[]{:S(2)}, u32[]{:S(2)}) %collective-permute-start.55) | collective-permute-done | bytes 153632 | tf_op jit(solution)/shard_map/ppermute | solution.py:44
  174.1 3.2 %shard_map.202 = (f32[192,2304]{1,0:T(8,128)}, f32[192,768]{1,0:T(8,128)}, f32[1,192]{1,0:T(1,128)}, f32[1,192]{1,0:T(1,128)}, f32[8,192]{1,0:T(8,128)}) custom-call(bf16[5,24,640]{2,1,0:T(8,128)(2,1)} %copy-done.11, bf16[5,24,640]{2,1,0:T(8,128)(2,1)} %copy-done.14, bf16[5,24,640]{2,1,0:T(8,128)(2,1)} %copy-done.13, bf16[5,24,640]{2,1,0:T(8,128)(2,1)} %copy-done.16, ...), custom_call_target="tpu_custom_call" | custom-call | tf_op jit(solution)/shard_map/pallas_call | solution.py:66
  (226 shorter events, 58.1 us)
Async XLA Ops:
  0.7 8.7 %collective-permute-start = (bf16[128,768]{1,0:T(8,128)(2,1)}, bf16[128,768]{1,0:T(8,128)(2,1)S(1)}, u32[]{:S(2)}, u32[]{:S(2)}) collective-permute-start(bf16[128,768]{1,0:T(8,128)(2,1)} %refs_2_.2), channel_id=1, source_target_pairs={{0,2},{1,3},{2,0},{3,1},{4,6},{5,7},{6,4},{7,5},{8,10},{9,11},{10,... | collective-permute-start | bytes 589832 | tf_op jit(solution)/shard_map/ppermute | solution.py:44
  3.7 6.5 %collective-permute-start.1 = (bf16[128,768]{1,0:T(8,128)(2,1)}, bf16[128,768]{1,0:T(8,128)(2,1)S(1)}, u32[]{:S(2)}, u32[]{:S(2)}) collective-permute-start(bf16[128,768]{1,0:T(8,128)(2,1)} %refs_2_.2), channel_id=1, source_target_pairs={{0,1},{1,0},{2,3},{3,2},{4,5},{5,4},{6,7},{7,6},{8,9},{9,8},{10,11... | collective-permute-start | bytes 589832 | tf_op jit(solution)/shard_map/ppermute | solution.py:44
  6.7 9.0 %collective-permute-start.4 = (bf16[192,640]{1,0:T(8,128)(2,1)}, bf16[192,640]{1,0:T(8,128)(2,1)S(1)}, u32[]{:S(2)}, u32[]{:S(2)}) collective-permute-start(bf16[192,640]{1,0:T(8,128)(2,1)} %get-tuple-element.126), channel_id=1, source_target_pairs={{0,2},{1,3},{2,0},{3,1},{4,6},{5,7},{6,4},{7,5},{8,10},{9,11},{10,... | collective-permute-start | bytes 737288 | tf_op jit(solution)/shard_map/ppermute | solution.py:44
  6.8 12.3 %collective-permute-start.5 = (bf16[192,640]{1,0:T(8,128)(2,1)}, bf16[192,640]{1,0:T(8,128)(2,1)S(1)}, u32[]{:S(2)}, u32[]{:S(2)}) collective-permute-start(bf16[192,640]{1,0:T(8,128)(2,1)} %get-tuple-element.127), channel_id=1, source_target_pairs={{0,3},{1,2},{2,1},{3,0},{4,7},{5,6},{6,5},{7,4},{8,11},{9,10},{10,... | collective-permute-start | bytes 737288 | tf_op jit(solution)/shard_map/ppermute | solution.py:44
  9.3 18.8 %collective-permute-start.6 = (bf16[1,768,768]{2,1,0:T(8,128)(2,1)}, bf16[1,768,768]{2,1,0:T(8,128)(2,1)S(1)}, u32[]{:S(2)}, u32[]{:S(2)}) collective-permute-start(bf16[1,768,768]{2,1,0:T(8,128)(2,1)} %refs_2_.4), channel_id=1, source_target_pairs={{0,1},{1,0},{2,3},{3,2},{4,5},{5,4},{6,7},{7,6},{8,9},{9,8},{10,11... | collective-permute-start | bytes 3538952 | tf_op jit(solution)/shard_map/ppermute | solution.py:44
  10.1 18.0 %collective-permute-start.7 = (bf16[1,768,768]{2,1,0:T(8,128)(2,1)}, bf16[1,768,768]{2,1,0:T(8,128)(2,1)}, u32[]{:S(2)}, u32[]{:S(2)}) collective-permute-start(bf16[1,768,768]{2,1,0:T(8,128)(2,1)} %refs_4_.1), channel_id=1, source_target_pairs={{0,1},{1,0},{2,3},{3,2},{4,5},{5,4},{6,7},{7,6},{8,9},{9,8},{10,11... | collective-permute-start | bytes 3538952 | tf_op jit(solution)/shard_map/ppermute | solution.py:44
  11.1 8.0 %collective-permute-start.2 = (bf16[128,768]{1,0:T(8,128)(2,1)S(1)}, bf16[128,768]{1,0:T(8,128)(2,1)S(1)}, u32[]{:S(2)}, u32[]{:S(2)}) collective-permute-start(bf16[128,768]{1,0:T(8,128)(2,1)S(1)} %collective-permute-done.refs_4_), channel_id=1, source_target_pairs={{0,1},{1,0},{2,3},{3,2},{4,5},{5,4},{6,7},{7,6},{8,9},{9,8},{10,11... | collective-permute-start | bytes 589832 | tf_op jit(solution)/shard_map/ppermute | solution.py:44
  19.1 9.0 %collective-permute-start.8 = (bf16[192,768]{1,0:T(8,128)(2,1)}, bf16[192,768]{1,0:T(8,128)(2,1)S(1)}, u32[]{:S(2)}, u32[]{:S(2)}) collective-permute-start(bf16[192,768]{1,0:T(8,128)(2,1)} %refs_6_), channel_id=1, source_target_pairs={{0,1},{1,0},{2,3},{3,2},{4,5},{5,4},{6,7},{7,6},{8,9},{9,8},{10,11... | collective-permute-start | bytes 884744 | tf_op jit(solution)/shard_map/ppermute | solution.py:44
  20.0 9.4 %collective-permute-start.11 = (bf16[192,768]{1,0:T(8,128)(2,1)}, bf16[192,768]{1,0:T(8,128)(2,1)S(1)}, u32[]{:S(2)}, u32[]{:S(2)}) collective-permute-start(bf16[192,768]{1,0:T(8,128)(2,1)} %refs_6_), channel_id=1, source_target_pairs={{0,2},{1,3},{2,0},{3,1},{4,6},{5,7},{6,4},{7,5},{8,10},{9,11},{10,... | collective-permute-start | bytes 884744 | tf_op jit(solution)/shard_map/ppermute | solution.py:44
  41.2 6.4 %collective-permute-start.15 = (bf16[80,768]{1,0:T(8,128)(2,1)S(1)}, bf16[80,768]{1,0:T(8,128)(2,1)S(1)}, u32[]{:S(2)}, u32[]{:S(2)}) collective-permute-start(bf16[80,768]{1,0:T(8,128)(2,1)S(1)} %convolution_convert_fusion.1), channel_id=1, source_target_pairs={{0,4},{4,0},{8,12},{12,8},{16,20},{20,16},{24,28},{28,24},{1,5},{5... | collective-permute-start | bytes 368648 | tf_op jit(solution)/shard_map/ppermute | solution.py:44
  44.8 6.4 %collective-permute-start.17 = (bf16[40,768]{1,0:T(8,128)(2,1)S(1)}, bf16[40,768]{1,0:T(8,128)(2,1)S(1)}, u32[]{:S(2)}, u32[]{:S(2)}) collective-permute-start(bf16[40,768]{1,0:T(8,128)(2,1)S(1)} %get-tuple-element.247), channel_id=1, source_target_pairs={{0,16},{4,20},{8,24},{12,28},{16,0},{20,4},{24,8},{28,12},{1,17},{... | collective-permute-start | bytes 184328 | tf_op jit(solution)/shard_map/ppermute | solution.py:44
  53.4 9.7 %collective-permute-start.19 = (bf16[160,768]{1,0:T(8,128)(2,1)S(1)}, bf16[160,768]{1,0:T(8,128)(2,1)S(1)}, u32[]{:S(2)}, u32[]{:S(2)}) collective-permute-start(bf16[160,768]{1,0:T(8,128)(2,1)S(1)} %pad_maximum_fusion.1.refs_0_.own), channel_id=1, source_target_pairs={{0,2},{1,3},{2,0},{3,1},{4,6},{5,7},{6,4},{7,5},{8,10},{9,11},{10,... | collective-permute-start | bytes 737288 | tf_op jit(solution)/shard_map/ppermute | solution.py:44
  62.0 8.8 %collective-permute-start.24 = (bf16[160,768]{1,0:T(8,128)(2,1)S(1)}, bf16[160,768]{1,0:T(8,128)(2,1)S(1)}, u32[]{:S(2)}, u32[]{:S(2)}) collective-permute-start(bf16[160,768]{1,0:T(8,128)(2,1)S(1)} %pad_maximum_fusion.2.refs_0_.own_grad), channel_id=1, source_target_pairs={{0,2},{1,3},{2,0},{3,1},{4,6},{5,7},{6,4},{7,5},{8,10},{9,11},{10,... | collective-permute-start | bytes 737288 | tf_op jit(solution)/shard_map/ppermute | solution.py:44
  69.8 8.6 %collective-permute-start.20 = (bf16[160,768]{1,0:T(8,128)(2,1)}, bf16[160,768]{1,0:T(8,128)(2,1)S(1)}, u32[]{:S(2)}, u32[]{:S(2)}) collective-permute-start(bf16[160,768]{1,0:T(8,128)(2,1)} %get-tuple-element.155), channel_id=1, source_target_pairs={{0,2},{1,3},{2,0},{3,1},{4,6},{5,7},{6,4},{7,5},{8,10},{9,11},{10,... | collective-permute-start | bytes 737288 | tf_op jit(solution)/shard_map/ppermute | solution.py:44
  77.3 6.4 %collective-permute-start.25 = (bf16[160,768]{1,0:T(8,128)(2,1)}, bf16[160,768]{1,0:T(8,128)(2,1)S(1)}, u32[]{:S(2)}, u32[]{:S(2)}) collective-permute-start(bf16[160,768]{1,0:T(8,128)(2,1)} %get-tuple-element.158), channel_id=1, source_target_pairs={{0,2},{1,3},{2,0},{3,1},{4,6},{5,7},{6,4},{7,5},{8,10},{9,11},{10,... | collective-permute-start | bytes 737288 | tf_op jit(solution)/shard_map/ppermute | solution.py:44
  79.1 9.1 %collective-permute-start.27 = (bf16[40,768]{1,0:T(8,128)(2,1)S(1)}, bf16[40,768]{1,0:T(8,128)(2,1)S(1)}, u32[]{:S(2)}, u32[]{:S(2)}) collective-permute-start(bf16[40,768]{1,0:T(8,128)(2,1)S(1)} %get-tuple-element.253), channel_id=1, source_target_pairs={{0,16},{4,20},{8,24},{12,28},{16,0},{20,4},{24,8},{28,12},{1,17},{... | collective-permute-start | bytes 184328 | tf_op jit(solution)/shard_map/ppermute | solution.py:44
  82.1 6.2 %collective-permute-start.28 = (bf16[40,768]{1,0:T(8,128)(2,1)S(1)}, bf16[40,768]{1,0:T(8,128)(2,1)S(1)}, u32[]{:S(2)}, u32[]{:S(2)}) collective-permute-start(bf16[40,768]{1,0:T(8,128)(2,1)S(1)} %get-tuple-element.252), channel_id=1, source_target_pairs={{0,24},{4,28},{8,16},{12,20},{16,8},{20,12},{24,0},{28,4},{1,25},{... | collective-permute-start | bytes 184328 | tf_op jit(solution)/shard_map/ppermute | solution.py:44
  93.7 6.3 %collective-permute-start.32 = (bf16[80,1536]{1,0:T(8,128)(2,1)S(1)}, bf16[80,1536]{1,0:T(8,128)(2,1)S(1)}, u32[]{:S(2)}, u32[]{:S(2)}) collective-permute-start(bf16[80,1536]{1,0:T(8,128)(2,1)S(1)} %maximum_maximum_fusion), channel_id=1, source_target_pairs={{0,4},{4,0},{8,12},{12,8},{16,20},{20,16},{24,28},{28,24},{1,5},{5... | collective-permute-start | bytes 737288 | tf_op jit(solution)/shard_map/ppermute | solution.py:44
  109.7 16.6 %collective-permute-start.37 = (bf16[1,768,768]{2,1,0:T(8,128)(2,1)}, bf16[1,768,768]{2,1,0:T(8,128)(2,1)S(1)}, u32[]{:S(2)}, u32[]{:S(2)}) collective-permute-start(bf16[1,768,768]{2,1,0:T(8,128)(2,1)} %get-tuple-element.196), channel_id=1, source_target_pairs={{0,1},{1,0},{2,3},{3,2},{4,5},{5,4},{6,7},{7,6},{8,9},{9,8},{10,11... | collective-permute-start | bytes 3538952 | tf_op jit(solution)/shard_map/ppermute | solution.py:44
  109.8 16.5 %collective-permute-start.38 = (bf16[1,768,768]{2,1,0:T(8,128)(2,1)}, bf16[1,768,768]{2,1,0:T(8,128)(2,1)}, u32[]{:S(2)}, u32[]{:S(2)}) collective-permute-start(bf16[1,768,768]{2,1,0:T(8,128)(2,1)} %get-tuple-element.197), channel_id=1, source_target_pairs={{0,1},{1,0},{2,3},{3,2},{4,5},{5,4},{6,7},{7,6},{8,9},{9,8},{10,11... | collective-permute-start | bytes 3538952 | tf_op jit(solution)/shard_map/ppermute | solution.py:44
  119.2 7.1 %collective-permute-start.36 = (bf16[1,5,24,640]{3,2,1,0:T(8,128)(2,1)}, bf16[1,5,24,640]{3,2,1,0:T(8,128)(2,1)S(1)}, u32[]{:S(2)}, u32[]{:S(2)}) collective-permute-start(bf16[1,5,24,640]{3,2,1,0:T(8,128)(2,1)} %get-tuple-element.194), channel_id=1, source_target_pairs={{0,4},{4,0},{8,12},{12,8},{16,20},{20,16},{24,28},{28,24},{1,5},{5... | collective-permute-start | bytes 460808 | tf_op jit(solution)/shard_map/ppermute | solution.py:44
  119.9 9.7 %collective-permute-start.42 = (bf16[1,5,24,640]{3,2,1,0:T(8,128)(2,1)}, bf16[1,5,24,640]{3,2,1,0:T(8,128)(2,1)S(1)}, u32[]{:S(2)}, u32[]{:S(2)}) collective-permute-start(bf16[1,5,24,640]{3,2,1,0:T(8,128)(2,1)} %get-tuple-element.203), channel_id=1, source_target_pairs={{0,4},{4,0},{8,12},{12,8},{16,20},{20,16},{24,28},{28,24},{1,5},{5... | collective-permute-start | bytes 460808 | tf_op jit(solution)/shard_map/ppermute | solution.py:44
  121.3 11.2 %collective-permute-start.40 = (bf16[2,128,768]{2,1,0:T(8,128)(2,1)}, bf16[2,128,768]{2,1,0:T(8,128)(2,1)S(1)}, u32[]{:S(2)}, u32[]{:S(2)}) collective-permute-start(bf16[2,128,768]{2,1,0:T(8,128)(2,1)} %get-tuple-element.199), channel_id=1, source_target_pairs={{0,1},{1,0},{2,3},{3,2},{4,5},{5,4},{6,7},{7,6},{8,9},{9,8},{10,11... | collective-permute-start | bytes 1179656 | tf_op jit(solution)/shard_map/ppermute | solution.py:44
  126.3 9.1 %collective-permute-start.39 = (bf16[2,5,24,640]{3,2,1,0:T(8,128)(2,1)}, bf16[2,5,24,640]{3,2,1,0:T(8,128)(2,1)S(1)}, u32[]{:S(2)}, u32[]{:S(2)}) collective-permute-start(bf16[2,5,24,640]{3,2,1,0:T(8,128)(2,1)} %get-tuple-element.198), channel_id=1, source_target_pairs={{0,4},{4,0},{8,12},{12,8},{16,20},{20,16},{24,28},{28,24},{1,5},{5... | collective-permute-start | bytes 921608 | tf_op jit(solution)/shard_map/ppermute | solution.py:44
  130.5 12.1 %collective-permute-start.43 = (bf16[5,24,640]{2,1,0:T(8,128)(2,1)S(1)}, bf16[5,24,640]{2,1,0:T(8,128)(2,1)S(1)}, u32[]{:S(2)}, u32[]{:S(2)}) collective-permute-start(bf16[5,24,640]{2,1,0:T(8,128)(2,1)S(1)} %fusion.35), channel_id=1, source_target_pairs={{0,16},{4,20},{8,24},{12,28},{16,0},{20,4},{24,8},{28,12},{1,17},{... | collective-permute-start | bytes 460808 | tf_op jit(solution)/shard_map/ppermute | solution.py:44
  131.6 11.0 %collective-permute-start.41 = (bf16[5,24,640]{2,1,0:T(8,128)(2,1)S(1)}, bf16[5,24,640]{2,1,0:T(8,128)(2,1)S(1)}, u32[]{:S(2)}, u32[]{:S(2)}) collective-permute-start(bf16[5,24,640]{2,1,0:T(8,128)(2,1)S(1)} %fusion.17), channel_id=1, source_target_pairs={{0,24},{4,28},{8,16},{12,20},{16,8},{20,12},{24,0},{28,4},{1,25},{... | collective-permute-start | bytes 460808 | tf_op jit(solution)/shard_map/ppermute | solution.py:44
  135.5 8.6 %collective-permute-start.45 = (bf16[128,768]{1,0:T(8,128)(2,1)S(1)}, bf16[128,768]{1,0:T(8,128)(2,1)S(1)}, u32[]{:S(2)}, u32[]{:S(2)}) collective-permute-start(bf16[128,768]{1,0:T(8,128)(2,1)S(1)} %fusion.34), channel_id=1, source_target_pairs={{0,2},{1,3},{2,0},{3,1},{4,6},{5,7},{6,4},{7,5},{8,10},{9,11},{10,... | collective-permute-start | bytes 589832 | tf_op jit(solution)/shard_map/ppermute | solution.py:44
  136.7 7.4 %collective-permute-start.44 = (bf16[5,24,640]{2,1,0:T(8,128)(2,1)S(1)}, bf16[5,24,640]{2,1,0:T(8,128)(2,1)S(1)}, u32[]{:S(2)}, u32[]{:S(2)}) collective-permute-start(bf16[5,24,640]{2,1,0:T(8,128)(2,1)S(1)} %fusion.36), channel_id=1, source_target_pairs={{0,8},{4,12},{8,0},{12,4},{16,24},{20,28},{24,16},{28,20},{1,9},{5... | collective-permute-start | bytes 460808 | tf_op jit(solution)/shard_map/ppermute | solution.py:44
  148.8 8.9 %collective-permute-start.50 = (bf16[5,24,640]{2,1,0:T(8,128)(2,1)S(1)}, bf16[5,24,640]{2,1,0:T(8,128)(2,1)S(1)}, u32[]{:S(2)}, u32[]{:S(2)}) collective-permute-start(bf16[5,24,640]{2,1,0:T(8,128)(2,1)S(1)} %slice_dynamic-update-slice_fusion.refs_0_), channel_id=1, source_target_pairs={{0,8},{4,12},{8,0},{12,4},{16,24},{20,28},{24,16},{28,20},{1,9},{5... | collective-permute-start | bytes 460808 | tf_op jit(solution)/shard_map/ppermute | solution.py:44
  149.5 8.2 %collective-permute-start.51 = (bf16[5,24,640]{2,1,0:T(8,128)(2,1)S(1)}, bf16[5,24,640]{2,1,0:T(8,128)(2,1)S(1)}, u32[]{:S(2)}, u32[]{:S(2)}) collective-permute-start(bf16[5,24,640]{2,1,0:T(8,128)(2,1)S(1)} %slice_dynamic-update-slice_fusion.refs_0_), channel_id=1, source_target_pairs={{0,4},{4,0},{8,12},{12,8},{16,20},{20,16},{24,28},{28,24},{1,5},{5... | collective-permute-start | bytes 460808 | tf_op jit(solution)/shard_map/ppermute | solution.py:44
  150.1 9.7 %collective-permute-start.49 = (bf16[5,24,640]{2,1,0:T(8,128)(2,1)S(1)}, bf16[5,24,640]{2,1,0:T(8,128)(2,1)S(1)}, u32[]{:S(2)}, u32[]{:S(2)}) collective-permute-start(bf16[5,24,640]{2,1,0:T(8,128)(2,1)S(1)} %slice_dynamic-update-slice_fusion.refs_0_), channel_id=1, source_target_pairs={{0,16},{4,20},{8,24},{12,28},{16,0},{20,4},{24,8},{28,12},{1,17},{... | collective-permute-start | bytes 460808 | tf_op jit(solution)/shard_map/ppermute | solution.py:44
  163.9 6.6 %collective-permute-start.54 = (bf16[5,24,640]{2,1,0:T(8,128)(2,1)S(1)}, bf16[5,24,640]{2,1,0:T(8,128)(2,1)S(1)}, u32[]{:S(2)}, u32[]{:S(2)}) collective-permute-start(bf16[5,24,640]{2,1,0:T(8,128)(2,1)S(1)} %collective-permute-done.49.refs_4_), channel_id=1, source_target_pairs={{0,4},{4,0},{8,12},{12,8},{16,20},{20,16},{24,28},{28,24},{1,5},{5... | collective-permute-start | bytes 460808 | tf_op jit(solution)/shard_map/ppermute | solution.py:44
  (60 other events, 385.5 us)

commit v11 on v8

--- a/solution.py
+++ b/solution.py
@@ -69,7 +69,7 @@
         in_specs=in_specs,
         out_specs=jax.tree.map(lambda _: vmem, out_shape),
         scratch_shapes=list(scratch),
-        compiler_params=pltpu.CompilerParams(vmem_limit_bytes=56 * 2**20),
+        compiler_params=pltpu.CompilerParams(vmem_limit_bytes=28 * 2**20),
         cost_estimate=pl.CostEstimate(flops=work, bytes_accessed=0, transcendentals=0),
     )(*operands)
 

time: 177 us -> 175 us (0.989)
  Pallas kernels: 43.9 us -> 26.5 us
  local copies, waits for them, and re-layouts: 3.66 us -> 12.4 us
  waiting for transfers between devices: 63.4 us -> 71 us
    pallas_call x8, Pallas kernels: 43.9 us -> 26.5 us  [call(): pl.pallas_call(kernel, out_shape=out_shape, in_specs=in_specs, out_specs=...]
    unnamed x72 -> x76, local copies, waits for them, and re-layouts: 2.4 us -> 10.4 us
    ppermute x55, waiting for transfers between devices: 63.4 us -> 71 us  [swap(): return lax.ppermute(value, axis, [(i, i ^ bit) for i in range(size)])]
  transfers between devices with their start and end apart: 55 -> 55, of which waited for: 29 -> 28; matrix products, arithmetic and copies ran while one was open for 5% -> 5% of each run, Pallas kernels for 23% -> 14%
where the time goes in v11:
time: 175 us
  waiting for transfers between devices  71 us (41%)
  starting transfers between devices  51.3 us (29%)
  Pallas kernels  26.5 us (15%)
  local copies, waits for them, and re-layouts  12.4 us (7%)
  other arithmetic  7.66 us (4%)
  matrix products  4.85 us (3%)
    ppermute x55, waiting for transfers between devices, swap(): return lax.ppermute(value, axis, [(i, i ^ bit) for i in range(size)])  71 us
    ppermute x55, starting transfers between devices, swap(): return lax.ppermute(value, axis, [(i, i ^ bit) for i in range(size)])  51.3 us
    pallas_call x8, Pallas kernels, call(): pl.pallas_call(kernel, out_shape=out_shape, in_specs=in_specs, out_specs=...  26.5 us
    unnamed x76, local copies, waits for them, and re-layouts  10.4 us
  transfers between devices with their start and end apart: 55, of which 28 were waited for; matrix products, arithmetic and copies ran while one was open for 5% of the time, Pallas kernels for 14%

profile of v11, /device:TPU:0, one launch (start us, length us, event | category | flops | bytes accessed | tf_op | source)
XLA Modules:
  0.0 175.0 jit_solution(10655354512150297236)
XLA Ops:
  0.7 3.0 %collective-permute-start = (bf16[128,768]{1,0:T(8,128)(2,1)}, bf16[128,768]{1,0:T(8,128)(2,1)S(1)}, u32[]{:S(2)}, u32[]{:S(2)}) collective-permute-start(bf16[128,768]{1,0:T(8,128)(2,1)} %refs_2_.2), channel_id=1, source_target_pairs={{0,2},{1,3},{2,0},{3,1},{4,6},{5,7},{6,4},{7,5},{8,10},{9,11},{10,... | collective-permute-start | bytes 589832 | tf_op jit(solution)/shard_map/ppermute | solution.py:44
  12.1 3.8 %collective-permute-done.4.refs_8_ = bf16[192,640]{1,0:T(8,128)(2,1)S(1)} collective-permute-done((bf16[192,640]{1,0:T(8,128)(2,1)S(1)}, bf16[192,640]{1,0:T(8,128)(2,1)S(1)}, u32[]{:S(2)}, u32[]{:S(2)}) %collective-permute-start.4) | collective-permute-done | bytes 245792 | tf_op jit(solution)/shard_map/ppermute | solution.py:44
  16.0 3.5 %collective-permute-done.5.refs_9_ = bf16[192,640]{1,0:T(8,128)(2,1)S(1)} collective-permute-done((bf16[192,640]{1,0:T(8,128)(2,1)S(1)}, bf16[192,640]{1,0:T(8,128)(2,1)S(1)}, u32[]{:S(2)}, u32[]{:S(2)}) %collective-permute-start.5) | collective-permute-done | bytes 245792 | tf_op jit(solution)/shard_map/ppermute | solution.py:44
  22.5 4.2 %shard_map.196 = (bf16[4,128,768]{2,1,0:T(8,128)(2,1)S(1)}, bf16[768,640]{1,0:T(8,128)(2,1)S(1)}, bf16[512,576]{1,0:T(8,128)(2,1)S(1)}, bf16[3,512,512]{2,1,0:T(...) custom-call(s32[1,3]{1,0:T(1,128)S(1)} %copy-done.14, ...), custom_call_target="tpu_custom_call" | custom-call | flops 10000000000 | tf_op jit(solution)/shard_map/pallas_call | solution.py:66
  31.8 1.9 %collective-permute-done.10 = bf16[128,192]{1,0:T(8,128)(2,1)S(1)} collective-permute-done((bf16[128,192]{1,0:T(8,128)(2,1)S(1)}, bf16[128,192]{1,0:T(8,128)(2,1)S(1)}, u32[]{:S(2)}, u32[]{:S(2)}) %collective-permute-start.10) | collective-permute-done | bytes 49184 | tf_op jit(solution)/shard_map/ppermute | solution.py:44
  39.0 3.5 %collective-permute-done.14 = bf16[80,768]{1,0:T(8,128)(2,1)S(1)} collective-permute-done((bf16[80,768]{1,0:T(8,128)(2,1)S(1)}, bf16[80,768]{1,0:T(8,128)(2,1)S(1)}, u32[]{:S(2)}, u32[]{:S(2)}) %collective-permute-start.14) | collective-permute-done | bytes 122912 | tf_op jit(solution)/shard_map/ppermute | solution.py:44
  46.6 2.6 %collective-permute-start.17 = (bf16[40,768]{1,0:T(8,128)(2,1)S(1)}, bf16[40,768]{1,0:T(8,128)(2,1)}, u32[]{:S(2)}, u32[]{:S(2)}) collective-permute-start(bf16[40,768]{1,0:T(8,128)(2,1)S(1)} %get-tuple-element.237), channel_id=1, source_target_pairs={{0,16},{4,20},{8,24},{12,28},{16,0},{20,4},{24,8},{28,12},{1,17},{... | collective-permute-start | bytes 184328 | tf_op jit(solution)/shard_map/ppermute | solution.py:44
  50.1 3.0 %collective-permute-done.17 = bf16[40,768]{1,0:T(8,128)(2,1)} collective-permute-done((bf16[40,768]{1,0:T(8,128)(2,1)S(1)}, bf16[40,768]{1,0:T(8,128)(2,1)}, u32[]{:S(2)}, u32[]{:S(2)}) %collective-permute-start.17) | collective-permute-done | bytes 61472 | tf_op jit(solution)/shard_map/ppermute | solution.py:44
  53.2 2.2 %collective-permute-done.18 = bf16[40,768]{1,0:T(8,128)(2,1)} collective-permute-done((bf16[40,768]{1,0:T(8,128)(2,1)S(1)}, bf16[40,768]{1,0:T(8,128)(2,1)}, u32[]{:S(2)}, u32[]{:S(2)}) %collective-permute-start.18) | collective-permute-done | bytes 61472 | tf_op jit(solution)/shard_map/ppermute | solution.py:44
  58.5 2.9 %collective-permute-start.23 = (bf16[40,768]{1,0:T(8,128)(2,1)S(1)}, bf16[40,768]{1,0:T(8,128)(2,1)S(1)}, u32[]{:S(2)}, u32[]{:S(2)}) collective-permute-start(bf16[40,768]{1,0:T(8,128)(2,1)S(1)} %get-tuple-element.247), channel_id=1, source_target_pairs={{0,24},{4,28},{8,16},{12,20},{16,8},{20,12},{24,0},{28,4},{1,25},{... | collective-permute-start | bytes 184328 | tf_op jit(solution)/shard_map/ppermute | solution.py:44
  62.3 2.4 %collective-permute-done.23 = bf16[40,768]{1,0:T(8,128)(2,1)S(1)} collective-permute-done((bf16[40,768]{1,0:T(8,128)(2,1)S(1)}, bf16[40,768]{1,0:T(8,128)(2,1)S(1)}, u32[]{:S(2)}, u32[]{:S(2)}) %collective-permute-start.23) | collective-permute-done | bytes 61472 | tf_op jit(solution)/shard_map/ppermute | solution.py:44
  68.6 3.8 %shard_map.197 = (bf16[2,320,768]{2,1,0:T(8,128)(2,1)S(1)}, bf16[2,320,768]{2,1,0:T(8,128)(2,1)S(1)}, f32[160,768]{1,0:T(8,128)S(1)}, bf16[160,768]{1,0:T(8,128)(2,1)S(1)}) custom-call(bf16[160,768]{1,0:T(8,128)(2,1)S(1)} %pad_maximum_fusion.1.refs_0_.own, bf16[160,768]{1,0:T(8,128)(2,1)S(1)} %collective-permute-done.19.refs_1_.came, ...), custom_call_target="tpu_custom_call" | custom-call | flops 6000000000 | tf_op jit(solution)/shard_map/pallas_call | solution.py:66
  73.2 3.5 %shard_map.198 = (bf16[2,320,768]{2,1,0:T(8,128)(2,1)S(1)}, f32[160,768]{1,0:T(8,128)S(1)}, bf16[160,768]{1,0:T(8,128)(2,1)S(1)}) custom-call(bf16[160,768]{1,0:T(8,128)(2,1)S(1)} %pad_maximum_fusion.2.refs_0_.own_grad, bf16[160,768]{1,0:T(8,128)(2,1)S(1)} %collective-permute-done.24.refs_1_.came_grad, bf16[1,768,768]{2,1,0:T(8,128)(2,1)S(1)} %copy-done.7, ...), custom_call_target="tpu_custom_call" | custom-call | flops 6000000000 | tf_op jit(solution)/shard_map/pallas_call | solution.py:66
  78.0 1.8 %collective-permute-done.20 = bf16[160,768]{1,0:T(8,128)(2,1)S(1)} collective-permute-done((bf16[160,768]{1,0:T(8,128)(2,1)S(1)}, bf16[160,768]{1,0:T(8,128)(2,1)S(1)}, u32[]{:S(2)}, u32[]{:S(2)}) %collective-permute-start.20) | collective-permute-done | bytes 245792 | tf_op jit(solution)/shard_map/ppermute | solution.py:44
  80.0 3.7 %collective-permute-start.27 = (bf16[40,768]{1,0:T(8,128)(2,1)S(1)}, bf16[40,768]{1,0:T(8,128)(2,1)S(1)}, u32[]{:S(2)}, u32[]{:S(2)}) collective-permute-start(bf16[40,768]{1,0:T(8,128)(2,1)S(1)} %get-tuple-element.243), channel_id=1, source_target_pairs={{0,16},{4,20},{8,24},{12,28},{16,0},{20,4},{24,8},{28,12},{1,17},{... | collective-permute-start | bytes 184328 | tf_op jit(solution)/shard_map/ppermute | solution.py:44
  84.6 3.7 %collective-permute-start.30 = (bf16[40,768]{1,0:T(8,128)(2,1)S(1)}, bf16[40,768]{1,0:T(8,128)(2,1)S(1)}, u32[]{:S(2)}, u32[]{:S(2)}) collective-permute-start(bf16[40,768]{1,0:T(8,128)(2,1)S(1)} %get-tuple-element.239), channel_id=1, source_target_pairs={{0,16},{4,20},{8,24},{12,28},{16,0},{20,4},{24,8},{28,12},{1,17},{... | collective-permute-start | bytes 184328 | tf_op jit(solution)/shard_map/ppermute | solution.py:44
  90.5 3.8 %collective-permute-done.31 = bf16[40,768]{1,0:T(8,128)(2,1)S(1)} collective-permute-done((bf16[40,768]{1,0:T(8,128)(2,1)S(1)}, bf16[40,768]{1,0:T(8,128)(2,1)S(1)}, u32[]{:S(2)}, u32[]{:S(2)}) %collective-permute-start.31) | collective-permute-done | bytes 61472 | tf_op jit(solution)/shard_map/ppermute | solution.py:44
  95.0 2.2 %shard_map.199 = (bf16[1,768,768]{2,1,0:T(8,128)(2,1)}, bf16[1,768,768]{2,1,0:T(8,128)(2,1)S(1)}) custom-call(bf16[160,768]{1,0:T(8,128)(2,1)S(1)} %pad_maximum_fusion.1.refs_0_.own, bf16[160,768]{1,0:T(8,128)(2,1)S(1)} %collective-permute-done.19.refs_1_.came, bf16[160,768]{1,0:T(8,128)(2,1)S(1)} %pad_maximum_fusion.2.refs_0_.own_grad, ...), custom_call_target="tpu_custom_call" | custom-call | flops 4000000000 | tf_op jit(solution)/shard_map/pallas_call | solution.py:66
  97.5 3.3 %collective-permute-done.32 = bf16[80,1536]{1,0:T(8,128)(2,1)S(1)} collective-permute-done((bf16[80,1536]{1,0:T(8,128)(2,1)S(1)}, bf16[80,1536]{1,0:T(8,128)(2,1)S(1)}, u32[]{:S(2)}, u32[]{:S(2)}) %collective-permute-start.32) | collective-permute-done | bytes 245792 | tf_op jit(solution)/shard_map/ppermute | solution.py:44
  105.4 3.8 %collective-permute-done.33.refs_11_ = bf16[128,768]{1,0:T(8,128)(2,1)S(1)} collective-permute-done((bf16[128,768]{1,0:T(8,128)(2,1)S(1)}, bf16[128,768]{1,0:T(8,128)(2,1)S(1)}, u32[]{:S(2)}, u32[]{:S(2)}) %collective-permute-start.33) | collective-permute-done | bytes 196640 | tf_op jit(solution)/shard_map/ppermute | solution.py:44
  111.2 5.7 %shard_map.200 = (bf16[2,5,24,640]{3,2,1,0:T(8,128)(2,1)S(1)}, bf16[2,5,24,640]{3,2,1,0:T(8,128)(2,1)S(1)}, bf16[2,5,24,640]{3,2,1,0:T(8,128)(2,1)S(1)}, bf16[2,...) custom-call(bf16[512,576]{1,0:T(8,128)(2,1)S(1)} %copy-done.26, ...), custom_call_target="tpu_custom_call" | custom-call | flops 8000000000 | tf_op jit(solution)/shard_map/pallas_call | solution.py:66
  121.9 5.6 %collective-permute-done.52 = bf16[128,768]{1,0:T(8,128)(2,1)S(1)} collective-permute-done((bf16[128,768]{1,0:T(8,128)(2,1)}, bf16[128,768]{1,0:T(8,128)(2,1)S(1)}, u32[]{:S(2)}, u32[]{:S(2)}) %collective-permute-start.52) | collective-permute-done | bytes 196640 | tf_op jit(solution)/shard_map/ppermute | solution.py:44
  130.2 5.9 %collective-permute-done.39 = bf16[2,5,24,640]{3,2,1,0:T(8,128)(2,1)S(1)} collective-permute-done((bf16[2,5,24,640]{3,2,1,0:T(8,128)(2,1)S(1)}, bf16[2,5,24,640]{3,2,1,0:T(8,128)(2,1)S(1)}, u32[]{:S(2)}, u32[]{:S(2)}) %collective-permute-start.39) | collective-permute-done | bytes 307232 | tf_op jit(solution)/shard_map/ppermute | solution.py:44
  136.3 4.8 %shard_map.201 = (f32[1,768,768]{2,1,0:T(8,128)}, f32[1,768,768]{2,1,0:T(8,128)}) custom-call(bf16[160,768]{1,0:T(8,128)(2,1)S(1)} %pad_maximum_fusion.1.refs_0_.own, bf16[160,768]{1,0:T(8,128)(2,1)S(1)} %collective-permute-done.19.refs_1_.came, bf16[160,768]{1,0:T(8,128)(2,1)S(1)} %pad_maximum_fusion.2.refs_0_.own_grad, bf16[160,768]{1,0:T(8,128)(2,1)S(1)} %copy-done.13, ...), custom_call_target="tpu_custom_call" | custom-call | flops 4000000000 | tf_op jit(solution)/shard_map/pallas_call | solution.py:66
  141.2 2.3 %collective-permute-done.42 = bf16[5,24,640]{2,1,0:T(8,128)(2,1)S(1)} collective-permute-done((bf16[5,24,640]{2,1,0:T(8,128)(2,1)S(1)}, bf16[5,24,640]{2,1,0:T(8,128)(2,1)S(1)}, u32[]{:S(2)}, u32[]{:S(2)}) %collective-permute-start.42) | collective-permute-done | bytes 153632 | tf_op jit(solution)/shard_map/ppermute | solution.py:44
  145.8 2.0 %collective-permute-done.44 = bf16[24,640]{1,0:T(8,128)(2,1)S(1)} collective-permute-done((bf16[24,640]{1,0:T(8,128)(2,1)S(1)}, bf16[24,640]{1,0:T(8,128)(2,1)S(1)}, u32[]{:S(2)}, u32[]{:S(2)}) %collective-permute-start.44) | collective-permute-done | bytes 30752 | tf_op jit(solution)/shard_map/ppermute | solution.py:44
  150.7 2.0 %collective-permute-start.46 = (bf16[5,24,640]{2,1,0:T(8,128)(2,1)S(1)}, bf16[5,24,640]{2,1,0:T(8,128)(2,1)S(1)}, u32[]{:S(2)}, u32[]{:S(2)}) collective-permute-start(bf16[5,24,640]{2,1,0:T(8,128)(2,1)S(1)} %slice_dynamic-update-slice_fusion.refs_0_), channel_id=1, source_target_pairs={{0,16},{4,20},{8,24},{12,28},{16,0},{20,4},{24,8},{28,12},{1,17},{... | collective-permute-start | bytes 460808 | tf_op jit(solution)/shard_map/ppermute | solution.py:44
  152.7 4.7 %collective-permute-done.47.refs_2_ = bf16[5,24,640]{2,1,0:T(8,128)(2,1)S(1)} collective-permute-done((bf16[5,24,640]{2,1,0:T(8,128)(2,1)S(1)}, bf16[5,24,640]{2,1,0:T(8,128)(2,1)S(1)}, u32[]{:S(2)}, u32[]{:S(2)}) %collective-permute-start.47) | collective-permute-done | bytes 153632 | tf_op jit(solution)/shard_map/ppermute | solution.py:44
  160.5 2.2 %collective-permute-done.49.refs_3_ = bf16[5,24,640]{2,1,0:T(8,128)(2,1)S(1)} collective-permute-done((bf16[5,24,640]{2,1,0:T(8,128)(2,1)S(1)}, bf16[5,24,640]{2,1,0:T(8,128)(2,1)S(1)}, u32[]{:S(2)}, u32[]{:S(2)}) %collective-permute-start.49) | collective-permute-done | bytes 153632 | tf_op jit(solution)/shard_map/ppermute | solution.py:44
  165.0 2.9 %collective-permute-done.50.refs_6_ = bf16[5,24,640]{2,1,0:T(8,128)(2,1)S(1)} collective-permute-done((bf16[5,24,640]{2,1,0:T(8,128)(2,1)S(1)}, bf16[5,24,640]{2,1,0:T(8,128)(2,1)S(1)}, u32[]{:S(2)}, u32[]{:S(2)}) %collective-permute-start.50) | collective-permute-done | bytes 153632 | tf_op jit(solution)/shard_map/ppermute | solution.py:44
  170.3 2.8 %collective-permute-done.54.refs_7_ = bf16[5,24,640]{2,1,0:T(8,128)(2,1)S(1)} collective-permute-done((bf16[5,24,640]{2,1,0:T(8,128)(2,1)S(1)}, bf16[5,24,640]{2,1,0:T(8,128)(2,1)S(1)}, u32[]{:S(2)}, u32[]{:S(2)}) %collective-permute-start.54) | collective-permute-done | bytes 153632 | tf_op jit(solution)/shard_map/ppermute | solution.py:44
  173.1 1.9 %shard_map.202 = (f32[192,2304]{1,0:T(8,128)}, f32[192,768]{1,0:T(8,128)}, f32[1,192]{1,0:T(1,128)}, f32[1,192]{1,0:T(1,128)}, f32[8,192]{1,0:T(8,128)}) custom-call(bf16[5,24,640]{2,1,0:T(8,128)(2,1)S(1)} %slice_dynamic-update-slice_fusion.refs_0_, bf16[5,24,640]{2,1,0:T(8,128)(2,1)S(1)} %collective-permute-done.48.refs_1_, ...), custom_call_target="tpu_custom_call" | custom-call | tf_op jit(solution)/shard_map/pallas_call | solution.py:66
  (228 shorter events, 68.0 us)
Async XLA Ops:
  0.7 8.6 %collective-permute-start = (bf16[128,768]{1,0:T(8,128)(2,1)}, bf16[128,768]{1,0:T(8,128)(2,1)S(1)}, u32[]{:S(2)}, u32[]{:S(2)}) collective-permute-start(bf16[128,768]{1,0:T(8,128)(2,1)} %refs_2_.2), channel_id=1, source_target_pairs={{0,2},{1,3},{2,0},{3,1},{4,6},{5,7},{6,4},{7,5},{8,10},{9,11},{10,... | collective-permute-start | bytes 589832 | tf_op jit(solution)/shard_map/ppermute | solution.py:44
  3.7 6.3 %collective-permute-start.1 = (bf16[128,768]{1,0:T(8,128)(2,1)}, bf16[128,768]{1,0:T(8,128)(2,1)S(1)}, u32[]{:S(2)}, u32[]{:S(2)}) collective-permute-start(bf16[128,768]{1,0:T(8,128)(2,1)} %refs_2_.2), channel_id=1, source_target_pairs={{0,1},{1,0},{2,3},{3,2},{4,5},{5,4},{6,7},{7,6},{8,9},{9,8},{10,11... | collective-permute-start | bytes 589832 | tf_op jit(solution)/shard_map/ppermute | solution.py:44
  7.2 8.8 %collective-permute-start.4 = (bf16[192,640]{1,0:T(8,128)(2,1)S(1)}, bf16[192,640]{1,0:T(8,128)(2,1)S(1)}, u32[]{:S(2)}, u32[]{:S(2)}) collective-permute-start(bf16[192,640]{1,0:T(8,128)(2,1)S(1)} %get-tuple-element.120), channel_id=1, source_target_pairs={{0,2},{1,3},{2,0},{3,1},{4,6},{5,7},{6,4},{7,5},{8,10},{9,11},{10,... | collective-permute-start | bytes 737288 | tf_op jit(solution)/shard_map/ppermute | solution.py:44
  7.2 12.2 %collective-permute-start.5 = (bf16[192,640]{1,0:T(8,128)(2,1)S(1)}, bf16[192,640]{1,0:T(8,128)(2,1)S(1)}, u32[]{:S(2)}, u32[]{:S(2)}) collective-permute-start(bf16[192,640]{1,0:T(8,128)(2,1)S(1)} %get-tuple-element.121), channel_id=1, source_target_pairs={{0,3},{1,2},{2,1},{3,0},{4,7},{5,6},{6,5},{7,4},{8,11},{9,10},{10,... | collective-permute-start | bytes 737288 | tf_op jit(solution)/shard_map/ppermute | solution.py:44
  9.3 20.0 %collective-permute-start.6 = (bf16[1,768,768]{2,1,0:T(8,128)(2,1)}, bf16[1,768,768]{2,1,0:T(8,128)(2,1)S(1)}, u32[]{:S(2)}, u32[]{:S(2)}) collective-permute-start(bf16[1,768,768]{2,1,0:T(8,128)(2,1)} %refs_2_.4), channel_id=1, source_target_pairs={{0,1},{1,0},{2,3},{3,2},{4,5},{5,4},{6,7},{7,6},{8,9},{9,8},{10,11... | collective-permute-start | bytes 3538952 | tf_op jit(solution)/shard_map/ppermute | solution.py:44
  10.0 19.4 %collective-permute-start.7 = (bf16[1,768,768]{2,1,0:T(8,128)(2,1)}, bf16[1,768,768]{2,1,0:T(8,128)(2,1)}, u32[]{:S(2)}, u32[]{:S(2)}) collective-permute-start(bf16[1,768,768]{2,1,0:T(8,128)(2,1)} %refs_4_.1), channel_id=1, source_target_pairs={{0,1},{1,0},{2,3},{3,2},{4,5},{5,4},{6,7},{7,6},{8,9},{9,8},{10,11... | collective-permute-start | bytes 3538952 | tf_op jit(solution)/shard_map/ppermute | solution.py:44
  10.9 8.5 %collective-permute-start.2 = (bf16[128,768]{1,0:T(8,128)(2,1)S(1)}, bf16[128,768]{1,0:T(8,128)(2,1)S(1)}, u32[]{:S(2)}, u32[]{:S(2)}) collective-permute-start(bf16[128,768]{1,0:T(8,128)(2,1)S(1)} %collective-permute-done.refs_4_), channel_id=1, source_target_pairs={{0,1},{1,0},{2,3},{3,2},{4,5},{5,4},{6,7},{7,6},{8,9},{9,8},{10,11... | collective-permute-start | bytes 589832 | tf_op jit(solution)/shard_map/ppermute | solution.py:44
  19.5 9.8 %collective-permute-start.8 = (bf16[192,768]{1,0:T(8,128)(2,1)}, bf16[192,768]{1,0:T(8,128)(2,1)S(1)}, u32[]{:S(2)}, u32[]{:S(2)}) collective-permute-start(bf16[192,768]{1,0:T(8,128)(2,1)} %refs_6_), channel_id=1, source_target_pairs={{0,1},{1,0},{2,3},{3,2},{4,5},{5,4},{6,7},{7,6},{8,9},{9,8},{10,11... | collective-permute-start | bytes 884744 | tf_op jit(solution)/shard_map/ppermute | solution.py:44
  20.2 10.7 %collective-permute-start.11 = (bf16[192,768]{1,0:T(8,128)(2,1)}, bf16[192,768]{1,0:T(8,128)(2,1)S(1)}, u32[]{:S(2)}, u32[]{:S(2)}) collective-permute-start(bf16[192,768]{1,0:T(8,128)(2,1)} %refs_6_), channel_id=1, source_target_pairs={{0,2},{1,3},{2,0},{3,1},{4,6},{5,7},{6,4},{7,5},{8,10},{9,11},{10,... | collective-permute-start | bytes 884744 | tf_op jit(solution)/shard_map/ppermute | solution.py:44
  42.5 7.0 %collective-permute-start.15 = (bf16[80,768]{1,0:T(8,128)(2,1)S(1)}, bf16[80,768]{1,0:T(8,128)(2,1)S(1)}, u32[]{:S(2)}, u32[]{:S(2)}) collective-permute-start(bf16[80,768]{1,0:T(8,128)(2,1)S(1)} %convolution_convert_fusion.1), channel_id=1, source_target_pairs={{0,4},{4,0},{8,12},{12,8},{16,20},{20,16},{24,28},{28,24},{1,5},{5... | collective-permute-start | bytes 368648 | tf_op jit(solution)/shard_map/ppermute | solution.py:44
  46.6 6.5 %collective-permute-start.17 = (bf16[40,768]{1,0:T(8,128)(2,1)S(1)}, bf16[40,768]{1,0:T(8,128)(2,1)}, u32[]{:S(2)}, u32[]{:S(2)}) collective-permute-start(bf16[40,768]{1,0:T(8,128)(2,1)S(1)} %get-tuple-element.237), channel_id=1, source_target_pairs={{0,16},{4,20},{8,24},{12,28},{16,0},{20,4},{24,8},{28,12},{1,17},{... | collective-permute-start | bytes 184328 | tf_op jit(solution)/shard_map/ppermute | solution.py:44
  49.2 6.1 %collective-permute-start.18 = (bf16[40,768]{1,0:T(8,128)(2,1)S(1)}, bf16[40,768]{1,0:T(8,128)(2,1)}, u32[]{:S(2)}, u32[]{:S(2)}) collective-permute-start(bf16[40,768]{1,0:T(8,128)(2,1)S(1)} %get-tuple-element.236), channel_id=1, source_target_pairs={{0,24},{4,28},{8,16},{12,20},{16,8},{20,12},{24,0},{28,4},{1,25},{... | collective-permute-start | bytes 184328 | tf_op jit(solution)/shard_map/ppermute | solution.py:44
  56.2 9.8 %collective-permute-start.19 = (bf16[160,768]{1,0:T(8,128)(2,1)S(1)}, bf16[160,768]{1,0:T(8,128)(2,1)S(1)}, u32[]{:S(2)}, u32[]{:S(2)}) collective-permute-start(bf16[160,768]{1,0:T(8,128)(2,1)S(1)} %pad_maximum_fusion.1.refs_0_.own), channel_id=1, source_target_pairs={{0,2},{1,3},{2,0},{3,1},{4,6},{5,7},{6,4},{7,5},{8,10},{9,11},{10,... | collective-permute-start | bytes 737288 | tf_op jit(solution)/shard_map/ppermute | solution.py:44
  58.5 6.1 %collective-permute-start.23 = (bf16[40,768]{1,0:T(8,128)(2,1)S(1)}, bf16[40,768]{1,0:T(8,128)(2,1)S(1)}, u32[]{:S(2)}, u32[]{:S(2)}) collective-permute-start(bf16[40,768]{1,0:T(8,128)(2,1)S(1)} %get-tuple-element.247), channel_id=1, source_target_pairs={{0,24},{4,28},{8,16},{12,20},{16,8},{20,12},{24,0},{28,4},{1,25},{... | collective-permute-start | bytes 184328 | tf_op jit(solution)/shard_map/ppermute | solution.py:44
  64.6 8.5 %collective-permute-start.24 = (bf16[160,768]{1,0:T(8,128)(2,1)S(1)}, bf16[160,768]{1,0:T(8,128)(2,1)S(1)}, u32[]{:S(2)}, u32[]{:S(2)}) collective-permute-start(bf16[160,768]{1,0:T(8,128)(2,1)S(1)} %pad_maximum_fusion.2.refs_0_.own_grad), channel_id=1, source_target_pairs={{0,2},{1,3},{2,0},{3,1},{4,6},{5,7},{6,4},{7,5},{8,10},{9,11},{10,... | collective-permute-start | bytes 737288 | tf_op jit(solution)/shard_map/ppermute | solution.py:44
  72.4 7.5 %collective-permute-start.20 = (bf16[160,768]{1,0:T(8,128)(2,1)S(1)}, bf16[160,768]{1,0:T(8,128)(2,1)S(1)}, u32[]{:S(2)}, u32[]{:S(2)}) collective-permute-start(bf16[160,768]{1,0:T(8,128)(2,1)S(1)} %get-tuple-element.149), channel_id=1, source_target_pairs={{0,2},{1,3},{2,0},{3,1},{4,6},{5,7},{6,4},{7,5},{8,10},{9,11},{10,... | collective-permute-start | bytes 737288 | tf_op jit(solution)/shard_map/ppermute | solution.py:44
  76.6 7.8 %collective-permute-start.25 = (bf16[160,768]{1,0:T(8,128)(2,1)S(1)}, bf16[160,768]{1,0:T(8,128)(2,1)S(1)}, u32[]{:S(2)}, u32[]{:S(2)}) collective-permute-start(bf16[160,768]{1,0:T(8,128)(2,1)S(1)} %get-tuple-element.152), channel_id=1, source_target_pairs={{0,2},{1,3},{2,0},{3,1},{4,6},{5,7},{6,4},{7,5},{8,10},{9,11},{10,... | collective-permute-start | bytes 737288 | tf_op jit(solution)/shard_map/ppermute | solution.py:44
  80.0 8.9 %collective-permute-start.27 = (bf16[40,768]{1,0:T(8,128)(2,1)S(1)}, bf16[40,768]{1,0:T(8,128)(2,1)S(1)}, u32[]{:S(2)}, u32[]{:S(2)}) collective-permute-start(bf16[40,768]{1,0:T(8,128)(2,1)S(1)} %get-tuple-element.243), channel_id=1, source_target_pairs={{0,16},{4,20},{8,24},{12,28},{16,0},{20,4},{24,8},{28,12},{1,17},{... | collective-permute-start | bytes 184328 | tf_op jit(solution)/shard_map/ppermute | solution.py:44
  83.7 6.0 %collective-permute-start.28 = (bf16[40,768]{1,0:T(8,128)(2,1)S(1)}, bf16[40,768]{1,0:T(8,128)(2,1)S(1)}, u32[]{:S(2)}, u32[]{:S(2)}) collective-permute-start(bf16[40,768]{1,0:T(8,128)(2,1)S(1)} %get-tuple-element.242), channel_id=1, source_target_pairs={{0,24},{4,28},{8,16},{12,20},{16,8},{20,12},{24,0},{28,4},{1,25},{... | collective-permute-start | bytes 184328 | tf_op jit(solution)/shard_map/ppermute | solution.py:44
  94.5 6.3 %collective-permute-start.32 = (bf16[80,1536]{1,0:T(8,128)(2,1)S(1)}, bf16[80,1536]{1,0:T(8,128)(2,1)S(1)}, u32[]{:S(2)}, u32[]{:S(2)}) collective-permute-start(bf16[80,1536]{1,0:T(8,128)(2,1)S(1)} %maximum_maximum_fusion), channel_id=1, source_target_pairs={{0,4},{4,0},{8,12},{12,8},{16,20},{20,16},{24,28},{28,24},{1,5},{5... | collective-permute-start | bytes 737288 | tf_op jit(solution)/shard_map/ppermute | solution.py:44
  110.7 16.8 %collective-permute-start.37 = (bf16[1,768,768]{2,1,0:T(8,128)(2,1)}, bf16[1,768,768]{2,1,0:T(8,128)(2,1)}, u32[]{:S(2)}, u32[]{:S(2)}) collective-permute-start(bf16[1,768,768]{2,1,0:T(8,128)(2,1)} %get-tuple-element.190), channel_id=1, source_target_pairs={{0,1},{1,0},{2,3},{3,2},{4,5},{5,4},{6,7},{7,6},{8,9},{9,8},{10,11... | collective-permute-start | bytes 3538952 | tf_op jit(solution)/shard_map/ppermute | solution.py:44
  110.8 16.7 %collective-permute-start.38 = (bf16[1,768,768]{2,1,0:T(8,128)(2,1)S(1)}, bf16[1,768,768]{2,1,0:T(8,128)(2,1)}, u32[]{:S(2)}, u32[]{:S(2)}) collective-permute-start(bf16[1,768,768]{2,1,0:T(8,128)(2,1)S(1)} %get-tuple-element.191), channel_id=1, source_target_pairs={{0,1},{1,0},{2,3},{3,2},{4,5},{5,4},{6,7},{7,6},{8,9},{9,8},{10,11... | collective-permute-start | bytes 3538952 | tf_op jit(solution)/shard_map/ppermute | solution.py:44
  117.1 10.4 %collective-permute-start.36 = (bf16[2,5,24,640]{3,2,1,0:T(8,128)(2,1)S(1)}, bf16[2,5,24,640]{3,2,1,0:T(8,128)(2,1)}, u32[]{:S(2)}, u32[]{:S(2)}) collective-permute-start(bf16[2,5,24,640]{3,2,1,0:T(8,128)(2,1)S(1)} %get-tuple-element.188), channel_id=1, source_target_pairs={{0,4},{4,0},{8,12},{12,8},{16,20},{20,16},{24,28},{28,24},{1,5},{5... | collective-permute-start | bytes 921608 | tf_op jit(solution)/shard_map/ppermute | solution.py:44
  120.3 7.2 %collective-permute-start.52 = (bf16[128,768]{1,0:T(8,128)(2,1)}, bf16[128,768]{1,0:T(8,128)(2,1)S(1)}, u32[]{:S(2)}, u32[]{:S(2)}) collective-permute-start(bf16[128,768]{1,0:T(8,128)(2,1)} %fusion.33), channel_id=1, source_target_pairs={{0,2},{1,3},{2,0},{3,1},{4,6},{5,7},{6,4},{7,5},{8,10},{9,11},{10,... | collective-permute-start | bytes 589832 | tf_op jit(solution)/shard_map/ppermute | solution.py:44
  127.5 8.6 %collective-permute-start.39 = (bf16[2,5,24,640]{3,2,1,0:T(8,128)(2,1)S(1)}, bf16[2,5,24,640]{3,2,1,0:T(8,128)(2,1)S(1)}, u32[]{:S(2)}, u32[]{:S(2)}) collective-permute-start(bf16[2,5,24,640]{3,2,1,0:T(8,128)(2,1)S(1)} %get-tuple-element.192), channel_id=1, source_target_pairs={{0,4},{4,0},{8,12},{12,8},{16,20},{20,16},{24,28},{28,24},{1,5},{5... | collective-permute-start | bytes 921608 | tf_op jit(solution)/shard_map/ppermute | solution.py:44
  129.4 11.8 %collective-permute-start.40 = (bf16[5,24,640]{2,1,0:T(8,128)(2,1)S(1)}, bf16[5,24,640]{2,1,0:T(8,128)(2,1)S(1)}, u32[]{:S(2)}, u32[]{:S(2)}) collective-permute-start(bf16[5,24,640]{2,1,0:T(8,128)(2,1)S(1)} %get-tuple-element.233), channel_id=1, source_target_pairs={{0,16},{4,20},{8,24},{12,28},{16,0},{20,4},{24,8},{28,12},{1,17},{... | collective-permute-start | bytes 460808 | tf_op jit(solution)/shard_map/ppermute | solution.py:44
  129.5 11.7 %collective-permute-start.41 = (bf16[5,24,640]{2,1,0:T(8,128)(2,1)S(1)}, bf16[5,24,640]{2,1,0:T(8,128)(2,1)S(1)}, u32[]{:S(2)}, u32[]{:S(2)}) collective-permute-start(bf16[5,24,640]{2,1,0:T(8,128)(2,1)S(1)} %get-tuple-element.232), channel_id=1, source_target_pairs={{0,24},{4,28},{8,16},{12,20},{16,8},{20,12},{24,0},{28,4},{1,25},{... | collective-permute-start | bytes 460808 | tf_op jit(solution)/shard_map/ppermute | solution.py:44
  136.2 7.3 %collective-permute-start.42 = (bf16[5,24,640]{2,1,0:T(8,128)(2,1)S(1)}, bf16[5,24,640]{2,1,0:T(8,128)(2,1)S(1)}, u32[]{:S(2)}, u32[]{:S(2)}) collective-permute-start(bf16[5,24,640]{2,1,0:T(8,128)(2,1)S(1)} %fusion.34), channel_id=1, source_target_pairs={{0,8},{4,12},{8,0},{12,4},{16,24},{20,28},{24,16},{28,20},{1,9},{5... | collective-permute-start | bytes 460808 | tf_op jit(solution)/shard_map/ppermute | solution.py:44
  148.9 8.6 %collective-permute-start.47 = (bf16[5,24,640]{2,1,0:T(8,128)(2,1)S(1)}, bf16[5,24,640]{2,1,0:T(8,128)(2,1)S(1)}, u32[]{:S(2)}, u32[]{:S(2)}) collective-permute-start(bf16[5,24,640]{2,1,0:T(8,128)(2,1)S(1)} %slice_dynamic-update-slice_fusion.refs_0_), channel_id=1, source_target_pairs={{0,8},{4,12},{8,0},{12,4},{16,24},{20,28},{24,16},{28,20},{1,9},{5... | collective-permute-start | bytes 460808 | tf_op jit(solution)/shard_map/ppermute | solution.py:44
  149.6 7.9 %collective-permute-start.48 = (bf16[5,24,640]{2,1,0:T(8,128)(2,1)S(1)}, bf16[5,24,640]{2,1,0:T(8,128)(2,1)S(1)}, u32[]{:S(2)}, u32[]{:S(2)}) collective-permute-start(bf16[5,24,640]{2,1,0:T(8,128)(2,1)S(1)} %slice_dynamic-update-slice_fusion.refs_0_), channel_id=1, source_target_pairs={{0,4},{4,0},{8,12},{12,8},{16,20},{20,16},{24,28},{28,24},{1,5},{5... | collective-permute-start | bytes 460808 | tf_op jit(solution)/shard_map/ppermute | solution.py:44
  150.7 9.8 %collective-permute-start.46 = (bf16[5,24,640]{2,1,0:T(8,128)(2,1)S(1)}, bf16[5,24,640]{2,1,0:T(8,128)(2,1)S(1)}, u32[]{:S(2)}, u32[]{:S(2)}) collective-permute-start(bf16[5,24,640]{2,1,0:T(8,128)(2,1)S(1)} %slice_dynamic-update-slice_fusion.refs_0_), channel_id=1, source_target_pairs={{0,16},{4,20},{8,24},{12,28},{16,0},{20,4},{24,8},{28,12},{1,17},{... | collective-permute-start | bytes 460808 | tf_op jit(solution)/shard_map/ppermute | solution.py:44
  163.6 6.7 %collective-permute-start.53 = (bf16[5,24,640]{2,1,0:T(8,128)(2,1)S(1)}, bf16[5,24,640]{2,1,0:T(8,128)(2,1)S(1)}, u32[]{:S(2)}, u32[]{:S(2)}) collective-permute-start(bf16[5,24,640]{2,1,0:T(8,128)(2,1)S(1)} %collective-permute-done.46.refs_4_), channel_id=1, source_target_pairs={{0,4},{4,0},{8,12},{12,8},{16,20},{20,16},{24,28},{28,24},{1,5},{5... | collective-permute-start | bytes 460808 | tf_op jit(solution)/shard_map/ppermute | solution.py:44
  (61 other events, 357.8 us)

commit v12 on v11

--- a/solution.py
+++ b/solution.py
@@ -59,7 +59,7 @@
     return [blocks[0]] + [swap(block, axis, p) for p, block in enumerate(blocks) if p]
 
 
-def call(kernel, out_shape, operands, spaces="", scratch=(), work=0):
+def call(kernel, out_shape, operands, spaces="", scratch=(), work=0, room=24):
     vmem = pl.BlockSpec(memory_space=pltpu.VMEM)
     smem = pl.BlockSpec(memory_space=pltpu.SMEM)
     in_specs = [smem if spaces[i : i + 1] == "s" else vmem for i in range(len(operands))]
@@ -69,7 +69,7 @@
         in_specs=in_specs,
         out_specs=jax.tree.map(lambda _: vmem, out_shape),
         scratch_shapes=list(scratch),
-        compiler_params=pltpu.CompilerParams(vmem_limit_bytes=28 * 2**20),
+        compiler_params=pltpu.CompilerParams(vmem_limit_bytes=room * 2**20),
         cost_estimate=pl.CostEstimate(flops=work, bytes_accessed=0, transcendentals=0),
     )(*operands)
 
@@ -469,6 +469,7 @@
             lambda *refs: prepare_weight(n, part, *refs),
             [shape((part, full))] * n,
             (attention_in, first_gain, second_gain),
+            room=56,
         ),
         "shard",
     )
@@ -499,6 +500,7 @@
         "ss",
         [pltpu.VMEM((group, width), bf16), pltpu.VMEM((group, group), f32)],
         work=10 * micro,
+        room=56,
     )
     tokens_all, weight, projected, weights, gain_one, gain_two, mixed = answers[:7]
     mixed_mine, pair_up, pair_down, pair_out = lax.optimization_barrier(

time: 175 us -> 173 us (0.989)
  local copies, waits for them, and re-layouts: 12.4 us -> 7.46 us
  Pallas kernels: 26.5 us -> 28.8 us
    unnamed x76, local copies, waits for them, and re-layouts: 10.4 us -> 5.52 us
    pallas_call x8, Pallas kernels: 26.5 us -> 28.8 us  [call(): pl.pallas_call(kernel, out_shape=out_shape, in_specs=in_specs, out_specs=...]
  transfers between devices with their start and end apart: 55 -> 55, of which waited for: 28 -> 28; matrix products, arithmetic and copies ran while one was open for 5% -> 6% of each run, Pallas kernels for 14% -> 16%
where the time goes in v12:
time: 173 us
  waiting for transfers between devices  70.6 us (41%)
  starting transfers between devices  51.2 us (30%)
  Pallas kernels  28.8 us (17%)
  other arithmetic  8.29 us (5%)
  local copies, waits for them, and re-layouts  7.46 us (4%)
  matrix products  4.85 us (3%)
    ppermute x55, waiting for transfers between devices, swap(): return lax.ppermute(value, axis, [(i, i ^ bit) for i in range(size)])  70.6 us
    ppermute x55, starting transfers between devices, swap(): return lax.ppermute(value, axis, [(i, i ^ bit) for i in range(size)])  51.2 us
    pallas_call x8, Pallas kernels, call(): pl.pallas_call(kernel, out_shape=out_shape, in_specs=in_specs, out_specs=...  28.8 us
    unnamed x76, local copies, waits for them, and re-layouts  5.52 us
  transfers between devices with their start and end apart: 55, of which 28 were waited for; matrix products, arithmetic and copies ran while one was open for 6% of the time, Pallas kernels for 16%

profile of v12, /device:TPU:0, one launch (start us, length us, event | category | flops | bytes accessed | tf_op | source)
XLA Modules:
  0.0 172.5 jit_solution(14491489561728750342)
XLA Ops:
  0.7 3.0 %collective-permute-start = (bf16[128,768]{1,0:T(8,128)(2,1)}, bf16[128,768]{1,0:T(8,128)(2,1)}, u32[]{:S(2)}, u32[]{:S(2)}) collective-permute-start(bf16[128,768]{1,0:T(8,128)(2,1)} %refs_2_.2), channel_id=1, source_target_pairs={{0,2},{1,3},{2,0},{3,1},{4,6},{5,7},{6,4},{7,5},{8,10},{9,11},{10,... | collective-permute-start | bytes 589832 | tf_op jit(solution)/shard_map/ppermute | solution.py:44
  3.7 2.5 %shard_map.195 = (bf16[192,640]{1,0:T(8,128)(2,1)}, bf16[192,640]{1,0:T(8,128)(2,1)}, bf16[192,640]{1,0:T(8,128)(2,1)}, bf16[192,640]{1,0:T(8,128)(2,1)}) custom-call(bf16[192,2304]{1,0:T(8,128)(2,1)} %refs_0_.2, bf16[192]{0:T(256)(128)(2,1)} %refs_1_.1, bf16[192]{0:T(256)(128)(2,1)} %refs_2_.1), custom_call_target="tpu_custom_call" | custom-call | tf_op jit(solution)/shard_map/pallas_call | solution.py:66
  12.5 3.3 %collective-permute-done.4.refs_8_ = bf16[192,640]{1,0:T(8,128)(2,1)S(1)} collective-permute-done((bf16[192,640]{1,0:T(8,128)(2,1)}, bf16[192,640]{1,0:T(8,128)(2,1)S(1)}, u32[]{:S(2)}, u32[]{:S(2)}) %collective-permute-start.4) | collective-permute-done | bytes 245792 | tf_op jit(solution)/shard_map/ppermute | solution.py:44
  15.8 3.3 %collective-permute-done.5.refs_9_ = bf16[192,640]{1,0:T(8,128)(2,1)S(1)} collective-permute-done((bf16[192,640]{1,0:T(8,128)(2,1)}, bf16[192,640]{1,0:T(8,128)(2,1)S(1)}, u32[]{:S(2)}, u32[]{:S(2)}) %collective-permute-start.5) | collective-permute-done | bytes 245792 | tf_op jit(solution)/shard_map/ppermute | solution.py:44
  21.0 7.1 %shard_map.196 = (bf16[4,128,768]{2,1,0:T(8,128)(2,1)}, bf16[768,640]{1,0:T(8,128)(2,1)}, bf16[512,576]{1,0:T(8,128)(2,1)}, bf16[3,512,512]{2,1,0:T(8,128)(2,1)}...) custom-call(s32[1,3]{1,0:T(1,128)} %refs_0_.3, ...), custom_call_target="tpu_custom_call" | custom-call | flops 10000000000 | tf_op jit(solution)/shard_map/pallas_call | solution.py:66
  30.6 2.1 %collective-permute-done.10 = bf16[128,192]{1,0:T(8,128)(2,1)S(1)} collective-permute-done((bf16[128,192]{1,0:T(8,128)(2,1)}, bf16[128,192]{1,0:T(8,128)(2,1)S(1)}, u32[]{:S(2)}, u32[]{:S(2)}) %collective-permute-start.10) | collective-permute-done | bytes 49184 | tf_op jit(solution)/shard_map/ppermute | solution.py:44
  37.6 3.5 %collective-permute-done.14 = bf16[80,768]{1,0:T(8,128)(2,1)S(1)} collective-permute-done((bf16[80,768]{1,0:T(8,128)(2,1)S(1)}, bf16[80,768]{1,0:T(8,128)(2,1)S(1)}, u32[]{:S(2)}, u32[]{:S(2)}) %collective-permute-start.14) | collective-permute-done | bytes 122912 | tf_op jit(solution)/shard_map/ppermute | solution.py:44
  45.3 2.6 %collective-permute-start.17 = (bf16[40,768]{1,0:T(8,128)(2,1)}, bf16[40,768]{1,0:T(8,128)(2,1)}, u32[]{:S(2)}, u32[]{:S(2)}) collective-permute-start(bf16[40,768]{1,0:T(8,128)(2,1)} %get-tuple-element.237), channel_id=1, source_target_pairs={{0,16},{4,20},{8,24},{12,28},{16,0},{20,4},{24,8},{28,12},{1,17},{... | collective-permute-start | bytes 184328 | tf_op jit(solution)/shard_map/ppermute | solution.py:44
  48.8 3.3 %collective-permute-done.17 = bf16[40,768]{1,0:T(8,128)(2,1)} collective-permute-done((bf16[40,768]{1,0:T(8,128)(2,1)}, bf16[40,768]{1,0:T(8,128)(2,1)}, u32[]{:S(2)}, u32[]{:S(2)}) %collective-permute-start.17) | collective-permute-done | bytes 61472 | tf_op jit(solution)/shard_map/ppermute | solution.py:44
  52.1 2.0 %collective-permute-done.18 = bf16[40,768]{1,0:T(8,128)(2,1)} collective-permute-done((bf16[40,768]{1,0:T(8,128)(2,1)S(1)}, bf16[40,768]{1,0:T(8,128)(2,1)}, u32[]{:S(2)}, u32[]{:S(2)}) %collective-permute-start.18) | collective-permute-done | bytes 61472 | tf_op jit(solution)/shard_map/ppermute | solution.py:44
  57.6 2.8 %collective-permute-start.23 = (bf16[40,768]{1,0:T(8,128)(2,1)S(1)}, bf16[40,768]{1,0:T(8,128)(2,1)S(1)}, u32[]{:S(2)}, u32[]{:S(2)}) collective-permute-start(bf16[40,768]{1,0:T(8,128)(2,1)S(1)} %get-tuple-element.247), channel_id=1, source_target_pairs={{0,24},{4,28},{8,16},{12,20},{16,8},{20,12},{24,0},{28,4},{1,25},{... | collective-permute-start | bytes 184328 | tf_op jit(solution)/shard_map/ppermute | solution.py:44
  61.2 2.4 %collective-permute-done.23 = bf16[40,768]{1,0:T(8,128)(2,1)S(1)} collective-permute-done((bf16[40,768]{1,0:T(8,128)(2,1)S(1)}, bf16[40,768]{1,0:T(8,128)(2,1)S(1)}, u32[]{:S(2)}, u32[]{:S(2)}) %collective-permute-start.23) | collective-permute-done | bytes 61472 | tf_op jit(solution)/shard_map/ppermute | solution.py:44
  68.6 2.4 %shard_map.197 = (bf16[2,320,768]{2,1,0:T(8,128)(2,1)S(1)}, bf16[2,320,768]{2,1,0:T(8,128)(2,1)S(1)}, f32[160,768]{1,0:T(8,128)S(1)}, bf16[160,768]{1,0:T(8,128)(2,1)S(1)}) custom-call(bf16[160,768]{1,0:T(8,128)(2,1)S(1)} %pad_maximum_fusion.1.refs_0_.own, bf16[160,768]{1,0:T(8,128)(2,1)S(1)} %collective-permute-done.19.refs_1_.came, ...), custom_call_target="tpu_custom_call" | custom-call | flops 6000000000 | tf_op jit(solution)/shard_map/pallas_call | solution.py:66
  72.1 2.1 %shard_map.198 = (bf16[2,320,768]{2,1,0:T(8,128)(2,1)S(1)}, f32[160,768]{1,0:T(8,128)S(1)}, bf16[160,768]{1,0:T(8,128)(2,1)S(1)}) custom-call(bf16[160,768]{1,0:T(8,128)(2,1)S(1)} %pad_maximum_fusion.2.refs_0_.own_grad, bf16[160,768]{1,0:T(8,128)(2,1)S(1)} %collective-permute-done.24.refs_1_.came_grad, bf16[1,768,768]{2,1,0:T(8,128)(2,1)S(1)} %copy-done.3, ...), custom_call_target="tpu_custom_call" | custom-call | flops 6000000000 | tf_op jit(solution)/shard_map/pallas_call | solution.py:66
  75.3 2.5 %collective-permute-done.20 = bf16[160,768]{1,0:T(8,128)(2,1)S(1)} collective-permute-done((bf16[160,768]{1,0:T(8,128)(2,1)S(1)}, bf16[160,768]{1,0:T(8,128)(2,1)S(1)}, u32[]{:S(2)}, u32[]{:S(2)}) %collective-permute-start.20) | collective-permute-done | bytes 245792 | tf_op jit(solution)/shard_map/ppermute | solution.py:44
  78.6 2.7 %collective-permute-start.27 = (bf16[40,768]{1,0:T(8,128)(2,1)S(1)}, bf16[40,768]{1,0:T(8,128)(2,1)S(1)}, u32[]{:S(2)}, u32[]{:S(2)}) collective-permute-start(bf16[40,768]{1,0:T(8,128)(2,1)S(1)} %get-tuple-element.243), channel_id=1, source_target_pairs={{0,16},{4,20},{8,24},{12,28},{16,0},{20,4},{24,8},{28,12},{1,17},{... | collective-permute-start | bytes 184328 | tf_op jit(solution)/shard_map/ppermute | solution.py:44
  83.6 2.3 %collective-permute-start.30 = (bf16[40,768]{1,0:T(8,128)(2,1)S(1)}, bf16[40,768]{1,0:T(8,128)(2,1)S(1)}, u32[]{:S(2)}, u32[]{:S(2)}) collective-permute-start(bf16[40,768]{1,0:T(8,128)(2,1)S(1)} %get-tuple-element.239), channel_id=1, source_target_pairs={{0,16},{4,20},{8,24},{12,28},{16,0},{20,4},{24,8},{28,12},{1,17},{... | collective-permute-start | bytes 184328 | tf_op jit(solution)/shard_map/ppermute | solution.py:44
  89.3 2.6 %collective-permute-done.31 = bf16[40,768]{1,0:T(8,128)(2,1)S(1)} collective-permute-done((bf16[40,768]{1,0:T(8,128)(2,1)S(1)}, bf16[40,768]{1,0:T(8,128)(2,1)S(1)}, u32[]{:S(2)}, u32[]{:S(2)}) %collective-permute-start.31) | collective-permute-done | bytes 61472 | tf_op jit(solution)/shard_map/ppermute | solution.py:44
  92.7 2.2 %shard_map.199 = (bf16[1,768,768]{2,1,0:T(8,128)(2,1)}, bf16[1,768,768]{2,1,0:T(8,128)(2,1)S(1)}) custom-call(bf16[160,768]{1,0:T(8,128)(2,1)S(1)} %pad_maximum_fusion.1.refs_0_.own, bf16[160,768]{1,0:T(8,128)(2,1)S(1)} %collective-permute-done.19.refs_1_.came, bf16[160,768]{1,0:T(8,128)(2,1)S(1)} %pad_maximum_fusion.2.refs_0_.own_grad, ...), custom_call_target="tpu_custom_call" | custom-call | flops 4000000000 | tf_op jit(solution)/shard_map/pallas_call | solution.py:66
  95.1 3.2 %collective-permute-done.32 = bf16[80,1536]{1,0:T(8,128)(2,1)S(1)} collective-permute-done((bf16[80,1536]{1,0:T(8,128)(2,1)S(1)}, bf16[80,1536]{1,0:T(8,128)(2,1)S(1)}, u32[]{:S(2)}, u32[]{:S(2)}) %collective-permute-start.32) | collective-permute-done | bytes 245792 | tf_op jit(solution)/shard_map/ppermute | solution.py:44
  102.5 4.3 %collective-permute-done.33.refs_11_ = bf16[128,768]{1,0:T(8,128)(2,1)S(1)} collective-permute-done((bf16[128,768]{1,0:T(8,128)(2,1)S(1)}, bf16[128,768]{1,0:T(8,128)(2,1)S(1)}, u32[]{:S(2)}, u32[]{:S(2)}) %collective-permute-start.33) | collective-permute-done | bytes 196640 | tf_op jit(solution)/shard_map/ppermute | solution.py:44
  108.8 5.7 %shard_map.200 = (bf16[2,5,24,640]{3,2,1,0:T(8,128)(2,1)S(1)}, bf16[2,5,24,640]{3,2,1,0:T(8,128)(2,1)S(1)}, bf16[2,5,24,640]{3,2,1,0:T(8,128)(2,1)S(1)}, bf16[2,...) custom-call(bf16[512,576]{1,0:T(8,128)(2,1)S(1)} %copy-done.19, ...), custom_call_target="tpu_custom_call" | custom-call | flops 8000000000 | tf_op jit(solution)/shard_map/pallas_call | solution.py:66
  119.0 6.1 %collective-permute-done.52 = bf16[128,768]{1,0:T(8,128)(2,1)S(1)} collective-permute-done((bf16[128,768]{1,0:T(8,128)(2,1)}, bf16[128,768]{1,0:T(8,128)(2,1)S(1)}, u32[]{:S(2)}, u32[]{:S(2)}) %collective-permute-start.52) | collective-permute-done | bytes 196640 | tf_op jit(solution)/shard_map/ppermute | solution.py:44
  128.2 5.6 %collective-permute-done.39 = bf16[2,5,24,640]{3,2,1,0:T(8,128)(2,1)S(1)} collective-permute-done((bf16[2,5,24,640]{3,2,1,0:T(8,128)(2,1)S(1)}, bf16[2,5,24,640]{3,2,1,0:T(8,128)(2,1)S(1)}, u32[]{:S(2)}, u32[]{:S(2)}) %collective-permute-start.39) | collective-permute-done | bytes 307232 | tf_op jit(solution)/shard_map/ppermute | solution.py:44
  134.0 4.8 %shard_map.201 = (f32[1,768,768]{2,1,0:T(8,128)}, f32[1,768,768]{2,1,0:T(8,128)}) custom-call(bf16[160,768]{1,0:T(8,128)(2,1)S(1)} %pad_maximum_fusion.1.refs_0_.own, bf16[160,768]{1,0:T(8,128)(2,1)S(1)} %collective-permute-done.19.refs_1_.came, bf16[160,768]{1,0:T(8,128)(2,1)S(1)} %pad_maximum_fusion.2.refs_0_.own_grad, bf16[160,768]{1,0:T(8,128)(2,1)S(1)} %copy-done.11, ...), custom_call_target="tpu_custom_call" | custom-call | flops 4000000000 | tf_op jit(solution)/shard_map/pallas_call | solution.py:66
  138.8 2.7 %collective-permute-done.42 = bf16[5,24,640]{2,1,0:T(8,128)(2,1)S(1)} collective-permute-done((bf16[5,24,640]{2,1,0:T(8,128)(2,1)S(1)}, bf16[5,24,640]{2,1,0:T(8,128)(2,1)S(1)}, u32[]{:S(2)}, u32[]{:S(2)}) %collective-permute-start.42) | collective-permute-done | bytes 153632 | tf_op jit(solution)/shard_map/ppermute | solution.py:44
  143.8 2.0 %collective-permute-done.44 = bf16[24,640]{1,0:T(8,128)(2,1)S(1)} collective-permute-done((bf16[24,640]{1,0:T(8,128)(2,1)S(1)}, bf16[24,640]{1,0:T(8,128)(2,1)S(1)}, u32[]{:S(2)}, u32[]{:S(2)}) %collective-permute-start.44) | collective-permute-done | bytes 30752 | tf_op jit(solution)/shard_map/ppermute | solution.py:44
  148.2 2.2 %collective-permute-start.46 = (bf16[5,24,640]{2,1,0:T(8,128)(2,1)S(1)}, bf16[5,24,640]{2,1,0:T(8,128)(2,1)S(1)}, u32[]{:S(2)}, u32[]{:S(2)}) collective-permute-start(bf16[5,24,640]{2,1,0:T(8,128)(2,1)S(1)} %slice_dynamic-update-slice_fusion.refs_0_), channel_id=1, source_target_pairs={{0,16},{4,20},{8,24},{12,28},{16,0},{20,4},{24,8},{28,12},{1,17},{... | collective-permute-start | bytes 460808 | tf_op jit(solution)/shard_map/ppermute | solution.py:44
  150.4 4.6 %collective-permute-done.47.refs_2_ = bf16[5,24,640]{2,1,0:T(8,128)(2,1)S(1)} collective-permute-done((bf16[5,24,640]{2,1,0:T(8,128)(2,1)S(1)}, bf16[5,24,640]{2,1,0:T(8,128)(2,1)S(1)}, u32[]{:S(2)}, u32[]{:S(2)}) %collective-permute-start.47) | collective-permute-done | bytes 153632 | tf_op jit(solution)/shard_map/ppermute | solution.py:44
  158.0 2.2 %collective-permute-done.49.refs_3_ = bf16[5,24,640]{2,1,0:T(8,128)(2,1)S(1)} collective-permute-done((bf16[5,24,640]{2,1,0:T(8,128)(2,1)S(1)}, bf16[5,24,640]{2,1,0:T(8,128)(2,1)S(1)}, u32[]{:S(2)}, u32[]{:S(2)}) %collective-permute-start.49) | collective-permute-done | bytes 153632 | tf_op jit(solution)/shard_map/ppermute | solution.py:44
  162.5 2.9 %collective-permute-done.50.refs_6_ = bf16[5,24,640]{2,1,0:T(8,128)(2,1)S(1)} collective-permute-done((bf16[5,24,640]{2,1,0:T(8,128)(2,1)S(1)}, bf16[5,24,640]{2,1,0:T(8,128)(2,1)S(1)}, u32[]{:S(2)}, u32[]{:S(2)}) %collective-permute-start.50) | collective-permute-done | bytes 153632 | tf_op jit(solution)/shard_map/ppermute | solution.py:44
  167.8 2.8 %collective-permute-done.54.refs_7_ = bf16[5,24,640]{2,1,0:T(8,128)(2,1)S(1)} collective-permute-done((bf16[5,24,640]{2,1,0:T(8,128)(2,1)S(1)}, bf16[5,24,640]{2,1,0:T(8,128)(2,1)S(1)}, u32[]{:S(2)}, u32[]{:S(2)}) %collective-permute-start.54) | collective-permute-done | bytes 153632 | tf_op jit(solution)/shard_map/ppermute | solution.py:44
  (228 shorter events, 67.2 us)
Async XLA Ops:
  0.7 8.7 %collective-permute-start = (bf16[128,768]{1,0:T(8,128)(2,1)}, bf16[128,768]{1,0:T(8,128)(2,1)}, u32[]{:S(2)}, u32[]{:S(2)}) collective-permute-start(bf16[128,768]{1,0:T(8,128)(2,1)} %refs_2_.2), channel_id=1, source_target_pairs={{0,2},{1,3},{2,0},{3,1},{4,6},{5,7},{6,4},{7,5},{8,10},{9,11},{10,... | collective-permute-start | bytes 589832 | tf_op jit(solution)/shard_map/ppermute | solution.py:44
  3.7 6.5 %collective-permute-start.1 = (bf16[128,768]{1,0:T(8,128)(2,1)}, bf16[128,768]{1,0:T(8,128)(2,1)S(1)}, u32[]{:S(2)}, u32[]{:S(2)}) collective-permute-start(bf16[128,768]{1,0:T(8,128)(2,1)} %refs_2_.2), channel_id=1, source_target_pairs={{0,1},{1,0},{2,3},{3,2},{4,5},{5,4},{6,7},{7,6},{8,9},{9,8},{10,11... | collective-permute-start | bytes 589832 | tf_op jit(solution)/shard_map/ppermute | solution.py:44
  6.7 9.0 %collective-permute-start.4 = (bf16[192,640]{1,0:T(8,128)(2,1)}, bf16[192,640]{1,0:T(8,128)(2,1)S(1)}, u32[]{:S(2)}, u32[]{:S(2)}) collective-permute-start(bf16[192,640]{1,0:T(8,128)(2,1)} %get-tuple-element.120), channel_id=1, source_target_pairs={{0,2},{1,3},{2,0},{3,1},{4,6},{5,7},{6,4},{7,5},{8,10},{9,11},{10,... | collective-permute-start | bytes 737288 | tf_op jit(solution)/shard_map/ppermute | solution.py:44
  6.8 12.3 %collective-permute-start.5 = (bf16[192,640]{1,0:T(8,128)(2,1)}, bf16[192,640]{1,0:T(8,128)(2,1)S(1)}, u32[]{:S(2)}, u32[]{:S(2)}) collective-permute-start(bf16[192,640]{1,0:T(8,128)(2,1)} %get-tuple-element.121), channel_id=1, source_target_pairs={{0,3},{1,2},{2,1},{3,0},{4,7},{5,6},{6,5},{7,4},{8,11},{9,10},{10,... | collective-permute-start | bytes 737288 | tf_op jit(solution)/shard_map/ppermute | solution.py:44
  9.3 18.7 %collective-permute-start.6 = (bf16[1,768,768]{2,1,0:T(8,128)(2,1)}, bf16[1,768,768]{2,1,0:T(8,128)(2,1)S(1)}, u32[]{:S(2)}, u32[]{:S(2)}) collective-permute-start(bf16[1,768,768]{2,1,0:T(8,128)(2,1)} %refs_2_.4), channel_id=1, source_target_pairs={{0,1},{1,0},{2,3},{3,2},{4,5},{5,4},{6,7},{7,6},{8,9},{9,8},{10,11... | collective-permute-start | bytes 3538952 | tf_op jit(solution)/shard_map/ppermute | solution.py:44
  10.1 18.0 %collective-permute-start.7 = (bf16[1,768,768]{2,1,0:T(8,128)(2,1)}, bf16[1,768,768]{2,1,0:T(8,128)(2,1)S(1)}, u32[]{:S(2)}, u32[]{:S(2)}) collective-permute-start(bf16[1,768,768]{2,1,0:T(8,128)(2,1)} %refs_4_.1), channel_id=1, source_target_pairs={{0,1},{1,0},{2,3},{3,2},{4,5},{5,4},{6,7},{7,6},{8,9},{9,8},{10,11... | collective-permute-start | bytes 3538952 | tf_op jit(solution)/shard_map/ppermute | solution.py:44
  11.7 7.4 %collective-permute-start.2 = (bf16[128,768]{1,0:T(8,128)(2,1)}, bf16[128,768]{1,0:T(8,128)(2,1)S(1)}, u32[]{:S(2)}, u32[]{:S(2)}) collective-permute-start(bf16[128,768]{1,0:T(8,128)(2,1)} %collective-permute-done.refs_4_), channel_id=1, source_target_pairs={{0,1},{1,0},{2,3},{3,2},{4,5},{5,4},{6,7},{7,6},{8,9},{9,8},{10,11... | collective-permute-start | bytes 589832 | tf_op jit(solution)/shard_map/ppermute | solution.py:44
  19.1 8.9 %collective-permute-start.8 = (bf16[192,768]{1,0:T(8,128)(2,1)}, bf16[192,768]{1,0:T(8,128)(2,1)S(1)}, u32[]{:S(2)}, u32[]{:S(2)}) collective-permute-start(bf16[192,768]{1,0:T(8,128)(2,1)} %refs_6_), channel_id=1, source_target_pairs={{0,1},{1,0},{2,3},{3,2},{4,5},{5,4},{6,7},{7,6},{8,9},{9,8},{10,11... | collective-permute-start | bytes 884744 | tf_op jit(solution)/shard_map/ppermute | solution.py:44
  20.0 9.4 %collective-permute-start.11 = (bf16[192,768]{1,0:T(8,128)(2,1)}, bf16[192,768]{1,0:T(8,128)(2,1)S(1)}, u32[]{:S(2)}, u32[]{:S(2)}) collective-permute-start(bf16[192,768]{1,0:T(8,128)(2,1)} %refs_6_), channel_id=1, source_target_pairs={{0,2},{1,3},{2,0},{3,1},{4,6},{5,7},{6,4},{7,5},{8,10},{9,11},{10,... | collective-permute-start | bytes 884744 | tf_op jit(solution)/shard_map/ppermute | solution.py:44
  41.1 7.0 %collective-permute-start.15 = (bf16[80,768]{1,0:T(8,128)(2,1)S(1)}, bf16[80,768]{1,0:T(8,128)(2,1)S(1)}, u32[]{:S(2)}, u32[]{:S(2)}) collective-permute-start(bf16[80,768]{1,0:T(8,128)(2,1)S(1)} %convolution_convert_fusion.1), channel_id=1, source_target_pairs={{0,4},{4,0},{8,12},{12,8},{16,20},{20,16},{24,28},{28,24},{1,5},{5... | collective-permute-start | bytes 368648 | tf_op jit(solution)/shard_map/ppermute | solution.py:44
  45.3 6.8 %collective-permute-start.17 = (bf16[40,768]{1,0:T(8,128)(2,1)}, bf16[40,768]{1,0:T(8,128)(2,1)}, u32[]{:S(2)}, u32[]{:S(2)}) collective-permute-start(bf16[40,768]{1,0:T(8,128)(2,1)} %get-tuple-element.237), channel_id=1, source_target_pairs={{0,16},{4,20},{8,24},{12,28},{16,0},{20,4},{24,8},{28,12},{1,17},{... | collective-permute-start | bytes 184328 | tf_op jit(solution)/shard_map/ppermute | solution.py:44
  47.9 6.1 %collective-permute-start.18 = (bf16[40,768]{1,0:T(8,128)(2,1)S(1)}, bf16[40,768]{1,0:T(8,128)(2,1)}, u32[]{:S(2)}, u32[]{:S(2)}) collective-permute-start(bf16[40,768]{1,0:T(8,128)(2,1)S(1)} %get-tuple-element.236), channel_id=1, source_target_pairs={{0,24},{4,28},{8,16},{12,20},{16,8},{20,12},{24,0},{28,4},{1,25},{... | collective-permute-start | bytes 184328 | tf_op jit(solution)/shard_map/ppermute | solution.py:44
  54.9 9.9 %collective-permute-start.19 = (bf16[160,768]{1,0:T(8,128)(2,1)S(1)}, bf16[160,768]{1,0:T(8,128)(2,1)S(1)}, u32[]{:S(2)}, u32[]{:S(2)}) collective-permute-start(bf16[160,768]{1,0:T(8,128)(2,1)S(1)} %pad_maximum_fusion.1.refs_0_.own), channel_id=1, source_target_pairs={{0,2},{1,3},{2,0},{3,1},{4,6},{5,7},{6,4},{7,5},{8,10},{9,11},{10,... | collective-permute-start | bytes 737288 | tf_op jit(solution)/shard_map/ppermute | solution.py:44
  57.6 6.1 %collective-permute-start.23 = (bf16[40,768]{1,0:T(8,128)(2,1)S(1)}, bf16[40,768]{1,0:T(8,128)(2,1)S(1)}, u32[]{:S(2)}, u32[]{:S(2)}) collective-permute-start(bf16[40,768]{1,0:T(8,128)(2,1)S(1)} %get-tuple-element.247), channel_id=1, source_target_pairs={{0,24},{4,28},{8,16},{12,20},{16,8},{20,12},{24,0},{28,4},{1,25},{... | collective-permute-start | bytes 184328 | tf_op jit(solution)/shard_map/ppermute | solution.py:44
  63.7 8.4 %collective-permute-start.24 = (bf16[160,768]{1,0:T(8,128)(2,1)S(1)}, bf16[160,768]{1,0:T(8,128)(2,1)S(1)}, u32[]{:S(2)}, u32[]{:S(2)}) collective-permute-start(bf16[160,768]{1,0:T(8,128)(2,1)S(1)} %pad_maximum_fusion.2.refs_0_.own_grad), channel_id=1, source_target_pairs={{0,2},{1,3},{2,0},{3,1},{4,6},{5,7},{6,4},{7,5},{8,10},{9,11},{10,... | collective-permute-start | bytes 737288 | tf_op jit(solution)/shard_map/ppermute | solution.py:44
  71.0 6.8 %collective-permute-start.20 = (bf16[160,768]{1,0:T(8,128)(2,1)S(1)}, bf16[160,768]{1,0:T(8,128)(2,1)S(1)}, u32[]{:S(2)}, u32[]{:S(2)}) collective-permute-start(bf16[160,768]{1,0:T(8,128)(2,1)S(1)} %get-tuple-element.149), channel_id=1, source_target_pairs={{0,2},{1,3},{2,0},{3,1},{4,6},{5,7},{6,4},{7,5},{8,10},{9,11},{10,... | collective-permute-start | bytes 737288 | tf_op jit(solution)/shard_map/ppermute | solution.py:44
  74.2 8.2 %collective-permute-start.25 = (bf16[160,768]{1,0:T(8,128)(2,1)S(1)}, bf16[160,768]{1,0:T(8,128)(2,1)S(1)}, u32[]{:S(2)}, u32[]{:S(2)}) collective-permute-start(bf16[160,768]{1,0:T(8,128)(2,1)S(1)} %get-tuple-element.152), channel_id=1, source_target_pairs={{0,2},{1,3},{2,0},{3,1},{4,6},{5,7},{6,4},{7,5},{8,10},{9,11},{10,... | collective-permute-start | bytes 737288 | tf_op jit(solution)/shard_map/ppermute | solution.py:44
  78.6 8.3 %collective-permute-start.27 = (bf16[40,768]{1,0:T(8,128)(2,1)S(1)}, bf16[40,768]{1,0:T(8,128)(2,1)S(1)}, u32[]{:S(2)}, u32[]{:S(2)}) collective-permute-start(bf16[40,768]{1,0:T(8,128)(2,1)S(1)} %get-tuple-element.243), channel_id=1, source_target_pairs={{0,16},{4,20},{8,24},{12,28},{16,0},{20,4},{24,8},{28,12},{1,17},{... | collective-permute-start | bytes 184328 | tf_op jit(solution)/shard_map/ppermute | solution.py:44
  81.3 6.1 %collective-permute-start.28 = (bf16[40,768]{1,0:T(8,128)(2,1)S(1)}, bf16[40,768]{1,0:T(8,128)(2,1)S(1)}, u32[]{:S(2)}, u32[]{:S(2)}) collective-permute-start(bf16[40,768]{1,0:T(8,128)(2,1)S(1)} %get-tuple-element.242), channel_id=1, source_target_pairs={{0,24},{4,28},{8,16},{12,20},{16,8},{20,12},{24,0},{28,4},{1,25},{... | collective-permute-start | bytes 184328 | tf_op jit(solution)/shard_map/ppermute | solution.py:44
  92.1 6.3 %collective-permute-start.32 = (bf16[80,1536]{1,0:T(8,128)(2,1)S(1)}, bf16[80,1536]{1,0:T(8,128)(2,1)S(1)}, u32[]{:S(2)}, u32[]{:S(2)}) collective-permute-start(bf16[80,1536]{1,0:T(8,128)(2,1)S(1)} %maximum_maximum_fusion), channel_id=1, source_target_pairs={{0,4},{4,0},{8,12},{12,8},{16,20},{20,16},{24,28},{28,24},{1,5},{5... | collective-permute-start | bytes 737288 | tf_op jit(solution)/shard_map/ppermute | solution.py:44
  108.3 16.8 %collective-permute-start.37 = (bf16[1,768,768]{2,1,0:T(8,128)(2,1)}, bf16[1,768,768]{2,1,0:T(8,128)(2,1)}, u32[]{:S(2)}, u32[]{:S(2)}) collective-permute-start(bf16[1,768,768]{2,1,0:T(8,128)(2,1)} %get-tuple-element.190), channel_id=1, source_target_pairs={{0,1},{1,0},{2,3},{3,2},{4,5},{5,4},{6,7},{7,6},{8,9},{9,8},{10,11... | collective-permute-start | bytes 3538952 | tf_op jit(solution)/shard_map/ppermute | solution.py:44
  108.4 16.7 %collective-permute-start.38 = (bf16[1,768,768]{2,1,0:T(8,128)(2,1)S(1)}, bf16[1,768,768]{2,1,0:T(8,128)(2,1)}, u32[]{:S(2)}, u32[]{:S(2)}) collective-permute-start(bf16[1,768,768]{2,1,0:T(8,128)(2,1)S(1)} %get-tuple-element.191), channel_id=1, source_target_pairs={{0,1},{1,0},{2,3},{3,2},{4,5},{5,4},{6,7},{7,6},{8,9},{9,8},{10,11... | collective-permute-start | bytes 3538952 | tf_op jit(solution)/shard_map/ppermute | solution.py:44
  114.7 10.4 %collective-permute-start.36 = (bf16[2,5,24,640]{3,2,1,0:T(8,128)(2,1)S(1)}, bf16[2,5,24,640]{3,2,1,0:T(8,128)(2,1)}, u32[]{:S(2)}, u32[]{:S(2)}) collective-permute-start(bf16[2,5,24,640]{3,2,1,0:T(8,128)(2,1)S(1)} %get-tuple-element.188), channel_id=1, source_target_pairs={{0,4},{4,0},{8,12},{12,8},{16,20},{20,16},{24,28},{28,24},{1,5},{5... | collective-permute-start | bytes 921608 | tf_op jit(solution)/shard_map/ppermute | solution.py:44
  118.0 7.2 %collective-permute-start.52 = (bf16[128,768]{1,0:T(8,128)(2,1)}, bf16[128,768]{1,0:T(8,128)(2,1)S(1)}, u32[]{:S(2)}, u32[]{:S(2)}) collective-permute-start(bf16[128,768]{1,0:T(8,128)(2,1)} %fusion.33), channel_id=1, source_target_pairs={{0,2},{1,3},{2,0},{3,1},{4,6},{5,7},{6,4},{7,5},{8,10},{9,11},{10,... | collective-permute-start | bytes 589832 | tf_op jit(solution)/shard_map/ppermute | solution.py:44
  125.2 8.6 %collective-permute-start.39 = (bf16[2,5,24,640]{3,2,1,0:T(8,128)(2,1)S(1)}, bf16[2,5,24,640]{3,2,1,0:T(8,128)(2,1)S(1)}, u32[]{:S(2)}, u32[]{:S(2)}) collective-permute-start(bf16[2,5,24,640]{3,2,1,0:T(8,128)(2,1)S(1)} %get-tuple-element.192), channel_id=1, source_target_pairs={{0,4},{4,0},{8,12},{12,8},{16,20},{20,16},{24,28},{28,24},{1,5},{5... | collective-permute-start | bytes 921608 | tf_op jit(solution)/shard_map/ppermute | solution.py:44
  127.0 11.8 %collective-permute-start.40 = (bf16[5,24,640]{2,1,0:T(8,128)(2,1)S(1)}, bf16[5,24,640]{2,1,0:T(8,128)(2,1)S(1)}, u32[]{:S(2)}, u32[]{:S(2)}) collective-permute-start(bf16[5,24,640]{2,1,0:T(8,128)(2,1)S(1)} %get-tuple-element.233), channel_id=1, source_target_pairs={{0,16},{4,20},{8,24},{12,28},{16,0},{20,4},{24,8},{28,12},{1,17},{... | collective-permute-start | bytes 460808 | tf_op jit(solution)/shard_map/ppermute | solution.py:44
  127.1 11.7 %collective-permute-start.41 = (bf16[5,24,640]{2,1,0:T(8,128)(2,1)S(1)}, bf16[5,24,640]{2,1,0:T(8,128)(2,1)S(1)}, u32[]{:S(2)}, u32[]{:S(2)}) collective-permute-start(bf16[5,24,640]{2,1,0:T(8,128)(2,1)S(1)} %get-tuple-element.232), channel_id=1, source_target_pairs={{0,24},{4,28},{8,16},{12,20},{16,8},{20,12},{24,0},{28,4},{1,25},{... | collective-permute-start | bytes 460808 | tf_op jit(solution)/shard_map/ppermute | solution.py:44
  133.9 7.6 %collective-permute-start.42 = (bf16[5,24,640]{2,1,0:T(8,128)(2,1)S(1)}, bf16[5,24,640]{2,1,0:T(8,128)(2,1)S(1)}, u32[]{:S(2)}, u32[]{:S(2)}) collective-permute-start(bf16[5,24,640]{2,1,0:T(8,128)(2,1)S(1)} %fusion.34), channel_id=1, source_target_pairs={{0,8},{4,12},{8,0},{12,4},{16,24},{20,28},{24,16},{28,20},{1,9},{5... | collective-permute-start | bytes 460808 | tf_op jit(solution)/shard_map/ppermute | solution.py:44
  146.4 8.6 %collective-permute-start.47 = (bf16[5,24,640]{2,1,0:T(8,128)(2,1)S(1)}, bf16[5,24,640]{2,1,0:T(8,128)(2,1)S(1)}, u32[]{:S(2)}, u32[]{:S(2)}) collective-permute-start(bf16[5,24,640]{2,1,0:T(8,128)(2,1)S(1)} %slice_dynamic-update-slice_fusion.refs_0_), channel_id=1, source_target_pairs={{0,8},{4,12},{8,0},{12,4},{16,24},{20,28},{24,16},{28,20},{1,9},{5... | collective-permute-start | bytes 460808 | tf_op jit(solution)/shard_map/ppermute | solution.py:44
  147.1 7.9 %collective-permute-start.48 = (bf16[5,24,640]{2,1,0:T(8,128)(2,1)S(1)}, bf16[5,24,640]{2,1,0:T(8,128)(2,1)S(1)}, u32[]{:S(2)}, u32[]{:S(2)}) collective-permute-start(bf16[5,24,640]{2,1,0:T(8,128)(2,1)S(1)} %slice_dynamic-update-slice_fusion.refs_0_), channel_id=1, source_target_pairs={{0,4},{4,0},{8,12},{12,8},{16,20},{20,16},{24,28},{28,24},{1,5},{5... | collective-permute-start | bytes 460808 | tf_op jit(solution)/shard_map/ppermute | solution.py:44
  148.2 9.8 %collective-permute-start.46 = (bf16[5,24,640]{2,1,0:T(8,128)(2,1)S(1)}, bf16[5,24,640]{2,1,0:T(8,128)(2,1)S(1)}, u32[]{:S(2)}, u32[]{:S(2)}) collective-permute-start(bf16[5,24,640]{2,1,0:T(8,128)(2,1)S(1)} %slice_dynamic-update-slice_fusion.refs_0_), channel_id=1, source_target_pairs={{0,16},{4,20},{8,24},{12,28},{16,0},{20,4},{24,8},{28,12},{1,17},{... | collective-permute-start | bytes 460808 | tf_op jit(solution)/shard_map/ppermute | solution.py:44
  161.1 6.7 %collective-permute-start.53 = (bf16[5,24,640]{2,1,0:T(8,128)(2,1)S(1)}, bf16[5,24,640]{2,1,0:T(8,128)(2,1)S(1)}, u32[]{:S(2)}, u32[]{:S(2)}) collective-permute-start(bf16[5,24,640]{2,1,0:T(8,128)(2,1)S(1)} %collective-permute-done.46.refs_4_), channel_id=1, source_target_pairs={{0,4},{4,0},{8,12},{12,8},{16,20},{20,16},{24,28},{28,24},{1,5},{5... | collective-permute-start | bytes 460808 | tf_op jit(solution)/shard_map/ppermute | solution.py:44
  (61 other events, 378.5 us)
